TPU v7x, 32 devices: a whole 2x2x4 slice. The times are simulated.
32 devices in a mesh: section: 4 (over z), dp: 4 (over y, x), tensor: 2 (over core).
Axes of the slice: x: 2, y: 2, z: 4, core: 2. Of those that a mesh axis runs over, the one named last changes fastest.
Arguments:
- tokens: bfloat16 [4, 512, 4096], P('section', 'dp', 'tensor'), may hold values from -6 to 6
- lengths: int32 [4, 4], P(None, 'dp'), may hold values from 16 to 128, as said below
- w_query: bfloat16 [4, 4096, 256], P('section', None, 'tensor')
- w_key: bfloat16 [4, 4096, 256], P('section', None, 'tensor')
- w_value: bfloat16 [4, 4096, 256], P('section', None, 'tensor'), may hold values from -0.09375 to 0.09375
- w_out: bfloat16 [4, 256, 4096], P('section', 'tensor'), may hold values from -0.375 to 0.375
- w_embed: bfloat16 [4096, 1024], P('tensor'), may hold values from -0.09375 to 0.09375
Outputs:
- penalty_grad: float32 [4, 512, 1024], P('section', 'dp', 'tensor')
Inputs may be any that keep to these rules, and one draw needn't show every extreme that they name: `lengths`: every length is at least 16; at least one length equals 128.
All inputs are finite; a program needn't handle non-finite values.
Results may differ from a plain program's by a relative error of at most 0.02.
Values may be sent and summed in bfloat16 or wider, within the bound.
No kernel may reach another device: no remote copies, remote signals or barrier semaphores. Data moves between devices by JAX's collectives and lax.ppermute only.
A program may use at most 64 MiB of HBM per device.

v0:
```python
import math

import jax
import jax.numpy as jnp
from jax import lax
from jax.sharding import PartitionSpec as P

HD = 128
HOPS = 2


EPSILON = 1e-05


def shifted(value, axis, steps):
    count = lax.axis_size(axis)
    pairs = [(source, (source + steps) % count) for source in range(count)]
    return lax.ppermute(value, axis, pairs)


def attend(features, w_query, w_key, w_value, w_out, live_len):
    seq_rows = features.shape[0]
    local_heads = w_query.shape[1] // HD
    values32 = features.astype(jnp.float32)
    normed = (
        values32 * lax.rsqrt(jnp.mean(values32 * values32, axis=-1, keepdims=True) + EPSILON)
    ).astype(jnp.bfloat16)
    query_rows = jnp.dot(normed, w_query, preferred_element_type=jnp.float32).astype(jnp.bfloat16)
    key_rows = jnp.dot(normed, w_key, preferred_element_type=jnp.float32).astype(jnp.bfloat16)
    value_rows = jnp.dot(normed, w_value, preferred_element_type=jnp.float32).astype(jnp.bfloat16)
    query_h = query_rows.reshape(seq_rows, local_heads, HD)
    key_h = key_rows.reshape(seq_rows, local_heads, HD)
    value_h = value_rows.reshape(seq_rows, local_heads, HD)
    scores = jnp.einsum("qhd,khd->hqk", query_h, key_h, preferred_element_type=jnp.float32) * (
        1.0 / math.sqrt(HD)
    )
    key_mask = lax.broadcasted_iota(jnp.int32, (1, 1, seq_rows), 2) < live_len
    scores = jnp.where(key_mask, scores, -1e30)
    row_max = jnp.max(scores, axis=-1, keepdims=True)
    exp_scores = jnp.exp(scores - row_max)
    attn_probs = (exp_scores / jnp.sum(exp_scores, axis=-1, keepdims=True)).astype(jnp.bfloat16)
    mixed = jnp.einsum(
        "hqk,khd->qhd", attn_probs, value_h, preferred_element_type=jnp.float32
    ).astype(jnp.bfloat16)
    mixed = mixed.reshape(seq_rows, local_heads * HD)
    return jnp.dot(mixed, w_out, preferred_element_type=jnp.float32)


def shards(tokens, lengths, w_query, w_key, w_value, w_out, w_embed):
    section_idx = lax.axis_index("section")
    section_count = lax.axis_size("section")
    core_idx = lax.axis_index("tensor")
    core_count = lax.axis_size("tensor")
    group_idx = lax.axis_index("dp")
    group_count = lax.axis_size("dp")
    per_section = lengths[:, 0]
    state = tokens[0]
    live_len = per_section[0]
    for hop in range(HOPS):
        if hop > 0:
            state = shifted(state, "section", 1)
        anchor = (section_idx - hop) % section_count
        live_len = lax.dynamic_index_in_dim(per_section, anchor, 0, keepdims=False)
        features = lax.all_gather(state, "tensor", axis=1, tiled=True)
        update = attend(features, w_query[0], w_key[0], w_value[0], w_out[0], live_len)
        summed = lax.psum_scatter(
            update.astype(jnp.bfloat16), "tensor", scatter_dimension=1, tiled=True
        ).astype(jnp.float32)
        state = (state.astype(jnp.float32) + summed).astype(jnp.bfloat16)
    seq_rows = state.shape[0]
    embed_part = jnp.dot(state, w_embed, preferred_element_type=jnp.float32)
    embed = lax.psum(embed_part.astype(jnp.bfloat16), "tensor")
    row_live = lax.broadcasted_iota(jnp.int32, (seq_rows, 1), 0) < live_len
    masked = jnp.where(row_live, embed, jnp.zeros_like(embed))
    embed_cols = masked.shape[1]
    half_cols = embed_cols // core_count
    col_start = core_idx * half_cols
    own_cols = lax.dynamic_slice_in_dim(masked, col_start, half_cols, 1)
    moment_part = lax.dot_general(
        masked, own_cols, (((0,), (0,)), ((), ())), preferred_element_type=jnp.float32
    ) / float(seq_rows * group_count)
    moment_block = lax.psum_scatter(
        moment_part.astype(jnp.bfloat16), "dp", scatter_dimension=0, tiled=True
    ).astype(jnp.float32)
    block_rows = moment_block.shape[0]
    row_ids = group_idx * block_rows + lax.broadcasted_iota(jnp.int32, (block_rows, half_cols), 0)
    col_ids = col_start + lax.broadcasted_iota(jnp.int32, (block_rows, half_cols), 1)
    penalty_rows = (moment_block - (row_ids == col_ids).astype(jnp.float32)).astype(jnp.bfloat16)
    result = jnp.dot(
        masked,
        lax.all_gather(penalty_rows, "dp", axis=0, tiled=True),
        preferred_element_type=jnp.float32,
    )
    return result[None]


def solution(mesh):
    return jax.shard_map(
        shards,
        mesh=mesh,
        in_specs=(
            P("section", "dp", "tensor"),
            P(None, "dp"),
            P("section", None, "tensor"),
            P("section", None, "tensor"),
            P("section", None, "tensor"),
            P("section", "tensor", None),
            P("tensor", None),
        ),
        out_specs=P("section", "dp", "tensor"),
        check_vma=False,
    )
```

profile of v0, /device:TPU:0, one launch (start us, length us, event | category | flops | bytes accessed | tf_op | source)
XLA Modules:
  0.0 175.2 jit_solution(7092905573895423525)
XLA Ops:
  6.5 0.0 copy-start
  6.5 0.0 copy-start.7
  6.5 0.0 all-gather.9.cloned.1.call-start
  6.5 0.7 all-gather.9.cloned.1.call-update
  7.3 0.0 reduce-scatter.4.cloned.1.call-start
  7.3 1.4 constant_dynamic-slice_fusion.1
  8.7 0.7 iota_compare_fusion
  9.4 11.2 %all-gather.9.cloned.1.call-done = bf16[1,128,4096]{2,1,0:T(8,128)(2,1)} async-done(((bf16[1,128,2048]{2,1,0:T(8,128)(2,1)}), bf16[1,128,4096]{2,1,0:T(8,128)(2,1)}) %all-gather.9.cloned.1.call-update) | async-done | bytes 1048592 | tf_op jit(solution)/shard_map/all_gather | solution.py:64
  20.7 0.0 copy-start.4
  20.7 1.6 fusion.2
  22.3 2.0 %convolution_convert_fusion.8 = bf16[128,128]{1,0:T(8,128)(2,1)S(1)} fusion(bf16[1,4096,128]{2,1,0:T(8,128)(2,1)} %param.10, bf16[1,128,4096]{2,1,0:T(8,128)(2,1)} %all-gather.9.cloned.1.call-done, f32[128]{0:T(128)S(1)} %add_rsqrt_fusion.1), kind=kOutput, calls=%fused_computation.22 | convolution fusion | flops 135806976 | bytes 2130432 | tf_op jit(solution)/shard_map/dot_general | solution.py:29
  24.3 0.0 copy-done.7
  24.4 0.0 copy-done.4
  24.4 0.7 fusion.39
  25.1 1.9 %fusion.6 = bf16[128,128]{0,1:T(8,128)(2,1)S(1)} fusion(bf16[1,4096,128]{2,1,0:T(8,128)(2,1)} %param.11, f32[128,128]{0,1:T(8,128)S(1)} %get-tuple-element.8, f32[128]{0:T(128)S(1)} %fusion.22, f32[128]{0:T(128)S(1)} %get-tuple-element.7, bf16[1,128,4096]{2,1,0:T(8,128)(2,1)S(1)} %copy-done.4, f32[128]{0:T(128)S(1)} %add_rsqrt_fusion.1), kind=kOutput, calls=%fused_computation.25 | convolution fusion | flops 140066816 | bytes 2196992 | tf_op jit(solution)/shard_map/hqk,khd->qhd/dot_general | solution.py:42
  26.9 0.0 copy-done
  27.0 0.0 copy-start.1
  27.0 1.4 convolution_convert_fusion.1
  28.4 0.0 copy-start.6
  28.4 0.0 reduce-scatter.4.cloned.1.call-update
  28.4 0.0 all-gather.5.cloned.1.call-start
  28.5 9.8 %reduce-scatter.4.cloned.1.call-done = bf16[128,2048]{1,0:T(8,128)(2,1)} async-done(((bf16[128,4096]{1,0:T(8,128)(2,1)}), bf16[128,2048]{1,0:T(8,128)(2,1)}) %reduce-scatter.4.cloned.1.call-update) | async-done | bytes 524304 | tf_op jit(solution)/shard_map/reduce_scatter | solution.py:66
  38.3 0.0 copy-done.1
  38.3 1.2 fusion.8
  39.4 1.8 %collective-permute-start = (bf16[128,2048]{1,0:T(8,128)(2,1)S(1)}, bf16[128,2048]{1,0:T(8,128)(2,1)S(1)}, u32[]{:S(2)}, u32[]{:S(2)}) collective-permute-start(bf16[128,2048]{1,0:T(8,128)(2,1)S(1)} %fusion.8), channel_id=1, source_target_pairs={{0,8},{8,16},{16,24},{24,0},{1,9},{9,17},{17,25},{25,1},{2,10},{10... | collective-permute-start | bytes 1572872 | tf_op jit(solution)/shard_map/ppermute | solution.py:18
  41.2 14.2 %collective-permute-done = bf16[128,2048]{1,0:T(8,128)(2,1)S(1)} collective-permute-done((bf16[128,2048]{1,0:T(8,128)(2,1)S(1)}, bf16[128,2048]{1,0:T(8,128)(2,1)S(1)}, u32[]{:S(2)}, u32[]{:S(2)}) %collective-permute-start) | collective-permute-done | bytes 524320 | tf_op jit(solution)/shard_map/ppermute | solution.py:18
  55.5 0.0 copy-start.2
  55.5 0.8 copy-done.2
  56.3 0.0 all-gather.5.cloned.1.call-update
  56.3 0.0 reduce-scatter.6.cloned.1.call-start
  56.3 0.7 iota_compare_fusion.1
  57.0 7.8 %all-gather.5.cloned.1.call-done = bf16[128,4096]{1,0:T(8,128)(2,1)} async-done(((bf16[128,2048]{1,0:T(8,128)(2,1)}), bf16[128,4096]{1,0:T(8,128)(2,1)}) %all-gather.5.cloned.1.call-update) | async-done | bytes 1048592 | tf_op jit(solution)/shard_map/all_gather | solution.py:64
  64.8 0.0 copy-start.5
  64.8 1.6 fusion
  66.4 0.0 copy-done.6
  66.4 1.7 convolution_convert_fusion.4
  68.2 0.0 copy-done.5
  68.2 0.0 copy-start.8
  68.2 1.9 %fusion.44 = (f32[128]{0:T(128)S(1)}, f32[128,128]{0,1:T(8,128)S(1)}) fusion(bf16[128,128]{1,0:T(8,128)(2,1)S(1)} %convolution_convert_fusion.4, bf16[1,4096,128]{2,1,0:T(8,128)(2,1)} %param.9, bf16[128,4096]{1,0:T(8,128)(2,1)S(1)} %copy-done.5, f32[128]{0:T(128)S(1)} %add_rsqrt_fusion, pred[128]{0:T(512)(128)(4,1)S(1)} %iota_compare_fusion.1), kind=kOutput, calls=%fused_computation.61 | convolution fusion | flops 140050304 | bytes 2196608 | tf_op jit(solution)/shard_map/qhd,khd->hqk/dot_general | solution.py:34
  70.2 0.0 copy-done.8
  70.2 0.7 fusion.7
  70.9 0.0 copy-start.3
  70.9 1.4 convolution_convert_fusion
  72.3 0.0 reduce-scatter.6.cloned.1.call-update
  72.3 0.0 all-reduce.2.cloned.1.call-start
  72.4 9.8 %reduce-scatter.6.cloned.1.call-done = bf16[128,2048]{1,0:T(8,128)(2,1)} async-done(((bf16[128,4096]{1,0:T(8,128)(2,1)}), bf16[128,2048]{1,0:T(8,128)(2,1)}) %reduce-scatter.6.cloned.1.call-update) | async-done | bytes 524304 | tf_op jit(solution)/shard_map/reduce_scatter | solution.py:66
  82.2 0.0 copy-done.3
  82.2 3.8 %convolution_convert_fusion.2 = bf16[128,1024]{1,0:T(8,128)(2,1)} fusion(bf16[2048,1024]{1,0:T(8,128)(2,1)} %param.13, bf16[128,2048]{1,0:T(8,128)(2,1)} %reduce-scatter.6.cloned.1.call-done, bf16[128,2048]{1,0:T(8,128)(2,1)S(1)} %copy-done.3), kind=kOutput, calls=%fused_computation.11 | convolution fusion | flops 538050560 | bytes 5505024 | tf_op jit(solution)/shard_map/dot_general | solution.py:71
  86.0 0.0 all-reduce.2.cloned.1.call-update
  86.0 0.0 reduce-scatter.8.cloned.1.call-start
  86.0 19.5 %all-reduce.2.cloned.1.call-done = bf16[128,1024]{1,0:T(8,128)(2,1)} async-done(((bf16[128,1024]{1,0:T(8,128)(2,1)}), bf16[128,1024]{1,0:T(8,128)(2,1)}) %all-reduce.2.cloned.1.call-update) | async-done | bytes 262160 | tf_op jit(solution)/shard_map/psum | solution.py:72
  105.6 1.0 broadcast_select_fusion
  106.6 1.4 multiply_convert_fusion
  108.0 0.0 reduce-scatter.8.cloned.1.call-update
  108.1 0.0 all-gather.7.cloned.1.call-start
  108.1 29.4 %reduce-scatter.8.cloned.1.call-done = bf16[256,512]{1,0:T(8,128)(2,1)} async-done(((bf16[1024,512]{1,0:T(8,128)(2,1)}), bf16[256,512]{1,0:T(8,128)(2,1)}) %reduce-scatter.8.cloned.1.call-update) | async-done | bytes 262160 | tf_op jit(solution)/shard_map/reduce_scatter | solution.py:82
  137.5 1.8 %subtract_convert_fusion = bf16[256,512]{1,0:T(8,128)(2,1)} fusion(bf16[256,512]{1,0:T(8,128)(2,1)} %reduce-scatter.8.cloned.1.call-done, s32[512]{0:T(512)S(1)} %iota_add_fusion, s32[256]{0:T(256)S(1)} %iota_add_fusion.1), kind=kLoop, calls=%fused_computation.38 | loop fusion | flops 655360 | bytes 527360 | tf_op jit(solution)/shard_map/convert_element_type | solution.py:88
  139.3 0.0 all-gather.7.cloned.1.call-update
  139.3 26.8 %all-gather.7.cloned.1.call-done = bf16[1024,512]{1,0:T(8,128)(2,1)} async-done(((bf16[256,512]{1,0:T(8,128)(2,1)}), bf16[1024,512]{1,0:T(8,128)(2,1)}) %all-gather.7.cloned.1.call-update) | async-done | bytes 1048592 | tf_op jit(solution)/shard_map/all_gather | solution.py:91
  166.1 2.2 %convolution_bitcast_fusion = f32[1,128,512]{2,1,0:T(8,128)} fusion(bf16[128,1024]{1,0:T(8,128)(2,1)S(1)} %broadcast_select_fusion, bf16[1024,512]{1,0:T(8,128)(2,1)} %all-gather.7.cloned.1.call-done), kind=kOutput, calls=%fused_computation.12 | convolution fusion | flops 134217728 | bytes 1572864 | tf_op jit(solution)/shard_map/dot_general | solution.py:89
  (6 shorter events, 0.1 us)
Async XLA Ops:
  6.5 20.4 %copy-start = (bf16[1,128,4096]{2,1,0:T(8,128)(2,1)S(1)}, bf16[1,128,4096]{2,1,0:T(8,128)(2,1)}, u32[]{:S(2)}) copy-start(bf16[1,128,4096]{2,1,0:T(8,128)(2,1)} %param.12) | copy-start | bytes 3145732
  6.5 17.8 %copy-start.7 = (bf16[1,4096,128]{2,1,0:T(8,128)(2,1)S(1)}, bf16[1,4096,128]{2,1,0:T(8,128)(2,1)}, u32[]{:S(2)}) copy-start(bf16[1,4096,128]{2,1,0:T(8,128)(2,1)} %param.9) | copy-start | bytes 3145732
  6.5 14.1 %all-gather.9.cloned.1.call-start = ((), (), s32[]{:S(2)}) async-start(), calls=%async_computation.9 | async-start | bytes 1572864 | tf_op jit(solution)/shard_map/all_gather | solution.py:64
  7.3 31.0 %reduce-scatter.4.cloned.1.call-start = ((), (), s32[]{:S(2)}) async-start(), calls=%async_computation.3 | async-start | bytes 1572864 | tf_op jit(solution)/shard_map/reduce_scatter | solution.py:66
  20.7 3.7 %copy-start.4 = (bf16[1,128,4096]{2,1,0:T(8,128)(2,1)S(1)}, bf16[1,128,4096]{2,1,0:T(8,128)(2,1)}, u32[]{:S(2)}) copy-start(bf16[1,128,4096]{2,1,0:T(8,128)(2,1)} %all-gather.9.cloned.1.call-done) | copy-start | bytes 3145732
  27.0 11.3 %copy-start.1 = (bf16[1,128,2048]{2,1,0:T(8,128)(2,1)S(1)}, bf16[1,128,2048]{2,1,0:T(8,128)(2,1)}, u32[]{:S(2)}) copy-start(bf16[1,128,2048]{2,1,0:T(8,128)(2,1)} %param.7) | copy-start | bytes 1572868
  28.4 38.0 %copy-start.6 = (bf16[1,4096,128]{2,1,0:T(8,128)(2,1)S(1)}, bf16[1,4096,128]{2,1,0:T(8,128)(2,1)}, u32[]{:S(2)}) copy-start(bf16[1,4096,128]{2,1,0:T(8,128)(2,1)} %param.10) | copy-start | bytes 3145732
  28.4 36.4 %all-gather.5.cloned.1.call-start = ((), (), s32[]{:S(2)}) async-start(), calls=%async_computation.4 | async-start | bytes 1572864 | tf_op jit(solution)/shard_map/all_gather | solution.py:64
  39.4 16.0 %collective-permute-start = (bf16[128,2048]{1,0:T(8,128)(2,1)S(1)}, bf16[128,2048]{1,0:T(8,128)(2,1)S(1)}, u32[]{:S(2)}, u32[]{:S(2)}) collective-permute-start(bf16[128,2048]{1,0:T(8,128)(2,1)S(1)} %fusion.8), channel_id=1, source_target_pairs={{0,8},{8,16},{16,24},{24,0},{1,9},{9,17},{17,25},{25,1},{2,10},{10... | collective-permute-start | bytes 1572872 | tf_op jit(solution)/shard_map/ppermute | solution.py:18
  55.5 0.8 copy-start.2
  56.3 25.9 %reduce-scatter.6.cloned.1.call-start = ((), (), s32[]{:S(2)}) async-start(), calls=%async_computation.5 | async-start | bytes 1572864 | tf_op jit(solution)/shard_map/reduce_scatter | solution.py:66
  64.8 3.4 %copy-start.5 = (bf16[128,4096]{1,0:T(8,128)(2,1)S(1)}, bf16[128,4096]{1,0:T(8,128)(2,1)}, u32[]{:S(2)}) copy-start(bf16[128,4096]{1,0:T(8,128)(2,1)} %all-gather.5.cloned.1.call-done) | copy-start | bytes 3145732
  68.2 2.0 %copy-start.8 = (bf16[1,4096,128]{2,1,0:T(8,128)(2,1)S(1)}, bf16[1,4096,128]{2,1,0:T(8,128)(2,1)}, u32[]{:S(2)}) copy-start(bf16[1,4096,128]{2,1,0:T(8,128)(2,1)} %param.11) | copy-start | bytes 3145732
  70.9 11.3 %copy-start.3 = (bf16[128,2048]{1,0:T(8,128)(2,1)S(1)}, bf16[128,2048]{1,0:T(8,128)(2,1)}, u32[]{:S(2)}) copy-start(bf16[128,2048]{1,0:T(8,128)(2,1)} %copy-done.2) | copy-start | bytes 1572868
  72.3 33.2 %all-reduce.2.cloned.1.call-start = ((), (), s32[]{:S(2)}) async-start(), calls=%async_computation.6 | async-start | bytes 524288 | tf_op jit(solution)/shard_map/psum | solution.py:72
  86.0 51.5 %reduce-scatter.8.cloned.1.call-start = ((), (), s32[]{:S(2)}) async-start(), calls=%async_computation.7 | async-start | bytes 1310720 | tf_op jit(solution)/shard_map/reduce_scatter | solution.py:82
  108.1 58.0 %all-gather.7.cloned.1.call-start = ((), (), s32[]{:S(2)}) async-start(), calls=%async_computation.8 | async-start | bytes 1310720 | tf_op jit(solution)/shard_map/all_gather | solution.py:91
Sparse Core Ops, SparseCore 0:
  8.9 11.7 all-gather.8
  28.5 9.6 reduce-scatter.3
  56.4 8.3 all-gather.4
  72.4 9.6 reduce-scatter.5
  86.1 19.4 all-reduce.1
  108.6 28.8 reduce-scatter.7
  139.4 26.6 all-gather.6
where the time goes:
time: 176 us; the launch traced here: 175 us
  waiting for transfers between devices  129 us (73%)
  matrix products  19.2 us (11%)
  between operations  13.7 us (8%)
  other arithmetic  8.66 us (5%)
  local copies, waits for them, and re-layouts  2.24 us (1%)
  starting transfers between devices  2.04 us (1%)
    reduce_scatter x1, waiting for transfers between devices, shards(): lax.psum_scatter(moment_part.astype(jnp.bfloat16), 'dp', scatter_dimensio...  29.4 us
    all_gather x1, waiting for transfers between devices, shards(): lax.all_gather(penalty_rows, 'dp', axis=0, tiled=True)  26.8 us
    reduce_scatter x2, waiting for transfers between devices, shards(): lax.psum_scatter(update.astype(jnp.bfloat16), 'tensor', scatter_dimension...  19.6 us
    psum x1, waiting for transfers between devices, shards(): embed = lax.psum(embed_part.astype(jnp.bfloat16), 'tensor')  19.5 us
    all_gather x2, waiting for transfers between devices, shards(): features = lax.all_gather(state, 'tensor', axis=1, tiled=True)  19.1 us
    ppermute x1, waiting for transfers between devices, shifted(): return lax.ppermute(value, axis, pairs)  14.2 us
    dot_general x1, matrix products, shards(): embed_part = jnp.dot(state, w_embed, preferred_element_type=jnp.float32)  3.78 us
    dot_general x2, matrix products, attend(): jnp.dot(normed, w_key, preferred_element_type=jnp.float32)  3.77 us
  transfers between devices with their start and end apart: 8, of which 8 were waited for; matrix products, arithmetic and copies ran while one was open for 2% of the time, Pallas kernels for 0%

commit v1 on v0

v1 whole, which is shorter than its diff:
```python
import functools
import math

import jax
import jax.numpy as jnp
from jax import lax
from jax.experimental import pallas as pl
from jax.experimental.pallas import tpu as pltpu
from jax.sharding import PartitionSpec as P

HD = 128
HOPS = 2
EPSILON = 1e-05
BF16 = jnp.bfloat16
F32 = jnp.float32
VMEM_BYTES = 16 * 1024 * 1024


def shifted(value, axis, steps):
    count = lax.axis_size(axis)
    pairs = [(source, (source + steps) % count) for source in range(count)]
    return lax.ppermute(value, axis, pairs)


def exchanged(value, axis, mask):
    count = lax.axis_size(axis)
    return lax.ppermute(value, axis, [(source, source ^ mask) for source in range(count)])


def dot(left, right):
    return lax.dot_general(left, right, (((1,), (0,)), ((), ())), preferred_element_type=F32)


def dot_t(left, right):
    return lax.dot_general(left, right, (((1,), (1,)), ((), ())), preferred_element_type=F32)


def call(body, out_shapes, n_smem, n_vmem, flops, scratch=()):
    return pl.pallas_call(
        body,
        out_shape=out_shapes,
        in_specs=[pl.BlockSpec(memory_space=pltpu.SMEM)] * n_smem
        + [pl.BlockSpec(memory_space=pltpu.VMEM)] * n_vmem,
        out_specs=jax.tree.map(lambda _: pl.BlockSpec(memory_space=pltpu.VMEM), out_shapes),
        scratch_shapes=scratch,
        compiler_params=pltpu.CompilerParams(vmem_limit_bytes=VMEM_BYTES),
        cost_estimate=pl.CostEstimate(flops=flops, bytes_accessed=2_000_000, transcendentals=0),
    )


def softmax_mix(query, key, value, live_len):
    rows = query.shape[0]
    scores = dot_t(query, key) * (1.0 / math.sqrt(HD))
    key_pos = lax.broadcasted_iota(jnp.int32, (rows, rows), 1)
    scores = jnp.where(key_pos < live_len, scores, -1e30)
    weights = jnp.exp(scores - jnp.max(scores, axis=-1, keepdims=True))
    probs = (weights / jnp.sum(weights, axis=-1, keepdims=True)).astype(BF16)
    return dot(probs, value).astype(BF16)


def project(state_refs, row_starts, w_refs, width, block):
    wq_ref, wk_ref, wv_ref = w_refs
    rows = state_refs[0].shape[0]
    qk = jnp.zeros((rows, 2 * HD), F32)
    val = jnp.zeros((rows, HD), F32)
    square = jnp.zeros((rows, HD), F32)
    for state_ref, row_start in zip(state_refs, row_starts):
        for at in range(0, width, block):
            x = state_ref[:, at : at + block]
            src = pl.ds(pl.multiple_of(row_start + at, block), block)
            qk += dot(x, jnp.concatenate([wq_ref[src, :], wk_ref[src, :]], axis=1))
            val += dot(x, wv_ref[src, :])
            x32 = x.astype(F32)
            x2 = x32 * x32
            for lane in range(0, block, HD):
                square += x2[:, lane : lane + HD]
    return qk, val, square


def attend(parts, row_starts, w_refs, live_len, width, block):
    qk, val, square = project(parts, row_starts, w_refs, width, block)
    features = w_refs[0].shape[0]
    scale = lax.rsqrt(jnp.sum(square, axis=-1, keepdims=True) * (1.0 / features) + EPSILON)
    query = (qk[:, :HD] * scale).astype(BF16)
    key = (qk[:, HD:] * scale).astype(BF16)
    value = (val * scale).astype(BF16)
    return softmax_mix(query, key, value, live_len)


def first_body(place_ref, own_ref, oth_ref, wq_ref, wk_ref, wv_ref, mixed_ref):
    half = own_ref.shape[1]
    core = place_ref[0]
    mixed_ref[...] = attend(
        [own_ref, oth_ref],
        [core * half, (1 - core) * half],
        (wq_ref, wk_ref, wv_ref),
        place_ref[1],
        half,
        512,
    )


def update_body(pieces, place_ref, own_ref, mix_own_ref, mix_oth_ref, w_own_ref, w_oth_ref, *outs):
    half = own_ref.shape[1]
    core = place_ref[0]
    width = half // pieces
    mixed = jnp.concatenate([mix_own_ref[...], mix_oth_ref[...]], axis=1)
    for piece in range(pieces):
        lower = piece * width
        cols = pl.ds(pl.multiple_of(core * half + lower, width), width)
        weight = jnp.concatenate([w_own_ref[:, cols], w_oth_ref[:, cols]], axis=0)
        held = own_ref[:, lower : lower + width].astype(F32)
        outs[piece][...] = (held + dot(mixed, weight)).astype(BF16)


def combine_body(place_ref, w_own_ref, w_oth_ref, e_own_ref, e_oth_ref, out_ref):
    half = e_own_ref.shape[0]
    cols_half = out_ref.shape[1]
    core = place_ref[0]
    cols = pl.ds(pl.multiple_of(core * cols_half, cols_half), cols_half)
    total = jnp.zeros(out_ref.shape, F32)
    block = 512
    for e_ref, start in ((e_own_ref, core * half), (e_oth_ref, (1 - core) * half)):
        for at in range(0, half, block):
            src = pl.ds(pl.multiple_of(start + at, block), block)
            weight = jnp.concatenate([w_own_ref[:, src], w_oth_ref[:, src]], axis=0)
            total += dot(weight, e_ref[at : at + block, cols])
    out_ref[...] = total.astype(BF16)


def second_body(pieces, place_ref, *refs):
    owns, oths = refs[:pieces], refs[pieces : 2 * pieces]
    wq_ref, wk_ref, wv_ref, e_own_ref, e_oth_ref, mixed_ref, embed_ref = refs[2 * pieces :]
    half = e_own_ref.shape[0]
    width = half // pieces
    core = place_ref[0]
    starts = [core * half + piece * width for piece in range(pieces)]
    starts += [(1 - core) * half + piece * width for piece in range(pieces)]
    mixed_ref[...] = attend(
        list(owns) + list(oths), starts, (wq_ref, wk_ref, wv_ref), place_ref[2], width, 512
    )
    cols_half = embed_ref.shape[1]
    cols = pl.ds(pl.multiple_of(core * cols_half, cols_half), cols_half)
    total = jnp.zeros(embed_ref.shape, F32)
    for e_ref, parts in ((e_own_ref, owns), (e_oth_ref, oths)):
        for piece in range(pieces):
            total += dot(parts[piece][...], e_ref[piece * width : (piece + 1) * width, cols])
    embed_ref[...] = total


def embed_body(place_ref, embed_ref, mix_own_ref, mix_oth_ref, combined_ref, out_ref):
    rows = out_ref.shape[0]
    mixed = jnp.concatenate([mix_own_ref[...], mix_oth_ref[...]], axis=1)
    embed = embed_ref[...] + dot(mixed, combined_ref[...])
    row_pos = lax.broadcasted_iota(jnp.int32, embed.shape, 0)
    out_ref[...] = jnp.where(row_pos < place_ref[2], embed, 0.0).astype(BF16)


def gram_body(*refs):
    embeds, out_ref = refs[:-1], refs[-1]
    rows = embeds[0].shape[0]
    own = embeds[0][...]
    for at, other in enumerate(embeds):
        out_ref[:, at * rows : (at + 1) * rows] = dot_t(own, other[...])


def result_body(*refs):
    embeds, (gram_own_ref, gram_oth_ref, out_ref) = refs[:-3], refs[-3:]
    rows = embeds[0].shape[0]
    tokens = rows * len(embeds)
    total = jnp.zeros(out_ref.shape, F32)
    for at, embed in enumerate(embeds):
        cols = slice(at * rows, (at + 1) * rows)
        gram = (gram_own_ref[:, cols] + gram_oth_ref[:, cols]) * (1.0 / tokens)
        if at == 0:
            row = lax.broadcasted_iota(jnp.int32, gram.shape, 0)
            col = lax.broadcasted_iota(jnp.int32, gram.shape, 1)
            gram = gram - (row == col).astype(F32)
        total += dot(gram.astype(BF16), embed[...])
    out_ref[...] = total


def shards(tokens, lengths, w_query, w_key, w_value, w_out, w_embed):
    section_idx = lax.axis_index("section")
    section_count = lax.axis_size("section")
    core_idx = lax.axis_index("tensor")
    group_count = lax.axis_size("dp")
    wq, wk, wv, wo = w_query[0], w_key[0], w_value[0], w_out[0]
    own = tokens[0]
    rows, half = own.shape
    pieces = 4
    width = half // pieces
    embed_half = w_embed.shape[1] // 2
    lens = lengths[:, 0]
    first_len = lax.dynamic_index_in_dim(lens, section_idx, 0, keepdims=False)
    last_len = lax.dynamic_index_in_dim(
        lens, (section_idx - (HOPS - 1)) % section_count, 0, keepdims=False
    )
    place = jnp.stack([core_idx.astype(jnp.int32), first_len, last_len])

    def shape(*dims, dtype=BF16):
        return jax.ShapeDtypeStruct(dims, dtype)

    with jax.named_scope("tokens_swap"):
        oth = exchanged(own, "tensor", 1)
    with jax.named_scope("weights_swap"):
        wo_oth = exchanged(wo, "tensor", 1)
        we_oth = exchanged(w_embed, "tensor", 1)
    with jax.named_scope("layer_one"):
        mixed = call(first_body, shape(rows, HD), 1, 5, 2 * rows * 2 * half * 3 * HD)(
            place, own, oth, wq, wk, wv
        )
        mixed_oth = exchanged(mixed, "tensor", 1)
        state = call(
            functools.partial(update_body, pieces),
            [shape(rows, width)] * pieces,
            1,
            5,
            2 * rows * 2 * HD * half,
        )(place, own, mixed, mixed_oth, wo, wo_oth)
    with jax.named_scope("hop"):
        state = [shifted(piece, "section", 1) for piece in state]
    with jax.named_scope("combine"):
        combined = call(
            combine_body, shape(2 * HD, embed_half), 1, 4, 2 * 2 * HD * 2 * half * embed_half
        )(place, wo, wo_oth, w_embed, we_oth)
    with jax.named_scope("layer_two"):
        state_oth = [exchanged(piece, "tensor", 1) for piece in state]
        mixed, embed_one = call(
            functools.partial(second_body, pieces),
            [shape(rows, HD), shape(rows, embed_half, dtype=F32)],
            1,
            2 * pieces + 5,
            2 * rows * 2 * half * (3 * HD + embed_half),
        )(place, *state, *state_oth, wq, wk, wv, w_embed, we_oth)
        mixed_oth = exchanged(mixed, "tensor", 1)
    with jax.named_scope("embed"):
        embed = call(embed_body, shape(rows, embed_half), 1, 4, 2 * rows * 2 * HD * embed_half)(
            place, embed_one, mixed, mixed_oth, combined
        )
        embeds = [embed] + [exchanged(embed, "dp", mask) for mask in range(1, group_count)]
    with jax.named_scope("moments"):
        gram = call(
            gram_body,
            shape(rows, rows * group_count, dtype=F32),
            0,
            group_count,
            2 * rows * rows * group_count * embed_half,
        )(*embeds)
        gram_oth = exchanged(gram, "tensor", 1)
        result = call(
            result_body,
            shape(rows, embed_half, dtype=F32),
            0,
            group_count + 2,
            2 * rows * rows * group_count * embed_half,
        )(*embeds, gram, gram_oth)
    return result[None]


def solution(mesh):
    return jax.shard_map(
        shards,
        mesh=mesh,
        in_specs=(
            P("section", "dp", "tensor"),
            P(None, "dp"),
            P("section", None, "tensor"),
            P("section", None, "tensor"),
            P("section", None, "tensor"),
            P("section", "tensor", None),
            P("tensor", None),
        ),
        out_specs=P("section", "dp", "tensor"),
        check_vma=False,
    )
```

time: 176 us -> 60.6 us (0.34)
  waiting for transfers between devices: 129 us -> 27 us
  matrix products: 19.2 us -> 0 us
  between operations: 13.7 us -> 0.11 us
  Pallas kernels: 0 us -> 12.1 us
  starting transfers between devices: 2.04 us -> 11 us
  other arithmetic: 8.66 us -> 1.4 us
  local copies, waits for them, and re-layouts: 2.24 us -> 8.65 us
    reduce_scatter x3 -> x0, waiting for transfers between devices: 49 us -> none  [the longest x1 29.4 us: shards(): lax.psum_scatter(moment_part.astype(jnp.bfloat16), 'dp', scatter_dimensio...]
    all_gather x3 -> x0, waiting for transfers between devices: 45.8 us -> none  [the longest x1 26.8 us: shards(): lax.all_gather(penalty_rows, 'dp', axis=0, tiled=True)]
    psum x1 -> x0, waiting for transfers between devices: 19.5 us -> none  [shards(): embed = lax.psum(embed_part.astype(jnp.bfloat16), 'tensor')]
    dot_general x11 -> x0, matrix products: 19.2 us -> none  [the longest x1 3.78 us: shards(): embed_part = jnp.dot(state, w_embed, preferred_element_type=jnp.float32)]
    ppermute x0 -> x13, waiting for transfers between devices: none -> 15.8 us  [exchanged(): lax.ppermute(value, axis, [(source, source ^ mask) for source in range(co...]
    pallas_call x0 -> x7, Pallas kernels: none -> 12.1 us  [the longest x1 4.04 us: shards(): call(functools.partial(second_body, pieces), [shape(rows, HD), shape(rows...]
    unnamed x18 -> x20, local copies, waits for them, and re-layouts: 0.84 us -> 7.17 us
    ppermute x0 -> x13, starting transfers between devices: none -> 5.02 us  [exchanged(): lax.ppermute(value, axis, [(source, source ^ mask) for source in range(co...]
  transfers between devices with their start and end apart: 8 -> 17, of which waited for: 8 -> 11; matrix products, arithmetic and copies ran while one was open for 2% -> 5% of each run, Pallas kernels for 0% -> 10%
where the time goes in v1:
time: 60.6 us; the launch traced here: 60.2 us
  waiting for transfers between devices  27 us (45%)
  Pallas kernels  12.1 us (20%)
  starting transfers between devices  11 us (18%)
  local copies, waits for them, and re-layouts  8.65 us (14%)
  other arithmetic  1.4 us (2%)
    ppermute x13, waiting for transfers between devices, exchanged(): lax.ppermute(value, axis, [(source, source ^ mask) for source in range(co...  15.8 us
    ppermute x4, waiting for transfers between devices, shifted(): return lax.ppermute(value, axis, pairs)  11.2 us
    unnamed x20, local copies, waits for them, and re-layouts  7.17 us
    ppermute x4, starting transfers between devices, shifted(): return lax.ppermute(value, axis, pairs)  5.95 us
    ppermute x13, starting transfers between devices, exchanged(): lax.ppermute(value, axis, [(source, source ^ mask) for source in range(co...  5.02 us
    pallas_call x1, Pallas kernels, shards(): call(functools.partial(second_body, pieces), [shape(rows, HD), shape(rows...  4.04 us
    pallas_call x1, Pallas kernels, shards(): call(combine_body, shape(2 * HD, embed_half), 1, 4, 2 * 2 * HD * 2 * half...  3.46 us
    pallas_call x1, Pallas kernels, shards(): call(first_body, shape(rows, HD), 1, 5, 2 * rows * 2 * half * 3 * HD)  1.7 us
  transfers between devices with their start and end apart: 17, of which 11 were waited for; matrix products, arithmetic and copies ran while one was open for 5% of the time, Pallas kernels for 10%

profile of v1, /device:TPU:0, one launch (start us, length us, event | category | flops | bytes accessed | tf_op | source)
XLA Modules:
  0.0 60.2 jit_solution(9201979529361686895)
XLA Ops:
  0.0 0.5 collective-permute-start.11
  0.5 0.1 collective-permute-start.2
  0.5 0.5 collective-permute-start
  1.0 0.0 copy-start
  1.0 1.5 %constant_dynamic-slice_fusion.1 = (s32[1,1]{0,1:T(1,128)}, s32[1,1]{0,1:T(1,128)}) fusion(s32[4,1]{0,1:T(1,128)} %param.8, s32[]{:T(128)S(6)} %select_n.14, s32[]{:T(128)S(6)} %select_n.16), kind=kLoop, calls=%fused_computation.2 | loop fusion | bytes 24 | tf_op jit(solution)/shard_map/jit(dynamic_index_in_dim)/dynamic_slice | solution.py:195
  2.4 1.4 %pad_add_fusion.place_ref = s32[3]{0:T(128)S(1)} fusion(s32[1]{0:T(128)} %bitcast.2, s32[1]{0:T(128)} %bitcast.1, s32[1]{0:T(128)} %bitcast), kind=kLoop, calls=%fused_computation | loop fusion | flops 6 | bytes 24 | tf_op jit(solution)/shard_map/stack | solution.py:199
  3.8 5.8 %collective-permute-done.oth_ref = bf16[128,2048]{1,0:T(8,128)(2,1)S(1)} collective-permute-done((bf16[128,2048]{1,0:T(8,128)(2,1)}, bf16[128,2048]{1,0:T(8,128)(2,1)S(1)}, u32[]{:S(2)}, u32[]{:S(2)}) %collective-permute-start) | collective-permute-done | bytes 524320 | tf_op jit(solution)/shard_map/tokens_swap/ppermute | solution.py:27
  9.6 0.0 copy-start.1
  9.6 1.2 %copy-done.1 = bf16[1,4096,128]{2,1,0:T(8,128)(2,1)S(1)} copy-done((bf16[1,4096,128]{2,1,0:T(8,128)(2,1)S(1)}, bf16[1,4096,128]{2,1,0:T(8,128)(2,1)}, u32[]{:S(2)}) %copy-start.1) | copy-done | bytes 1048600
  10.8 0.0 copy-start.3
  10.8 1.2 %copy-done.3 = bf16[1,4096,128]{2,1,0:T(8,128)(2,1)S(1)} copy-done((bf16[1,4096,128]{2,1,0:T(8,128)(2,1)S(1)}, bf16[1,4096,128]{2,1,0:T(8,128)(2,1)}, u32[]{:S(2)}) %copy-start.3) | copy-done | bytes 1048600
  12.1 0.0 copy-start.5
  12.1 1.2 %copy-done.5 = bf16[1,4096,128]{2,1,0:T(8,128)(2,1)S(1)} copy-done((bf16[1,4096,128]{2,1,0:T(8,128)(2,1)S(1)}, bf16[1,4096,128]{2,1,0:T(8,128)(2,1)}, u32[]{:S(2)}) %copy-start.5) | copy-done | bytes 1048600
  13.3 0.0 copy-start.9
  13.3 1.0 %copy-done.9 = bf16[1,128,2048]{2,1,0:T(8,128)(2,1)S(1)} copy-done((bf16[1,128,2048]{2,1,0:T(8,128)(2,1)S(1)}, bf16[1,128,2048]{2,1,0:T(8,128)(2,1)}, u32[]{:S(2)}) %copy-start.9) | copy-done | bytes 524312
  14.3 0.0 copy-start.2
  14.3 0.0 copy-start.4
  14.3 1.7 %layer_one.2.mix_own_ref = bf16[128,128]{1,0:T(8,128)(2,1)S(1)} custom-call(s32[3]{0:T(128)S(1)} %pad_add_fusion.place_ref, bf16[128,2048]{1,0:T(8,128)(2,1)S(1)} %bitcast.19, bf16[128,2048]{1,0:T(8,128)(2,1)S(1)} %collective-permute-done.oth_ref, bf16[4096,128]{1,0:T(8,128)(2,1)S(1)} %bitcast.9, bf16[4096,128]{1,0:T(8,128)(2,1)S(1)} %bitcast.11, ...), custom_call_target="tpu_custom_call" | custom-call | flops 402653184 | bytes 2000000 | tf_op jit(solution)/shard_map/layer_one/pallas_call | solution.py:210
  16.1 0.2 collective-permute-start.1
  16.3 1.1 %collective-permute-done.1.mix_oth_ref = bf16[128,128]{1,0:T(8,128)(2,1)S(1)} collective-permute-done((bf16[128,128]{1,0:T(8,128)(2,1)S(1)}, bf16[128,128]{1,0:T(8,128)(2,1)S(1)}, u32[]{:S(2)}, u32[]{:S(2)}) %collective-permute-start.1) | collective-permute-done | bytes 32800 | tf_op jit(solution)/shard_map/layer_one/ppermute | solution.py:27
  17.3 0.0 collective-permute-done.2.w_oth_ref
  17.3 0.0 copy-start.7
  17.3 1.2 %copy-done.7 = bf16[1,128,4096]{2,1,0:T(8,128)(2,1)S(1)} copy-done((bf16[1,128,4096]{2,1,0:T(8,128)(2,1)S(1)}, bf16[1,128,4096]{2,1,0:T(8,128)(2,1)}, u32[]{:S(2)}) %copy-start.7) | copy-done | bytes 1048600
  18.6 0.9 %layer_one.3 = (bf16[128,512]{1,0:T(8,128)(2,1)S(1)}, bf16[128,512]{1,0:T(8,128)(2,1)S(1)}, bf16[128,512]{1,0:T(8,128)(2,1)S(1)}, bf16[128,512]{1,0:T(8,128)(2,1)S(1)}) custom-call(s32[3]{0:T(128)S(1)} %pad_add_fusion.place_ref, bf16[128,2048]{1,0:T(8,128)(2,1)S(1)} %bitcast.20, bf16[128,128]{1,0:T(8,128)(2,1)S(1)} %layer_one.2.mix_own_ref, ...), custom_call_target="tpu_custom_call" | custom-call | flops 134217728 | bytes 2000000 | tf_op jit(solution)/shard_map/layer_one/pallas_call | solution.py:214
  19.4 2.7 %collective-permute-start.3 = (bf16[128,512]{1,0:T(8,128)(2,1)S(1)}, bf16[128,512]{1,0:T(8,128)(2,1)S(1)}, u32[]{:S(2)}, u32[]{:S(2)}) collective-permute-start(bf16[128,512]{1,0:T(8,128)(2,1)S(1)} %get-tuple-element.11), channel_id=1, source_target_pairs={{0,8},{8,16},{16,24},{24,0},{1,9},{9,17},{17,25},{25,1},{2,10},{10... | collective-permute-start | bytes 393224 | tf_op jit(solution)/shard_map/hop/ppermute | solution.py:22
  22.2 1.6 %collective-permute-start.4 = (bf16[128,512]{1,0:T(8,128)(2,1)S(1)}, bf16[128,512]{1,0:T(8,128)(2,1)S(1)}, u32[]{:S(2)}, u32[]{:S(2)}) collective-permute-start(bf16[128,512]{1,0:T(8,128)(2,1)S(1)} %get-tuple-element.12), channel_id=1, source_target_pairs={{0,8},{8,16},{16,24},{24,0},{1,9},{9,17},{17,25},{25,1},{2,10},{10... | collective-permute-start | bytes 393224 | tf_op jit(solution)/shard_map/hop/ppermute | solution.py:22
  23.7 1.6 %collective-permute-start.5 = (bf16[128,512]{1,0:T(8,128)(2,1)S(1)}, bf16[128,512]{1,0:T(8,128)(2,1)S(1)}, u32[]{:S(2)}, u32[]{:S(2)}) collective-permute-start(bf16[128,512]{1,0:T(8,128)(2,1)S(1)} %get-tuple-element.13), channel_id=1, source_target_pairs={{0,8},{8,16},{16,24},{24,0},{1,9},{9,17},{17,25},{25,1},{2,10},{10... | collective-permute-start | bytes 393224 | tf_op jit(solution)/shard_map/hop/ppermute | solution.py:22
  25.3 0.1 collective-permute-start.6
  25.4 3.2 %collective-permute-done.3.refs_0_ = bf16[128,512]{1,0:T(8,128)(2,1)S(1)} collective-permute-done((bf16[128,512]{1,0:T(8,128)(2,1)S(1)}, bf16[128,512]{1,0:T(8,128)(2,1)S(1)}, u32[]{:S(2)}, u32[]{:S(2)}) %collective-permute-start.3) | collective-permute-done | bytes 131104 | tf_op jit(solution)/shard_map/hop/ppermute | solution.py:22
  28.5 0.0 collective-permute-start.7
  28.5 2.8 %collective-permute-done.4.refs_1_ = bf16[128,512]{1,0:T(8,128)(2,1)S(1)} collective-permute-done((bf16[128,512]{1,0:T(8,128)(2,1)S(1)}, bf16[128,512]{1,0:T(8,128)(2,1)S(1)}, u32[]{:S(2)}, u32[]{:S(2)}) %collective-permute-start.4) | collective-permute-done | bytes 131104 | tf_op jit(solution)/shard_map/hop/ppermute | solution.py:22
  31.3 0.0 collective-permute-start.8
  31.3 2.8 %collective-permute-done.5.refs_2_ = bf16[128,512]{1,0:T(8,128)(2,1)S(1)} collective-permute-done((bf16[128,512]{1,0:T(8,128)(2,1)S(1)}, bf16[128,512]{1,0:T(8,128)(2,1)S(1)}, u32[]{:S(2)}, u32[]{:S(2)}) %collective-permute-start.5) | collective-permute-done | bytes 131104 | tf_op jit(solution)/shard_map/hop/ppermute | solution.py:22
  34.1 0.0 collective-permute-start.9
  34.1 2.5 %collective-permute-done.6.refs_3_ = bf16[128,512]{1,0:T(8,128)(2,1)S(1)} collective-permute-done((bf16[128,512]{1,0:T(8,128)(2,1)S(1)}, bf16[128,512]{1,0:T(8,128)(2,1)S(1)}, u32[]{:S(2)}, u32[]{:S(2)}) %collective-permute-start.6) | collective-permute-done | bytes 131104 | tf_op jit(solution)/shard_map/hop/ppermute | solution.py:22
  36.6 0.0 collective-permute-start.10
  36.6 0.0 collective-permute-done.7.refs_4_
  36.6 0.0 collective-permute-done.8.refs_5_
  36.6 0.0 collective-permute-done.9.refs_6_
  36.6 1.3 %collective-permute-done.10.refs_7_ = bf16[128,512]{1,0:T(8,128)(2,1)S(1)} collective-permute-done((bf16[128,512]{1,0:T(8,128)(2,1)S(1)}, bf16[128,512]{1,0:T(8,128)(2,1)S(1)}, u32[]{:S(2)}, u32[]{:S(2)}) %collective-permute-start.10) | collective-permute-done | bytes 131104 | tf_op jit(solution)/shard_map/layer_two/ppermute | solution.py:27
  38.0 0.0 collective-permute-done.11.refs_12_.e_oth_ref
  38.0 0.0 copy-done
  38.0 0.0 copy-done.2
  38.0 0.0 copy-done.4
  38.0 0.0 copy-start.6
  38.0 1.2 %copy-done.6 = bf16[1,4096,128]{2,1,0:T(8,128)(2,1)S(1)} copy-done((bf16[1,4096,128]{2,1,0:T(8,128)(2,1)S(1)}, bf16[1,4096,128]{2,1,0:T(8,128)(2,1)}, u32[]{:S(2)}) %copy-start.6) | copy-done | bytes 1048600
  39.2 0.0 copy-start.8
  39.2 4.0 %layer_two.1 = (bf16[128,128]{1,0:T(8,128)(2,1)S(1)}, f32[128,512]{1,0:T(8,128)S(1)}) custom-call(s32[3]{0:T(128)S(1)} %pad_add_fusion.place_ref, bf16[128,512]{1,0:T(8,128)(2,1)S(1)} %collective-permute-done.3.refs_0_, bf16[128,512]{1,0:T(8,128)(2,1)S(1)} %collective-permute-done.4.refs_1_, bf16[128,512]{1,0:T(8,128)(2,1)S(1)} %collective-permute-done.5.refs_2_, ...), custom_call_target="tpu_custom_call" | custom-call | flops 939524096 | bytes 2000000 | tf_op jit(solution)/shard_map/layer_two/pallas_call | solution.py:229
  43.3 0.2 collective-permute-start.12
  43.5 0.0 copy-done.8
  43.5 3.5 %combine.1.combined_ref = bf16[256,512]{1,0:T(8,128)(2,1)S(1)} custom-call(s32[3]{0:T(128)S(1)} %pad_add_fusion.place_ref, bf16[128,4096]{1,0:T(8,128)(2,1)S(1)} %bitcast.17, bf16[128,4096]{1,0:T(8,128)(2,1)S(1)} %collective-permute-done.2.w_oth_ref, bf16[2048,1024]{1,0:T(8,128)(2,1)S(1)} %copy-done, ...), custom_call_target="tpu_custom_call" | custom-call | flops 1073741824 | bytes 2000000 | tf_op jit(solution)/shard_map/combine/pallas_call | solution.py:224
  46.9 0.0 collective-permute-done.12.mix_oth_ref
  46.9 0.7 %embed.1.refs_0_ = bf16[128,512]{1,0:T(8,128)(2,1)S(1)} custom-call(s32[3]{0:T(128)S(1)} %pad_add_fusion.place_ref, f32[128,512]{1,0:T(8,128)S(1)} %get-tuple-element.15.embed_ref, bf16[128,128]{1,0:T(8,128)(2,1)S(1)} %get-tuple-element.16.mix_own_ref, bf16[128,128]{1,0:T(8,128)(2,1)S(1)} %collective-permute-done.12.mix_oth_ref, ...), custom_call_target="tpu_custom_call" | custom-call | flops 33554432 | bytes 2000000 | tf_op jit(solution)/shard_map/embed/pallas_call | solution.py:238
  47.7 2.5 %collective-permute-start.15 = (bf16[128,512]{1,0:T(8,128)(2,1)S(1)}, bf16[128,512]{1,0:T(8,128)(2,1)S(1)}, u32[]{:S(2)}, u32[]{:S(2)}) collective-permute-start(bf16[128,512]{1,0:T(8,128)(2,1)S(1)} %embed.1.refs_0_), channel_id=1, source_target_pairs={{0,6},{2,4},{4,2},{6,0},{1,7},{3,5},{5,3},{7,1},{8,14},{10,12},{12... | collective-permute-start | bytes 393224 | tf_op jit(solution)/shard_map/embed/ppermute | solution.py:27
  50.2 0.5 collective-permute-start.14
  50.7 0.5 collective-permute-start.13
  51.3 3.4 %collective-permute-done.15.refs_3_ = bf16[128,512]{1,0:T(8,128)(2,1)S(1)} collective-permute-done((bf16[128,512]{1,0:T(8,128)(2,1)S(1)}, bf16[128,512]{1,0:T(8,128)(2,1)S(1)}, u32[]{:S(2)}, u32[]{:S(2)}) %collective-permute-start.15) | collective-permute-done | bytes 131104 | tf_op jit(solution)/shard_map/embed/ppermute | solution.py:27
  54.7 2.5 %collective-permute-done.14.refs_2_ = bf16[128,512]{1,0:T(8,128)(2,1)S(1)} collective-permute-done((bf16[128,512]{1,0:T(8,128)(2,1)S(1)}, bf16[128,512]{1,0:T(8,128)(2,1)S(1)}, u32[]{:S(2)}, u32[]{:S(2)}) %collective-permute-start.14) | collective-permute-done | bytes 131104 | tf_op jit(solution)/shard_map/embed/ppermute | solution.py:27
  57.2 0.1 collective-permute-done.13.refs_1_
  57.3 0.3 moments.2.refs_4_
  57.6 0.1 collective-permute-start.16
  57.7 1.5 %collective-permute-done.16.refs_5_ = f32[128,512]{1,0:T(8,128)S(1)} collective-permute-done((f32[128,512]{1,0:T(8,128)S(1)}, f32[128,512]{1,0:T(8,128)S(1)}, u32[]{:S(2)}, u32[]{:S(2)}) %collective-permute-start.16) | collective-permute-done | bytes 262176 | tf_op jit(solution)/shard_map/moments/ppermute | solution.py:27
  59.2 1.0 %moments.3 = f32[128,512]{1,0:T(8,128)} custom-call(bf16[128,512]{1,0:T(8,128)(2,1)S(1)} %embed.1.refs_0_, bf16[128,512]{1,0:T(8,128)(2,1)S(1)} %collective-permute-done.13.refs_1_, bf16[128,512]{1,0:T(8,128)(2,1)S(1)} %collective-permute-done.14.refs_2_, bf16[128,512]{1,0:T(8,128)(2,1)S(1)} %collective-permute-done.15.refs_3_, ...), custom_call_target="tpu_custom_call" | custom-call | flops 67108864 | bytes 2000000 | tf_op jit(solution)/shard_map/moments/pallas_call | solution.py:251
Async XLA Ops:
  0.0 38.0 %collective-permute-start.11 = (bf16[2048,1024]{1,0:T(8,128)(2,1)}, bf16[2048,1024]{1,0:T(8,128)(2,1)}, u32[]{:S(2)}, u32[]{:S(2)}) collective-permute-start(bf16[2048,1024]{1,0:T(8,128)(2,1)} %e_own_ref.1), channel_id=1, source_target_pairs={{0,1},{1,0},{2,3},{3,2},{4,5},{5,4},{6,7},{7,6},{8,9},{9,8},{10,11... | collective-permute-start | bytes 12582920 | tf_op jit(solution)/shard_map/weights_swap/ppermute | solution.py:27
  0.5 16.9 %collective-permute-start.2 = (bf16[128,4096]{1,0:T(8,128)(2,1)}, bf16[128,4096]{1,0:T(8,128)(2,1)S(1)}, u32[]{:S(2)}, u32[]{:S(2)}) collective-permute-start(bf16[128,4096]{1,0:T(8,128)(2,1)} %bitcast.15), channel_id=1, source_target_pairs={{0,1},{1,0},{2,3},{3,2},{4,5},{5,4},{6,7},{7,6},{8,9},{9,8},{10,11... | collective-permute-start | bytes 3145736 | tf_op jit(solution)/shard_map/weights_swap/ppermute | solution.py:27
  0.5 9.1 %collective-permute-start = (bf16[128,2048]{1,0:T(8,128)(2,1)}, bf16[128,2048]{1,0:T(8,128)(2,1)S(1)}, u32[]{:S(2)}, u32[]{:S(2)}) collective-permute-start(bf16[128,2048]{1,0:T(8,128)(2,1)} %bitcast.18), channel_id=1, source_target_pairs={{0,1},{1,0},{2,3},{3,2},{4,5},{5,4},{6,7},{7,6},{8,9},{9,8},{10,11... | collective-permute-start | bytes 1572872 | tf_op jit(solution)/shard_map/tokens_swap/ppermute | solution.py:27
  1.0 37.0 %copy-start = (bf16[2048,1024]{1,0:T(8,128)(2,1)S(1)}, bf16[2048,1024]{1,0:T(8,128)(2,1)}, u32[]{:S(2)}) copy-start(bf16[2048,1024]{1,0:T(8,128)(2,1)} %e_own_ref.1) | copy-start | bytes 12582916
  9.6 1.2 %copy-start.1 = (bf16[1,4096,128]{2,1,0:T(8,128)(2,1)S(1)}, bf16[1,4096,128]{2,1,0:T(8,128)(2,1)}, u32[]{:S(2)}) copy-start(bf16[1,4096,128]{2,1,0:T(8,128)(2,1)} %param.9) | copy-start | bytes 3145732
  10.8 1.2 %copy-start.3 = (bf16[1,4096,128]{2,1,0:T(8,128)(2,1)S(1)}, bf16[1,4096,128]{2,1,0:T(8,128)(2,1)}, u32[]{:S(2)}) copy-start(bf16[1,4096,128]{2,1,0:T(8,128)(2,1)} %param.10) | copy-start | bytes 3145732
  12.1 1.2 %copy-start.5 = (bf16[1,4096,128]{2,1,0:T(8,128)(2,1)S(1)}, bf16[1,4096,128]{2,1,0:T(8,128)(2,1)}, u32[]{:S(2)}) copy-start(bf16[1,4096,128]{2,1,0:T(8,128)(2,1)} %param.11) | copy-start | bytes 3145732
  13.3 1.0 %copy-start.9 = (bf16[1,128,2048]{2,1,0:T(8,128)(2,1)S(1)}, bf16[1,128,2048]{2,1,0:T(8,128)(2,1)}, u32[]{:S(2)}) copy-start(bf16[1,128,2048]{2,1,0:T(8,128)(2,1)} %param.7) | copy-start | bytes 1572868
  14.3 23.6 %copy-start.2 = (bf16[1,4096,128]{2,1,0:T(8,128)(2,1)S(1)}, bf16[1,4096,128]{2,1,0:T(8,128)(2,1)}, u32[]{:S(2)}) copy-start(bf16[1,4096,128]{2,1,0:T(8,128)(2,1)} %param.9) | copy-start | bytes 3145732
  14.3 23.6 %copy-start.4 = (bf16[1,4096,128]{2,1,0:T(8,128)(2,1)S(1)}, bf16[1,4096,128]{2,1,0:T(8,128)(2,1)}, u32[]{:S(2)}) copy-start(bf16[1,4096,128]{2,1,0:T(8,128)(2,1)} %param.10) | copy-start | bytes 3145732
  16.1 1.3 %collective-permute-start.1 = (bf16[128,128]{1,0:T(8,128)(2,1)S(1)}, bf16[128,128]{1,0:T(8,128)(2,1)S(1)}, u32[]{:S(2)}, u32[]{:S(2)}) collective-permute-start(bf16[128,128]{1,0:T(8,128)(2,1)S(1)} %layer_one.2.mix_own_ref), channel_id=1, source_target_pairs={{0,1},{1,0},{2,3},{3,2},{4,5},{5,4},{6,7},{7,6},{8,9},{9,8},{10,11... | collective-permute-start | bytes 98312 | tf_op jit(solution)/shard_map/layer_one/ppermute | solution.py:27
  17.3 1.2 %copy-start.7 = (bf16[1,128,4096]{2,1,0:T(8,128)(2,1)S(1)}, bf16[1,128,4096]{2,1,0:T(8,128)(2,1)}, u32[]{:S(2)}) copy-start(bf16[1,128,4096]{2,1,0:T(8,128)(2,1)} %param.12) | copy-start | bytes 3145732
  19.4 9.1 %collective-permute-start.3 = (bf16[128,512]{1,0:T(8,128)(2,1)S(1)}, bf16[128,512]{1,0:T(8,128)(2,1)S(1)}, u32[]{:S(2)}, u32[]{:S(2)}) collective-permute-start(bf16[128,512]{1,0:T(8,128)(2,1)S(1)} %get-tuple-element.11), channel_id=1, source_target_pairs={{0,8},{8,16},{16,24},{24,0},{1,9},{9,17},{17,25},{25,1},{2,10},{10... | collective-permute-start | bytes 393224 | tf_op jit(solution)/shard_map/hop/ppermute | solution.py:22
  22.2 9.2 %collective-permute-start.4 = (bf16[128,512]{1,0:T(8,128)(2,1)S(1)}, bf16[128,512]{1,0:T(8,128)(2,1)S(1)}, u32[]{:S(2)}, u32[]{:S(2)}) collective-permute-start(bf16[128,512]{1,0:T(8,128)(2,1)S(1)} %get-tuple-element.12), channel_id=1, source_target_pairs={{0,8},{8,16},{16,24},{24,0},{1,9},{9,17},{17,25},{25,1},{2,10},{10... | collective-permute-start | bytes 393224 | tf_op jit(solution)/shard_map/hop/ppermute | solution.py:22
  23.7 10.4 %collective-permute-start.5 = (bf16[128,512]{1,0:T(8,128)(2,1)S(1)}, bf16[128,512]{1,0:T(8,128)(2,1)S(1)}, u32[]{:S(2)}, u32[]{:S(2)}) collective-permute-start(bf16[128,512]{1,0:T(8,128)(2,1)S(1)} %get-tuple-element.13), channel_id=1, source_target_pairs={{0,8},{8,16},{16,24},{24,0},{1,9},{9,17},{17,25},{25,1},{2,10},{10... | collective-permute-start | bytes 393224 | tf_op jit(solution)/shard_map/hop/ppermute | solution.py:22
  25.3 11.3 %collective-permute-start.6 = (bf16[128,512]{1,0:T(8,128)(2,1)S(1)}, bf16[128,512]{1,0:T(8,128)(2,1)S(1)}, u32[]{:S(2)}, u32[]{:S(2)}) collective-permute-start(bf16[128,512]{1,0:T(8,128)(2,1)S(1)} %get-tuple-element.14), channel_id=1, source_target_pairs={{0,8},{8,16},{16,24},{24,0},{1,9},{9,17},{17,25},{25,1},{2,10},{10... | collective-permute-start | bytes 393224 | tf_op jit(solution)/shard_map/hop/ppermute | solution.py:22
  28.5 8.1 %collective-permute-start.7 = (bf16[128,512]{1,0:T(8,128)(2,1)S(1)}, bf16[128,512]{1,0:T(8,128)(2,1)S(1)}, u32[]{:S(2)}, u32[]{:S(2)}) collective-permute-start(bf16[128,512]{1,0:T(8,128)(2,1)S(1)} %collective-permute-done.3.refs_0_), channel_id=1, source_target_pairs={{0,1},{1,0},{2,3},{3,2},{4,5},{5,4},{6,7},{7,6},{8,9},{9,8},{10,11... | collective-permute-start | bytes 393224 | tf_op jit(solution)/shard_map/layer_two/ppermute | solution.py:27
  31.3 5.3 %collective-permute-start.8 = (bf16[128,512]{1,0:T(8,128)(2,1)S(1)}, bf16[128,512]{1,0:T(8,128)(2,1)S(1)}, u32[]{:S(2)}, u32[]{:S(2)}) collective-permute-start(bf16[128,512]{1,0:T(8,128)(2,1)S(1)} %collective-permute-done.4.refs_1_), channel_id=1, source_target_pairs={{0,1},{1,0},{2,3},{3,2},{4,5},{5,4},{6,7},{7,6},{8,9},{9,8},{10,11... | collective-permute-start | bytes 393224 | tf_op jit(solution)/shard_map/layer_two/ppermute | solution.py:27
  34.1 2.5 %collective-permute-start.9 = (bf16[128,512]{1,0:T(8,128)(2,1)S(1)}, bf16[128,512]{1,0:T(8,128)(2,1)S(1)}, u32[]{:S(2)}, u32[]{:S(2)}) collective-permute-start(bf16[128,512]{1,0:T(8,128)(2,1)S(1)} %collective-permute-done.5.refs_2_), channel_id=1, source_target_pairs={{0,1},{1,0},{2,3},{3,2},{4,5},{5,4},{6,7},{7,6},{8,9},{9,8},{10,11... | collective-permute-start | bytes 393224 | tf_op jit(solution)/shard_map/layer_two/ppermute | solution.py:27
  36.6 1.3 %collective-permute-start.10 = (bf16[128,512]{1,0:T(8,128)(2,1)S(1)}, bf16[128,512]{1,0:T(8,128)(2,1)S(1)}, u32[]{:S(2)}, u32[]{:S(2)}) collective-permute-start(bf16[128,512]{1,0:T(8,128)(2,1)S(1)} %collective-permute-done.6.refs_3_), channel_id=1, source_target_pairs={{0,1},{1,0},{2,3},{3,2},{4,5},{5,4},{6,7},{7,6},{8,9},{9,8},{10,11... | collective-permute-start | bytes 393224 | tf_op jit(solution)/shard_map/layer_two/ppermute | solution.py:27
  38.0 1.2 %copy-start.6 = (bf16[1,4096,128]{2,1,0:T(8,128)(2,1)S(1)}, bf16[1,4096,128]{2,1,0:T(8,128)(2,1)}, u32[]{:S(2)}) copy-start(bf16[1,4096,128]{2,1,0:T(8,128)(2,1)} %param.11) | copy-start | bytes 3145732
  39.2 4.3 %copy-start.8 = (bf16[1,128,4096]{2,1,0:T(8,128)(2,1)S(1)}, bf16[1,128,4096]{2,1,0:T(8,128)(2,1)}, u32[]{:S(2)}) copy-start(bf16[1,128,4096]{2,1,0:T(8,128)(2,1)} %param.12) | copy-start | bytes 3145732
  43.3 3.7 %collective-permute-start.12 = (bf16[128,128]{1,0:T(8,128)(2,1)S(1)}, bf16[128,128]{1,0:T(8,128)(2,1)S(1)}, u32[]{:S(2)}, u32[]{:S(2)}) collective-permute-start(bf16[128,128]{1,0:T(8,128)(2,1)S(1)} %get-tuple-element.16.mix_own_ref), channel_id=1, source_target_pairs={{0,1},{1,0},{2,3},{3,2},{4,5},{5,4},{6,7},{7,6},{8,9},{9,8},{10,11... | collective-permute-start | bytes 98312 | tf_op jit(solution)/shard_map/layer_two/ppermute | solution.py:27
  47.7 7.0 %collective-permute-start.15 = (bf16[128,512]{1,0:T(8,128)(2,1)S(1)}, bf16[128,512]{1,0:T(8,128)(2,1)S(1)}, u32[]{:S(2)}, u32[]{:S(2)}) collective-permute-start(bf16[128,512]{1,0:T(8,128)(2,1)S(1)} %embed.1.refs_0_), channel_id=1, source_target_pairs={{0,6},{2,4},{4,2},{6,0},{1,7},{3,5},{5,3},{7,1},{8,14},{10,12},{12... | collective-permute-start | bytes 393224 | tf_op jit(solution)/shard_map/embed/ppermute | solution.py:27
  50.2 7.0 %collective-permute-start.14 = (bf16[128,512]{1,0:T(8,128)(2,1)S(1)}, bf16[128,512]{1,0:T(8,128)(2,1)S(1)}, u32[]{:S(2)}, u32[]{:S(2)}) collective-permute-start(bf16[128,512]{1,0:T(8,128)(2,1)S(1)} %embed.1.refs_0_), channel_id=1, source_target_pairs={{0,4},{2,6},{4,0},{6,2},{1,5},{3,7},{5,1},{7,3},{8,12},{10,14},{12... | collective-permute-start | bytes 393224 | tf_op jit(solution)/shard_map/embed/ppermute | solution.py:27
  50.7 6.6 %collective-permute-start.13 = (bf16[128,512]{1,0:T(8,128)(2,1)S(1)}, bf16[128,512]{1,0:T(8,128)(2,1)S(1)}, u32[]{:S(2)}, u32[]{:S(2)}) collective-permute-start(bf16[128,512]{1,0:T(8,128)(2,1)S(1)} %embed.1.refs_0_), channel_id=1, source_target_pairs={{0,2},{2,0},{4,6},{6,4},{1,3},{3,1},{5,7},{7,5},{8,10},{10,8},{12,... | collective-permute-start | bytes 393224 | tf_op jit(solution)/shard_map/embed/ppermute | solution.py:27
  57.6 1.6 %collective-permute-start.16 = (f32[128,512]{1,0:T(8,128)S(1)}, f32[128,512]{1,0:T(8,128)S(1)}, u32[]{:S(2)}, u32[]{:S(2)}) collective-permute-start(f32[128,512]{1,0:T(8,128)S(1)} %moments.2.refs_4_), channel_id=1, source_target_pairs={{0,1},{1,0},{2,3},{3,2},{4,5},{5,4},{6,7},{7,6},{8,9},{9,8},{10,11... | collective-permute-start | bytes 786440 | tf_op jit(solution)/shard_map/moments/ppermute | solution.py:27

commit v2 on v0

v2 whole, which is shorter than its diff:
```python
import functools
import math

import jax
import jax.numpy as jnp
from jax import lax
from jax.experimental import pallas as pl
from jax.experimental.pallas import tpu as pltpu
from jax.sharding import PartitionSpec as P

HD = 128
QKV = 3 * HD
EPSILON = 1e-05
BF16 = jnp.bfloat16
F32 = jnp.float32
VMEM_BYTES = 18 * 1024 * 1024
SHARES = (8, 8)


def shifted(value, axis, steps):
    count = lax.axis_size(axis)
    pairs = [(source, (source + steps) % count) for source in range(count)]
    return lax.ppermute(value, axis, pairs)


def exchanged(value, axis, mask):
    count = lax.axis_size(axis)
    return lax.ppermute(value, axis, [(source, source ^ mask) for source in range(count)])


def after(value, *others):
    return lax.optimization_barrier((value, *others))[0]


def dot(left, right):
    return lax.dot_general(left, right, (((1,), (0,)), ((), ())), preferred_element_type=F32)


def dot_t(left, right):
    return lax.dot_general(left, right, (((1,), (1,)), ((), ())), preferred_element_type=F32)


def shape(*dims, dtype=BF16):
    return jax.ShapeDtypeStruct(dims, dtype)


SPACES = {"s": pltpu.SMEM, "v": pltpu.VMEM, "h": pltpu.HBM}


def call(body, out_shapes, spaces, copies=0, last=False, scratch=()):
    kernel = pl.pallas_call(
        body,
        out_shape=out_shapes
        if last
        else jax.tree.map(lambda out: pltpu.VMEM(out.shape, out.dtype), out_shapes),
        in_specs=[pl.BlockSpec(memory_space=SPACES[space]) for space in spaces],
        out_specs=jax.tree.map(lambda _: pl.BlockSpec(memory_space=pltpu.VMEM), out_shapes),
        scratch_shapes=([pltpu.SemaphoreType.DMA((copies,))] if copies else []) + list(scratch),
        compiler_params=pltpu.CompilerParams(vmem_limit_bytes=VMEM_BYTES),
        cost_estimate=pl.CostEstimate(flops=0, bytes_accessed=0, transcendentals=0),
    )

    def place(operand, space):
        if space == "s":
            return operand
        return pltpu.with_memory_space_constraint(operand, SPACES[space])

    return lambda *operands: kernel(*map(place, operands, spaces))


def span(start, size):
    return pl.ds(pl.multiple_of(start, size), size)


def lane_sums(x):
    x32 = x.astype(F32)
    x2 = x32 * x32
    total = x2[:, :HD]
    for lane in range(HD, x.shape[1], HD):
        total += x2[:, lane : lane + HD]
    return total


def rms_scale(square, features):
    return lax.rsqrt(jnp.sum(square, axis=-1, keepdims=True) * (1.0 / features) + EPSILON)


def softmax_mix(qkv, live_len):
    query, key, value = (qkv[:, at : at + HD].astype(BF16) for at in range(0, QKV, HD))
    rows = query.shape[0]
    scores = dot_t(query, key) * (1.0 / math.sqrt(HD))
    key_pos = lax.broadcasted_iota(jnp.int32, (rows, rows), 1)
    scores = jnp.where(key_pos < live_len, scores, -1e30)
    weights = jnp.exp(scores - jnp.max(scores, axis=-1, keepdims=True))
    probs = (weights / jnp.sum(weights, axis=-1, keepdims=True)).astype(BF16)
    return dot(probs, value).astype(BF16)


def load_body(own_hbm, wq_hbm, wk_hbm, wv_hbm, own_ref, w_ref, qkv_ref, square_ref, sems):
    half = own_ref.shape[1]
    core = lax.axis_index("tensor")
    copies = [pltpu.make_async_copy(own_hbm.at[0], own_ref, sems.at[0])]
    for part in range(2):
        rows = span((core if part == 0 else 1 - core) * half, half)
        for at, w_hbm in enumerate((wq_hbm, wk_hbm, wv_hbm)):
            copies.append(
                pltpu.make_async_copy(
                    w_hbm.at[0, rows, :],
                    w_ref.at[rows, at * HD : (at + 1) * HD],
                    sems.at[len(copies)],
                )
            )
    for copy in copies:
        copy.start()
    copies[0].wait()
    own = own_ref[...]
    square_ref[...] = lane_sums(own)
    for copy in copies[1:4]:
        copy.wait()
    qkv_ref[...] = dot(own, w_ref[span(core * half, half), :])
    for copy in copies[4:]:
        copy.wait()


def first_body(
    lens_hbm, own_ref, oth_ref, w_ref, qkv_ref, square_ref, wo_hbm,
    held_ref, part_ref, wo_own_ref, wo_send_ref, sems, lens_ref,
):
    half = oth_ref.shape[1]
    core = lax.axis_index("tensor")
    copies = [
        pltpu.make_async_copy(wo_hbm.at[0, :, span(side * half, half)], ref, sems.at[index])
        for index, (side, ref) in enumerate(((1 - core, wo_send_ref), (core, wo_own_ref)))
    ]
    copies.append(pltpu.make_async_copy(lens_hbm, lens_ref, sems.at[2]))
    for copy in copies:
        copy.start()
    oth = oth_ref[...]
    qkv = qkv_ref[...] + dot(oth, w_ref[span((1 - core) * half, half), :])
    scale = rms_scale(square_ref[...] + lane_sums(oth), 2 * half)
    copies.pop().wait()
    mixed = softmax_mix(qkv * scale, lens_ref[lax.axis_index("section")])
    for copy in copies:
        copy.wait()
    part_ref[...] = dot(mixed, wo_send_ref[...]).astype(BF16)
    held_ref[...] = own_ref[...].astype(F32) + dot(mixed, wo_own_ref[...])


def update_body(held_ref, part_ref, *outs):
    lower = 0
    for out_ref in outs:
        upper = lower + out_ref.shape[1]
        held, part = held_ref[:, lower:upper], part_ref[:, lower:upper]
        out_ref[...] = (held + part.astype(F32)).astype(BF16)
        lower = upper


def combine_body(w_own_ref, w_oth_ref, e_hbm, e_ref, mine_ref, send_ref, sems):
    blocks = sems.shape[0]
    depth = e_ref.shape[0] // blocks
    copies = []
    for block in range(blocks):
        rows = slice(block * depth, (block + 1) * depth)
        copies.append(pltpu.make_async_copy(e_hbm.at[rows, :], e_ref.at[rows, :], sems.at[block]))
        copies[-1].start()
    cols = mine_ref.shape[1]
    core = lax.axis_index("tensor")
    weight = jnp.concatenate([w_own_ref[...], w_oth_ref[...]], axis=0)
    for copy in copies:
        copy.wait()
    mine_ref[...] = dot(weight, e_ref[:, span(core * cols, cols)])
    send_ref[...] = dot(weight, e_ref[:, span((1 - core) * cols, cols)])


def own_body(lower, own_ref, w_ref, e_ref, *refs):
    sums, (qkv_ref, square_ref, embed_ref) = refs[:-3], refs[-3:]
    width = own_ref.shape[1]
    half = e_ref.shape[0]
    src = pl.ds(pl.multiple_of(lax.axis_index("tensor") * half + lower, HD), width)
    x = own_ref[...]
    qkv, square, embed = dot(x, w_ref[src, :]), lane_sums(x), dot(x, e_ref[lower : lower + width, :])
    if sums:
        qkv, square = qkv + sums[0][...], square + sums[1][...]
        embed = embed + sums[2][...]
    qkv_ref[...], square_ref[...], embed_ref[...] = qkv, square, embed


def own_last_body(lower, own_ref, w_ref, e_ref, sum_ref, square_in_ref, embed_in_ref, *refs):
    qkv_ref, square_ref, mine_ref, send_ref = refs
    width = own_ref.shape[1]
    half = e_ref.shape[0]
    cols = mine_ref.shape[1]
    core = lax.axis_index("tensor")
    src = pl.ds(pl.multiple_of(core * half + lower, HD), width)
    x = own_ref[...]
    for side, out_ref in ((1 - core, send_ref), (core, mine_ref)):
        at = span(side * cols, cols)
        embed = embed_in_ref[:, at] + dot(x, e_ref[lower : lower + width, at])
        out_ref[...] = embed.astype(out_ref.dtype)
    qkv_ref[...] = sum_ref[...] + dot(x, w_ref[src, :])
    square_ref[...] = square_in_ref[...] + lane_sums(x)


def other_sums(lower, half, oth_ref, w_ref):
    src = pl.ds(
        pl.multiple_of((1 - lax.axis_index("tensor")) * half + lower, HD), oth_ref.shape[1]
    )
    x = oth_ref[...]
    return dot(x, w_ref[src, :]), lane_sums(x)


def other_body(lower, half, oth_ref, w_ref, sum_ref, square_in_ref, qkv_ref, square_ref):
    qkv, square = other_sums(lower, half, oth_ref, w_ref)
    qkv_ref[...] = sum_ref[...] + qkv
    square_ref[...] = square_in_ref[...] + square


def hop_anchor():
    sections = lax.axis_size("section")
    return lax.rem(lax.axis_index("section") + sections - 1, sections)


def second_body(lower, half, lens_ref, oth_ref, w_ref, sum_ref, square_in_ref, mixed_ref):
    qkv, square = other_sums(lower, half, oth_ref, w_ref)
    scale = rms_scale(square_in_ref[...] + square, 2 * half)
    mixed_ref[...] = softmax_mix((sum_ref[...] + qkv) * scale, lens_ref[hop_anchor()])


def combine_sum_body(mine_ref, recv_ref, out_ref):
    rows = mine_ref.shape[0] // 2
    out_ref[:rows, :] = (mine_ref[:rows, :] + recv_ref[rows:, :]).astype(BF16)
    out_ref[rows:, :] = (mine_ref[rows:, :] + recv_ref[:rows, :]).astype(BF16)


def embed_own_body(mine_ref, recv_ref, mixed_ref, combined_ref, out_ref):
    product = dot(mixed_ref[...], combined_ref[: mixed_ref.shape[1], :])
    out_ref[...] = mine_ref[...] + recv_ref[...].astype(F32) + product


def embed_body(lens_ref, sum_ref, mixed_ref, combined_ref, out_ref):
    embed = sum_ref[...] + dot(mixed_ref[...], combined_ref[mixed_ref.shape[1] :, :])
    row_pos = lax.broadcasted_iota(jnp.int32, embed.shape, 0)
    out_ref[...] = jnp.where(row_pos < lens_ref[hop_anchor()], embed, 0.0).astype(BF16)


def gram_body(*refs):
    own, embeds, out_ref = refs[0][...], refs[1:-1], refs[-1]
    rows = own.shape[0]
    for at, embed in enumerate(embeds):
        out_ref[:, at * rows : (at + 1) * rows] = dot_t(own, embed[...])


def result_body(tokens, first, *refs):
    (gram_own_ref, gram_oth_ref), embeds, out_ref = refs[:2], refs[2:-1], refs[-1]
    total = None
    if not first:
        embeds, total = embeds[:-1], embeds[-1][...]
    rows = embeds[0].shape[0]
    for at, embed in enumerate(embeds):
        cols = slice(at * rows, (at + 1) * rows)
        gram = (gram_own_ref[:, cols] + gram_oth_ref[:, cols]) * (1.0 / tokens)
        if first and at == 0:
            row = lax.broadcasted_iota(jnp.int32, gram.shape, 0)
            col = lax.broadcasted_iota(jnp.int32, gram.shape, 1)
            gram = gram - (row == col).astype(F32)
        product = dot(gram.astype(BF16), embed[...])
        total = product if total is None else total + product
    out_ref[...] = total


def shards(tokens, lengths, w_query, w_key, w_value, w_out, w_embed):
    group_count = lax.axis_size("dp")
    own_in = tokens[0]
    rows, half = own_in.shape
    features = 2 * half
    widths = [half * share // sum(SHARES) for share in SHARES]
    lowers = [sum(widths[:at]) for at in range(len(widths))]
    cols = w_embed.shape[1] // 2

    lens = lengths.reshape(-1)

    with jax.named_scope("layer_one"):
        oth = exchanged(own_in, "tensor", 1)
        own, w_own, qkv, square = call(
            load_body,
            [shape(rows, half), shape(features, QKV), shape(rows, QKV, dtype=F32), shape(rows, HD, dtype=F32)],
            "hhhh",
            7,
                    )(tokens, w_query, w_key, w_value)
        held, part, wo_own, wo_send = call(
            first_body,
            [shape(rows, half, dtype=F32)] + [shape(rows, half)] + [shape(HD, half)] * 2,
            "hvvvvvh",
            3,
            scratch=(pltpu.SMEM(lens.shape, jnp.int32),),
        )(lens, own, oth, w_own, qkv, square, w_out)
        part = exchanged(part, "tensor", 1)
        state = call(update_body, [shape(rows, width) for width in widths], "vv")(held, part)
    with jax.named_scope("weights"):
        wo_oth = exchanged(after(wo_send, state[0]), "tensor", 1)
    with jax.named_scope("hop"):
        state = [shifted(piece, "section", 1) for piece in state]
    with jax.named_scope("weights"):
        w_embed_own, c_mine, c_send = call(
            combine_body,
            [shape(*w_embed.shape)] + [shape(2 * HD, cols, dtype=F32)] * 2,
            "vvh",
            4,
        )(wo_own, wo_oth, after(w_embed, state[0]))
        combined = call(combine_sum_body, shape(2 * HD, cols), "vv")(
            c_mine, exchanged(c_send, "tensor", 1)
        )
    with jax.named_scope("layer_two"):
        sums = ()
        for lower, piece in zip(lowers, state):
            oth = exchanged(piece, "tensor", 1)
            if lower != lowers[-1]:
                qkv, square, embed = call(
                    functools.partial(own_body, lower),
                    [shape(rows, QKV, dtype=F32), shape(rows, HD, dtype=F32), shape(rows, 2 * cols, dtype=F32)],
                    "v" * (3 + len(sums)),
                )(piece, w_own, w_embed_own, *sums)
                qkv, square = call(
                    functools.partial(other_body, lower, half),
                    [shape(rows, QKV, dtype=F32), shape(rows, HD, dtype=F32)],
                    "vvvv",
                )(oth, w_own, qkv, square)
                sums = (qkv, square, embed)
            else:
                qkv, square, e_mine, e_send = call(
                    functools.partial(own_last_body, lower),
                    [shape(rows, QKV, dtype=F32), shape(rows, HD, dtype=F32)]
                    + [shape(rows, cols, dtype=F32), shape(rows, cols)],
                    "v" * 6,
                )(piece, w_own, w_embed_own, *sums)
        e_recv = exchanged(e_send, "tensor", 1)
        mixed = call(
            functools.partial(second_body, lower, half), shape(rows, HD), "svvvv"
        )(lens, oth, w_own, qkv, square)
        mixed_oth = exchanged(mixed, "tensor", 1)
        embed = call(embed_own_body, shape(rows, cols, dtype=F32), "vvvv")(
            e_mine, e_recv, mixed, combined
        )
        embed = call(embed_body, shape(rows, cols), "svvv")(lens, embed, mixed_oth, combined)
    with jax.named_scope("moments"):
        embeds = [embed] + [exchanged(embed, "dp", mask) for mask in range(1, group_count)]
        result = ()
        for part in (embeds[:2], embeds[2:]):
            gram = call(gram_body, shape(rows, rows * len(part), dtype=F32), "v" * (1 + len(part)))(
                embed, *part
            )
            operands = (gram, exchanged(gram, "tensor", 1), *part, *result)
            result = (
                call(
                    functools.partial(result_body, rows * group_count, not result),
                    shape(rows, cols, dtype=F32),
                    "v" * len(operands),
                    last=bool(result),
                )(*operands),
            )
    return result[0][None]


def solution(mesh):
    return jax.shard_map(
        shards,
        mesh=mesh,
        in_specs=(
            P("section", "dp", "tensor"),
            P(None, "dp"),
            P("section", None, "tensor"),
            P("section", None, "tensor"),
            P("section", None, "tensor"),
            P("section", "tensor", None),
            P("tensor", None),
        ),
        out_specs=P("section", "dp", "tensor"),
        check_vma=False,
    )
```

time: 176 us -> 42 us (0.24)
  waiting for transfers between devices: 129 us -> 18.6 us
  matrix products: 19.2 us -> 0 us
  between operations: 13.7 us -> 0.17 us
  Pallas kernels: 0 us -> 12.9 us
  other arithmetic: 8.66 us -> 0 us
  starting transfers between devices: 2.04 us -> 10.2 us
  local copies, waits for them, and re-layouts: 2.24 us -> 0.01 us
    reduce_scatter x3 -> x0, waiting for transfers between devices: 49 us -> none  [the longest x1 29.4 us: shards(): lax.psum_scatter(moment_part.astype(jnp.bfloat16), 'dp', scatter_dimensio...]
    all_gather x3 -> x0, waiting for transfers between devices: 45.8 us -> none  [the longest x1 26.8 us: shards(): lax.all_gather(penalty_rows, 'dp', axis=0, tiled=True)]
    psum x1 -> x0, waiting for transfers between devices: 19.5 us -> none  [shards(): embed = lax.psum(embed_part.astype(jnp.bfloat16), 'tensor')]
    dot_general x11 -> x0, matrix products: 19.2 us -> none  [the longest x1 3.78 us: shards(): embed_part = jnp.dot(state, w_embed, preferred_element_type=jnp.float32)]
    pallas_call x0 -> x15, Pallas kernels: none -> 12.9 us  [call(): return lambda *operands: kernel(*map(place, operands, spaces))]
    ppermute x0 -> x13, waiting for transfers between devices: none -> 9.94 us  [exchanged(): lax.ppermute(value, axis, [(source, source ^ mask) for source in range(co...]
    ppermute x0 -> x13, starting transfers between devices: none -> 5.68 us  [exchanged(): lax.ppermute(value, axis, [(source, source ^ mask) for source in range(co...]
    ppermute x1 -> x2, waiting for transfers between devices: 14.2 us -> 8.62 us  [shifted(): return lax.ppermute(value, axis, pairs)]
  transfers between devices with their start and end apart: 8 -> 15, of which waited for: 8 -> 8; matrix products, arithmetic and copies ran while one was open for 2% -> 0% of each run, Pallas kernels for 0% -> 22%
where the time goes in v2:
time: 42 us; the launch traced here: 41.8 us
  waiting for transfers between devices  18.6 us (44%)
  Pallas kernels  12.9 us (31%)
  starting transfers between devices  10.2 us (24%)
    pallas_call x15, Pallas kernels, call(): return lambda *operands: kernel(*map(place, operands, spaces))  12.9 us
    ppermute x13, waiting for transfers between devices, exchanged(): lax.ppermute(value, axis, [(source, source ^ mask) for source in range(co...  9.94 us
    ppermute x2, waiting for transfers between devices, shifted(): return lax.ppermute(value, axis, pairs)  8.62 us
    ppermute x13, starting transfers between devices, exchanged(): lax.ppermute(value, axis, [(source, source ^ mask) for source in range(co...  5.68 us
    ppermute x2, starting transfers between devices, shifted(): return lax.ppermute(value, axis, pairs)  4.52 us
  transfers between devices with their start and end apart: 15, of which 8 were waited for; matrix products, arithmetic and copies ran while one was open for 0% of the time, Pallas kernels for 22%

profile of v2, /device:TPU:0, one launch (start us, length us, event | category | flops | bytes accessed | tf_op | source)
XLA Modules:
  0.0 41.8 jit_solution(6702557045662411163)
XLA Ops:
  0.0 0.5 %collective-permute-start = (bf16[128,2048]{1,0:T(8,128)(2,1)}, bf16[128,2048]{1,0:T(8,128)(2,1)S(1)}, u32[]{:S(2)}, u32[]{:S(2)}) collective-permute-start(bf16[128,2048]{1,0:T(8,128)(2,1)} %bitcast.6), channel_id=1, source_target_pairs={{0,1},{1,0},{2,3},{3,2},{4,5},{5,4},{6,7},{7,6},{8,9},{9,8},{10,11... | collective-permute-start | bytes 1572872 | tf_op jit(solution)/shard_map/layer_one/ppermute | solution.py:28
  0.5 2.0 %layer_one.3 = (bf16[128,2048]{1,0:T(8,128)(2,1)S(1)}, bf16[4096,384]{1,0:T(8,128)(2,1)S(1)}, f32[128,384]{1,0:T(8,128)S(1)}, f32[128,128]{1,0:T(8,128)S(1)}) custom-call(bf16[1,128,2048]{2,1,0:T(8,128)(2,1)} %own_hbm.1, bf16[1,4096,128]{2,1,0:T(8,128)(2,1)} %wq_hbm.1, bf16[1,4096,128]{2,1,0:T(8,128)(2,1)} %wk_hbm.1, bf16[1,4096,128]{2,1,0:T(8,128)(2,1)} %wv_hbm.1), custom_call_target="tpu_custom_call" | custom-call | tf_op jit(solution)/shard_map/layer_one/pallas_call | solution.py:68
  2.5 0.0 collective-permute-done.oth_ref
  2.5 2.0 %layer_one.4 = (f32[128,2048]{1,0:T(8,128)S(1)}, bf16[128,2048]{1,0:T(8,128)(2,1)S(1)}, bf16[128,2048]{1,0:T(8,128)(2,1)S(1)}, bf16[128,2048]{1,0:T(8,128)(2,1)S(1)}) custom-call(s32[4]{0:T(128)} %bitcast.3, bf16[128,2048]{1,0:T(8,128)(2,1)S(1)} %get-tuple-element.29.own_ref, bf16[128,2048]{1,0:T(8,128)(2,1)S(1)} %collective-permute-done.oth_ref, ...), custom_call_target="tpu_custom_call" | custom-call | tf_op jit(solution)/shard_map/layer_one/pallas_call | solution.py:68
  4.6 0.1 collective-permute-start.1
  4.7 1.9 %collective-permute-done.1.part_ref = bf16[128,2048]{1,0:T(8,128)(2,1)S(1)} collective-permute-done((bf16[128,2048]{1,0:T(8,128)(2,1)S(1)}, bf16[128,2048]{1,0:T(8,128)(2,1)S(1)}, u32[]{:S(2)}, u32[]{:S(2)}) %collective-permute-start.1) | collective-permute-done | bytes 524320 | tf_op jit(solution)/shard_map/layer_one/ppermute | solution.py:28
  6.5 0.1 layer_one.5
  6.6 0.2 collective-permute-start.3
  6.8 2.9 %collective-permute-start.4 = (bf16[128,1024]{1,0:T(8,128)(2,1)S(1)}, bf16[128,1024]{1,0:T(8,128)(2,1)S(1)}, u32[]{:S(2)}, u32[]{:S(2)}) collective-permute-start(bf16[128,1024]{1,0:T(8,128)(2,1)S(1)} %get-tuple-element.38), channel_id=1, source_target_pairs={{0,8},{8,16},{16,24},{24,0},{1,9},{9,17},{17,25},{25,1},{2,10},{10... | collective-permute-start | bytes 786440 | tf_op jit(solution)/shard_map/hop/ppermute | solution.py:23
  9.8 1.6 %collective-permute-start.2 = (bf16[128,1024]{1,0:T(8,128)(2,1)S(1)}, bf16[128,1024]{1,0:T(8,128)(2,1)S(1)}, u32[]{:S(2)}, u32[]{:S(2)}) collective-permute-start(bf16[128,1024]{1,0:T(8,128)(2,1)S(1)} %get-tuple-element.35), channel_id=1, source_target_pairs={{0,8},{8,16},{16,24},{24,0},{1,9},{9,17},{17,25},{25,1},{2,10},{10... | collective-permute-start | bytes 786440 | tf_op jit(solution)/shard_map/hop/ppermute | solution.py:23
  11.3 7.5 %collective-permute-done.4.own_ref = bf16[128,1024]{1,0:T(8,128)(2,1)S(1)} collective-permute-done((bf16[128,1024]{1,0:T(8,128)(2,1)S(1)}, bf16[128,1024]{1,0:T(8,128)(2,1)S(1)}, u32[]{:S(2)}, u32[]{:S(2)}) %collective-permute-start.4) | collective-permute-done | bytes 262176 | tf_op jit(solution)/shard_map/hop/ppermute | solution.py:23
  18.9 0.0 collective-permute-done.3.w_oth_ref
  18.9 3.5 %weights.2 = (bf16[2048,1024]{1,0:T(8,128)(2,1)S(1)}, f32[256,512]{1,0:T(8,128)S(1)}, f32[256,512]{1,0:T(8,128)S(1)}) custom-call(bf16[128,2048]{1,0:T(8,128)(2,1)S(1)} %get-tuple-element.36.w_own_ref, bf16[128,2048]{1,0:T(8,128)(2,1)S(1)} %collective-permute-done.3.w_oth_ref, bf16[2048,1024]{1,0:T(8,128)(2,1)} %e_hbm), custom_call_target="tpu_custom_call" | custom-call | tf_op jit(solution)/shard_map/weights/pallas_call | solution.py:68
  22.4 0.1 collective-permute-start.8
  22.4 0.5 %collective-permute-start.5 = (bf16[128,1024]{1,0:T(8,128)(2,1)S(1)}, bf16[128,1024]{1,0:T(8,128)(2,1)S(1)}, u32[]{:S(2)}, u32[]{:S(2)}) collective-permute-start(bf16[128,1024]{1,0:T(8,128)(2,1)S(1)} %collective-permute-done.4.own_ref), channel_id=1, source_target_pairs={{0,1},{1,0},{2,3},{3,2},{4,5},{5,4},{6,7},{7,6},{8,9},{9,8},{10,11... | collective-permute-start | bytes 786440 | tf_op jit(solution)/shard_map/layer_two/ppermute | solution.py:28
  22.9 1.1 %collective-permute-done.2.own_ref = bf16[128,1024]{1,0:T(8,128)(2,1)S(1)} collective-permute-done((bf16[128,1024]{1,0:T(8,128)(2,1)S(1)}, bf16[128,1024]{1,0:T(8,128)(2,1)S(1)}, u32[]{:S(2)}, u32[]{:S(2)}) %collective-permute-start.2) | collective-permute-done | bytes 262176 | tf_op jit(solution)/shard_map/hop/ppermute | solution.py:23
  24.0 0.0 collective-permute-start.7
  24.0 0.6 %layer_two.6 = (f32[128,384]{1,0:T(8,128)S(1)}, f32[128,128]{1,0:T(8,128)S(1)}, f32[128,1024]{1,0:T(8,128)S(1)}) custom-call(bf16[128,1024]{1,0:T(8,128)(2,1)S(1)} %collective-permute-done.4.own_ref, bf16[4096,384]{1,0:T(8,128)(2,1)S(1)} %get-tuple-element.30.w_ref, bf16[2048,1024]{1,0:T(8,128)(2,1)S(1)} %get-tuple-element.41.e_ref), custom_call_target="tpu_custom_call" | custom-call | tf_op jit(solution)/shard_map/layer_two/pallas_call | solution.py:68
  24.6 0.1 collective-permute-done.5.oth_ref
  24.7 0.3 layer_two.7
  25.0 0.0 copy-start
  25.0 0.6 %layer_two.8 = (f32[128,384]{1,0:T(8,128)S(1)}, f32[128,128]{1,0:T(8,128)S(1)}, f32[128,512]{1,0:T(8,128)S(1)}, bf16[128,512]{1,0:T(8,128)(2,1)S(1)}) custom-call(bf16[128,1024]{1,0:T(8,128)(2,1)S(1)} %collective-permute-done.2.own_ref, bf16[4096,384]{1,0:T(8,128)(2,1)S(1)} %get-tuple-element.30.w_ref, bf16[2048,1024]{1,0:T(8,128)(2,1)S(1)} %get-tuple-element.41.e_ref, ...), custom_call_target="tpu_custom_call" | custom-call | tf_op jit(solution)/shard_map/layer_two/pallas_call | solution.py:68
  25.7 0.5 %collective-permute-start.6 = (bf16[128,512]{1,0:T(8,128)(2,1)S(1)}, bf16[128,512]{1,0:T(8,128)(2,1)S(1)}, u32[]{:S(2)}, u32[]{:S(2)}) collective-permute-start(bf16[128,512]{1,0:T(8,128)(2,1)S(1)} %get-tuple-element.48), channel_id=1, source_target_pairs={{0,1},{1,0},{2,3},{3,2},{4,5},{5,4},{6,7},{7,6},{8,9},{9,8},{10,11... | collective-permute-start | bytes 393224 | tf_op jit(solution)/shard_map/layer_two/ppermute | solution.py:28
  26.1 0.0 collective-permute-done.7.oth_ref
  26.1 0.0 copy-done
  26.1 1.3 %layer_two.9.mixed_ref = bf16[128,128]{1,0:T(8,128)(2,1)S(1)} custom-call(s32[4]{0:T(128)S(1)} %bitcast.4, bf16[128,1024]{1,0:T(8,128)(2,1)S(1)} %collective-permute-done.7.oth_ref, bf16[4096,384]{1,0:T(8,128)(2,1)S(1)} %get-tuple-element.30.w_ref, f32[128,384]{1,0:T(8,128)S(1)} %get-tuple-element.49.sum_ref, f32[128,128]{1,0:T(8,128)S(1)} %get-tuple-element.50.square_in_ref), custom_call_target="tpu_custom_call" | custom-call | tf_op jit(solution)/shard_map/layer_two/pallas_call | solution.py:68
  27.4 0.2 collective-permute-start.9
  27.6 0.0 collective-permute-done.8.recv_ref
  27.6 0.0 collective-permute-done.6.recv_ref
  27.6 0.2 layer_two.10.sum_ref
  27.8 0.9 %collective-permute-done.9.mixed_ref = bf16[128,128]{1,0:T(8,128)(2,1)S(1)} collective-permute-done((bf16[128,128]{1,0:T(8,128)(2,1)S(1)}, bf16[128,128]{1,0:T(8,128)(2,1)S(1)}, u32[]{:S(2)}, u32[]{:S(2)}) %collective-permute-start.9) | collective-permute-done | bytes 32800 | tf_op jit(solution)/shard_map/layer_two/ppermute | solution.py:28
  28.7 0.7 %layer_two.11.refs_0_.refs_1_.refs_2_ = bf16[128,512]{1,0:T(8,128)(2,1)S(1)} custom-call(s32[4]{0:T(128)S(1)} %bitcast.5, f32[128,512]{1,0:T(8,128)S(1)} %layer_two.10.sum_ref, bf16[128,128]{1,0:T(8,128)(2,1)S(1)} %collective-permute-done.9.mixed_ref, bf16[256,512]{1,0:T(8,128)(2,1)S(1)} %weights.3.combined_ref), custom_call_target="tpu_custom_call" | custom-call | tf_op jit(solution)/shard_map/layer_two/pallas_call | solution.py:68
  29.4 1.6 %collective-permute-start.13 = (bf16[128,512]{1,0:T(8,128)(2,1)S(1)}, bf16[128,512]{1,0:T(8,128)(2,1)S(1)}, u32[]{:S(2)}, u32[]{:S(2)}) collective-permute-start(bf16[128,512]{1,0:T(8,128)(2,1)S(1)} %layer_two.11.refs_0_.refs_1_.refs_2_), channel_id=1, source_target_pairs={{0,2},{2,0},{4,6},{6,4},{1,3},{3,1},{5,7},{7,5},{8,10},{10,8},{12,... | collective-permute-start | bytes 393224 | tf_op jit(solution)/shard_map/moments/ppermute | solution.py:28
  31.0 1.5 %collective-permute-start.10 = (bf16[128,512]{1,0:T(8,128)(2,1)S(1)}, bf16[128,512]{1,0:T(8,128)(2,1)S(1)}, u32[]{:S(2)}, u32[]{:S(2)}) collective-permute-start(bf16[128,512]{1,0:T(8,128)(2,1)S(1)} %layer_two.11.refs_0_.refs_1_.refs_2_), channel_id=1, source_target_pairs={{0,4},{2,6},{4,0},{6,2},{1,5},{3,7},{5,1},{7,3},{8,12},{10,14},{12... | collective-permute-start | bytes 393224 | tf_op jit(solution)/shard_map/moments/ppermute | solution.py:28
  32.5 0.5 %collective-permute-start.11 = (bf16[128,512]{1,0:T(8,128)(2,1)S(1)}, bf16[128,512]{1,0:T(8,128)(2,1)S(1)}, u32[]{:S(2)}, u32[]{:S(2)}) collective-permute-start(bf16[128,512]{1,0:T(8,128)(2,1)S(1)} %layer_two.11.refs_0_.refs_1_.refs_2_), channel_id=1, source_target_pairs={{0,6},{2,4},{4,2},{6,0},{1,7},{3,5},{5,3},{7,1},{8,14},{10,12},{12... | collective-permute-start | bytes 393224 | tf_op jit(solution)/shard_map/moments/ppermute | solution.py:28
  32.9 2.2 %collective-permute-done.13.refs_2_.refs_3_ = bf16[128,512]{1,0:T(8,128)(2,1)S(1)} collective-permute-done((bf16[128,512]{1,0:T(8,128)(2,1)S(1)}, bf16[128,512]{1,0:T(8,128)(2,1)S(1)}, u32[]{:S(2)}, u32[]{:S(2)}) %collective-permute-start.13) | collective-permute-done | bytes 131104 | tf_op jit(solution)/shard_map/moments/ppermute | solution.py:28
  35.1 0.2 moments.5.refs_0_
  35.4 0.1 collective-permute-start.14
  35.5 3.8 %collective-permute-done.10.refs_1_.refs_2_ = bf16[128,512]{1,0:T(8,128)(2,1)S(1)} collective-permute-done((bf16[128,512]{1,0:T(8,128)(2,1)S(1)}, bf16[128,512]{1,0:T(8,128)(2,1)S(1)}, u32[]{:S(2)}, u32[]{:S(2)}) %collective-permute-start.10) | collective-permute-done | bytes 131104 | tf_op jit(solution)/shard_map/moments/ppermute | solution.py:28
  39.2 0.0 collective-permute-done.11.refs_2_.refs_3_
  39.2 0.2 moments.4.refs_0_
  39.5 0.1 collective-permute-start.12
  39.6 0.0 collective-permute-done.14.refs_1_
  39.6 0.2 moments.6.refs_4_
  39.8 1.1 %collective-permute-done.12.refs_1_ = f32[128,256]{1,0:T(8,128)S(1)} collective-permute-done((f32[128,256]{1,0:T(8,128)S(1)}, f32[128,256]{1,0:T(8,128)S(1)}, u32[]{:S(2)}, u32[]{:S(2)}) %collective-permute-start.12) | collective-permute-done | bytes 131104 | tf_op jit(solution)/shard_map/moments/ppermute | solution.py:28
  40.9 0.9 %moments.7 = f32[128,512]{1,0:T(8,128)} custom-call(f32[128,256]{1,0:T(8,128)S(1)} %moments.4.refs_0_, f32[128,256]{1,0:T(8,128)S(1)} %collective-permute-done.12.refs_1_, bf16[128,512]{1,0:T(8,128)(2,1)S(1)} %collective-permute-done.10.refs_1_.refs_2_, bf16[128,512]{1,0:T(8,128)(2,1)S(1)} %collective-permute-done.11.refs_2_.refs_3_, ...), custom_call_target="tpu_custom_call" | custom-call | tf_op jit(solution)/shard_map/moments/pallas_call | solution.py:68
  (1 shorter events, 0.0 us)
Async XLA Ops:
  0.0 2.5 %collective-permute-start = (bf16[128,2048]{1,0:T(8,128)(2,1)}, bf16[128,2048]{1,0:T(8,128)(2,1)S(1)}, u32[]{:S(2)}, u32[]{:S(2)}) collective-permute-start(bf16[128,2048]{1,0:T(8,128)(2,1)} %bitcast.6), channel_id=1, source_target_pairs={{0,1},{1,0},{2,3},{3,2},{4,5},{5,4},{6,7},{7,6},{8,9},{9,8},{10,11... | collective-permute-start | bytes 1572872 | tf_op jit(solution)/shard_map/layer_one/ppermute | solution.py:28
  4.6 2.0 %collective-permute-start.1 = (bf16[128,2048]{1,0:T(8,128)(2,1)S(1)}, bf16[128,2048]{1,0:T(8,128)(2,1)S(1)}, u32[]{:S(2)}, u32[]{:S(2)}) collective-permute-start(bf16[128,2048]{1,0:T(8,128)(2,1)S(1)} %get-tuple-element.34), channel_id=1, source_target_pairs={{0,1},{1,0},{2,3},{3,2},{4,5},{5,4},{6,7},{7,6},{8,9},{9,8},{10,11... | collective-permute-start | bytes 1572872 | tf_op jit(solution)/shard_map/layer_one/ppermute | solution.py:28
  6.6 12.3 %collective-permute-start.3 = (bf16[128,2048]{1,0:T(8,128)(2,1)S(1)}, bf16[128,2048]{1,0:T(8,128)(2,1)S(1)}, u32[]{:S(2)}, u32[]{:S(2)}) collective-permute-start(bf16[128,2048]{1,0:T(8,128)(2,1)S(1)} %get-tuple-element.39), channel_id=1, source_target_pairs={{0,1},{1,0},{2,3},{3,2},{4,5},{5,4},{6,7},{7,6},{8,9},{9,8},{10,11... | collective-permute-start | bytes 1572872 | tf_op jit(solution)/shard_map/weights/ppermute | solution.py:28
  6.8 12.1 %collective-permute-start.4 = (bf16[128,1024]{1,0:T(8,128)(2,1)S(1)}, bf16[128,1024]{1,0:T(8,128)(2,1)S(1)}, u32[]{:S(2)}, u32[]{:S(2)}) collective-permute-start(bf16[128,1024]{1,0:T(8,128)(2,1)S(1)} %get-tuple-element.38), channel_id=1, source_target_pairs={{0,8},{8,16},{16,24},{24,0},{1,9},{9,17},{17,25},{25,1},{2,10},{10... | collective-permute-start | bytes 786440 | tf_op jit(solution)/shard_map/hop/ppermute | solution.py:23
  9.8 14.2 %collective-permute-start.2 = (bf16[128,1024]{1,0:T(8,128)(2,1)S(1)}, bf16[128,1024]{1,0:T(8,128)(2,1)S(1)}, u32[]{:S(2)}, u32[]{:S(2)}) collective-permute-start(bf16[128,1024]{1,0:T(8,128)(2,1)S(1)} %get-tuple-element.35), channel_id=1, source_target_pairs={{0,8},{8,16},{16,24},{24,0},{1,9},{9,17},{17,25},{25,1},{2,10},{10... | collective-permute-start | bytes 786440 | tf_op jit(solution)/shard_map/hop/ppermute | solution.py:23
  22.4 5.2 %collective-permute-start.8 = (f32[256,512]{1,0:T(8,128)S(1)}, f32[256,512]{1,0:T(8,128)S(1)}, u32[]{:S(2)}, u32[]{:S(2)}) collective-permute-start(f32[256,512]{1,0:T(8,128)S(1)} %get-tuple-element.52), channel_id=1, source_target_pairs={{0,1},{1,0},{2,3},{3,2},{4,5},{5,4},{6,7},{7,6},{8,9},{9,8},{10,11... | collective-permute-start | bytes 1572872 | tf_op jit(solution)/shard_map/weights/ppermute | solution.py:28
  22.4 2.3 %collective-permute-start.5 = (bf16[128,1024]{1,0:T(8,128)(2,1)S(1)}, bf16[128,1024]{1,0:T(8,128)(2,1)S(1)}, u32[]{:S(2)}, u32[]{:S(2)}) collective-permute-start(bf16[128,1024]{1,0:T(8,128)(2,1)S(1)} %collective-permute-done.4.own_ref), channel_id=1, source_target_pairs={{0,1},{1,0},{2,3},{3,2},{4,5},{5,4},{6,7},{7,6},{8,9},{9,8},{10,11... | collective-permute-start | bytes 786440 | tf_op jit(solution)/shard_map/layer_two/ppermute | solution.py:28
  24.0 2.1 %collective-permute-start.7 = (bf16[128,1024]{1,0:T(8,128)(2,1)S(1)}, bf16[128,1024]{1,0:T(8,128)(2,1)S(1)}, u32[]{:S(2)}, u32[]{:S(2)}) collective-permute-start(bf16[128,1024]{1,0:T(8,128)(2,1)S(1)} %collective-permute-done.2.own_ref), channel_id=1, source_target_pairs={{0,1},{1,0},{2,3},{3,2},{4,5},{5,4},{6,7},{7,6},{8,9},{9,8},{10,11... | collective-permute-start | bytes 786440 | tf_op jit(solution)/shard_map/layer_two/ppermute | solution.py:28
  25.0 1.1 %copy-start = (s32[4,1]{0,1:T(1,128)S(1)}, s32[4,1]{0,1:T(1,128)}, u32[]{:S(2)}) copy-start(s32[4,1]{0,1:T(1,128)} %param.8) | copy-start | bytes 52
  25.7 2.0 %collective-permute-start.6 = (bf16[128,512]{1,0:T(8,128)(2,1)S(1)}, bf16[128,512]{1,0:T(8,128)(2,1)S(1)}, u32[]{:S(2)}, u32[]{:S(2)}) collective-permute-start(bf16[128,512]{1,0:T(8,128)(2,1)S(1)} %get-tuple-element.48), channel_id=1, source_target_pairs={{0,1},{1,0},{2,3},{3,2},{4,5},{5,4},{6,7},{7,6},{8,9},{9,8},{10,11... | collective-permute-start | bytes 393224 | tf_op jit(solution)/shard_map/layer_two/ppermute | solution.py:28
  27.4 1.3 %collective-permute-start.9 = (bf16[128,128]{1,0:T(8,128)(2,1)S(1)}, bf16[128,128]{1,0:T(8,128)(2,1)S(1)}, u32[]{:S(2)}, u32[]{:S(2)}) collective-permute-start(bf16[128,128]{1,0:T(8,128)(2,1)S(1)} %layer_two.9.mixed_ref), channel_id=1, source_target_pairs={{0,1},{1,0},{2,3},{3,2},{4,5},{5,4},{6,7},{7,6},{8,9},{9,8},{10,11... | collective-permute-start | bytes 98312 | tf_op jit(solution)/shard_map/layer_two/ppermute | solution.py:28
  29.4 5.8 %collective-permute-start.13 = (bf16[128,512]{1,0:T(8,128)(2,1)S(1)}, bf16[128,512]{1,0:T(8,128)(2,1)S(1)}, u32[]{:S(2)}, u32[]{:S(2)}) collective-permute-start(bf16[128,512]{1,0:T(8,128)(2,1)S(1)} %layer_two.11.refs_0_.refs_1_.refs_2_), channel_id=1, source_target_pairs={{0,2},{2,0},{4,6},{6,4},{1,3},{3,1},{5,7},{7,5},{8,10},{10,8},{12,... | collective-permute-start | bytes 393224 | tf_op jit(solution)/shard_map/moments/ppermute | solution.py:28
  31.0 8.3 %collective-permute-start.10 = (bf16[128,512]{1,0:T(8,128)(2,1)S(1)}, bf16[128,512]{1,0:T(8,128)(2,1)S(1)}, u32[]{:S(2)}, u32[]{:S(2)}) collective-permute-start(bf16[128,512]{1,0:T(8,128)(2,1)S(1)} %layer_two.11.refs_0_.refs_1_.refs_2_), channel_id=1, source_target_pairs={{0,4},{2,6},{4,0},{6,2},{1,5},{3,7},{5,1},{7,3},{8,12},{10,14},{12... | collective-permute-start | bytes 393224 | tf_op jit(solution)/shard_map/moments/ppermute | solution.py:28
  32.5 6.8 %collective-permute-start.11 = (bf16[128,512]{1,0:T(8,128)(2,1)S(1)}, bf16[128,512]{1,0:T(8,128)(2,1)S(1)}, u32[]{:S(2)}, u32[]{:S(2)}) collective-permute-start(bf16[128,512]{1,0:T(8,128)(2,1)S(1)} %layer_two.11.refs_0_.refs_1_.refs_2_), channel_id=1, source_target_pairs={{0,6},{2,4},{4,2},{6,0},{1,7},{3,5},{5,3},{7,1},{8,14},{10,12},{12... | collective-permute-start | bytes 393224 | tf_op jit(solution)/shard_map/moments/ppermute | solution.py:28
  35.4 4.2 %collective-permute-start.14 = (f32[128,256]{1,0:T(8,128)S(1)}, f32[128,256]{1,0:T(8,128)S(1)}, u32[]{:S(2)}, u32[]{:S(2)}) collective-permute-start(f32[128,256]{1,0:T(8,128)S(1)} %moments.5.refs_0_), channel_id=1, source_target_pairs={{0,1},{1,0},{2,3},{3,2},{4,5},{5,4},{6,7},{7,6},{8,9},{9,8},{10,11... | collective-permute-start | bytes 393224 | tf_op jit(solution)/shard_map/moments/ppermute | solution.py:28
  39.5 1.4 %collective-permute-start.12 = (f32[128,256]{1,0:T(8,128)S(1)}, f32[128,256]{1,0:T(8,128)S(1)}, u32[]{:S(2)}, u32[]{:S(2)}) collective-permute-start(f32[128,256]{1,0:T(8,128)S(1)} %moments.4.refs_0_), channel_id=1, source_target_pairs={{0,1},{1,0},{2,3},{3,2},{4,5},{5,4},{6,7},{7,6},{8,9},{9,8},{10,11... | collective-permute-start | bytes 393224 | tf_op jit(solution)/shard_map/moments/ppermute | solution.py:28

commit v3 on v2

--- a/solution.py
+++ b/solution.py
@@ -14,7 +14,8 @@
 BF16 = jnp.bfloat16
 F32 = jnp.float32
 VMEM_BYTES = 18 * 1024 * 1024
-SHARES = (8, 8)
+SHARES = (7, 9)
+DP_ORDER = lambda count: reversed(range(1, count))
 
 
 def shifted(value, axis, steps):
@@ -123,8 +124,8 @@
 
 
 def first_body(
-    lens_hbm, own_ref, oth_ref, w_ref, qkv_ref, square_ref, wo_hbm,
-    held_ref, part_ref, wo_own_ref, wo_send_ref, sems, lens_ref,
+    lens_hbm, oth_ref, w_ref, qkv_ref, square_ref, wo_hbm,
+    mixed_ref, part_ref, wo_own_ref, wo_send_ref, sems, lens_ref,
 ):
     half = oth_ref.shape[1]
     core = lax.axis_index("tensor")
@@ -140,10 +141,14 @@
     scale = rms_scale(square_ref[...] + lane_sums(oth), 2 * half)
     copies.pop().wait()
     mixed = softmax_mix(qkv * scale, lens_ref[lax.axis_index("section")])
-    for copy in copies:
-        copy.wait()
+    copies[0].wait()
     part_ref[...] = dot(mixed, wo_send_ref[...]).astype(BF16)
-    held_ref[...] = own_ref[...].astype(F32) + dot(mixed, wo_own_ref[...])
+    mixed_ref[...] = mixed
+    copies[1].wait()
+
+
+def held_body(own_ref, mixed_ref, wo_own_ref, held_ref):
+    held_ref[...] = own_ref[...].astype(F32) + dot(mixed_ref[...], wo_own_ref[...])
 
 
 def update_body(held_ref, part_ref, *outs):
@@ -155,7 +160,7 @@
         lower = upper
 
 
-def combine_body(w_own_ref, w_oth_ref, e_hbm, e_ref, mine_ref, send_ref, sems):
+def combine_body(lens_ref, w_own_ref, w_oth_ref, e_hbm, e_ref, mine_ref, send_ref, live_ref, sems):
     blocks = sems.shape[0]
     depth = e_ref.shape[0] // blocks
     copies = []
@@ -166,10 +171,11 @@
     cols = mine_ref.shape[1]
     core = lax.axis_index("tensor")
     weight = jnp.concatenate([w_own_ref[...], w_oth_ref[...]], axis=0)
+    live_ref[...] = jnp.full(live_ref.shape, lens_ref[hop_anchor()], jnp.int32)
     for copy in copies:
         copy.wait()
     mine_ref[...] = dot(weight, e_ref[:, span(core * cols, cols)])
-    send_ref[...] = dot(weight, e_ref[:, span((1 - core) * cols, cols)])
+    send_ref[...] = dot(weight, e_ref[:, span((1 - core) * cols, cols)]).astype(BF16)
 
 
 def own_body(lower, own_ref, w_ref, e_ref, *refs):
@@ -220,10 +226,10 @@
     return lax.rem(lax.axis_index("section") + sections - 1, sections)
 
 
-def second_body(lower, half, lens_ref, oth_ref, w_ref, sum_ref, square_in_ref, mixed_ref):
+def second_body(lower, half, live_ref, oth_ref, w_ref, sum_ref, square_in_ref, mixed_ref):
     qkv, square = other_sums(lower, half, oth_ref, w_ref)
     scale = rms_scale(square_in_ref[...] + square, 2 * half)
-    mixed_ref[...] = softmax_mix((sum_ref[...] + qkv) * scale, lens_ref[hop_anchor()])
+    mixed_ref[...] = softmax_mix((sum_ref[...] + qkv) * scale, live_ref[...])
 
 
 def combine_sum_body(mine_ref, recv_ref, out_ref):
@@ -237,10 +243,13 @@
     out_ref[...] = mine_ref[...] + recv_ref[...].astype(F32) + product
 
 
-def embed_body(lens_ref, sum_ref, mixed_ref, combined_ref, out_ref):
+def embed_body(live_ref, sum_ref, mixed_ref, combined_ref, out_ref):
     embed = sum_ref[...] + dot(mixed_ref[...], combined_ref[mixed_ref.shape[1] :, :])
-    row_pos = lax.broadcasted_iota(jnp.int32, embed.shape, 0)
-    out_ref[...] = jnp.where(row_pos < lens_ref[hop_anchor()], embed, 0.0).astype(BF16)
+    live = live_ref[...]
+    keep = lax.broadcasted_iota(jnp.int32, live.shape, 0) < live
+    for lane in range(0, embed.shape[1], HD):
+        cols = slice(lane, lane + HD)
+        out_ref[:, cols] = jnp.where(keep, embed[:, cols], 0.0).astype(BF16)
 
 
 def gram_body(*refs):
@@ -287,32 +296,37 @@
             "hhhh",
             7,
                     )(tokens, w_query, w_key, w_value)
-        held, part, wo_own, wo_send = call(
+        mixed, part, wo_own, wo_send = call(
             first_body,
-            [shape(rows, half, dtype=F32)] + [shape(rows, half)] + [shape(HD, half)] * 2,
-            "hvvvvvh",
+            [shape(rows, HD), shape(rows, half)] + [shape(HD, half)] * 2,
+            "hvvvvh",
             3,
             scratch=(pltpu.SMEM(lens.shape, jnp.int32),),
-        )(lens, own, oth, w_own, qkv, square, w_out)
+        )(lens, oth, w_own, qkv, square, w_out)
         part = exchanged(part, "tensor", 1)
+        held = call(held_body, shape(rows, half, dtype=F32), "vvv")(own, mixed, wo_own)
         state = call(update_body, [shape(rows, width) for width in widths], "vv")(held, part)
     with jax.named_scope("weights"):
         wo_oth = exchanged(after(wo_send, state[0]), "tensor", 1)
     with jax.named_scope("hop"):
         state = [shifted(piece, "section", 1) for piece in state]
     with jax.named_scope("weights"):
-        w_embed_own, c_mine, c_send = call(
+        w_embed_own, c_mine, c_send, live = call(
             combine_body,
-            [shape(*w_embed.shape)] + [shape(2 * HD, cols, dtype=F32)] * 2,
-            "vvh",
+            [shape(*w_embed.shape)]
+            + [shape(2 * HD, cols, dtype=F32), shape(2 * HD, cols)]
+            + [shape(rows, HD, dtype=jnp.int32)],
+            "svvh",
             4,
-        )(wo_own, wo_oth, after(w_embed, state[0]))
+        )(lens, wo_own, wo_oth, w_embed)
         combined = call(combine_sum_body, shape(2 * HD, cols), "vv")(
             c_mine, exchanged(c_send, "tensor", 1)
         )
     with jax.named_scope("layer_two"):
         sums = ()
         for lower, piece in zip(lowers, state):
+            if sums:
+                piece, combined, *sums = lax.optimization_barrier((piece, combined, *sums))
             oth = exchanged(piece, "tensor", 1)
             if lower != lowers[-1]:
                 qkv, square, embed = call(
@@ -335,15 +349,15 @@
                 )(piece, w_own, w_embed_own, *sums)
         e_recv = exchanged(e_send, "tensor", 1)
         mixed = call(
-            functools.partial(second_body, lower, half), shape(rows, HD), "svvvv"
-        )(lens, oth, w_own, qkv, square)
+            functools.partial(second_body, lower, half), shape(rows, HD), "vvvvv"
+        )(live, oth, w_own, qkv, square)
         mixed_oth = exchanged(mixed, "tensor", 1)
         embed = call(embed_own_body, shape(rows, cols, dtype=F32), "vvvv")(
             e_mine, e_recv, mixed, combined
         )
-        embed = call(embed_body, shape(rows, cols), "svvv")(lens, embed, mixed_oth, combined)
+        embed = call(embed_body, shape(rows, cols), "vvvv")(live, embed, mixed_oth, combined)
     with jax.named_scope("moments"):
-        embeds = [embed] + [exchanged(embed, "dp", mask) for mask in range(1, group_count)]
+        embeds = [embed] + [exchanged(embed, "dp", mask) for mask in DP_ORDER(group_count)]
         result = ()
         for part in (embeds[:2], embeds[2:]):
             gram = call(gram_body, shape(rows, rows * len(part), dtype=F32), "v" * (1 + len(part)))(

time: 42 us -> 39.8 us (0.948)
  waiting for transfers between devices: 18.6 us -> 17.1 us
    ppermute x2, waiting for transfers between devices: 8.62 us -> 6.72 us  [shifted(): return lax.ppermute(value, axis, pairs)]
    pallas_call x15 -> x16, Pallas kernels: 12.9 us -> 12.6 us  [call(): return lambda *operands: kernel(*map(place, operands, spaces))]
  transfers between devices with their start and end apart: 15 -> 15, of which waited for: 8 -> 10; matrix products, arithmetic and copies ran while one was open for 0% -> 0% of each run, Pallas kernels for 22% -> 24%
where the time goes in v3:
time: 39.8 us; the launch traced here: 39.7 us
  waiting for transfers between devices  17.1 us (43%)
  Pallas kernels  12.6 us (32%)
  starting transfers between devices  9.84 us (25%)
    pallas_call x16, Pallas kernels, call(): return lambda *operands: kernel(*map(place, operands, spaces))  12.6 us
    ppermute x13, waiting for transfers between devices, exchanged(): lax.ppermute(value, axis, [(source, source ^ mask) for source in range(co...  10.3 us
    ppermute x2, waiting for transfers between devices, shifted(): return lax.ppermute(value, axis, pairs)  6.72 us
    ppermute x13, starting transfers between devices, exchanged(): lax.ppermute(value, axis, [(source, source ^ mask) for source in range(co...  5.32 us
    ppermute x2, starting transfers between devices, shifted(): return lax.ppermute(value, axis, pairs)  4.52 us
  transfers between devices with their start and end apart: 15, of which 10 were waited for; matrix products, arithmetic and copies ran while one was open for 0% of the time, Pallas kernels for 24%

profile of v3, /device:TPU:0, one launch (start us, length us, event | category | flops | bytes accessed | tf_op | source)
XLA Modules:
  0.0 39.7 jit_solution(2995289527144496600)
XLA Ops:
  0.0 0.5 %collective-permute-start = (bf16[128,2048]{1,0:T(8,128)(2,1)}, bf16[128,2048]{1,0:T(8,128)(2,1)S(1)}, u32[]{:S(2)}, u32[]{:S(2)}) collective-permute-start(bf16[128,2048]{1,0:T(8,128)(2,1)} %bitcast.5), channel_id=1, source_target_pairs={{0,1},{1,0},{2,3},{3,2},{4,5},{5,4},{6,7},{7,6},{8,9},{9,8},{10,11... | collective-permute-start | bytes 1572872 | tf_op jit(solution)/shard_map/layer_one/ppermute | solution.py:29
  0.5 2.0 %layer_one.4 = (bf16[128,2048]{1,0:T(8,128)(2,1)S(1)}, bf16[4096,384]{1,0:T(8,128)(2,1)S(1)}, f32[128,384]{1,0:T(8,128)S(1)}, f32[128,128]{1,0:T(8,128)S(1)}) custom-call(bf16[1,128,2048]{2,1,0:T(8,128)(2,1)} %own_hbm.1, bf16[1,4096,128]{2,1,0:T(8,128)(2,1)} %wq_hbm.1, bf16[1,4096,128]{2,1,0:T(8,128)(2,1)} %wk_hbm.1, bf16[1,4096,128]{2,1,0:T(8,128)(2,1)} %wv_hbm.1), custom_call_target="tpu_custom_call" | custom-call | tf_op jit(solution)/shard_map/layer_one/pallas_call | solution.py:69
  2.5 0.0 collective-permute-done.oth_ref
  2.5 0.0 copy-start
  2.5 1.9 %layer_one.5 = (bf16[128,128]{1,0:T(8,128)(2,1)S(1)}, bf16[128,2048]{1,0:T(8,128)(2,1)S(1)}, bf16[128,2048]{1,0:T(8,128)(2,1)S(1)}, bf16[128,2048]{1,0:T(8,128)(2,1)S(1)}) custom-call(s32[4]{0:T(128)} %bitcast.3, bf16[128,2048]{1,0:T(8,128)(2,1)S(1)} %collective-permute-done.oth_ref, bf16[4096,384]{1,0:T(8,128)(2,1)S(1)} %get-tuple-element.34.w_ref, ...), custom_call_target="tpu_custom_call" | custom-call | tf_op jit(solution)/shard_map/layer_one/pallas_call | solution.py:69
  4.4 0.1 collective-permute-start.1
  4.5 0.3 layer_one.6.held_ref
  4.8 1.6 %collective-permute-done.1.part_ref = bf16[128,2048]{1,0:T(8,128)(2,1)S(1)} collective-permute-done((bf16[128,2048]{1,0:T(8,128)(2,1)S(1)}, bf16[128,2048]{1,0:T(8,128)(2,1)S(1)}, u32[]{:S(2)}, u32[]{:S(2)}) %collective-permute-start.1) | collective-permute-done | bytes 524320 | tf_op jit(solution)/shard_map/layer_one/ppermute | solution.py:29
  6.4 0.1 layer_one.7
  6.5 0.2 collective-permute-start.2
  6.7 2.9 %collective-permute-start.5 = (bf16[128,896]{1,0:T(8,128)(2,1)S(1)}, bf16[128,896]{1,0:T(8,128)(2,1)S(1)}, u32[]{:S(2)}, u32[]{:S(2)}) collective-permute-start(bf16[128,896]{1,0:T(8,128)(2,1)S(1)} %get-tuple-element.42), channel_id=1, source_target_pairs={{0,8},{8,16},{16,24},{24,0},{1,9},{9,17},{17,25},{25,1},{2,10},{10... | collective-permute-start | bytes 688136 | tf_op jit(solution)/shard_map/hop/ppermute | solution.py:24
  9.6 1.6 %collective-permute-start.3 = (bf16[128,1152]{1,0:T(8,128)(2,1)S(1)}, bf16[128,1152]{1,0:T(8,128)(2,1)S(1)}, u32[]{:S(2)}, u32[]{:S(2)}) collective-permute-start(bf16[128,1152]{1,0:T(8,128)(2,1)S(1)} %get-tuple-element.45), channel_id=1, source_target_pairs={{0,8},{8,16},{16,24},{24,0},{1,9},{9,17},{17,25},{25,1},{2,10},{10... | collective-permute-start | bytes 884744 | tf_op jit(solution)/shard_map/hop/ppermute | solution.py:24
  11.2 0.0 collective-permute-done.2.w_oth_ref
  11.2 0.0 copy-done
  11.2 4.0 %weights.2 = (bf16[2048,1024]{1,0:T(8,128)(2,1)S(1)}, f32[256,512]{1,0:T(8,128)S(1)}, bf16[256,512]{1,0:T(8,128)(2,1)S(1)}, s32[128,128]{1,0:T(8,128)S(1)}) custom-call(s32[4]{0:T(128)S(1)} %bitcast.4, bf16[128,2048]{1,0:T(8,128)(2,1)S(1)} %get-tuple-element.37.wo_own_ref.w_own_ref, bf16[128,2048]{1,0:T(8,128)(2,1)S(1)} %collective-permute-done.2.w_oth_ref, ...), custom_call_target="tpu_custom_call" | custom-call | tf_op jit(solution)/shard_map/weights/pallas_call | solution.py:69
  15.2 0.1 collective-permute-start.4
  15.3 2.7 %collective-permute-done.5.own_ref = bf16[128,896]{1,0:T(8,128)(2,1)S(1)} collective-permute-done((bf16[128,896]{1,0:T(8,128)(2,1)S(1)}, bf16[128,896]{1,0:T(8,128)(2,1)S(1)}, u32[]{:S(2)}, u32[]{:S(2)}) %collective-permute-start.5) | collective-permute-done | bytes 229408 | tf_op jit(solution)/shard_map/hop/ppermute | solution.py:24
  18.1 0.0 collective-permute-start.6
  18.1 0.6 %layer_two.6 = (f32[128,384]{1,0:T(8,128)S(1)}, f32[128,128]{1,0:T(8,128)S(1)}, f32[128,1024]{1,0:T(8,128)S(1)}) custom-call(bf16[128,896]{1,0:T(8,128)(2,1)S(1)} %collective-permute-done.5.own_ref, bf16[4096,384]{1,0:T(8,128)(2,1)S(1)} %get-tuple-element.34.w_ref, bf16[2048,1024]{1,0:T(8,128)(2,1)S(1)} %get-tuple-element.48.e_ref), custom_call_target="tpu_custom_call" | custom-call | tf_op jit(solution)/shard_map/layer_two/pallas_call | solution.py:69
  18.6 0.9 %collective-permute-done.6.oth_ref = bf16[128,896]{1,0:T(8,128)(2,1)S(1)} collective-permute-done((bf16[128,896]{1,0:T(8,128)(2,1)S(1)}, bf16[128,896]{1,0:T(8,128)(2,1)S(1)}, u32[]{:S(2)}, u32[]{:S(2)}) %collective-permute-start.6) | collective-permute-done | bytes 229408 | tf_op jit(solution)/shard_map/layer_two/ppermute | solution.py:29
  19.5 0.3 layer_two.7
  19.8 0.0 collective-permute-done.4.recv_ref
  19.9 4.0 %collective-permute-done.3.own_ref = bf16[128,1152]{1,0:T(8,128)(2,1)S(1)} collective-permute-done((bf16[128,1152]{1,0:T(8,128)(2,1)S(1)}, bf16[128,1152]{1,0:T(8,128)(2,1)S(1)}, u32[]{:S(2)}, u32[]{:S(2)}) %collective-permute-start.3) | collective-permute-done | bytes 294944 | tf_op jit(solution)/shard_map/hop/ppermute | solution.py:24
  23.9 0.0 collective-permute-start.8
  23.9 0.7 %layer_two.8 = (f32[128,384]{1,0:T(8,128)S(1)}, f32[128,128]{1,0:T(8,128)S(1)}, f32[128,512]{1,0:T(8,128)S(1)}, bf16[128,512]{1,0:T(8,128)(2,1)S(1)}) custom-call(bf16[128,1152]{1,0:T(8,128)(2,1)S(1)} %collective-permute-done.3.own_ref, bf16[4096,384]{1,0:T(8,128)(2,1)S(1)} %get-tuple-element.34.w_ref, bf16[2048,1024]{1,0:T(8,128)(2,1)S(1)} %get-tuple-element.48.e_ref, ...), custom_call_target="tpu_custom_call" | custom-call | tf_op jit(solution)/shard_map/layer_two/pallas_call | solution.py:69
  24.6 0.6 %collective-permute-start.7 = (bf16[128,512]{1,0:T(8,128)(2,1)S(1)}, bf16[128,512]{1,0:T(8,128)(2,1)S(1)}, u32[]{:S(2)}, u32[]{:S(2)}) collective-permute-start(bf16[128,512]{1,0:T(8,128)(2,1)S(1)} %get-tuple-element.59), channel_id=1, source_target_pairs={{0,1},{1,0},{2,3},{3,2},{4,5},{5,4},{6,7},{7,6},{8,9},{9,8},{10,11... | collective-permute-start | bytes 393224 | tf_op jit(solution)/shard_map/layer_two/ppermute | solution.py:29
  25.2 0.3 collective-permute-done.8.oth_ref
  25.5 0.8 %layer_two.9.mixed_ref = bf16[128,128]{1,0:T(8,128)(2,1)S(1)} custom-call(s32[128,128]{1,0:T(8,128)S(1)} %get-tuple-element.44.live_ref, bf16[128,1152]{1,0:T(8,128)(2,1)S(1)} %collective-permute-done.8.oth_ref, bf16[4096,384]{1,0:T(8,128)(2,1)S(1)} %get-tuple-element.34.w_ref, f32[128,384]{1,0:T(8,128)S(1)} %get-tuple-element.60.sum_ref, ...), custom_call_target="tpu_custom_call" | custom-call | tf_op jit(solution)/shard_map/layer_two/pallas_call | solution.py:69
  26.2 0.2 collective-permute-start.9
  26.4 0.0 collective-permute-done.7.recv_ref
  26.4 0.2 layer_two.10.sum_ref
  26.6 0.9 %collective-permute-done.9.mixed_ref = bf16[128,128]{1,0:T(8,128)(2,1)S(1)} collective-permute-done((bf16[128,128]{1,0:T(8,128)(2,1)S(1)}, bf16[128,128]{1,0:T(8,128)(2,1)S(1)}, u32[]{:S(2)}, u32[]{:S(2)}) %collective-permute-start.9) | collective-permute-done | bytes 32800 | tf_op jit(solution)/shard_map/layer_two/ppermute | solution.py:29
  27.5 0.2 layer_two.11.refs_0_.refs_1_.refs_2_
  27.7 2.5 %collective-permute-start.13 = (bf16[128,512]{1,0:T(8,128)(2,1)S(1)}, bf16[128,512]{1,0:T(8,128)(2,1)S(1)}, u32[]{:S(2)}, u32[]{:S(2)}) collective-permute-start(bf16[128,512]{1,0:T(8,128)(2,1)S(1)} %layer_two.11.refs_0_.refs_1_.refs_2_), channel_id=1, source_target_pairs={{0,6},{2,4},{4,2},{6,0},{1,7},{3,5},{5,3},{7,1},{8,14},{10,12},{12... | collective-permute-start | bytes 393224 | tf_op jit(solution)/shard_map/moments/ppermute | solution.py:29
  30.2 0.5 %collective-permute-start.10 = (bf16[128,512]{1,0:T(8,128)(2,1)S(1)}, bf16[128,512]{1,0:T(8,128)(2,1)S(1)}, u32[]{:S(2)}, u32[]{:S(2)}) collective-permute-start(bf16[128,512]{1,0:T(8,128)(2,1)S(1)} %layer_two.11.refs_0_.refs_1_.refs_2_), channel_id=1, source_target_pairs={{0,4},{2,6},{4,0},{6,2},{1,5},{3,7},{5,1},{7,3},{8,12},{10,14},{12... | collective-permute-start | bytes 393224 | tf_op jit(solution)/shard_map/moments/ppermute | solution.py:29
  30.7 0.5 %collective-permute-start.11 = (bf16[128,512]{1,0:T(8,128)(2,1)S(1)}, bf16[128,512]{1,0:T(8,128)(2,1)S(1)}, u32[]{:S(2)}, u32[]{:S(2)}) collective-permute-start(bf16[128,512]{1,0:T(8,128)(2,1)S(1)} %layer_two.11.refs_0_.refs_1_.refs_2_), channel_id=1, source_target_pairs={{0,2},{2,0},{4,6},{6,4},{1,3},{3,1},{5,7},{7,5},{8,10},{10,8},{12,... | collective-permute-start | bytes 393224 | tf_op jit(solution)/shard_map/moments/ppermute | solution.py:29
  31.2 3.3 %collective-permute-done.13.refs_2_.refs_3_ = bf16[128,512]{1,0:T(8,128)(2,1)S(1)} collective-permute-done((bf16[128,512]{1,0:T(8,128)(2,1)S(1)}, bf16[128,512]{1,0:T(8,128)(2,1)S(1)}, u32[]{:S(2)}, u32[]{:S(2)}) %collective-permute-start.13) | collective-permute-done | bytes 131104 | tf_op jit(solution)/shard_map/moments/ppermute | solution.py:29
  34.5 0.2 moments.5.refs_0_
  34.7 0.1 collective-permute-start.14
  34.8 2.2 %collective-permute-done.10.refs_1_.refs_2_ = bf16[128,512]{1,0:T(8,128)(2,1)S(1)} collective-permute-done((bf16[128,512]{1,0:T(8,128)(2,1)S(1)}, bf16[128,512]{1,0:T(8,128)(2,1)S(1)}, u32[]{:S(2)}, u32[]{:S(2)}) %collective-permute-start.10) | collective-permute-done | bytes 131104 | tf_op jit(solution)/shard_map/moments/ppermute | solution.py:29
  37.0 0.1 collective-permute-done.11.refs_2_.refs_3_
  37.1 0.2 moments.4.refs_0_
  37.3 0.1 collective-permute-start.12
  37.4 0.0 collective-permute-done.14.refs_1_
  37.4 0.2 moments.6.refs_4_
  37.6 1.1 %collective-permute-done.12.refs_1_ = f32[128,256]{1,0:T(8,128)S(1)} collective-permute-done((f32[128,256]{1,0:T(8,128)S(1)}, f32[128,256]{1,0:T(8,128)S(1)}, u32[]{:S(2)}, u32[]{:S(2)}) %collective-permute-start.12) | collective-permute-done | bytes 131104 | tf_op jit(solution)/shard_map/moments/ppermute | solution.py:29
  38.8 0.9 %moments.7 = f32[128,512]{1,0:T(8,128)} custom-call(f32[128,256]{1,0:T(8,128)S(1)} %moments.4.refs_0_, f32[128,256]{1,0:T(8,128)S(1)} %collective-permute-done.12.refs_1_, bf16[128,512]{1,0:T(8,128)(2,1)S(1)} %collective-permute-done.10.refs_1_.refs_2_, bf16[128,512]{1,0:T(8,128)(2,1)S(1)} %collective-permute-done.11.refs_2_.refs_3_, ...), custom_call_target="tpu_custom_call" | custom-call | tf_op jit(solution)/shard_map/moments/pallas_call | solution.py:69
  (1 shorter events, 0.0 us)
Async XLA Ops:
  0.0 2.5 %collective-permute-start = (bf16[128,2048]{1,0:T(8,128)(2,1)}, bf16[128,2048]{1,0:T(8,128)(2,1)S(1)}, u32[]{:S(2)}, u32[]{:S(2)}) collective-permute-start(bf16[128,2048]{1,0:T(8,128)(2,1)} %bitcast.5), channel_id=1, source_target_pairs={{0,1},{1,0},{2,3},{3,2},{4,5},{5,4},{6,7},{7,6},{8,9},{9,8},{10,11... | collective-permute-start | bytes 1572872 | tf_op jit(solution)/shard_map/layer_one/ppermute | solution.py:29
  2.5 8.7 %copy-start = (s32[4,1]{0,1:T(1,128)S(1)}, s32[4,1]{0,1:T(1,128)}, u32[]{:S(2)}) copy-start(s32[4,1]{0,1:T(1,128)} %param.8) | copy-start | bytes 52
  4.4 2.0 %collective-permute-start.1 = (bf16[128,2048]{1,0:T(8,128)(2,1)S(1)}, bf16[128,2048]{1,0:T(8,128)(2,1)S(1)}, u32[]{:S(2)}, u32[]{:S(2)}) collective-permute-start(bf16[128,2048]{1,0:T(8,128)(2,1)S(1)} %get-tuple-element.41), channel_id=1, source_target_pairs={{0,1},{1,0},{2,3},{3,2},{4,5},{5,4},{6,7},{7,6},{8,9},{9,8},{10,11... | collective-permute-start | bytes 1572872 | tf_op jit(solution)/shard_map/layer_one/ppermute | solution.py:29
  6.5 4.7 %collective-permute-start.2 = (bf16[128,2048]{1,0:T(8,128)(2,1)S(1)}, bf16[128,2048]{1,0:T(8,128)(2,1)S(1)}, u32[]{:S(2)}, u32[]{:S(2)}) collective-permute-start(bf16[128,2048]{1,0:T(8,128)(2,1)S(1)} %get-tuple-element.43), channel_id=1, source_target_pairs={{0,1},{1,0},{2,3},{3,2},{4,5},{5,4},{6,7},{7,6},{8,9},{9,8},{10,11... | collective-permute-start | bytes 1572872 | tf_op jit(solution)/shard_map/weights/ppermute | solution.py:29
  6.7 11.4 %collective-permute-start.5 = (bf16[128,896]{1,0:T(8,128)(2,1)S(1)}, bf16[128,896]{1,0:T(8,128)(2,1)S(1)}, u32[]{:S(2)}, u32[]{:S(2)}) collective-permute-start(bf16[128,896]{1,0:T(8,128)(2,1)S(1)} %get-tuple-element.42), channel_id=1, source_target_pairs={{0,8},{8,16},{16,24},{24,0},{1,9},{9,17},{17,25},{25,1},{2,10},{10... | collective-permute-start | bytes 688136 | tf_op jit(solution)/shard_map/hop/ppermute | solution.py:24
  9.6 14.2 %collective-permute-start.3 = (bf16[128,1152]{1,0:T(8,128)(2,1)S(1)}, bf16[128,1152]{1,0:T(8,128)(2,1)S(1)}, u32[]{:S(2)}, u32[]{:S(2)}) collective-permute-start(bf16[128,1152]{1,0:T(8,128)(2,1)S(1)} %get-tuple-element.45), channel_id=1, source_target_pairs={{0,8},{8,16},{16,24},{24,0},{1,9},{9,17},{17,25},{25,1},{2,10},{10... | collective-permute-start | bytes 884744 | tf_op jit(solution)/shard_map/hop/ppermute | solution.py:24
  15.2 4.6 %collective-permute-start.4 = (bf16[256,512]{1,0:T(8,128)(2,1)S(1)}, bf16[256,512]{1,0:T(8,128)(2,1)S(1)}, u32[]{:S(2)}, u32[]{:S(2)}) collective-permute-start(bf16[256,512]{1,0:T(8,128)(2,1)S(1)} %get-tuple-element.47), channel_id=1, source_target_pairs={{0,1},{1,0},{2,3},{3,2},{4,5},{5,4},{6,7},{7,6},{8,9},{9,8},{10,11... | collective-permute-start | bytes 786440 | tf_op jit(solution)/shard_map/weights/ppermute | solution.py:29
  18.1 1.5 %collective-permute-start.6 = (bf16[128,896]{1,0:T(8,128)(2,1)S(1)}, bf16[128,896]{1,0:T(8,128)(2,1)S(1)}, u32[]{:S(2)}, u32[]{:S(2)}) collective-permute-start(bf16[128,896]{1,0:T(8,128)(2,1)S(1)} %collective-permute-done.5.own_ref), channel_id=1, source_target_pairs={{0,1},{1,0},{2,3},{3,2},{4,5},{5,4},{6,7},{7,6},{8,9},{9,8},{10,11... | collective-permute-start | bytes 688136 | tf_op jit(solution)/shard_map/layer_two/ppermute | solution.py:29
  23.9 1.6 %collective-permute-start.8 = (bf16[128,1152]{1,0:T(8,128)(2,1)S(1)}, bf16[128,1152]{1,0:T(8,128)(2,1)S(1)}, u32[]{:S(2)}, u32[]{:S(2)}) collective-permute-start(bf16[128,1152]{1,0:T(8,128)(2,1)S(1)} %collective-permute-done.3.own_ref), channel_id=1, source_target_pairs={{0,1},{1,0},{2,3},{3,2},{4,5},{5,4},{6,7},{7,6},{8,9},{9,8},{10,11... | collective-permute-start | bytes 884744 | tf_op jit(solution)/shard_map/layer_two/ppermute | solution.py:29
  24.6 1.8 %collective-permute-start.7 = (bf16[128,512]{1,0:T(8,128)(2,1)S(1)}, bf16[128,512]{1,0:T(8,128)(2,1)S(1)}, u32[]{:S(2)}, u32[]{:S(2)}) collective-permute-start(bf16[128,512]{1,0:T(8,128)(2,1)S(1)} %get-tuple-element.59), channel_id=1, source_target_pairs={{0,1},{1,0},{2,3},{3,2},{4,5},{5,4},{6,7},{7,6},{8,9},{9,8},{10,11... | collective-permute-start | bytes 393224 | tf_op jit(solution)/shard_map/layer_two/ppermute | solution.py:29
  26.2 1.3 %collective-permute-start.9 = (bf16[128,128]{1,0:T(8,128)(2,1)S(1)}, bf16[128,128]{1,0:T(8,128)(2,1)S(1)}, u32[]{:S(2)}, u32[]{:S(2)}) collective-permute-start(bf16[128,128]{1,0:T(8,128)(2,1)S(1)} %layer_two.9.mixed_ref), channel_id=1, source_target_pairs={{0,1},{1,0},{2,3},{3,2},{4,5},{5,4},{6,7},{7,6},{8,9},{9,8},{10,11... | collective-permute-start | bytes 98312 | tf_op jit(solution)/shard_map/layer_two/ppermute | solution.py:29
  27.7 6.8 %collective-permute-start.13 = (bf16[128,512]{1,0:T(8,128)(2,1)S(1)}, bf16[128,512]{1,0:T(8,128)(2,1)S(1)}, u32[]{:S(2)}, u32[]{:S(2)}) collective-permute-start(bf16[128,512]{1,0:T(8,128)(2,1)S(1)} %layer_two.11.refs_0_.refs_1_.refs_2_), channel_id=1, source_target_pairs={{0,6},{2,4},{4,2},{6,0},{1,7},{3,5},{5,3},{7,1},{8,14},{10,12},{12... | collective-permute-start | bytes 393224 | tf_op jit(solution)/shard_map/moments/ppermute | solution.py:29
  30.2 6.8 %collective-permute-start.10 = (bf16[128,512]{1,0:T(8,128)(2,1)S(1)}, bf16[128,512]{1,0:T(8,128)(2,1)S(1)}, u32[]{:S(2)}, u32[]{:S(2)}) collective-permute-start(bf16[128,512]{1,0:T(8,128)(2,1)S(1)} %layer_two.11.refs_0_.refs_1_.refs_2_), channel_id=1, source_target_pairs={{0,4},{2,6},{4,0},{6,2},{1,5},{3,7},{5,1},{7,3},{8,12},{10,14},{12... | collective-permute-start | bytes 393224 | tf_op jit(solution)/shard_map/moments/ppermute | solution.py:29
  30.7 6.4 %collective-permute-start.11 = (bf16[128,512]{1,0:T(8,128)(2,1)S(1)}, bf16[128,512]{1,0:T(8,128)(2,1)S(1)}, u32[]{:S(2)}, u32[]{:S(2)}) collective-permute-start(bf16[128,512]{1,0:T(8,128)(2,1)S(1)} %layer_two.11.refs_0_.refs_1_.refs_2_), channel_id=1, source_target_pairs={{0,2},{2,0},{4,6},{6,4},{1,3},{3,1},{5,7},{7,5},{8,10},{10,8},{12,... | collective-permute-start | bytes 393224 | tf_op jit(solution)/shard_map/moments/ppermute | solution.py:29
  34.7 2.7 %collective-permute-start.14 = (f32[128,256]{1,0:T(8,128)S(1)}, f32[128,256]{1,0:T(8,128)S(1)}, u32[]{:S(2)}, u32[]{:S(2)}) collective-permute-start(f32[128,256]{1,0:T(8,128)S(1)} %moments.5.refs_0_), channel_id=1, source_target_pairs={{0,1},{1,0},{2,3},{3,2},{4,5},{5,4},{6,7},{7,6},{8,9},{9,8},{10,11... | collective-permute-start | bytes 393224 | tf_op jit(solution)/shard_map/moments/ppermute | solution.py:29
  37.3 1.4 %collective-permute-start.12 = (f32[128,256]{1,0:T(8,128)S(1)}, f32[128,256]{1,0:T(8,128)S(1)}, u32[]{:S(2)}, u32[]{:S(2)}) collective-permute-start(f32[128,256]{1,0:T(8,128)S(1)} %moments.4.refs_0_), channel_id=1, source_target_pairs={{0,1},{1,0},{2,3},{3,2},{4,5},{5,4},{6,7},{7,6},{8,9},{9,8},{10,11... | collective-permute-start | bytes 393224 | tf_op jit(solution)/shard_map/moments/ppermute | solution.py:29

commit v4 on v3

--- a/solution.py
+++ b/solution.py
@@ -15,6 +15,7 @@
 F32 = jnp.float32
 VMEM_BYTES = 18 * 1024 * 1024
 SHARES = (7, 9)
+WO_PARTS = 4
 DP_ORDER = lambda count: reversed(range(1, count))
 
 
@@ -55,7 +56,9 @@
         if last
         else jax.tree.map(lambda out: pltpu.VMEM(out.shape, out.dtype), out_shapes),
         in_specs=[pl.BlockSpec(memory_space=SPACES[space]) for space in spaces],
-        out_specs=jax.tree.map(lambda _: pl.BlockSpec(memory_space=pltpu.VMEM), out_shapes),
+        out_specs=jax.tree.map(
+            lambda _: pl.BlockSpec(memory_space=pltpu.HBM if last else pltpu.VMEM), out_shapes
+        ),
         scratch_shapes=([pltpu.SemaphoreType.DMA((copies,))] if copies else []) + list(scratch),
         compiler_params=pltpu.CompilerParams(vmem_limit_bytes=VMEM_BYTES),
         cost_estimate=pl.CostEstimate(flops=0, bytes_accessed=0, transcendentals=0),
@@ -97,70 +100,72 @@
     return dot(probs, value).astype(BF16)
 
 
-def load_body(own_hbm, wq_hbm, wk_hbm, wv_hbm, own_ref, w_ref, qkv_ref, square_ref, sems):
+def load_body(
+    lens_hbm, own_hbm, wq_hbm, wk_hbm, wv_hbm, wo_hbm,
+    own_ref, w_ref, qkv_ref, square_ref, live_ref, *rest,
+):
+    wo_own_ref, *wo_send_refs, sems, lens_ref = rest
     half = own_ref.shape[1]
     core = lax.axis_index("tensor")
-    copies = [pltpu.make_async_copy(own_hbm.at[0], own_ref, sems.at[0])]
-    for part in range(2):
-        rows = span((core if part == 0 else 1 - core) * half, half)
+    pairs = [(lens_hbm, lens_ref), (own_hbm.at[0], own_ref)]
+    for side in (core, 1 - core):
+        rows = span(side * half, half)
         for at, w_hbm in enumerate((wq_hbm, wk_hbm, wv_hbm)):
-            copies.append(
-                pltpu.make_async_copy(
-                    w_hbm.at[0, rows, :],
-                    w_ref.at[rows, at * HD : (at + 1) * HD],
-                    sems.at[len(copies)],
-                )
-            )
+            pairs.append((w_hbm.at[0, rows, :], w_ref.at[rows, at * HD : (at + 1) * HD]))
+    for at, ref in enumerate(wo_send_refs):
+        width = ref.shape[1]
+        pairs.append((wo_hbm.at[0, :, span((1 - core) * half + at * width, width)], ref))
+    pairs.append((wo_hbm.at[0, :, span(core * half, half)], wo_own_ref))
+    copies = [
+        pltpu.make_async_copy(source, target, sems.at[index])
+        for index, (source, target) in enumerate(pairs)
+    ]
     for copy in copies:
         copy.start()
     copies[0].wait()
+    live_ref[...] = jnp.full(live_ref.shape, lens_ref[lax.axis_index("section")], jnp.int32)
+    copies[1].wait()
     own = own_ref[...]
     square_ref[...] = lane_sums(own)
-    for copy in copies[1:4]:
+    for copy in copies[2:5]:
         copy.wait()
     qkv_ref[...] = dot(own, w_ref[span(core * half, half), :])
-    for copy in copies[4:]:
+    for copy in copies[5:]:
         copy.wait()
 
 
-def first_body(
-    lens_hbm, oth_ref, w_ref, qkv_ref, square_ref, wo_hbm,
-    mixed_ref, part_ref, wo_own_ref, wo_send_ref, sems, lens_ref,
-):
+def first_body(live_ref, oth_ref, w_ref, qkv_ref, square_ref, *refs):
+    wo_send_refs, mixed_ref, parts = refs[:WO_PARTS], refs[WO_PARTS], refs[WO_PARTS + 1 :]
     half = oth_ref.shape[1]
     core = lax.axis_index("tensor")
-    copies = [
-        pltpu.make_async_copy(wo_hbm.at[0, :, span(side * half, half)], ref, sems.at[index])
-        for index, (side, ref) in enumerate(((1 - core, wo_send_ref), (core, wo_own_ref)))
-    ]
-    copies.append(pltpu.make_async_copy(lens_hbm, lens_ref, sems.at[2]))
-    for copy in copies:
-        copy.start()
     oth = oth_ref[...]
     qkv = qkv_ref[...] + dot(oth, w_ref[span((1 - core) * half, half), :])
     scale = rms_scale(square_ref[...] + lane_sums(oth), 2 * half)
-    copies.pop().wait()
-    mixed = softmax_mix(qkv * scale, lens_ref[lax.axis_index("section")])
-    copies[0].wait()
-    part_ref[...] = dot(mixed, wo_send_ref[...]).astype(BF16)
+    mixed = softmax_mix(qkv * scale, live_ref[...])
     mixed_ref[...] = mixed
-    copies[1].wait()
+    weight = jnp.concatenate([ref[...] for ref in wo_send_refs], axis=1)
+    lower = 0
+    for part_ref in parts:
+        upper = lower + part_ref.shape[1]
+        part_ref[...] = dot(mixed, weight[:, lower:upper]).astype(BF16)
+        lower = upper
 
 
 def held_body(own_ref, mixed_ref, wo_own_ref, held_ref):
     held_ref[...] = own_ref[...].astype(F32) + dot(mixed_ref[...], wo_own_ref[...])
 
 
-def update_body(held_ref, part_ref, *outs):
-    lower = 0
-    for out_ref in outs:
-        upper = lower + out_ref.shape[1]
-        held, part = held_ref[:, lower:upper], part_ref[:, lower:upper]
-        out_ref[...] = (held + part.astype(F32)).astype(BF16)
-        lower = upper
-
-
-def combine_body(lens_ref, w_own_ref, w_oth_ref, e_hbm, e_ref, mine_ref, send_ref, live_ref, sems):
+def update_body(lower, held_ref, *refs):
+    parts, out_ref = refs[:-1], refs[-1]
+    width = out_ref.shape[1]
+    part = jnp.concatenate([ref[...] for ref in parts], axis=1)
+    part = part[:, part.shape[1] - width :] if len(parts) > 1 else part[:, :width]
+    held = held_ref[:, lower : lower + width]
+    out_ref[...] = (held + part.astype(F32)).astype(BF16)
+
+
+def combine_body(lens_ref, w_own_ref, e_hbm, *refs):
+    w_oth_refs, (e_ref, mine_ref, send_ref, live_ref, sems) = refs[:WO_PARTS], refs[WO_PARTS:]
     blocks = sems.shape[0]
     depth = e_ref.shape[0] // blocks
     copies = []
@@ -170,7 +175,8 @@
         copies[-1].start()
     cols = mine_ref.shape[1]
     core = lax.axis_index("tensor")
-    weight = jnp.concatenate([w_own_ref[...], w_oth_ref[...]], axis=0)
+    w_oth = jnp.concatenate([ref[...] for ref in w_oth_refs], axis=1)
+    weight = jnp.concatenate([w_own_ref[...], w_oth], axis=0)
     live_ref[...] = jnp.full(live_ref.shape, lens_ref[hop_anchor()], jnp.int32)
     for copy in copies:
         copy.wait()
@@ -259,22 +265,39 @@
         out_ref[:, at * rows : (at + 1) * rows] = dot_t(own, embed[...])
 
 
-def result_body(tokens, first, *refs):
-    (gram_own_ref, gram_oth_ref), embeds, out_ref = refs[:2], refs[2:-1], refs[-1]
-    total = None
-    if not first:
-        embeds, total = embeds[:-1], embeds[-1][...]
+def result_sums(tokens, first, gram_own_ref, gram_oth_ref, embeds):
     rows = embeds[0].shape[0]
-    for at, embed in enumerate(embeds):
-        cols = slice(at * rows, (at + 1) * rows)
-        gram = (gram_own_ref[:, cols] + gram_oth_ref[:, cols]) * (1.0 / tokens)
-        if first and at == 0:
-            row = lax.broadcasted_iota(jnp.int32, gram.shape, 0)
-            col = lax.broadcasted_iota(jnp.int32, gram.shape, 1)
-            gram = gram - (row == col).astype(F32)
-        product = dot(gram.astype(BF16), embed[...])
-        total = product if total is None else total + product
-    out_ref[...] = total
+    gram = (gram_own_ref[...] + gram_oth_ref[...]) * (1.0 / tokens)
+    if first:
+        row = lax.broadcasted_iota(jnp.int32, gram.shape, 0)
+        col = lax.broadcasted_iota(jnp.int32, gram.shape, 1)
+        gram = gram - (row == col).astype(F32)
+    gram = gram.astype(BF16)
+    return lambda cols: dot(
+        gram, jnp.concatenate([embed[:, cols] for embed in embeds], axis=0)
+    )
+
+
+def result_body(tokens, gram_own_ref, gram_oth_ref, *refs):
+    embeds, out_ref = refs[:-1], refs[-1]
+    out_ref[...] = result_sums(tokens, True, gram_own_ref, gram_oth_ref, embeds)(slice(None))
+
+
+def result_last_body(tokens, gram_own_ref, gram_oth_ref, *refs):
+    embeds, (sum_ref, out_hbm, sems, out_ref) = refs[:-4], refs[-4:]
+    product = result_sums(tokens, False, gram_own_ref, gram_oth_ref, embeds)
+    chunks = sems.shape[0]
+    width = out_ref.shape[1] // chunks
+    copies = []
+    for chunk in range(chunks):
+        cols = slice(chunk * width, (chunk + 1) * width)
+        out_ref[:, cols] = sum_ref[:, cols] + product(cols)
+        copies.append(
+            pltpu.make_async_copy(out_ref.at[:, cols], out_hbm.at[:, cols], sems.at[chunk])
+        )
+        copies[-1].start()
+    for copy in copies:
+        copy.wait()
 
 
 def shards(tokens, lengths, w_query, w_key, w_value, w_out, w_embed):
@@ -290,24 +313,33 @@
 
     with jax.named_scope("layer_one"):
         oth = exchanged(own_in, "tensor", 1)
-        own, w_own, qkv, square = call(
+        own, w_own, qkv, square, live, wo_own, *wo_send = call(
             load_body,
-            [shape(rows, half), shape(features, QKV), shape(rows, QKV, dtype=F32), shape(rows, HD, dtype=F32)],
-            "hhhh",
-            7,
-                    )(tokens, w_query, w_key, w_value)
-        mixed, part, wo_own, wo_send = call(
-            first_body,
-            [shape(rows, HD), shape(rows, half)] + [shape(HD, half)] * 2,
-            "hvvvvh",
-            3,
+            [
+                shape(rows, half),
+                shape(features, QKV),
+                shape(rows, QKV, dtype=F32),
+                shape(rows, HD, dtype=F32),
+                shape(rows, HD, dtype=jnp.int32),
+                shape(HD, half),
+            ]
+            + [shape(HD, half // WO_PARTS)] * WO_PARTS,
+            "hhhhhh",
+            9 + WO_PARTS,
             scratch=(pltpu.SMEM(lens.shape, jnp.int32),),
-        )(lens, oth, w_own, qkv, square, w_out)
-        part = exchanged(part, "tensor", 1)
+        )(lens, tokens, w_query, w_key, w_value, w_out)
+        mixed, *parts = call(
+            first_body, [shape(rows, HD)] + [shape(rows, half // 2)] * 2, "v" * (5 + WO_PARTS)
+        )(live, oth, w_own, qkv, square, *wo_send)
+        parts = [exchanged(part, "tensor", 1) for part in parts]
         held = call(held_body, shape(rows, half, dtype=F32), "vvv")(own, mixed, wo_own)
-        state = call(update_body, [shape(rows, width) for width in widths], "vv")(held, part)
+        state = []
+        for lower, width in zip(lowers, widths):
+            needed = parts if lower else parts[:1]
+            body = functools.partial(update_body, lower)
+            state.append(call(body, shape(rows, width), "v" * (1 + len(needed)))(held, *needed))
     with jax.named_scope("weights"):
-        wo_oth = exchanged(after(wo_send, state[0]), "tensor", 1)
+        wo_oth = [exchanged(after(part, state[-1]), "tensor", 1) for part in wo_send]
     with jax.named_scope("hop"):
         state = [shifted(piece, "section", 1) for piece in state]
     with jax.named_scope("weights"):
@@ -316,9 +348,9 @@
             [shape(*w_embed.shape)]
             + [shape(2 * HD, cols, dtype=F32), shape(2 * HD, cols)]
             + [shape(rows, HD, dtype=jnp.int32)],
-            "svvh",
+            "svh" + "v" * WO_PARTS,
             4,
-        )(lens, wo_own, wo_oth, w_embed)
+        )(lens, wo_own, w_embed, *wo_oth)
         combined = call(combine_sum_body, shape(2 * HD, cols), "vv")(
             c_mine, exchanged(c_send, "tensor", 1)
         )
@@ -358,21 +390,25 @@
         embed = call(embed_body, shape(rows, cols), "vvvv")(live, embed, mixed_oth, combined)
     with jax.named_scope("moments"):
         embeds = [embed] + [exchanged(embed, "dp", mask) for mask in DP_ORDER(group_count)]
-        result = ()
+        sums = ()
         for part in (embeds[:2], embeds[2:]):
             gram = call(gram_body, shape(rows, rows * len(part), dtype=F32), "v" * (1 + len(part)))(
                 embed, *part
             )
-            operands = (gram, exchanged(gram, "tensor", 1), *part, *result)
-            result = (
+            operands = (gram, exchanged(gram, "tensor", 1), *part, *sums)
+            out = shape(rows, cols, dtype=F32)
+            body = functools.partial(result_last_body if sums else result_body, rows * group_count)
+            sums = (
                 call(
-                    functools.partial(result_body, rows * group_count, not result),
-                    shape(rows, cols, dtype=F32),
+                    body,
+                    out,
                     "v" * len(operands),
-                    last=bool(result),
+                    copies=2 if sums else 0,
+                    last=bool(sums),
+                    scratch=(pltpu.VMEM(out.shape, out.dtype),) if sums else (),
                 )(*operands),
             )
-    return result[0][None]
+    return sums[0][None]
 
 
 def solution(mesh):

time: 39.8 us -> 38.9 us (0.977)
  waiting for transfers between devices: 17.1 us -> 15.3 us
  starting transfers between devices: 9.84 us -> 11 us
  Pallas kernels: 12.6 us -> 12.2 us
    ppermute x13 -> x17, starting transfers between devices: 5.32 us -> 6.67 us  [exchanged(): lax.ppermute(value, axis, [(source, source ^ mask) for source in range(co...]
    ppermute x2, waiting for transfers between devices: 6.72 us -> 5.5 us  [shifted(): return lax.ppermute(value, axis, pairs)]
    ppermute x13 -> x17, waiting for transfers between devices: 10.3 us -> 9.8 us  [exchanged(): lax.ppermute(value, axis, [(source, source ^ mask) for source in range(co...]
    pallas_call x16 -> x17, Pallas kernels: 12.6 us -> 12.2 us  [call(): return lambda *operands: kernel(*map(place, operands, spaces))]
  transfers between devices with their start and end apart: 15 -> 19, of which waited for: 10 -> 11; matrix products, arithmetic and copies ran while one was open for 0% -> 0% of each run, Pallas kernels for 24% -> 26%
where the time goes in v4:
time: 38.9 us; the launch traced here: 38.7 us
  waiting for transfers between devices  15.3 us (39%)
  Pallas kernels  12.2 us (31%)
  starting transfers between devices  11 us (28%)
    pallas_call x17, Pallas kernels, call(): return lambda *operands: kernel(*map(place, operands, spaces))  12.2 us
    ppermute x17, waiting for transfers between devices, exchanged(): lax.ppermute(value, axis, [(source, source ^ mask) for source in range(co...  9.8 us
    ppermute x17, starting transfers between devices, exchanged(): lax.ppermute(value, axis, [(source, source ^ mask) for source in range(co...  6.67 us
    ppermute x2, waiting for transfers between devices, shifted(): return lax.ppermute(value, axis, pairs)  5.5 us
    ppermute x2, starting transfers between devices, shifted(): return lax.ppermute(value, axis, pairs)  4.35 us
  transfers between devices with their start and end apart: 19, of which 11 were waited for; matrix products, arithmetic and copies ran while one was open for 0% of the time, Pallas kernels for 26%

profile of v4, /device:TPU:0, one launch (start us, length us, event | category | flops | bytes accessed | tf_op | source)
XLA Modules:
  0.0 38.7 jit_solution(5892286562276677598)
XLA Ops:
  0.0 0.5 %collective-permute-start = (bf16[128,2048]{1,0:T(8,128)(2,1)}, bf16[128,2048]{1,0:T(8,128)(2,1)S(1)}, u32[]{:S(2)}, u32[]{:S(2)}) collective-permute-start(bf16[128,2048]{1,0:T(8,128)(2,1)} %bitcast.5), channel_id=1, source_target_pairs={{0,1},{1,0},{2,3},{3,2},{4,5},{5,4},{6,7},{7,6},{8,9},{9,8},{10,11... | collective-permute-start | bytes 1572872 | tf_op jit(solution)/shard_map/layer_one/ppermute | solution.py:30
  0.5 2.4 %layer_one.5 = (bf16[128,2048]{1,0:T(8,128)(2,1)S(1)}, bf16[4096,384]{1,0:T(8,128)(2,1)S(1)}, f32[128,384]{1,0:T(8,128)S(1)}, f32[128,128]{1,0:T(8,128)S(1)}, s3...) custom-call(s32[4]{0:T(128)} %bitcast.3, ...), custom_call_target="tpu_custom_call" | custom-call | tf_op jit(solution)/shard_map/layer_one/pallas_call | solution.py:72
  2.9 0.0 collective-permute-done.oth_ref
  2.9 0.0 copy-start
  2.9 1.1 %layer_one.6 = (bf16[128,128]{1,0:T(8,128)(2,1)S(1)}, bf16[128,1024]{1,0:T(8,128)(2,1)S(1)}, bf16[128,1024]{1,0:T(8,128)(2,1)S(1)}) custom-call(s32[128,128]{1,0:T(8,128)S(1)} %get-tuple-element.43.live_ref, bf16[128,2048]{1,0:T(8,128)(2,1)S(1)} %collective-permute-done.oth_ref, bf16[4096,384]{1,0:T(8,128)(2,1)S(1)} %get-tuple-element.44.w_ref, ...), custom_call_target="tpu_custom_call" | custom-call | tf_op jit(solution)/shard_map/layer_one/pallas_call | solution.py:72
  4.0 0.1 collective-permute-start.1
  4.2 0.5 %collective-permute-start.2 = (bf16[128,1024]{1,0:T(8,128)(2,1)S(1)}, bf16[128,1024]{1,0:T(8,128)(2,1)S(1)}, u32[]{:S(2)}, u32[]{:S(2)}) collective-permute-start(bf16[128,1024]{1,0:T(8,128)(2,1)S(1)} %get-tuple-element.52), channel_id=1, source_target_pairs={{0,1},{1,0},{2,3},{3,2},{4,5},{5,4},{6,7},{7,6},{8,9},{9,8},{10,11... | collective-permute-start | bytes 786440 | tf_op jit(solution)/shard_map/layer_one/ppermute | solution.py:30
  4.6 0.3 layer_one.7.held_ref
  4.9 0.7 %collective-permute-done.1.refs_0_ = bf16[128,1024]{1,0:T(8,128)(2,1)S(1)} collective-permute-done((bf16[128,1024]{1,0:T(8,128)(2,1)S(1)}, bf16[128,1024]{1,0:T(8,128)(2,1)S(1)}, u32[]{:S(2)}, u32[]{:S(2)}) %collective-permute-start.1) | collective-permute-done | bytes 262176 | tf_op jit(solution)/shard_map/layer_one/ppermute | solution.py:30
  5.7 2.8 %collective-permute-start.9 = (bf16[128,896]{1,0:T(8,128)(2,1)S(1)}, bf16[128,896]{1,0:T(8,128)(2,1)S(1)}, u32[]{:S(2)}, u32[]{:S(2)}) collective-permute-start(bf16[128,896]{1,0:T(8,128)(2,1)S(1)} %layer_one.9), channel_id=1, source_target_pairs={{0,8},{8,16},{16,24},{24,0},{1,9},{9,17},{17,25},{25,1},{2,10},{10... | collective-permute-start | bytes 688136 | tf_op jit(solution)/shard_map/hop/ppermute | solution.py:25
  8.5 0.0 collective-permute-done.2.refs_1_
  8.5 0.1 layer_one.8
  8.5 0.1 collective-permute-start.6
  8.7 0.4 %collective-permute-start.5 = (bf16[128,512]{1,0:T(8,128)(2,1)S(1)}, bf16[128,512]{1,0:T(8,128)(2,1)S(1)}, u32[]{:S(2)}, u32[]{:S(2)}) collective-permute-start(bf16[128,512]{1,0:T(8,128)(2,1)S(1)} %get-tuple-element.55.refs_2_), channel_id=1, source_target_pairs={{0,1},{1,0},{2,3},{3,2},{4,5},{5,4},{6,7},{7,6},{8,9},{9,8},{10,11... | collective-permute-start | bytes 393224 | tf_op jit(solution)/shard_map/weights/ppermute | solution.py:30
  9.1 0.1 collective-permute-start.4
  9.2 0.4 %collective-permute-start.3 = (bf16[128,512]{1,0:T(8,128)(2,1)S(1)}, bf16[128,512]{1,0:T(8,128)(2,1)S(1)}, u32[]{:S(2)}, u32[]{:S(2)}) collective-permute-start(bf16[128,512]{1,0:T(8,128)(2,1)S(1)} %get-tuple-element.53.refs_0_), channel_id=1, source_target_pairs={{0,1},{1,0},{2,3},{3,2},{4,5},{5,4},{6,7},{7,6},{8,9},{9,8},{10,11... | collective-permute-start | bytes 393224 | tf_op jit(solution)/shard_map/weights/ppermute | solution.py:30
  9.6 0.3 collective-permute-done.6.refs_3_
  9.9 1.6 %collective-permute-start.7 = (bf16[128,1152]{1,0:T(8,128)(2,1)S(1)}, bf16[128,1152]{1,0:T(8,128)(2,1)S(1)}, u32[]{:S(2)}, u32[]{:S(2)}) collective-permute-start(bf16[128,1152]{1,0:T(8,128)(2,1)S(1)} %layer_one.8), channel_id=1, source_target_pairs={{0,8},{8,16},{16,24},{24,0},{1,9},{9,17},{17,25},{25,1},{2,10},{10... | collective-permute-start | bytes 884744 | tf_op jit(solution)/shard_map/hop/ppermute | solution.py:25
  11.5 0.0 collective-permute-done.5.refs_2_
  11.5 0.0 collective-permute-done.4.refs_1_
  11.5 0.0 collective-permute-done.3.refs_0_
  11.5 0.0 copy-done
  11.6 4.0 %weights.2 = (bf16[2048,1024]{1,0:T(8,128)(2,1)S(1)}, f32[256,512]{1,0:T(8,128)S(1)}, bf16[256,512]{1,0:T(8,128)(2,1)S(1)}, s32[128,128]{1,0:T(8,128)S(1)}) custom-call(s32[4]{0:T(128)S(1)} %bitcast.4, bf16[128,2048]{1,0:T(8,128)(2,1)S(1)} %get-tuple-element.40.wo_own_ref.w_own_ref, bf16[2048,1024]{1,0:T(8,128)(2,1)} %e_hbm.1, ...), custom_call_target="tpu_custom_call" | custom-call | tf_op jit(solution)/shard_map/weights/pallas_call | solution.py:72
  15.6 0.1 collective-permute-start.8
  15.6 1.3 %collective-permute-done.9.own_ref = bf16[128,896]{1,0:T(8,128)(2,1)S(1)} collective-permute-done((bf16[128,896]{1,0:T(8,128)(2,1)S(1)}, bf16[128,896]{1,0:T(8,128)(2,1)S(1)}, u32[]{:S(2)}, u32[]{:S(2)}) %collective-permute-start.9) | collective-permute-done | bytes 229408 | tf_op jit(solution)/shard_map/hop/ppermute | solution.py:25
  16.9 0.0 collective-permute-start.10
  16.9 0.6 %layer_two.6 = (f32[128,384]{1,0:T(8,128)S(1)}, f32[128,128]{1,0:T(8,128)S(1)}, f32[128,1024]{1,0:T(8,128)S(1)}) custom-call(bf16[128,896]{1,0:T(8,128)(2,1)S(1)} %collective-permute-done.9.own_ref, bf16[4096,384]{1,0:T(8,128)(2,1)S(1)} %get-tuple-element.44.w_ref, bf16[2048,1024]{1,0:T(8,128)(2,1)S(1)} %get-tuple-element.60.e_ref), custom_call_target="tpu_custom_call" | custom-call | tf_op jit(solution)/shard_map/layer_two/pallas_call | solution.py:72
  17.5 0.0 collective-permute-done.8.recv_ref
  17.5 0.1 weights.3.combined_ref
  17.6 0.8 %collective-permute-done.10.oth_ref = bf16[128,896]{1,0:T(8,128)(2,1)S(1)} collective-permute-done((bf16[128,896]{1,0:T(8,128)(2,1)S(1)}, bf16[128,896]{1,0:T(8,128)(2,1)S(1)}, u32[]{:S(2)}, u32[]{:S(2)}) %collective-permute-start.10) | collective-permute-done | bytes 229408 | tf_op jit(solution)/shard_map/layer_two/ppermute | solution.py:30
  18.4 0.3 layer_two.7
  18.7 4.2 %collective-permute-done.7.own_ref = bf16[128,1152]{1,0:T(8,128)(2,1)S(1)} collective-permute-done((bf16[128,1152]{1,0:T(8,128)(2,1)S(1)}, bf16[128,1152]{1,0:T(8,128)(2,1)S(1)}, u32[]{:S(2)}, u32[]{:S(2)}) %collective-permute-start.7) | collective-permute-done | bytes 294944 | tf_op jit(solution)/shard_map/hop/ppermute | solution.py:25
  22.9 0.0 collective-permute-start.12
  22.9 0.7 %layer_two.8 = (f32[128,384]{1,0:T(8,128)S(1)}, f32[128,128]{1,0:T(8,128)S(1)}, f32[128,512]{1,0:T(8,128)S(1)}, bf16[128,512]{1,0:T(8,128)(2,1)S(1)}) custom-call(bf16[128,1152]{1,0:T(8,128)(2,1)S(1)} %collective-permute-done.7.own_ref, bf16[4096,384]{1,0:T(8,128)(2,1)S(1)} %get-tuple-element.44.w_ref, bf16[2048,1024]{1,0:T(8,128)(2,1)S(1)} %get-tuple-element.60.e_ref, ...), custom_call_target="tpu_custom_call" | custom-call | tf_op jit(solution)/shard_map/layer_two/pallas_call | solution.py:72
  23.7 0.6 %collective-permute-start.11 = (bf16[128,512]{1,0:T(8,128)(2,1)S(1)}, bf16[128,512]{1,0:T(8,128)(2,1)S(1)}, u32[]{:S(2)}, u32[]{:S(2)}) collective-permute-start(bf16[128,512]{1,0:T(8,128)(2,1)S(1)} %get-tuple-element.71), channel_id=1, source_target_pairs={{0,1},{1,0},{2,3},{3,2},{4,5},{5,4},{6,7},{7,6},{8,9},{9,8},{10,11... | collective-permute-start | bytes 393224 | tf_op jit(solution)/shard_map/layer_two/ppermute | solution.py:30
  24.2 0.3 collective-permute-done.12.oth_ref
  24.5 0.8 %layer_two.9.mixed_ref = bf16[128,128]{1,0:T(8,128)(2,1)S(1)} custom-call(s32[128,128]{1,0:T(8,128)S(1)} %get-tuple-element.57.live_ref, bf16[128,1152]{1,0:T(8,128)(2,1)S(1)} %collective-permute-done.12.oth_ref, bf16[4096,384]{1,0:T(8,128)(2,1)S(1)} %get-tuple-element.44.w_ref, f32[128,384]{1,0:T(8,128)S(1)} %get-tuple-element.72.sum_ref, ...), custom_call_target="tpu_custom_call" | custom-call | tf_op jit(solution)/shard_map/layer_two/pallas_call | solution.py:72
  25.3 0.2 collective-permute-start.13
  25.5 0.0 collective-permute-done.11.recv_ref
  25.5 0.2 layer_two.10.sum_ref
  25.7 0.9 %collective-permute-done.13.mixed_ref = bf16[128,128]{1,0:T(8,128)(2,1)S(1)} collective-permute-done((bf16[128,128]{1,0:T(8,128)(2,1)S(1)}, bf16[128,128]{1,0:T(8,128)(2,1)S(1)}, u32[]{:S(2)}, u32[]{:S(2)}) %collective-permute-start.13) | collective-permute-done | bytes 32800 | tf_op jit(solution)/shard_map/layer_two/ppermute | solution.py:30
  26.6 0.2 layer_two.11.refs_0_.refs_1_
  26.7 2.5 %collective-permute-start.17 = (bf16[128,512]{1,0:T(8,128)(2,1)S(1)}, bf16[128,512]{1,0:T(8,128)(2,1)S(1)}, u32[]{:S(2)}, u32[]{:S(2)}) collective-permute-start(bf16[128,512]{1,0:T(8,128)(2,1)S(1)} %layer_two.11.refs_0_.refs_1_), channel_id=1, source_target_pairs={{0,6},{2,4},{4,2},{6,0},{1,7},{3,5},{5,3},{7,1},{8,14},{10,12},{12... | collective-permute-start | bytes 393224 | tf_op jit(solution)/shard_map/moments/ppermute | solution.py:30
  29.2 0.5 %collective-permute-start.14 = (bf16[128,512]{1,0:T(8,128)(2,1)S(1)}, bf16[128,512]{1,0:T(8,128)(2,1)S(1)}, u32[]{:S(2)}, u32[]{:S(2)}) collective-permute-start(bf16[128,512]{1,0:T(8,128)(2,1)S(1)} %layer_two.11.refs_0_.refs_1_), channel_id=1, source_target_pairs={{0,4},{2,6},{4,0},{6,2},{1,5},{3,7},{5,1},{7,3},{8,12},{10,14},{12... | collective-permute-start | bytes 393224 | tf_op jit(solution)/shard_map/moments/ppermute | solution.py:30
  29.8 0.5 %collective-permute-start.15 = (bf16[128,512]{1,0:T(8,128)(2,1)S(1)}, bf16[128,512]{1,0:T(8,128)(2,1)S(1)}, u32[]{:S(2)}, u32[]{:S(2)}) collective-permute-start(bf16[128,512]{1,0:T(8,128)(2,1)S(1)} %layer_two.11.refs_0_.refs_1_), channel_id=1, source_target_pairs={{0,2},{2,0},{4,6},{6,4},{1,3},{3,1},{5,7},{7,5},{8,10},{10,8},{12,... | collective-permute-start | bytes 393224 | tf_op jit(solution)/shard_map/moments/ppermute | solution.py:30
  30.3 3.3 %collective-permute-done.17.refs_2_.refs_1_ = bf16[128,512]{1,0:T(8,128)(2,1)S(1)} collective-permute-done((bf16[128,512]{1,0:T(8,128)(2,1)S(1)}, bf16[128,512]{1,0:T(8,128)(2,1)S(1)}, u32[]{:S(2)}, u32[]{:S(2)}) %collective-permute-start.17) | collective-permute-done | bytes 131104 | tf_op jit(solution)/shard_map/moments/ppermute | solution.py:30
  33.6 0.2 moments.5.gram_own_ref
  33.8 0.1 collective-permute-start.18
  33.9 2.2 %collective-permute-done.14.refs_1_.refs_0_ = bf16[128,512]{1,0:T(8,128)(2,1)S(1)} collective-permute-done((bf16[128,512]{1,0:T(8,128)(2,1)S(1)}, bf16[128,512]{1,0:T(8,128)(2,1)S(1)}, u32[]{:S(2)}, u32[]{:S(2)}) %collective-permute-start.14) | collective-permute-done | bytes 131104 | tf_op jit(solution)/shard_map/moments/ppermute | solution.py:30
  36.1 0.1 collective-permute-done.15.refs_2_.refs_1_
  36.2 0.2 moments.4.gram_own_ref
  36.4 0.1 collective-permute-start.16
  36.5 0.0 collective-permute-done.18.gram_oth_ref
  36.5 0.2 moments.6.refs_2_
  36.7 1.1 %collective-permute-done.16.gram_oth_ref = f32[128,256]{1,0:T(8,128)S(1)} collective-permute-done((f32[128,256]{1,0:T(8,128)S(1)}, f32[128,256]{1,0:T(8,128)S(1)}, u32[]{:S(2)}, u32[]{:S(2)}) %collective-permute-start.16) | collective-permute-done | bytes 131104 | tf_op jit(solution)/shard_map/moments/ppermute | solution.py:30
  37.8 0.9 %moments.7 = f32[128,512]{1,0:T(8,128)} custom-call(f32[128,256]{1,0:T(8,128)S(1)} %moments.4.gram_own_ref, f32[128,256]{1,0:T(8,128)S(1)} %collective-permute-done.16.gram_oth_ref, bf16[128,512]{1,0:T(8,128)(2,1)S(1)} %collective-permute-done.14.refs_1_.refs_0_, bf16[128,512]{1,0:T(8,128)(2,1)S(1)} %collective-permute-done.15.refs_2_.refs_1_, ...), custom_call_target="tpu_custom_call" | custom-call | tf_op jit(solution)/shard_map/moments/pallas_call | solution.py:72
  (1 shorter events, 0.0 us)
Async XLA Ops:
  0.0 2.9 %collective-permute-start = (bf16[128,2048]{1,0:T(8,128)(2,1)}, bf16[128,2048]{1,0:T(8,128)(2,1)S(1)}, u32[]{:S(2)}, u32[]{:S(2)}) collective-permute-start(bf16[128,2048]{1,0:T(8,128)(2,1)} %bitcast.5), channel_id=1, source_target_pairs={{0,1},{1,0},{2,3},{3,2},{4,5},{5,4},{6,7},{7,6},{8,9},{9,8},{10,11... | collective-permute-start | bytes 1572872 | tf_op jit(solution)/shard_map/layer_one/ppermute | solution.py:30
  2.9 8.7 %copy-start = (s32[4,1]{0,1:T(1,128)S(1)}, s32[4,1]{0,1:T(1,128)}, u32[]{:S(2)}) copy-start(s32[4,1]{0,1:T(1,128)} %param.8) | copy-start | bytes 52
  4.0 1.6 %collective-permute-start.1 = (bf16[128,1024]{1,0:T(8,128)(2,1)S(1)}, bf16[128,1024]{1,0:T(8,128)(2,1)S(1)}, u32[]{:S(2)}, u32[]{:S(2)}) collective-permute-start(bf16[128,1024]{1,0:T(8,128)(2,1)S(1)} %get-tuple-element.51), channel_id=1, source_target_pairs={{0,1},{1,0},{2,3},{3,2},{4,5},{5,4},{6,7},{7,6},{8,9},{9,8},{10,11... | collective-permute-start | bytes 786440 | tf_op jit(solution)/shard_map/layer_one/ppermute | solution.py:30
  4.2 4.3 %collective-permute-start.2 = (bf16[128,1024]{1,0:T(8,128)(2,1)S(1)}, bf16[128,1024]{1,0:T(8,128)(2,1)S(1)}, u32[]{:S(2)}, u32[]{:S(2)}) collective-permute-start(bf16[128,1024]{1,0:T(8,128)(2,1)S(1)} %get-tuple-element.52), channel_id=1, source_target_pairs={{0,1},{1,0},{2,3},{3,2},{4,5},{5,4},{6,7},{7,6},{8,9},{9,8},{10,11... | collective-permute-start | bytes 786440 | tf_op jit(solution)/shard_map/layer_one/ppermute | solution.py:30
  5.7 11.2 %collective-permute-start.9 = (bf16[128,896]{1,0:T(8,128)(2,1)S(1)}, bf16[128,896]{1,0:T(8,128)(2,1)S(1)}, u32[]{:S(2)}, u32[]{:S(2)}) collective-permute-start(bf16[128,896]{1,0:T(8,128)(2,1)S(1)} %layer_one.9), channel_id=1, source_target_pairs={{0,8},{8,16},{16,24},{24,0},{1,9},{9,17},{17,25},{25,1},{2,10},{10... | collective-permute-start | bytes 688136 | tf_op jit(solution)/shard_map/hop/ppermute | solution.py:25
  8.5 1.4 %collective-permute-start.6 = (bf16[128,512]{1,0:T(8,128)(2,1)S(1)}, bf16[128,512]{1,0:T(8,128)(2,1)S(1)}, u32[]{:S(2)}, u32[]{:S(2)}) collective-permute-start(bf16[128,512]{1,0:T(8,128)(2,1)S(1)} %get-tuple-element.56.refs_3_), channel_id=1, source_target_pairs={{0,1},{1,0},{2,3},{3,2},{4,5},{5,4},{6,7},{7,6},{8,9},{9,8},{10,11... | collective-permute-start | bytes 393224 | tf_op jit(solution)/shard_map/weights/ppermute | solution.py:30
  8.7 2.9 %collective-permute-start.5 = (bf16[128,512]{1,0:T(8,128)(2,1)S(1)}, bf16[128,512]{1,0:T(8,128)(2,1)S(1)}, u32[]{:S(2)}, u32[]{:S(2)}) collective-permute-start(bf16[128,512]{1,0:T(8,128)(2,1)S(1)} %get-tuple-element.55.refs_2_), channel_id=1, source_target_pairs={{0,1},{1,0},{2,3},{3,2},{4,5},{5,4},{6,7},{7,6},{8,9},{9,8},{10,11... | collective-permute-start | bytes 393224 | tf_op jit(solution)/shard_map/weights/ppermute | solution.py:30
  9.1 2.4 %collective-permute-start.4 = (bf16[128,512]{1,0:T(8,128)(2,1)S(1)}, bf16[128,512]{1,0:T(8,128)(2,1)S(1)}, u32[]{:S(2)}, u32[]{:S(2)}) collective-permute-start(bf16[128,512]{1,0:T(8,128)(2,1)S(1)} %get-tuple-element.54.refs_1_), channel_id=1, source_target_pairs={{0,1},{1,0},{2,3},{3,2},{4,5},{5,4},{6,7},{7,6},{8,9},{9,8},{10,11... | collective-permute-start | bytes 393224 | tf_op jit(solution)/shard_map/weights/ppermute | solution.py:30
  9.2 2.3 %collective-permute-start.3 = (bf16[128,512]{1,0:T(8,128)(2,1)S(1)}, bf16[128,512]{1,0:T(8,128)(2,1)S(1)}, u32[]{:S(2)}, u32[]{:S(2)}) collective-permute-start(bf16[128,512]{1,0:T(8,128)(2,1)S(1)} %get-tuple-element.53.refs_0_), channel_id=1, source_target_pairs={{0,1},{1,0},{2,3},{3,2},{4,5},{5,4},{6,7},{7,6},{8,9},{9,8},{10,11... | collective-permute-start | bytes 393224 | tf_op jit(solution)/shard_map/weights/ppermute | solution.py:30
  9.9 13.0 %collective-permute-start.7 = (bf16[128,1152]{1,0:T(8,128)(2,1)S(1)}, bf16[128,1152]{1,0:T(8,128)(2,1)S(1)}, u32[]{:S(2)}, u32[]{:S(2)}) collective-permute-start(bf16[128,1152]{1,0:T(8,128)(2,1)S(1)} %layer_one.8), channel_id=1, source_target_pairs={{0,8},{8,16},{16,24},{24,0},{1,9},{9,17},{17,25},{25,1},{2,10},{10... | collective-permute-start | bytes 884744 | tf_op jit(solution)/shard_map/hop/ppermute | solution.py:25
  15.6 1.9 %collective-permute-start.8 = (bf16[256,512]{1,0:T(8,128)(2,1)S(1)}, bf16[256,512]{1,0:T(8,128)(2,1)S(1)}, u32[]{:S(2)}, u32[]{:S(2)}) collective-permute-start(bf16[256,512]{1,0:T(8,128)(2,1)S(1)} %get-tuple-element.59), channel_id=1, source_target_pairs={{0,1},{1,0},{2,3},{3,2},{4,5},{5,4},{6,7},{7,6},{8,9},{9,8},{10,11... | collective-permute-start | bytes 786440 | tf_op jit(solution)/shard_map/weights/ppermute | solution.py:30
  16.9 1.5 %collective-permute-start.10 = (bf16[128,896]{1,0:T(8,128)(2,1)S(1)}, bf16[128,896]{1,0:T(8,128)(2,1)S(1)}, u32[]{:S(2)}, u32[]{:S(2)}) collective-permute-start(bf16[128,896]{1,0:T(8,128)(2,1)S(1)} %collective-permute-done.9.own_ref), channel_id=1, source_target_pairs={{0,1},{1,0},{2,3},{3,2},{4,5},{5,4},{6,7},{7,6},{8,9},{9,8},{10,11... | collective-permute-start | bytes 688136 | tf_op jit(solution)/shard_map/layer_two/ppermute | solution.py:30
  22.9 1.6 %collective-permute-start.12 = (bf16[128,1152]{1,0:T(8,128)(2,1)S(1)}, bf16[128,1152]{1,0:T(8,128)(2,1)S(1)}, u32[]{:S(2)}, u32[]{:S(2)}) collective-permute-start(bf16[128,1152]{1,0:T(8,128)(2,1)S(1)} %collective-permute-done.7.own_ref), channel_id=1, source_target_pairs={{0,1},{1,0},{2,3},{3,2},{4,5},{5,4},{6,7},{7,6},{8,9},{9,8},{10,11... | collective-permute-start | bytes 884744 | tf_op jit(solution)/shard_map/layer_two/ppermute | solution.py:30
  23.7 1.8 %collective-permute-start.11 = (bf16[128,512]{1,0:T(8,128)(2,1)S(1)}, bf16[128,512]{1,0:T(8,128)(2,1)S(1)}, u32[]{:S(2)}, u32[]{:S(2)}) collective-permute-start(bf16[128,512]{1,0:T(8,128)(2,1)S(1)} %get-tuple-element.71), channel_id=1, source_target_pairs={{0,1},{1,0},{2,3},{3,2},{4,5},{5,4},{6,7},{7,6},{8,9},{9,8},{10,11... | collective-permute-start | bytes 393224 | tf_op jit(solution)/shard_map/layer_two/ppermute | solution.py:30
  25.3 1.3 %collective-permute-start.13 = (bf16[128,128]{1,0:T(8,128)(2,1)S(1)}, bf16[128,128]{1,0:T(8,128)(2,1)S(1)}, u32[]{:S(2)}, u32[]{:S(2)}) collective-permute-start(bf16[128,128]{1,0:T(8,128)(2,1)S(1)} %layer_two.9.mixed_ref), channel_id=1, source_target_pairs={{0,1},{1,0},{2,3},{3,2},{4,5},{5,4},{6,7},{7,6},{8,9},{9,8},{10,11... | collective-permute-start | bytes 98312 | tf_op jit(solution)/shard_map/layer_two/ppermute | solution.py:30
  26.7 6.8 %collective-permute-start.17 = (bf16[128,512]{1,0:T(8,128)(2,1)S(1)}, bf16[128,512]{1,0:T(8,128)(2,1)S(1)}, u32[]{:S(2)}, u32[]{:S(2)}) collective-permute-start(bf16[128,512]{1,0:T(8,128)(2,1)S(1)} %layer_two.11.refs_0_.refs_1_), channel_id=1, source_target_pairs={{0,6},{2,4},{4,2},{6,0},{1,7},{3,5},{5,3},{7,1},{8,14},{10,12},{12... | collective-permute-start | bytes 393224 | tf_op jit(solution)/shard_map/moments/ppermute | solution.py:30
  29.2 6.8 %collective-permute-start.14 = (bf16[128,512]{1,0:T(8,128)(2,1)S(1)}, bf16[128,512]{1,0:T(8,128)(2,1)S(1)}, u32[]{:S(2)}, u32[]{:S(2)}) collective-permute-start(bf16[128,512]{1,0:T(8,128)(2,1)S(1)} %layer_two.11.refs_0_.refs_1_), channel_id=1, source_target_pairs={{0,4},{2,6},{4,0},{6,2},{1,5},{3,7},{5,1},{7,3},{8,12},{10,14},{12... | collective-permute-start | bytes 393224 | tf_op jit(solution)/shard_map/moments/ppermute | solution.py:30
  29.8 6.4 %collective-permute-start.15 = (bf16[128,512]{1,0:T(8,128)(2,1)S(1)}, bf16[128,512]{1,0:T(8,128)(2,1)S(1)}, u32[]{:S(2)}, u32[]{:S(2)}) collective-permute-start(bf16[128,512]{1,0:T(8,128)(2,1)S(1)} %layer_two.11.refs_0_.refs_1_), channel_id=1, source_target_pairs={{0,2},{2,0},{4,6},{6,4},{1,3},{3,1},{5,7},{7,5},{8,10},{10,8},{12,... | collective-permute-start | bytes 393224 | tf_op jit(solution)/shard_map/moments/ppermute | solution.py:30
  33.8 2.7 %collective-permute-start.18 = (f32[128,256]{1,0:T(8,128)S(1)}, f32[128,256]{1,0:T(8,128)S(1)}, u32[]{:S(2)}, u32[]{:S(2)}) collective-permute-start(f32[128,256]{1,0:T(8,128)S(1)} %moments.5.gram_own_ref), channel_id=1, source_target_pairs={{0,1},{1,0},{2,3},{3,2},{4,5},{5,4},{6,7},{7,6},{8,9},{9,8},{10,11... | collective-permute-start | bytes 393224 | tf_op jit(solution)/shard_map/moments/ppermute | solution.py:30
  36.4 1.4 %collective-permute-start.16 = (f32[128,256]{1,0:T(8,128)S(1)}, f32[128,256]{1,0:T(8,128)S(1)}, u32[]{:S(2)}, u32[]{:S(2)}) collective-permute-start(f32[128,256]{1,0:T(8,128)S(1)} %moments.4.gram_own_ref), channel_id=1, source_target_pairs={{0,1},{1,0},{2,3},{3,2},{4,5},{5,4},{6,7},{7,6},{8,9},{9,8},{10,11... | collective-permute-start | bytes 393224 | tf_op jit(solution)/shard_map/moments/ppermute | solution.py:30

commit v5 on v4

--- a/solution.py
+++ b/solution.py
@@ -96,8 +96,8 @@
     key_pos = lax.broadcasted_iota(jnp.int32, (rows, rows), 1)
     scores = jnp.where(key_pos < live_len, scores, -1e30)
     weights = jnp.exp(scores - jnp.max(scores, axis=-1, keepdims=True))
-    probs = (weights / jnp.sum(weights, axis=-1, keepdims=True)).astype(BF16)
-    return dot(probs, value).astype(BF16)
+    total = jnp.sum(weights, axis=-1, keepdims=True)
+    return (dot(weights.astype(BF16), value) / total).astype(BF16)
 
 
 def load_body(
@@ -135,7 +135,7 @@
 
 
 def first_body(live_ref, oth_ref, w_ref, qkv_ref, square_ref, *refs):
-    wo_send_refs, mixed_ref, parts = refs[:WO_PARTS], refs[WO_PARTS], refs[WO_PARTS + 1 :]
+    wo_send_refs, (mixed_ref, part_ref) = refs[:-2], refs[-2:]
     half = oth_ref.shape[1]
     core = lax.axis_index("tensor")
     oth = oth_ref[...]
@@ -144,15 +144,15 @@
     mixed = softmax_mix(qkv * scale, live_ref[...])
     mixed_ref[...] = mixed
     weight = jnp.concatenate([ref[...] for ref in wo_send_refs], axis=1)
-    lower = 0
-    for part_ref in parts:
-        upper = lower + part_ref.shape[1]
-        part_ref[...] = dot(mixed, weight[:, lower:upper]).astype(BF16)
-        lower = upper
-
-
-def held_body(own_ref, mixed_ref, wo_own_ref, held_ref):
-    held_ref[...] = own_ref[...].astype(F32) + dot(mixed_ref[...], wo_own_ref[...])
+    part_ref[...] = dot(mixed, weight).astype(BF16)
+
+
+def held_body(own_ref, mixed_ref, wo_own_ref, *refs):
+    wo_send_refs, (part_ref, held_ref) = refs[:-2], refs[-2:]
+    mixed = mixed_ref[...]
+    weight = jnp.concatenate([ref[...] for ref in wo_send_refs], axis=1)
+    part_ref[...] = dot(mixed, weight).astype(BF16)
+    held_ref[...] = own_ref[...].astype(F32) + dot(mixed, wo_own_ref[...])
 
 
 def update_body(lower, held_ref, *refs):
@@ -328,11 +328,16 @@
             9 + WO_PARTS,
             scratch=(pltpu.SMEM(lens.shape, jnp.int32),),
         )(lens, tokens, w_query, w_key, w_value, w_out)
-        mixed, *parts = call(
-            first_body, [shape(rows, HD)] + [shape(rows, half // 2)] * 2, "v" * (5 + WO_PARTS)
-        )(live, oth, w_own, qkv, square, *wo_send)
-        parts = [exchanged(part, "tensor", 1) for part in parts]
-        held = call(held_body, shape(rows, half, dtype=F32), "vvv")(own, mixed, wo_own)
+        mixed, part = call(
+            first_body, [shape(rows, HD), shape(rows, half // 2)], "v" * (5 + WO_PARTS // 2)
+        )(live, oth, w_own, qkv, square, *wo_send[: WO_PARTS // 2])
+        parts = [exchanged(part, "tensor", 1)]
+        part, held = call(
+            held_body,
+            [shape(rows, half // 2), shape(rows, half, dtype=F32)],
+            "v" * (3 + WO_PARTS // 2),
+        )(own, mixed, wo_own, *wo_send[WO_PARTS // 2 :])
+        parts.append(exchanged(part, "tensor", 1))
         state = []
         for lower, width in zip(lowers, widths):
             needed = parts if lower else parts[:1]

time: 38.9 us -> 38.6 us (level)
  no operation moved by 1% of the time
where the time goes in v5:
time: 38.6 us; the launch traced here: 38.5 us
  waiting for transfers between devices  15.1 us (39%)
  Pallas kernels  12 us (31%)
  starting transfers between devices  11.1 us (29%)
    pallas_call x17, Pallas kernels, call(): return lambda *operands: kernel(*map(place, operands, spaces))  12 us
    ppermute x17, waiting for transfers between devices, exchanged(): lax.ppermute(value, axis, [(source, source ^ mask) for source in range(co...  9.64 us
    ppermute x17, starting transfers between devices, exchanged(): lax.ppermute(value, axis, [(source, source ^ mask) for source in range(co...  6.74 us
    ppermute x2, waiting for transfers between devices, shifted(): return lax.ppermute(value, axis, pairs)  5.51 us
    ppermute x2, starting transfers between devices, shifted(): return lax.ppermute(value, axis, pairs)  4.35 us
  transfers between devices with their start and end apart: 19, of which 11 were waited for; matrix products, arithmetic and copies ran while one was open for 0% of the time, Pallas kernels for 26%

profile of v5, /device:TPU:0, one launch (start us, length us, event | category | flops | bytes accessed | tf_op | source)
XLA Modules:
  0.0 38.5 jit_solution(2444986257085545426)
XLA Ops:
  0.0 0.5 %collective-permute-start = (bf16[128,2048]{1,0:T(8,128)(2,1)}, bf16[128,2048]{1,0:T(8,128)(2,1)S(1)}, u32[]{:S(2)}, u32[]{:S(2)}) collective-permute-start(bf16[128,2048]{1,0:T(8,128)(2,1)} %bitcast.5), channel_id=1, source_target_pairs={{0,1},{1,0},{2,3},{3,2},{4,5},{5,4},{6,7},{7,6},{8,9},{9,8},{10,11... | collective-permute-start | bytes 1572872 | tf_op jit(solution)/shard_map/layer_one/ppermute | solution.py:30
  0.5 2.4 %layer_one.5 = (bf16[128,2048]{1,0:T(8,128)(2,1)S(1)}, bf16[4096,384]{1,0:T(8,128)(2,1)S(1)}, f32[128,384]{1,0:T(8,128)S(1)}, f32[128,128]{1,0:T(8,128)S(1)}, s3...) custom-call(s32[4]{0:T(128)} %bitcast.3, ...), custom_call_target="tpu_custom_call" | custom-call | tf_op jit(solution)/shard_map/layer_one/pallas_call | solution.py:72
  2.9 0.0 collective-permute-done.oth_ref
  2.9 0.0 copy-start
  2.9 1.0 %layer_one.6 = (bf16[128,128]{1,0:T(8,128)(2,1)S(1)}, bf16[128,1024]{1,0:T(8,128)(2,1)S(1)}) custom-call(s32[128,128]{1,0:T(8,128)S(1)} %get-tuple-element.44.live_ref, bf16[128,2048]{1,0:T(8,128)(2,1)S(1)} %collective-permute-done.oth_ref, bf16[4096,384]{1,0:T(8,128)(2,1)S(1)} %get-tuple-element.45.w_ref, f32[128,384]{1,0:T(8,128)S(1)} %get-tuple-element.46.qkv_ref, ...), custom_call_target="tpu_custom_call" | custom-call | tf_op jit(solution)/shard_map/layer_one/pallas_call | solution.py:72
  3.9 0.1 collective-permute-start.1
  4.0 0.3 layer_one.7
  4.4 0.5 %collective-permute-start.2 = (bf16[128,1024]{1,0:T(8,128)(2,1)S(1)}, bf16[128,1024]{1,0:T(8,128)(2,1)S(1)}, u32[]{:S(2)}, u32[]{:S(2)}) collective-permute-start(bf16[128,1024]{1,0:T(8,128)(2,1)S(1)} %get-tuple-element.54), channel_id=1, source_target_pairs={{0,1},{1,0},{2,3},{3,2},{4,5},{5,4},{6,7},{7,6},{8,9},{9,8},{10,11... | collective-permute-start | bytes 786440 | tf_op jit(solution)/shard_map/layer_one/ppermute | solution.py:30
  4.9 0.6 %collective-permute-done.1.refs_0_ = bf16[128,1024]{1,0:T(8,128)(2,1)S(1)} collective-permute-done((bf16[128,1024]{1,0:T(8,128)(2,1)S(1)}, bf16[128,1024]{1,0:T(8,128)(2,1)S(1)}, u32[]{:S(2)}, u32[]{:S(2)}) %collective-permute-start.1) | collective-permute-done | bytes 262176 | tf_op jit(solution)/shard_map/layer_one/ppermute | solution.py:30
  5.5 2.8 %collective-permute-start.9 = (bf16[128,896]{1,0:T(8,128)(2,1)S(1)}, bf16[128,896]{1,0:T(8,128)(2,1)S(1)}, u32[]{:S(2)}, u32[]{:S(2)}) collective-permute-start(bf16[128,896]{1,0:T(8,128)(2,1)S(1)} %layer_one.9), channel_id=1, source_target_pairs={{0,8},{8,16},{16,24},{24,0},{1,9},{9,17},{17,25},{25,1},{2,10},{10... | collective-permute-start | bytes 688136 | tf_op jit(solution)/shard_map/hop/ppermute | solution.py:25
  8.3 0.0 collective-permute-done.2.refs_1_
  8.3 0.1 layer_one.8
  8.4 0.1 collective-permute-start.6
  8.5 0.4 %collective-permute-start.5 = (bf16[128,512]{1,0:T(8,128)(2,1)S(1)}, bf16[128,512]{1,0:T(8,128)(2,1)S(1)}, u32[]{:S(2)}, u32[]{:S(2)}) collective-permute-start(bf16[128,512]{1,0:T(8,128)(2,1)S(1)} %get-tuple-element.57.refs_0_), channel_id=1, source_target_pairs={{0,1},{1,0},{2,3},{3,2},{4,5},{5,4},{6,7},{7,6},{8,9},{9,8},{10,11... | collective-permute-start | bytes 393224 | tf_op jit(solution)/shard_map/weights/ppermute | solution.py:30
  9.0 0.1 collective-permute-start.4
  9.0 0.4 %collective-permute-start.3 = (bf16[128,512]{1,0:T(8,128)(2,1)S(1)}, bf16[128,512]{1,0:T(8,128)(2,1)S(1)}, u32[]{:S(2)}, u32[]{:S(2)}) collective-permute-start(bf16[128,512]{1,0:T(8,128)(2,1)S(1)} %get-tuple-element.55.refs_0_), channel_id=1, source_target_pairs={{0,1},{1,0},{2,3},{3,2},{4,5},{5,4},{6,7},{7,6},{8,9},{9,8},{10,11... | collective-permute-start | bytes 393224 | tf_op jit(solution)/shard_map/weights/ppermute | solution.py:30
  9.5 0.3 collective-permute-done.6.refs_3_
  9.8 1.6 %collective-permute-start.7 = (bf16[128,1152]{1,0:T(8,128)(2,1)S(1)}, bf16[128,1152]{1,0:T(8,128)(2,1)S(1)}, u32[]{:S(2)}, u32[]{:S(2)}) collective-permute-start(bf16[128,1152]{1,0:T(8,128)(2,1)S(1)} %layer_one.8), channel_id=1, source_target_pairs={{0,8},{8,16},{16,24},{24,0},{1,9},{9,17},{17,25},{25,1},{2,10},{10... | collective-permute-start | bytes 884744 | tf_op jit(solution)/shard_map/hop/ppermute | solution.py:25
  11.4 0.0 collective-permute-done.5.refs_2_
  11.4 0.0 collective-permute-done.4.refs_1_
  11.4 0.0 collective-permute-done.3.refs_0_
  11.4 0.0 copy-done
  11.4 4.0 %weights.2 = (bf16[2048,1024]{1,0:T(8,128)(2,1)S(1)}, f32[256,512]{1,0:T(8,128)S(1)}, bf16[256,512]{1,0:T(8,128)(2,1)S(1)}, s32[128,128]{1,0:T(8,128)S(1)}) custom-call(s32[4]{0:T(128)S(1)} %bitcast.4, bf16[128,2048]{1,0:T(8,128)(2,1)S(1)} %get-tuple-element.41.wo_own_ref.w_own_ref, bf16[2048,1024]{1,0:T(8,128)(2,1)} %e_hbm.1, ...), custom_call_target="tpu_custom_call" | custom-call | tf_op jit(solution)/shard_map/weights/pallas_call | solution.py:72
  15.4 0.1 collective-permute-start.8
  15.5 1.3 %collective-permute-done.9.own_ref = bf16[128,896]{1,0:T(8,128)(2,1)S(1)} collective-permute-done((bf16[128,896]{1,0:T(8,128)(2,1)S(1)}, bf16[128,896]{1,0:T(8,128)(2,1)S(1)}, u32[]{:S(2)}, u32[]{:S(2)}) %collective-permute-start.9) | collective-permute-done | bytes 229408 | tf_op jit(solution)/shard_map/hop/ppermute | solution.py:25
  16.8 0.0 collective-permute-start.10
  16.8 0.6 %layer_two.6 = (f32[128,384]{1,0:T(8,128)S(1)}, f32[128,128]{1,0:T(8,128)S(1)}, f32[128,1024]{1,0:T(8,128)S(1)}) custom-call(bf16[128,896]{1,0:T(8,128)(2,1)S(1)} %collective-permute-done.9.own_ref, bf16[4096,384]{1,0:T(8,128)(2,1)S(1)} %get-tuple-element.45.w_ref, bf16[2048,1024]{1,0:T(8,128)(2,1)S(1)} %get-tuple-element.62.e_ref), custom_call_target="tpu_custom_call" | custom-call | tf_op jit(solution)/shard_map/layer_two/pallas_call | solution.py:72
  17.4 0.0 collective-permute-done.8.recv_ref
  17.4 0.1 weights.3.combined_ref
  17.4 0.8 %collective-permute-done.10.oth_ref = bf16[128,896]{1,0:T(8,128)(2,1)S(1)} collective-permute-done((bf16[128,896]{1,0:T(8,128)(2,1)S(1)}, bf16[128,896]{1,0:T(8,128)(2,1)S(1)}, u32[]{:S(2)}, u32[]{:S(2)}) %collective-permute-start.10) | collective-permute-done | bytes 229408 | tf_op jit(solution)/shard_map/layer_two/ppermute | solution.py:30
  18.3 0.3 layer_two.7
  18.6 4.2 %collective-permute-done.7.own_ref = bf16[128,1152]{1,0:T(8,128)(2,1)S(1)} collective-permute-done((bf16[128,1152]{1,0:T(8,128)(2,1)S(1)}, bf16[128,1152]{1,0:T(8,128)(2,1)S(1)}, u32[]{:S(2)}, u32[]{:S(2)}) %collective-permute-start.7) | collective-permute-done | bytes 294944 | tf_op jit(solution)/shard_map/hop/ppermute | solution.py:25
  22.8 0.0 collective-permute-start.12
  22.8 0.7 %layer_two.8 = (f32[128,384]{1,0:T(8,128)S(1)}, f32[128,128]{1,0:T(8,128)S(1)}, f32[128,512]{1,0:T(8,128)S(1)}, bf16[128,512]{1,0:T(8,128)(2,1)S(1)}) custom-call(bf16[128,1152]{1,0:T(8,128)(2,1)S(1)} %collective-permute-done.7.own_ref, bf16[4096,384]{1,0:T(8,128)(2,1)S(1)} %get-tuple-element.45.w_ref, bf16[2048,1024]{1,0:T(8,128)(2,1)S(1)} %get-tuple-element.62.e_ref, ...), custom_call_target="tpu_custom_call" | custom-call | tf_op jit(solution)/shard_map/layer_two/pallas_call | solution.py:72
  23.5 0.6 %collective-permute-start.11 = (bf16[128,512]{1,0:T(8,128)(2,1)S(1)}, bf16[128,512]{1,0:T(8,128)(2,1)S(1)}, u32[]{:S(2)}, u32[]{:S(2)}) collective-permute-start(bf16[128,512]{1,0:T(8,128)(2,1)S(1)} %get-tuple-element.73), channel_id=1, source_target_pairs={{0,1},{1,0},{2,3},{3,2},{4,5},{5,4},{6,7},{7,6},{8,9},{9,8},{10,11... | collective-permute-start | bytes 393224 | tf_op jit(solution)/shard_map/layer_two/ppermute | solution.py:30
  24.1 0.3 collective-permute-done.12.oth_ref
  24.4 0.7 %layer_two.9.mixed_ref = bf16[128,128]{1,0:T(8,128)(2,1)S(1)} custom-call(s32[128,128]{1,0:T(8,128)S(1)} %get-tuple-element.59.live_ref, bf16[128,1152]{1,0:T(8,128)(2,1)S(1)} %collective-permute-done.12.oth_ref, bf16[4096,384]{1,0:T(8,128)(2,1)S(1)} %get-tuple-element.45.w_ref, f32[128,384]{1,0:T(8,128)S(1)} %get-tuple-element.74.sum_ref, ...), custom_call_target="tpu_custom_call" | custom-call | tf_op jit(solution)/shard_map/layer_two/pallas_call | solution.py:72
  25.1 0.2 collective-permute-start.13
  25.3 0.0 collective-permute-done.11.recv_ref
  25.3 0.2 layer_two.10.sum_ref
  25.4 0.9 %collective-permute-done.13.mixed_ref = bf16[128,128]{1,0:T(8,128)(2,1)S(1)} collective-permute-done((bf16[128,128]{1,0:T(8,128)(2,1)S(1)}, bf16[128,128]{1,0:T(8,128)(2,1)S(1)}, u32[]{:S(2)}, u32[]{:S(2)}) %collective-permute-start.13) | collective-permute-done | bytes 32800 | tf_op jit(solution)/shard_map/layer_two/ppermute | solution.py:30
  26.3 0.2 layer_two.11.refs_0_.refs_1_
  26.5 2.5 %collective-permute-start.17 = (bf16[128,512]{1,0:T(8,128)(2,1)S(1)}, bf16[128,512]{1,0:T(8,128)(2,1)S(1)}, u32[]{:S(2)}, u32[]{:S(2)}) collective-permute-start(bf16[128,512]{1,0:T(8,128)(2,1)S(1)} %layer_two.11.refs_0_.refs_1_), channel_id=1, source_target_pairs={{0,6},{2,4},{4,2},{6,0},{1,7},{3,5},{5,3},{7,1},{8,14},{10,12},{12... | collective-permute-start | bytes 393224 | tf_op jit(solution)/shard_map/moments/ppermute | solution.py:30
  29.0 0.5 %collective-permute-start.14 = (bf16[128,512]{1,0:T(8,128)(2,1)S(1)}, bf16[128,512]{1,0:T(8,128)(2,1)S(1)}, u32[]{:S(2)}, u32[]{:S(2)}) collective-permute-start(bf16[128,512]{1,0:T(8,128)(2,1)S(1)} %layer_two.11.refs_0_.refs_1_), channel_id=1, source_target_pairs={{0,4},{2,6},{4,0},{6,2},{1,5},{3,7},{5,1},{7,3},{8,12},{10,14},{12... | collective-permute-start | bytes 393224 | tf_op jit(solution)/shard_map/moments/ppermute | solution.py:30
  29.5 0.5 %collective-permute-start.15 = (bf16[128,512]{1,0:T(8,128)(2,1)S(1)}, bf16[128,512]{1,0:T(8,128)(2,1)S(1)}, u32[]{:S(2)}, u32[]{:S(2)}) collective-permute-start(bf16[128,512]{1,0:T(8,128)(2,1)S(1)} %layer_two.11.refs_0_.refs_1_), channel_id=1, source_target_pairs={{0,2},{2,0},{4,6},{6,4},{1,3},{3,1},{5,7},{7,5},{8,10},{10,8},{12,... | collective-permute-start | bytes 393224 | tf_op jit(solution)/shard_map/moments/ppermute | solution.py:30
  30.1 3.3 %collective-permute-done.17.refs_2_.refs_1_ = bf16[128,512]{1,0:T(8,128)(2,1)S(1)} collective-permute-done((bf16[128,512]{1,0:T(8,128)(2,1)S(1)}, bf16[128,512]{1,0:T(8,128)(2,1)S(1)}, u32[]{:S(2)}, u32[]{:S(2)}) %collective-permute-start.17) | collective-permute-done | bytes 131104 | tf_op jit(solution)/shard_map/moments/ppermute | solution.py:30
  33.3 0.2 moments.5.gram_own_ref
  33.5 0.1 collective-permute-start.18
  33.6 2.2 %collective-permute-done.14.refs_1_.refs_0_ = bf16[128,512]{1,0:T(8,128)(2,1)S(1)} collective-permute-done((bf16[128,512]{1,0:T(8,128)(2,1)S(1)}, bf16[128,512]{1,0:T(8,128)(2,1)S(1)}, u32[]{:S(2)}, u32[]{:S(2)}) %collective-permute-start.14) | collective-permute-done | bytes 131104 | tf_op jit(solution)/shard_map/moments/ppermute | solution.py:30
  35.8 0.1 collective-permute-done.15.refs_2_.refs_1_
  35.9 0.2 moments.4.gram_own_ref
  36.2 0.1 collective-permute-start.16
  36.2 0.0 collective-permute-done.18.gram_oth_ref
  36.2 0.2 moments.6.refs_2_
  36.4 1.1 %collective-permute-done.16.gram_oth_ref = f32[128,256]{1,0:T(8,128)S(1)} collective-permute-done((f32[128,256]{1,0:T(8,128)S(1)}, f32[128,256]{1,0:T(8,128)S(1)}, u32[]{:S(2)}, u32[]{:S(2)}) %collective-permute-start.16) | collective-permute-done | bytes 131104 | tf_op jit(solution)/shard_map/moments/ppermute | solution.py:30
  37.6 0.9 %moments.7 = f32[128,512]{1,0:T(8,128)} custom-call(f32[128,256]{1,0:T(8,128)S(1)} %moments.4.gram_own_ref, f32[128,256]{1,0:T(8,128)S(1)} %collective-permute-done.16.gram_oth_ref, bf16[128,512]{1,0:T(8,128)(2,1)S(1)} %collective-permute-done.14.refs_1_.refs_0_, bf16[128,512]{1,0:T(8,128)(2,1)S(1)} %collective-permute-done.15.refs_2_.refs_1_, ...), custom_call_target="tpu_custom_call" | custom-call | tf_op jit(solution)/shard_map/moments/pallas_call | solution.py:72
  (1 shorter events, 0.0 us)
Async XLA Ops:
  0.0 2.9 %collective-permute-start = (bf16[128,2048]{1,0:T(8,128)(2,1)}, bf16[128,2048]{1,0:T(8,128)(2,1)S(1)}, u32[]{:S(2)}, u32[]{:S(2)}) collective-permute-start(bf16[128,2048]{1,0:T(8,128)(2,1)} %bitcast.5), channel_id=1, source_target_pairs={{0,1},{1,0},{2,3},{3,2},{4,5},{5,4},{6,7},{7,6},{8,9},{9,8},{10,11... | collective-permute-start | bytes 1572872 | tf_op jit(solution)/shard_map/layer_one/ppermute | solution.py:30
  2.9 8.5 %copy-start = (s32[4,1]{0,1:T(1,128)S(1)}, s32[4,1]{0,1:T(1,128)}, u32[]{:S(2)}) copy-start(s32[4,1]{0,1:T(1,128)} %param.8) | copy-start | bytes 52
  3.9 1.6 %collective-permute-start.1 = (bf16[128,1024]{1,0:T(8,128)(2,1)S(1)}, bf16[128,1024]{1,0:T(8,128)(2,1)S(1)}, u32[]{:S(2)}, u32[]{:S(2)}) collective-permute-start(bf16[128,1024]{1,0:T(8,128)(2,1)S(1)} %get-tuple-element.53), channel_id=1, source_target_pairs={{0,1},{1,0},{2,3},{3,2},{4,5},{5,4},{6,7},{7,6},{8,9},{9,8},{10,11... | collective-permute-start | bytes 786440 | tf_op jit(solution)/shard_map/layer_one/ppermute | solution.py:30
  4.4 3.9 %collective-permute-start.2 = (bf16[128,1024]{1,0:T(8,128)(2,1)S(1)}, bf16[128,1024]{1,0:T(8,128)(2,1)S(1)}, u32[]{:S(2)}, u32[]{:S(2)}) collective-permute-start(bf16[128,1024]{1,0:T(8,128)(2,1)S(1)} %get-tuple-element.54), channel_id=1, source_target_pairs={{0,1},{1,0},{2,3},{3,2},{4,5},{5,4},{6,7},{7,6},{8,9},{9,8},{10,11... | collective-permute-start | bytes 786440 | tf_op jit(solution)/shard_map/layer_one/ppermute | solution.py:30
  5.5 11.2 %collective-permute-start.9 = (bf16[128,896]{1,0:T(8,128)(2,1)S(1)}, bf16[128,896]{1,0:T(8,128)(2,1)S(1)}, u32[]{:S(2)}, u32[]{:S(2)}) collective-permute-start(bf16[128,896]{1,0:T(8,128)(2,1)S(1)} %layer_one.9), channel_id=1, source_target_pairs={{0,8},{8,16},{16,24},{24,0},{1,9},{9,17},{17,25},{25,1},{2,10},{10... | collective-permute-start | bytes 688136 | tf_op jit(solution)/shard_map/hop/ppermute | solution.py:25
  8.4 1.4 %collective-permute-start.6 = (bf16[128,512]{1,0:T(8,128)(2,1)S(1)}, bf16[128,512]{1,0:T(8,128)(2,1)S(1)}, u32[]{:S(2)}, u32[]{:S(2)}) collective-permute-start(bf16[128,512]{1,0:T(8,128)(2,1)S(1)} %get-tuple-element.58.refs_1_), channel_id=1, source_target_pairs={{0,1},{1,0},{2,3},{3,2},{4,5},{5,4},{6,7},{7,6},{8,9},{9,8},{10,11... | collective-permute-start | bytes 393224 | tf_op jit(solution)/shard_map/weights/ppermute | solution.py:30
  8.5 2.8 %collective-permute-start.5 = (bf16[128,512]{1,0:T(8,128)(2,1)S(1)}, bf16[128,512]{1,0:T(8,128)(2,1)S(1)}, u32[]{:S(2)}, u32[]{:S(2)}) collective-permute-start(bf16[128,512]{1,0:T(8,128)(2,1)S(1)} %get-tuple-element.57.refs_0_), channel_id=1, source_target_pairs={{0,1},{1,0},{2,3},{3,2},{4,5},{5,4},{6,7},{7,6},{8,9},{9,8},{10,11... | collective-permute-start | bytes 393224 | tf_op jit(solution)/shard_map/weights/ppermute | solution.py:30
  9.0 2.4 %collective-permute-start.4 = (bf16[128,512]{1,0:T(8,128)(2,1)S(1)}, bf16[128,512]{1,0:T(8,128)(2,1)S(1)}, u32[]{:S(2)}, u32[]{:S(2)}) collective-permute-start(bf16[128,512]{1,0:T(8,128)(2,1)S(1)} %get-tuple-element.56.refs_1_), channel_id=1, source_target_pairs={{0,1},{1,0},{2,3},{3,2},{4,5},{5,4},{6,7},{7,6},{8,9},{9,8},{10,11... | collective-permute-start | bytes 393224 | tf_op jit(solution)/shard_map/weights/ppermute | solution.py:30
  9.0 2.3 %collective-permute-start.3 = (bf16[128,512]{1,0:T(8,128)(2,1)S(1)}, bf16[128,512]{1,0:T(8,128)(2,1)S(1)}, u32[]{:S(2)}, u32[]{:S(2)}) collective-permute-start(bf16[128,512]{1,0:T(8,128)(2,1)S(1)} %get-tuple-element.55.refs_0_), channel_id=1, source_target_pairs={{0,1},{1,0},{2,3},{3,2},{4,5},{5,4},{6,7},{7,6},{8,9},{9,8},{10,11... | collective-permute-start | bytes 393224 | tf_op jit(solution)/shard_map/weights/ppermute | solution.py:30
  9.8 13.0 %collective-permute-start.7 = (bf16[128,1152]{1,0:T(8,128)(2,1)S(1)}, bf16[128,1152]{1,0:T(8,128)(2,1)S(1)}, u32[]{:S(2)}, u32[]{:S(2)}) collective-permute-start(bf16[128,1152]{1,0:T(8,128)(2,1)S(1)} %layer_one.8), channel_id=1, source_target_pairs={{0,8},{8,16},{16,24},{24,0},{1,9},{9,17},{17,25},{25,1},{2,10},{10... | collective-permute-start | bytes 884744 | tf_op jit(solution)/shard_map/hop/ppermute | solution.py:25
  15.4 2.0 %collective-permute-start.8 = (bf16[256,512]{1,0:T(8,128)(2,1)S(1)}, bf16[256,512]{1,0:T(8,128)(2,1)S(1)}, u32[]{:S(2)}, u32[]{:S(2)}) collective-permute-start(bf16[256,512]{1,0:T(8,128)(2,1)S(1)} %get-tuple-element.61), channel_id=1, source_target_pairs={{0,1},{1,0},{2,3},{3,2},{4,5},{5,4},{6,7},{7,6},{8,9},{9,8},{10,11... | collective-permute-start | bytes 786440 | tf_op jit(solution)/shard_map/weights/ppermute | solution.py:30
  16.8 1.5 %collective-permute-start.10 = (bf16[128,896]{1,0:T(8,128)(2,1)S(1)}, bf16[128,896]{1,0:T(8,128)(2,1)S(1)}, u32[]{:S(2)}, u32[]{:S(2)}) collective-permute-start(bf16[128,896]{1,0:T(8,128)(2,1)S(1)} %collective-permute-done.9.own_ref), channel_id=1, source_target_pairs={{0,1},{1,0},{2,3},{3,2},{4,5},{5,4},{6,7},{7,6},{8,9},{9,8},{10,11... | collective-permute-start | bytes 688136 | tf_op jit(solution)/shard_map/layer_two/ppermute | solution.py:30
  22.8 1.6 %collective-permute-start.12 = (bf16[128,1152]{1,0:T(8,128)(2,1)S(1)}, bf16[128,1152]{1,0:T(8,128)(2,1)S(1)}, u32[]{:S(2)}, u32[]{:S(2)}) collective-permute-start(bf16[128,1152]{1,0:T(8,128)(2,1)S(1)} %collective-permute-done.7.own_ref), channel_id=1, source_target_pairs={{0,1},{1,0},{2,3},{3,2},{4,5},{5,4},{6,7},{7,6},{8,9},{9,8},{10,11... | collective-permute-start | bytes 884744 | tf_op jit(solution)/shard_map/layer_two/ppermute | solution.py:30
  23.5 1.8 %collective-permute-start.11 = (bf16[128,512]{1,0:T(8,128)(2,1)S(1)}, bf16[128,512]{1,0:T(8,128)(2,1)S(1)}, u32[]{:S(2)}, u32[]{:S(2)}) collective-permute-start(bf16[128,512]{1,0:T(8,128)(2,1)S(1)} %get-tuple-element.73), channel_id=1, source_target_pairs={{0,1},{1,0},{2,3},{3,2},{4,5},{5,4},{6,7},{7,6},{8,9},{9,8},{10,11... | collective-permute-start | bytes 393224 | tf_op jit(solution)/shard_map/layer_two/ppermute | solution.py:30
  25.1 1.3 %collective-permute-start.13 = (bf16[128,128]{1,0:T(8,128)(2,1)S(1)}, bf16[128,128]{1,0:T(8,128)(2,1)S(1)}, u32[]{:S(2)}, u32[]{:S(2)}) collective-permute-start(bf16[128,128]{1,0:T(8,128)(2,1)S(1)} %layer_two.9.mixed_ref), channel_id=1, source_target_pairs={{0,1},{1,0},{2,3},{3,2},{4,5},{5,4},{6,7},{7,6},{8,9},{9,8},{10,11... | collective-permute-start | bytes 98312 | tf_op jit(solution)/shard_map/layer_two/ppermute | solution.py:30
  26.5 6.8 %collective-permute-start.17 = (bf16[128,512]{1,0:T(8,128)(2,1)S(1)}, bf16[128,512]{1,0:T(8,128)(2,1)S(1)}, u32[]{:S(2)}, u32[]{:S(2)}) collective-permute-start(bf16[128,512]{1,0:T(8,128)(2,1)S(1)} %layer_two.11.refs_0_.refs_1_), channel_id=1, source_target_pairs={{0,6},{2,4},{4,2},{6,0},{1,7},{3,5},{5,3},{7,1},{8,14},{10,12},{12... | collective-permute-start | bytes 393224 | tf_op jit(solution)/shard_map/moments/ppermute | solution.py:30
  29.0 6.8 %collective-permute-start.14 = (bf16[128,512]{1,0:T(8,128)(2,1)S(1)}, bf16[128,512]{1,0:T(8,128)(2,1)S(1)}, u32[]{:S(2)}, u32[]{:S(2)}) collective-permute-start(bf16[128,512]{1,0:T(8,128)(2,1)S(1)} %layer_two.11.refs_0_.refs_1_), channel_id=1, source_target_pairs={{0,4},{2,6},{4,0},{6,2},{1,5},{3,7},{5,1},{7,3},{8,12},{10,14},{12... | collective-permute-start | bytes 393224 | tf_op jit(solution)/shard_map/moments/ppermute | solution.py:30
  29.5 6.4 %collective-permute-start.15 = (bf16[128,512]{1,0:T(8,128)(2,1)S(1)}, bf16[128,512]{1,0:T(8,128)(2,1)S(1)}, u32[]{:S(2)}, u32[]{:S(2)}) collective-permute-start(bf16[128,512]{1,0:T(8,128)(2,1)S(1)} %layer_two.11.refs_0_.refs_1_), channel_id=1, source_target_pairs={{0,2},{2,0},{4,6},{6,4},{1,3},{3,1},{5,7},{7,5},{8,10},{10,8},{12,... | collective-permute-start | bytes 393224 | tf_op jit(solution)/shard_map/moments/ppermute | solution.py:30
  33.5 2.7 %collective-permute-start.18 = (f32[128,256]{1,0:T(8,128)S(1)}, f32[128,256]{1,0:T(8,128)S(1)}, u32[]{:S(2)}, u32[]{:S(2)}) collective-permute-start(f32[128,256]{1,0:T(8,128)S(1)} %moments.5.gram_own_ref), channel_id=1, source_target_pairs={{0,1},{1,0},{2,3},{3,2},{4,5},{5,4},{6,7},{7,6},{8,9},{9,8},{10,11... | collective-permute-start | bytes 393224 | tf_op jit(solution)/shard_map/moments/ppermute | solution.py:30
  36.2 1.4 %collective-permute-start.16 = (f32[128,256]{1,0:T(8,128)S(1)}, f32[128,256]{1,0:T(8,128)S(1)}, u32[]{:S(2)}, u32[]{:S(2)}) collective-permute-start(f32[128,256]{1,0:T(8,128)S(1)} %moments.4.gram_own_ref), channel_id=1, source_target_pairs={{0,1},{1,0},{2,3},{3,2},{4,5},{5,4},{6,7},{7,6},{8,9},{9,8},{10,11... | collective-permute-start | bytes 393224 | tf_op jit(solution)/shard_map/moments/ppermute | solution.py:30

commit v6 on v4

--- a/solution.py
+++ b/solution.py
@@ -15,7 +15,7 @@
 F32 = jnp.float32
 VMEM_BYTES = 18 * 1024 * 1024
 SHARES = (7, 9)
-WO_PARTS = 4
+WO_PARTS = 1
 DP_ORDER = lambda count: reversed(range(1, count))
 
 
@@ -96,8 +96,8 @@
     key_pos = lax.broadcasted_iota(jnp.int32, (rows, rows), 1)
     scores = jnp.where(key_pos < live_len, scores, -1e30)
     weights = jnp.exp(scores - jnp.max(scores, axis=-1, keepdims=True))
-    probs = (weights / jnp.sum(weights, axis=-1, keepdims=True)).astype(BF16)
-    return dot(probs, value).astype(BF16)
+    total = jnp.sum(weights, axis=-1, keepdims=True)
+    return (dot(weights.astype(BF16), value) / total).astype(BF16)
 
 
 def load_body(
@@ -134,34 +134,22 @@
         copy.wait()
 
 
-def first_body(live_ref, oth_ref, w_ref, qkv_ref, square_ref, *refs):
-    wo_send_refs, mixed_ref, parts = refs[:WO_PARTS], refs[WO_PARTS], refs[WO_PARTS + 1 :]
+def first_body(live_ref, oth_ref, w_ref, qkv_ref, square_ref, mixed_ref):
     half = oth_ref.shape[1]
     core = lax.axis_index("tensor")
     oth = oth_ref[...]
     qkv = qkv_ref[...] + dot(oth, w_ref[span((1 - core) * half, half), :])
     scale = rms_scale(square_ref[...] + lane_sums(oth), 2 * half)
-    mixed = softmax_mix(qkv * scale, live_ref[...])
-    mixed_ref[...] = mixed
-    weight = jnp.concatenate([ref[...] for ref in wo_send_refs], axis=1)
-    lower = 0
-    for part_ref in parts:
-        upper = lower + part_ref.shape[1]
-        part_ref[...] = dot(mixed, weight[:, lower:upper]).astype(BF16)
-        lower = upper
-
-
-def held_body(own_ref, mixed_ref, wo_own_ref, held_ref):
-    held_ref[...] = own_ref[...].astype(F32) + dot(mixed_ref[...], wo_own_ref[...])
-
-
-def update_body(lower, held_ref, *refs):
-    parts, out_ref = refs[:-1], refs[-1]
-    width = out_ref.shape[1]
-    part = jnp.concatenate([ref[...] for ref in parts], axis=1)
-    part = part[:, part.shape[1] - width :] if len(parts) > 1 else part[:, :width]
-    held = held_ref[:, lower : lower + width]
-    out_ref[...] = (held + part.astype(F32)).astype(BF16)
+    mixed_ref[...] = softmax_mix(qkv * scale, live_ref[...])
+
+
+def update_body(lower, own_ref, mix_own_ref, mix_oth_ref, w_own_ref, *refs):
+    w_oth_refs, out_ref = refs[:-1], refs[-1]
+    cols = slice(lower, lower + out_ref.shape[1])
+    w_oth = jnp.concatenate([ref[...] for ref in w_oth_refs], axis=1)
+    weight = jnp.concatenate([w_own_ref[:, cols], w_oth[:, cols]], axis=0)
+    mixed = jnp.concatenate([mix_own_ref[...], mix_oth_ref[...]], axis=1)
+    out_ref[...] = (own_ref[:, cols].astype(F32) + dot(mixed, weight)).astype(BF16)
 
 
 def combine_body(lens_ref, w_own_ref, e_hbm, *refs):
@@ -184,47 +172,36 @@
     send_ref[...] = dot(weight, e_ref[:, span((1 - core) * cols, cols)]).astype(BF16)
 
 
-def own_body(lower, own_ref, w_ref, e_ref, *refs):
-    sums, (qkv_ref, square_ref, embed_ref) = refs[:-3], refs[-3:]
-    width = own_ref.shape[1]
-    half = e_ref.shape[0]
-    src = pl.ds(pl.multiple_of(lax.axis_index("tensor") * half + lower, HD), width)
-    x = own_ref[...]
-    qkv, square, embed = dot(x, w_ref[src, :]), lane_sums(x), dot(x, e_ref[lower : lower + width, :])
+def heads_sums(lower, half, own_side, x_ref, w_own_ref, w_oth_ref):
+    core = lax.axis_index("tensor")
+    side = core if own_side else 1 - core
+    src = pl.ds(pl.multiple_of(side * half + lower, HD), x_ref.shape[1])
+    x = x_ref[...]
+    weight = jnp.concatenate([w_own_ref[src, :], w_oth_ref[src, :]], axis=1)
+    return dot(x, weight), lane_sums(x)
+
+
+def heads_body(lower, half, own_side, x_ref, w_own_ref, w_oth_ref, *refs):
+    sums, (qkv_ref, square_ref) = refs[:-2], refs[-2:]
+    qkv, square = heads_sums(lower, half, own_side, x_ref, w_own_ref, w_oth_ref)
     if sums:
         qkv, square = qkv + sums[0][...], square + sums[1][...]
-        embed = embed + sums[2][...]
-    qkv_ref[...], square_ref[...], embed_ref[...] = qkv, square, embed
-
-
-def own_last_body(lower, own_ref, w_ref, e_ref, sum_ref, square_in_ref, embed_in_ref, *refs):
-    qkv_ref, square_ref, mine_ref, send_ref = refs
-    width = own_ref.shape[1]
-    half = e_ref.shape[0]
+    qkv_ref[...], square_ref[...] = qkv, square
+
+
+def embed_piece_body(lower, x_ref, e_ref, *refs):
+    embed = dot(x_ref[...], e_ref[lower : lower + x_ref.shape[1], :])
+    refs[-1][...] = embed + refs[0][...] if lower else embed
+
+
+def embed_last_body(lower, x_ref, e_ref, embed_ref, mine_ref, send_ref):
     cols = mine_ref.shape[1]
     core = lax.axis_index("tensor")
-    src = pl.ds(pl.multiple_of(core * half + lower, HD), width)
-    x = own_ref[...]
+    x = x_ref[...]
+    src = slice(lower, lower + x.shape[1])
     for side, out_ref in ((1 - core, send_ref), (core, mine_ref)):
         at = span(side * cols, cols)
-        embed = embed_in_ref[:, at] + dot(x, e_ref[lower : lower + width, at])
-        out_ref[...] = embed.astype(out_ref.dtype)
-    qkv_ref[...] = sum_ref[...] + dot(x, w_ref[src, :])
-    square_ref[...] = square_in_ref[...] + lane_sums(x)
-
-
-def other_sums(lower, half, oth_ref, w_ref):
-    src = pl.ds(
-        pl.multiple_of((1 - lax.axis_index("tensor")) * half + lower, HD), oth_ref.shape[1]
-    )
-    x = oth_ref[...]
-    return dot(x, w_ref[src, :]), lane_sums(x)
-
-
-def other_body(lower, half, oth_ref, w_ref, sum_ref, square_in_ref, qkv_ref, square_ref):
-    qkv, square = other_sums(lower, half, oth_ref, w_ref)
-    qkv_ref[...] = sum_ref[...] + qkv
-    square_ref[...] = square_in_ref[...] + square
+        out_ref[...] = (embed_ref[:, at] + dot(x, e_ref[src, at])).astype(out_ref.dtype)
 
 
 def hop_anchor():
@@ -232,10 +209,15 @@
     return lax.rem(lax.axis_index("section") + sections - 1, sections)
 
 
-def second_body(lower, half, live_ref, oth_ref, w_ref, sum_ref, square_in_ref, mixed_ref):
-    qkv, square = other_sums(lower, half, oth_ref, w_ref)
-    scale = rms_scale(square_in_ref[...] + square, 2 * half)
-    mixed_ref[...] = softmax_mix((sum_ref[...] + qkv) * scale, live_ref[...])
+def second_body(
+    lower, half, live_ref, x_ref, w_own_ref, w_oth_ref, sum_ref, square_ref, mixed_ref
+):
+    qkv, square = heads_sums(lower, half, False, x_ref, w_own_ref, w_oth_ref)
+    qkv = (qkv + sum_ref[...]) * rms_scale(square + square_ref[...], 2 * half)
+    live = live_ref[...]
+    for head in range(2):
+        at = head * QKV
+        mixed_ref[:, head * HD : (head + 1) * HD] = softmax_mix(qkv[:, at : at + QKV], live)
 
 
 def combine_sum_body(mine_ref, recv_ref, out_ref):
@@ -244,13 +226,8 @@
     out_ref[rows:, :] = (mine_ref[rows:, :] + recv_ref[:rows, :]).astype(BF16)
 
 
-def embed_own_body(mine_ref, recv_ref, mixed_ref, combined_ref, out_ref):
-    product = dot(mixed_ref[...], combined_ref[: mixed_ref.shape[1], :])
-    out_ref[...] = mine_ref[...] + recv_ref[...].astype(F32) + product
-
-
-def embed_body(live_ref, sum_ref, mixed_ref, combined_ref, out_ref):
-    embed = sum_ref[...] + dot(mixed_ref[...], combined_ref[mixed_ref.shape[1] :, :])
+def embed_body(live_ref, mine_ref, recv_ref, mixed_ref, combined_ref, out_ref):
+    embed = mine_ref[...] + recv_ref[...].astype(F32) + dot(mixed_ref[...], combined_ref[...])
     live = live_ref[...]
     keep = lax.broadcasted_iota(jnp.int32, live.shape, 0) < live
     for lane in range(0, embed.shape[1], HD):
@@ -328,18 +305,17 @@
             9 + WO_PARTS,
             scratch=(pltpu.SMEM(lens.shape, jnp.int32),),
         )(lens, tokens, w_query, w_key, w_value, w_out)
-        mixed, *parts = call(
-            first_body, [shape(rows, HD)] + [shape(rows, half // 2)] * 2, "v" * (5 + WO_PARTS)
-        )(live, oth, w_own, qkv, square, *wo_send)
-        parts = [exchanged(part, "tensor", 1) for part in parts]
-        held = call(held_body, shape(rows, half, dtype=F32), "vvv")(own, mixed, wo_own)
-        state = []
-        for lower, width in zip(lowers, widths):
-            needed = parts if lower else parts[:1]
-            body = functools.partial(update_body, lower)
-            state.append(call(body, shape(rows, width), "v" * (1 + len(needed)))(held, *needed))
+        wo_oth = [exchanged(part, "tensor", 1) for part in wo_send]
+        mixed = call(first_body, shape(rows, HD), "vvvvv")(live, oth, w_own, qkv, square)
+        mixed_oth = exchanged(mixed, "tensor", 1)
+        state = [
+            call(functools.partial(update_body, lower), shape(rows, width), "v" * (4 + WO_PARTS))(
+                own, mixed, mixed_oth, wo_own, *wo_oth
+            )
+            for lower, width in zip(lowers, widths)
+        ]
     with jax.named_scope("weights"):
-        wo_oth = [exchanged(after(part, state[-1]), "tensor", 1) for part in wo_send]
+        w_oth = exchanged(after(w_own, state[0]), "tensor", 1)
     with jax.named_scope("hop"):
         state = [shifted(piece, "section", 1) for piece in state]
     with jax.named_scope("weights"):
@@ -356,38 +332,38 @@
         )
     with jax.named_scope("layer_two"):
         sums = ()
+        sum_shapes = [shape(rows, 2 * QKV, dtype=F32), shape(rows, HD, dtype=F32)]
         for lower, piece in zip(lowers, state):
-            if sums:
-                piece, combined, *sums = lax.optimization_barrier((piece, combined, *sums))
+            if lower == lowers[-1]:
+                piece, combined, embed, *sums = lax.optimization_barrier(
+                    (piece, combined, embed, *sums)
+                )
             oth = exchanged(piece, "tensor", 1)
             if lower != lowers[-1]:
-                qkv, square, embed = call(
-                    functools.partial(own_body, lower),
-                    [shape(rows, QKV, dtype=F32), shape(rows, HD, dtype=F32), shape(rows, 2 * cols, dtype=F32)],
-                    "v" * (3 + len(sums)),
-                )(piece, w_own, w_embed_own, *sums)
-                qkv, square = call(
-                    functools.partial(other_body, lower, half),
-                    [shape(rows, QKV, dtype=F32), shape(rows, HD, dtype=F32)],
-                    "vvvv",
-                )(oth, w_own, qkv, square)
-                sums = (qkv, square, embed)
+                operands = (piece, w_embed_own, embed) if lower else (piece, w_embed_own)
+                embed = call(
+                    functools.partial(embed_piece_body, lower),
+                    shape(rows, 2 * cols, dtype=F32),
+                    "v" * len(operands),
+                )(*operands)
             else:
-                qkv, square, e_mine, e_send = call(
-                    functools.partial(own_last_body, lower),
-                    [shape(rows, QKV, dtype=F32), shape(rows, HD, dtype=F32)]
-                    + [shape(rows, cols, dtype=F32), shape(rows, cols)],
-                    "v" * 6,
-                )(piece, w_own, w_embed_own, *sums)
+                e_mine, e_send = call(
+                    functools.partial(embed_last_body, lower),
+                    [shape(rows, cols, dtype=F32), shape(rows, cols)],
+                    "vvv",
+                )(piece, w_embed_own, embed)
+            sums = call(
+                functools.partial(heads_body, lower, half, True), sum_shapes, "v" * (3 + len(sums))
+            )(piece, w_own, w_oth, *sums)
+            if lower != lowers[-1]:
+                sums = call(
+                    functools.partial(heads_body, lower, half, False), sum_shapes, "v" * 5
+                )(oth, w_own, w_oth, *sums)
         e_recv = exchanged(e_send, "tensor", 1)
         mixed = call(
-            functools.partial(second_body, lower, half), shape(rows, HD), "vvvvv"
-        )(live, oth, w_own, qkv, square)
-        mixed_oth = exchanged(mixed, "tensor", 1)
-        embed = call(embed_own_body, shape(rows, cols, dtype=F32), "vvvv")(
-            e_mine, e_recv, mixed, combined
-        )
-        embed = call(embed_body, shape(rows, cols), "vvvv")(live, embed, mixed_oth, combined)
+            functools.partial(second_body, lower, half), shape(rows, 2 * HD), "v" * 6
+        )(live, oth, w_own, w_oth, *sums)
+        embed = call(embed_body, shape(rows, cols), "v" * 5)(live, e_mine, e_recv, mixed, combined)
     with jax.named_scope("moments"):
         embeds = [embed] + [exchanged(embed, "dp", mask) for mask in DP_ORDER(group_count)]
         sums = ()

time: 38.9 us -> 37.8 us (0.972)
  starting transfers between devices: 11 us -> 10.2 us
  waiting for transfers between devices: 15.3 us -> 14.7 us
    ppermute x17 -> x13, waiting for transfers between devices: 9.8 us -> 8.15 us  [exchanged(): lax.ppermute(value, axis, [(source, source ^ mask) for source in range(co...]
    ppermute x2, waiting for transfers between devices: 5.5 us -> 6.59 us  [shifted(): return lax.ppermute(value, axis, pairs)]
    ppermute x17 -> x13, starting transfers between devices: 6.67 us -> 5.86 us  [exchanged(): lax.ppermute(value, axis, [(source, source ^ mask) for source in range(co...]
  transfers between devices with their start and end apart: 19 -> 15, of which waited for: 11 -> 9; matrix products, arithmetic and copies ran while one was open for 0% -> 0% of each run, Pallas kernels for 26% -> 30%
where the time goes in v6:
time: 37.8 us; the launch traced here: 37.7 us
  waiting for transfers between devices  14.7 us (39%)
  Pallas kernels  12.5 us (33%)
  starting transfers between devices  10.2 us (27%)
    pallas_call x17, Pallas kernels, call(): return lambda *operands: kernel(*map(place, operands, spaces))  12.5 us
    ppermute x13, waiting for transfers between devices, exchanged(): lax.ppermute(value, axis, [(source, source ^ mask) for source in range(co...  8.15 us
    ppermute x2, waiting for transfers between devices, shifted(): return lax.ppermute(value, axis, pairs)  6.59 us
    ppermute x13, starting transfers between devices, exchanged(): lax.ppermute(value, axis, [(source, source ^ mask) for source in range(co...  5.86 us
    ppermute x2, starting transfers between devices, shifted(): return lax.ppermute(value, axis, pairs)  4.37 us
  transfers between devices with their start and end apart: 15, of which 9 were waited for; matrix products, arithmetic and copies ran while one was open for 0% of the time, Pallas kernels for 30%

profile of v6, /device:TPU:0, one launch (start us, length us, event | category | flops | bytes accessed | tf_op | source)
XLA Modules:
  0.0 37.7 jit_solution(7195916619873310017)
XLA Ops:
  0.0 0.5 %collective-permute-start.1 = (bf16[128,2048]{1,0:T(8,128)(2,1)}, bf16[128,2048]{1,0:T(8,128)(2,1)S(1)}, u32[]{:S(2)}, u32[]{:S(2)}) collective-permute-start(bf16[128,2048]{1,0:T(8,128)(2,1)} %bitcast.5), channel_id=1, source_target_pairs={{0,1},{1,0},{2,3},{3,2},{4,5},{5,4},{6,7},{7,6},{8,9},{9,8},{10,11... | collective-permute-start | bytes 1572872 | tf_op jit(solution)/shard_map/layer_one/ppermute | solution.py:30
  0.5 2.4 %layer_one.4 = (bf16[128,2048]{1,0:T(8,128)(2,1)S(1)}, bf16[4096,384]{1,0:T(8,128)(2,1)S(1)}, f32[128,384]{1,0:T(8,128)S(1)}, f32[128,128]{1,0:T(8,128)S(1)}, s3...) custom-call(s32[4]{0:T(128)} %bitcast.3, bf16[1,128,2048]{2,1,0:T(8,128)(2,1)} %own_hbm.1, ...), custom_call_target="tpu_custom_call" | custom-call | tf_op jit(solution)/shard_map/layer_one/pallas_call | solution.py:72
  2.9 0.0 copy-start
  2.9 0.1 collective-permute-start
  3.0 0.0 collective-permute-done.1.oth_ref
  3.0 0.8 %layer_one.5.mix_own_ref = bf16[128,128]{1,0:T(8,128)(2,1)S(1)} custom-call(s32[128,128]{1,0:T(8,128)S(1)} %get-tuple-element.34.live_ref, bf16[128,2048]{1,0:T(8,128)(2,1)S(1)} %collective-permute-done.1.oth_ref, bf16[4096,384]{1,0:T(8,128)(2,1)S(1)} %get-tuple-element.41.w_ref.w_own_ref, f32[128,384]{1,0:T(8,128)S(1)} %get-tuple-element.36.qkv_ref, ...), custom_call_target="tpu_custom_call" | custom-call | tf_op jit(solution)/shard_map/layer_one/pallas_call | solution.py:72
  3.8 0.5 %collective-permute-start.2 = (bf16[128,128]{1,0:T(8,128)(2,1)S(1)}, bf16[128,128]{1,0:T(8,128)(2,1)S(1)}, u32[]{:S(2)}, u32[]{:S(2)}) collective-permute-start(bf16[128,128]{1,0:T(8,128)(2,1)S(1)} %layer_one.5.mix_own_ref), channel_id=1, source_target_pairs={{0,1},{1,0},{2,3},{3,2},{4,5},{5,4},{6,7},{7,6},{8,9},{9,8},{10,11... | collective-permute-start | bytes 98312 | tf_op jit(solution)/shard_map/layer_one/ppermute | solution.py:30
  4.3 0.5 %collective-permute-done.refs_0_ = bf16[128,2048]{1,0:T(8,128)(2,1)S(1)} collective-permute-done((bf16[128,2048]{1,0:T(8,128)(2,1)S(1)}, bf16[128,2048]{1,0:T(8,128)(2,1)S(1)}, u32[]{:S(2)}, u32[]{:S(2)}) %collective-permute-start) | collective-permute-done | bytes 524320 | tf_op jit(solution)/shard_map/layer_one/ppermute | solution.py:30
  4.8 0.3 collective-permute-done.2.mix_oth_ref
  5.2 0.2 layer_one.7
  5.4 0.4 %collective-permute-start.7 = (bf16[4096,384]{1,0:T(8,128)(2,1)S(1)}, bf16[4096,384]{1,0:T(8,128)(2,1)S(1)}, u32[]{:S(2)}, u32[]{:S(2)}) collective-permute-start(bf16[4096,384]{1,0:T(8,128)(2,1)S(1)} %get-tuple-element.41.w_ref.w_own_ref), channel_id=1, source_target_pairs={{0,1},{1,0},{2,3},{3,2},{4,5},{5,4},{6,7},{7,6},{8,9},{9,8},{10,11... | collective-permute-start | bytes 9437192 | tf_op jit(solution)/shard_map/weights/ppermute | solution.py:30
  5.8 2.7 %collective-permute-start.5 = (bf16[128,896]{1,0:T(8,128)(2,1)S(1)}, bf16[128,896]{1,0:T(8,128)(2,1)S(1)}, u32[]{:S(2)}, u32[]{:S(2)}) collective-permute-start(bf16[128,896]{1,0:T(8,128)(2,1)S(1)} %layer_one.7), channel_id=1, source_target_pairs={{0,8},{8,16},{16,24},{24,0},{1,9},{9,17},{17,25},{25,1},{2,10},{10... | collective-permute-start | bytes 688136 | tf_op jit(solution)/shard_map/hop/ppermute | solution.py:25
  8.6 0.3 layer_one.6
  8.8 1.6 %collective-permute-start.3 = (bf16[128,1152]{1,0:T(8,128)(2,1)S(1)}, bf16[128,1152]{1,0:T(8,128)(2,1)S(1)}, u32[]{:S(2)}, u32[]{:S(2)}) collective-permute-start(bf16[128,1152]{1,0:T(8,128)(2,1)S(1)} %layer_one.6), channel_id=1, source_target_pairs={{0,8},{8,16},{16,24},{24,0},{1,9},{9,17},{17,25},{25,1},{2,10},{10... | collective-permute-start | bytes 884744 | tf_op jit(solution)/shard_map/hop/ppermute | solution.py:25
  10.4 0.0 copy-done
  10.4 4.0 %weights.2 = (bf16[2048,1024]{1,0:T(8,128)(2,1)S(1)}, f32[256,512]{1,0:T(8,128)S(1)}, bf16[256,512]{1,0:T(8,128)(2,1)S(1)}, s32[128,128]{1,0:T(8,128)S(1)}) custom-call(s32[4]{0:T(128)S(1)} %bitcast.4, bf16[128,2048]{1,0:T(8,128)(2,1)S(1)} %get-tuple-element.30.w_own_ref, bf16[2048,1024]{1,0:T(8,128)(2,1)} %e_hbm.1, ...), custom_call_target="tpu_custom_call" | custom-call | tf_op jit(solution)/shard_map/weights/pallas_call | solution.py:72
  14.5 0.1 collective-permute-start.4
  14.5 2.5 %collective-permute-done.5.x_ref = bf16[128,896]{1,0:T(8,128)(2,1)S(1)} collective-permute-done((bf16[128,896]{1,0:T(8,128)(2,1)S(1)}, bf16[128,896]{1,0:T(8,128)(2,1)S(1)}, u32[]{:S(2)}, u32[]{:S(2)}) %collective-permute-start.5) | collective-permute-done | bytes 229408 | tf_op jit(solution)/shard_map/hop/ppermute | solution.py:25
  17.0 0.0 collective-permute-start.6
  17.0 0.0 collective-permute-done.4.recv_ref
  17.1 0.5 %layer_two.7.embed_ref = f32[128,1024]{1,0:T(8,128)S(1)} custom-call(bf16[128,896]{1,0:T(8,128)(2,1)S(1)} %collective-permute-done.5.x_ref, bf16[2048,1024]{1,0:T(8,128)(2,1)S(1)} %get-tuple-element.40.e_ref), custom_call_target="tpu_custom_call" | custom-call | tf_op jit(solution)/shard_map/layer_two/pallas_call | solution.py:72
  17.5 0.0 collective-permute-done.7.w_oth_ref
  17.6 0.4 %layer_two.8 = (f32[128,768]{1,0:T(8,128)S(1)}, f32[128,128]{1,0:T(8,128)S(1)}) custom-call(bf16[128,896]{1,0:T(8,128)(2,1)S(1)} %collective-permute-done.5.x_ref, bf16[4096,384]{1,0:T(8,128)(2,1)S(1)} %get-tuple-element.41.w_ref.w_own_ref, bf16[4096,384]{1,0:T(8,128)(2,1)S(1)} %collective-permute-done.7.w_oth_ref), custom_call_target="tpu_custom_call" | custom-call | tf_op jit(solution)/shard_map/layer_two/pallas_call | solution.py:72
  17.9 0.6 %collective-permute-done.6.x_ref = bf16[128,896]{1,0:T(8,128)(2,1)S(1)} collective-permute-done((bf16[128,896]{1,0:T(8,128)(2,1)S(1)}, bf16[128,896]{1,0:T(8,128)(2,1)S(1)}, u32[]{:S(2)}, u32[]{:S(2)}) %collective-permute-start.6) | collective-permute-done | bytes 229408 | tf_op jit(solution)/shard_map/layer_two/ppermute | solution.py:30
  18.5 0.4 %layer_two.9 = (f32[128,768]{1,0:T(8,128)S(1)}, f32[128,128]{1,0:T(8,128)S(1)}) custom-call(bf16[128,896]{1,0:T(8,128)(2,1)S(1)} %collective-permute-done.6.x_ref, bf16[4096,384]{1,0:T(8,128)(2,1)S(1)} %get-tuple-element.41.w_ref.w_own_ref, bf16[4096,384]{1,0:T(8,128)(2,1)S(1)} %collective-permute-done.7.w_oth_ref, ...), custom_call_target="tpu_custom_call" | custom-call | tf_op jit(solution)/shard_map/layer_two/pallas_call | solution.py:72
  18.9 4.1 %collective-permute-done.3.x_ref = bf16[128,1152]{1,0:T(8,128)(2,1)S(1)} collective-permute-done((bf16[128,1152]{1,0:T(8,128)(2,1)S(1)}, bf16[128,1152]{1,0:T(8,128)(2,1)S(1)}, u32[]{:S(2)}, u32[]{:S(2)}) %collective-permute-start.3) | collective-permute-done | bytes 294944 | tf_op jit(solution)/shard_map/hop/ppermute | solution.py:25
  23.0 0.0 collective-permute-start.9
  23.0 0.5 %layer_two.10 = (f32[128,512]{1,0:T(8,128)S(1)}, bf16[128,512]{1,0:T(8,128)(2,1)S(1)}) custom-call(bf16[128,1152]{1,0:T(8,128)(2,1)S(1)} %collective-permute-done.3.x_ref, bf16[2048,1024]{1,0:T(8,128)(2,1)S(1)} %get-tuple-element.40.e_ref, f32[128,1024]{1,0:T(8,128)S(1)} %layer_two.7.embed_ref), custom_call_target="tpu_custom_call" | custom-call | tf_op jit(solution)/shard_map/layer_two/pallas_call | solution.py:72
  23.6 0.6 %collective-permute-start.8 = (bf16[128,512]{1,0:T(8,128)(2,1)S(1)}, bf16[128,512]{1,0:T(8,128)(2,1)S(1)}, u32[]{:S(2)}, u32[]{:S(2)}) collective-permute-start(bf16[128,512]{1,0:T(8,128)(2,1)S(1)} %get-tuple-element.49), channel_id=1, source_target_pairs={{0,1},{1,0},{2,3},{3,2},{4,5},{5,4},{6,7},{7,6},{8,9},{9,8},{10,11... | collective-permute-start | bytes 393224 | tf_op jit(solution)/shard_map/layer_two/ppermute | solution.py:30
  24.1 0.4 %layer_two.11 = (f32[128,768]{1,0:T(8,128)S(1)}, f32[128,128]{1,0:T(8,128)S(1)}) custom-call(bf16[128,1152]{1,0:T(8,128)(2,1)S(1)} %collective-permute-done.3.x_ref, bf16[4096,384]{1,0:T(8,128)(2,1)S(1)} %get-tuple-element.41.w_ref.w_own_ref, bf16[4096,384]{1,0:T(8,128)(2,1)S(1)} %collective-permute-done.7.w_oth_ref, ...), custom_call_target="tpu_custom_call" | custom-call | tf_op jit(solution)/shard_map/layer_two/pallas_call | solution.py:72
  24.6 0.0 collective-permute-done.9.x_ref
  24.6 0.9 %layer_two.12.mixed_ref = bf16[128,256]{1,0:T(8,128)(2,1)S(1)} custom-call(s32[128,128]{1,0:T(8,128)S(1)} %get-tuple-element.32.live_ref, bf16[128,1152]{1,0:T(8,128)(2,1)S(1)} %collective-permute-done.9.x_ref, bf16[4096,384]{1,0:T(8,128)(2,1)S(1)} %get-tuple-element.41.w_ref.w_own_ref, bf16[4096,384]{1,0:T(8,128)(2,1)S(1)} %collective-permute-done.7.w_oth_ref, ...), custom_call_target="tpu_custom_call" | custom-call | tf_op jit(solution)/shard_map/layer_two/pallas_call | solution.py:72
  25.5 0.0 collective-permute-done.8.recv_ref
  25.5 0.2 layer_two.13.refs_0_.refs_1_
  25.7 2.5 %collective-permute-start.13 = (bf16[128,512]{1,0:T(8,128)(2,1)S(1)}, bf16[128,512]{1,0:T(8,128)(2,1)S(1)}, u32[]{:S(2)}, u32[]{:S(2)}) collective-permute-start(bf16[128,512]{1,0:T(8,128)(2,1)S(1)} %layer_two.13.refs_0_.refs_1_), channel_id=1, source_target_pairs={{0,6},{2,4},{4,2},{6,0},{1,7},{3,5},{5,3},{7,1},{8,14},{10,12},{12... | collective-permute-start | bytes 393224 | tf_op jit(solution)/shard_map/moments/ppermute | solution.py:30
  28.2 0.5 %collective-permute-start.10 = (bf16[128,512]{1,0:T(8,128)(2,1)S(1)}, bf16[128,512]{1,0:T(8,128)(2,1)S(1)}, u32[]{:S(2)}, u32[]{:S(2)}) collective-permute-start(bf16[128,512]{1,0:T(8,128)(2,1)S(1)} %layer_two.13.refs_0_.refs_1_), channel_id=1, source_target_pairs={{0,4},{2,6},{4,0},{6,2},{1,5},{3,7},{5,1},{7,3},{8,12},{10,14},{12... | collective-permute-start | bytes 393224 | tf_op jit(solution)/shard_map/moments/ppermute | solution.py:30
  28.7 0.5 %collective-permute-start.11 = (bf16[128,512]{1,0:T(8,128)(2,1)S(1)}, bf16[128,512]{1,0:T(8,128)(2,1)S(1)}, u32[]{:S(2)}, u32[]{:S(2)}) collective-permute-start(bf16[128,512]{1,0:T(8,128)(2,1)S(1)} %layer_two.13.refs_0_.refs_1_), channel_id=1, source_target_pairs={{0,2},{2,0},{4,6},{6,4},{1,3},{3,1},{5,7},{7,5},{8,10},{10,8},{12,... | collective-permute-start | bytes 393224 | tf_op jit(solution)/shard_map/moments/ppermute | solution.py:30
  29.3 3.2 %collective-permute-done.13.refs_2_.refs_1_ = bf16[128,512]{1,0:T(8,128)(2,1)S(1)} collective-permute-done((bf16[128,512]{1,0:T(8,128)(2,1)S(1)}, bf16[128,512]{1,0:T(8,128)(2,1)S(1)}, u32[]{:S(2)}, u32[]{:S(2)}) %collective-permute-start.13) | collective-permute-done | bytes 131104 | tf_op jit(solution)/shard_map/moments/ppermute | solution.py:30
  32.5 0.2 moments.5.gram_own_ref
  32.7 0.1 collective-permute-start.14
  32.8 2.2 %collective-permute-done.10.refs_1_.refs_0_ = bf16[128,512]{1,0:T(8,128)(2,1)S(1)} collective-permute-done((bf16[128,512]{1,0:T(8,128)(2,1)S(1)}, bf16[128,512]{1,0:T(8,128)(2,1)S(1)}, u32[]{:S(2)}, u32[]{:S(2)}) %collective-permute-start.10) | collective-permute-done | bytes 131104 | tf_op jit(solution)/shard_map/moments/ppermute | solution.py:30
  35.0 0.1 collective-permute-done.11.refs_2_.refs_1_
  35.1 0.2 moments.4.gram_own_ref
  35.3 0.1 collective-permute-start.12
  35.4 0.0 collective-permute-done.14.gram_oth_ref
  35.4 0.2 moments.6.refs_2_
  35.6 1.1 %collective-permute-done.12.gram_oth_ref = f32[128,256]{1,0:T(8,128)S(1)} collective-permute-done((f32[128,256]{1,0:T(8,128)S(1)}, f32[128,256]{1,0:T(8,128)S(1)}, u32[]{:S(2)}, u32[]{:S(2)}) %collective-permute-start.12) | collective-permute-done | bytes 131104 | tf_op jit(solution)/shard_map/moments/ppermute | solution.py:30
  36.8 0.9 %moments.7 = f32[128,512]{1,0:T(8,128)} custom-call(f32[128,256]{1,0:T(8,128)S(1)} %moments.4.gram_own_ref, f32[128,256]{1,0:T(8,128)S(1)} %collective-permute-done.12.gram_oth_ref, bf16[128,512]{1,0:T(8,128)(2,1)S(1)} %collective-permute-done.10.refs_1_.refs_0_, bf16[128,512]{1,0:T(8,128)(2,1)S(1)} %collective-permute-done.11.refs_2_.refs_1_, ...), custom_call_target="tpu_custom_call" | custom-call | tf_op jit(solution)/shard_map/moments/pallas_call | solution.py:72
  (1 shorter events, 0.0 us)
Async XLA Ops:
  0.0 3.0 %collective-permute-start.1 = (bf16[128,2048]{1,0:T(8,128)(2,1)}, bf16[128,2048]{1,0:T(8,128)(2,1)S(1)}, u32[]{:S(2)}, u32[]{:S(2)}) collective-permute-start(bf16[128,2048]{1,0:T(8,128)(2,1)} %bitcast.5), channel_id=1, source_target_pairs={{0,1},{1,0},{2,3},{3,2},{4,5},{5,4},{6,7},{7,6},{8,9},{9,8},{10,11... | collective-permute-start | bytes 1572872 | tf_op jit(solution)/shard_map/layer_one/ppermute | solution.py:30
  2.9 7.6 %copy-start = (s32[4,1]{0,1:T(1,128)S(1)}, s32[4,1]{0,1:T(1,128)}, u32[]{:S(2)}) copy-start(s32[4,1]{0,1:T(1,128)} %param.8) | copy-start | bytes 52
  2.9 2.0 %collective-permute-start = (bf16[128,2048]{1,0:T(8,128)(2,1)S(1)}, bf16[128,2048]{1,0:T(8,128)(2,1)S(1)}, u32[]{:S(2)}, u32[]{:S(2)}) collective-permute-start(bf16[128,2048]{1,0:T(8,128)(2,1)S(1)} %get-tuple-element.31), channel_id=1, source_target_pairs={{0,1},{1,0},{2,3},{3,2},{4,5},{5,4},{6,7},{7,6},{8,9},{9,8},{10,11... | collective-permute-start | bytes 1572872 | tf_op jit(solution)/shard_map/layer_one/ppermute | solution.py:30
  3.8 1.4 %collective-permute-start.2 = (bf16[128,128]{1,0:T(8,128)(2,1)S(1)}, bf16[128,128]{1,0:T(8,128)(2,1)S(1)}, u32[]{:S(2)}, u32[]{:S(2)}) collective-permute-start(bf16[128,128]{1,0:T(8,128)(2,1)S(1)} %layer_one.5.mix_own_ref), channel_id=1, source_target_pairs={{0,1},{1,0},{2,3},{3,2},{4,5},{5,4},{6,7},{7,6},{8,9},{9,8},{10,11... | collective-permute-start | bytes 98312 | tf_op jit(solution)/shard_map/layer_one/ppermute | solution.py:30
  5.4 12.1 %collective-permute-start.7 = (bf16[4096,384]{1,0:T(8,128)(2,1)S(1)}, bf16[4096,384]{1,0:T(8,128)(2,1)S(1)}, u32[]{:S(2)}, u32[]{:S(2)}) collective-permute-start(bf16[4096,384]{1,0:T(8,128)(2,1)S(1)} %get-tuple-element.41.w_ref.w_own_ref), channel_id=1, source_target_pairs={{0,1},{1,0},{2,3},{3,2},{4,5},{5,4},{6,7},{7,6},{8,9},{9,8},{10,11... | collective-permute-start | bytes 9437192 | tf_op jit(solution)/shard_map/weights/ppermute | solution.py:30
  5.8 11.2 %collective-permute-start.5 = (bf16[128,896]{1,0:T(8,128)(2,1)S(1)}, bf16[128,896]{1,0:T(8,128)(2,1)S(1)}, u32[]{:S(2)}, u32[]{:S(2)}) collective-permute-start(bf16[128,896]{1,0:T(8,128)(2,1)S(1)} %layer_one.7), channel_id=1, source_target_pairs={{0,8},{8,16},{16,24},{24,0},{1,9},{9,17},{17,25},{25,1},{2,10},{10... | collective-permute-start | bytes 688136 | tf_op jit(solution)/shard_map/hop/ppermute | solution.py:25
  8.8 14.2 %collective-permute-start.3 = (bf16[128,1152]{1,0:T(8,128)(2,1)S(1)}, bf16[128,1152]{1,0:T(8,128)(2,1)S(1)}, u32[]{:S(2)}, u32[]{:S(2)}) collective-permute-start(bf16[128,1152]{1,0:T(8,128)(2,1)S(1)} %layer_one.6), channel_id=1, source_target_pairs={{0,8},{8,16},{16,24},{24,0},{1,9},{9,17},{17,25},{25,1},{2,10},{10... | collective-permute-start | bytes 884744 | tf_op jit(solution)/shard_map/hop/ppermute | solution.py:25
  14.5 2.6 %collective-permute-start.4 = (bf16[256,512]{1,0:T(8,128)(2,1)S(1)}, bf16[256,512]{1,0:T(8,128)(2,1)S(1)}, u32[]{:S(2)}, u32[]{:S(2)}) collective-permute-start(bf16[256,512]{1,0:T(8,128)(2,1)S(1)} %get-tuple-element.39), channel_id=1, source_target_pairs={{0,1},{1,0},{2,3},{3,2},{4,5},{5,4},{6,7},{7,6},{8,9},{9,8},{10,11... | collective-permute-start | bytes 786440 | tf_op jit(solution)/shard_map/weights/ppermute | solution.py:30
  17.0 1.5 %collective-permute-start.6 = (bf16[128,896]{1,0:T(8,128)(2,1)S(1)}, bf16[128,896]{1,0:T(8,128)(2,1)S(1)}, u32[]{:S(2)}, u32[]{:S(2)}) collective-permute-start(bf16[128,896]{1,0:T(8,128)(2,1)S(1)} %collective-permute-done.5.x_ref), channel_id=1, source_target_pairs={{0,1},{1,0},{2,3},{3,2},{4,5},{5,4},{6,7},{7,6},{8,9},{9,8},{10,11... | collective-permute-start | bytes 688136 | tf_op jit(solution)/shard_map/layer_two/ppermute | solution.py:30
  23.0 1.6 %collective-permute-start.9 = (bf16[128,1152]{1,0:T(8,128)(2,1)S(1)}, bf16[128,1152]{1,0:T(8,128)(2,1)S(1)}, u32[]{:S(2)}, u32[]{:S(2)}) collective-permute-start(bf16[128,1152]{1,0:T(8,128)(2,1)S(1)} %collective-permute-done.3.x_ref), channel_id=1, source_target_pairs={{0,1},{1,0},{2,3},{3,2},{4,5},{5,4},{6,7},{7,6},{8,9},{9,8},{10,11... | collective-permute-start | bytes 884744 | tf_op jit(solution)/shard_map/layer_two/ppermute | solution.py:30
  23.6 1.9 %collective-permute-start.8 = (bf16[128,512]{1,0:T(8,128)(2,1)S(1)}, bf16[128,512]{1,0:T(8,128)(2,1)S(1)}, u32[]{:S(2)}, u32[]{:S(2)}) collective-permute-start(bf16[128,512]{1,0:T(8,128)(2,1)S(1)} %get-tuple-element.49), channel_id=1, source_target_pairs={{0,1},{1,0},{2,3},{3,2},{4,5},{5,4},{6,7},{7,6},{8,9},{9,8},{10,11... | collective-permute-start | bytes 393224 | tf_op jit(solution)/shard_map/layer_two/ppermute | solution.py:30
  25.7 6.8 %collective-permute-start.13 = (bf16[128,512]{1,0:T(8,128)(2,1)S(1)}, bf16[128,512]{1,0:T(8,128)(2,1)S(1)}, u32[]{:S(2)}, u32[]{:S(2)}) collective-permute-start(bf16[128,512]{1,0:T(8,128)(2,1)S(1)} %layer_two.13.refs_0_.refs_1_), channel_id=1, source_target_pairs={{0,6},{2,4},{4,2},{6,0},{1,7},{3,5},{5,3},{7,1},{8,14},{10,12},{12... | collective-permute-start | bytes 393224 | tf_op jit(solution)/shard_map/moments/ppermute | solution.py:30
  28.2 6.8 %collective-permute-start.10 = (bf16[128,512]{1,0:T(8,128)(2,1)S(1)}, bf16[128,512]{1,0:T(8,128)(2,1)S(1)}, u32[]{:S(2)}, u32[]{:S(2)}) collective-permute-start(bf16[128,512]{1,0:T(8,128)(2,1)S(1)} %layer_two.13.refs_0_.refs_1_), channel_id=1, source_target_pairs={{0,4},{2,6},{4,0},{6,2},{1,5},{3,7},{5,1},{7,3},{8,12},{10,14},{12... | collective-permute-start | bytes 393224 | tf_op jit(solution)/shard_map/moments/ppermute | solution.py:30
  28.7 6.4 %collective-permute-start.11 = (bf16[128,512]{1,0:T(8,128)(2,1)S(1)}, bf16[128,512]{1,0:T(8,128)(2,1)S(1)}, u32[]{:S(2)}, u32[]{:S(2)}) collective-permute-start(bf16[128,512]{1,0:T(8,128)(2,1)S(1)} %layer_two.13.refs_0_.refs_1_), channel_id=1, source_target_pairs={{0,2},{2,0},{4,6},{6,4},{1,3},{3,1},{5,7},{7,5},{8,10},{10,8},{12,... | collective-permute-start | bytes 393224 | tf_op jit(solution)/shard_map/moments/ppermute | solution.py:30
  32.7 2.7 %collective-permute-start.14 = (f32[128,256]{1,0:T(8,128)S(1)}, f32[128,256]{1,0:T(8,128)S(1)}, u32[]{:S(2)}, u32[]{:S(2)}) collective-permute-start(f32[128,256]{1,0:T(8,128)S(1)} %moments.5.gram_own_ref), channel_id=1, source_target_pairs={{0,1},{1,0},{2,3},{3,2},{4,5},{5,4},{6,7},{7,6},{8,9},{9,8},{10,11... | collective-permute-start | bytes 393224 | tf_op jit(solution)/shard_map/moments/ppermute | solution.py:30
  35.3 1.4 %collective-permute-start.12 = (f32[128,256]{1,0:T(8,128)S(1)}, f32[128,256]{1,0:T(8,128)S(1)}, u32[]{:S(2)}, u32[]{:S(2)}) collective-permute-start(f32[128,256]{1,0:T(8,128)S(1)} %moments.4.gram_own_ref), channel_id=1, source_target_pairs={{0,1},{1,0},{2,3},{3,2},{4,5},{5,4},{6,7},{7,6},{8,9},{9,8},{10,11... | collective-permute-start | bytes 393224 | tf_op jit(solution)/shard_map/moments/ppermute | solution.py:30

commit v7 on v6

--- a/solution.py
+++ b/solution.py
@@ -14,8 +14,9 @@
 BF16 = jnp.bfloat16
 F32 = jnp.float32
 VMEM_BYTES = 18 * 1024 * 1024
-SHARES = (7, 9)
+SHARES = (9, 7)
 WO_PARTS = 1
+SWAP_CUTS = 2
 DP_ORDER = lambda count: reversed(range(1, count))
 
 
@@ -172,18 +173,19 @@
     send_ref[...] = dot(weight, e_ref[:, span((1 - core) * cols, cols)]).astype(BF16)
 
 
-def heads_sums(lower, half, own_side, x_ref, w_own_ref, w_oth_ref):
+def heads_sums(lower, half, own_side, x_refs, w_own_ref, w_oth_ref):
     core = lax.axis_index("tensor")
     side = core if own_side else 1 - core
-    src = pl.ds(pl.multiple_of(side * half + lower, HD), x_ref.shape[1])
-    x = x_ref[...]
+    x = jnp.concatenate([x_ref[...] for x_ref in x_refs], axis=1)
+    src = pl.ds(pl.multiple_of(side * half + lower, HD), x.shape[1])
     weight = jnp.concatenate([w_own_ref[src, :], w_oth_ref[src, :]], axis=1)
     return dot(x, weight), lane_sums(x)
 
 
-def heads_body(lower, half, own_side, x_ref, w_own_ref, w_oth_ref, *refs):
-    sums, (qkv_ref, square_ref) = refs[:-2], refs[-2:]
-    qkv, square = heads_sums(lower, half, own_side, x_ref, w_own_ref, w_oth_ref)
+def heads_body(lower, half, own_side, count, *refs):
+    x_refs, (w_own_ref, w_oth_ref, *sums) = refs[:count], refs[count:-2]
+    qkv_ref, square_ref = refs[-2:]
+    qkv, square = heads_sums(lower, half, own_side, x_refs, w_own_ref, w_oth_ref)
     if sums:
         qkv, square = qkv + sums[0][...], square + sums[1][...]
     qkv_ref[...], square_ref[...] = qkv, square
@@ -212,7 +214,7 @@
 def second_body(
     lower, half, live_ref, x_ref, w_own_ref, w_oth_ref, sum_ref, square_ref, mixed_ref
 ):
-    qkv, square = heads_sums(lower, half, False, x_ref, w_own_ref, w_oth_ref)
+    qkv, square = heads_sums(lower, half, False, [x_ref], w_own_ref, w_oth_ref)
     qkv = (qkv + sum_ref[...]) * rms_scale(square + square_ref[...], 2 * half)
     live = live_ref[...]
     for head in range(2):
@@ -338,7 +340,13 @@
                 piece, combined, embed, *sums = lax.optimization_barrier(
                     (piece, combined, embed, *sums)
                 )
-            oth = exchanged(piece, "tensor", 1)
+            cuts = SWAP_CUTS if lower != lowers[-1] else 1
+            step = piece.shape[1] // HD // cuts * HD
+            ends = [step * at for at in range(cuts)] + [piece.shape[1]]
+            oth = [
+                exchanged(piece[:, start:end] if cuts > 1 else piece, "tensor", 1)
+                for start, end in zip(ends, ends[1:])
+            ]
             if lower != lowers[-1]:
                 operands = (piece, w_embed_own, embed) if lower else (piece, w_embed_own)
                 embed = call(
@@ -353,16 +361,20 @@
                     "vvv",
                 )(piece, w_embed_own, embed)
             sums = call(
-                functools.partial(heads_body, lower, half, True), sum_shapes, "v" * (3 + len(sums))
+                functools.partial(heads_body, lower, half, True, 1),
+                sum_shapes,
+                "v" * (3 + len(sums)),
             )(piece, w_own, w_oth, *sums)
             if lower != lowers[-1]:
                 sums = call(
-                    functools.partial(heads_body, lower, half, False), sum_shapes, "v" * 5
-                )(oth, w_own, w_oth, *sums)
+                    functools.partial(heads_body, lower, half, False, cuts),
+                    sum_shapes,
+                    "v" * (4 + cuts),
+                )(*oth, w_own, w_oth, *sums)
         e_recv = exchanged(e_send, "tensor", 1)
         mixed = call(
             functools.partial(second_body, lower, half), shape(rows, 2 * HD), "v" * 6
-        )(live, oth, w_own, w_oth, *sums)
+        )(live, *oth, w_own, w_oth, *sums)
         embed = call(embed_body, shape(rows, cols), "v" * 5)(live, e_mine, e_recv, mixed, combined)
     with jax.named_scope("moments"):
         embeds = [embed] + [exchanged(embed, "dp", mask) for mask in DP_ORDER(group_count)]

time: 37.8 us -> 37.7 us (level)
  waiting for transfers between devices: 14.7 us -> 13.9 us
  starting transfers between devices: 10.2 us -> 10.9 us
    ppermute x13 -> x14, starting transfers between devices: 5.86 us -> 6.53 us  [exchanged(): lax.ppermute(value, axis, [(source, source ^ mask) for source in range(co...]
    ppermute x13 -> x14, waiting for transfers between devices: 8.15 us -> 7.63 us  [exchanged(): lax.ppermute(value, axis, [(source, source ^ mask) for source in range(co...]
  transfers between devices with their start and end apart: 15 -> 16, of which waited for: 9 -> 9; matrix products, arithmetic and copies ran while one was open for 0% -> 0% of each run, Pallas kernels for 30% -> 30%
where the time goes in v7:
time: 37.7 us; the launch traced here: 37.5 us
  waiting for transfers between devices  13.9 us (37%)
  Pallas kernels  12.5 us (33%)
  starting transfers between devices  10.9 us (29%)
    pallas_call x17, Pallas kernels, call(): return lambda *operands: kernel(*map(place, operands, spaces))  12.5 us
    ppermute x14, waiting for transfers between devices, exchanged(): lax.ppermute(value, axis, [(source, source ^ mask) for source in range(co...  7.63 us
    ppermute x14, starting transfers between devices, exchanged(): lax.ppermute(value, axis, [(source, source ^ mask) for source in range(co...  6.53 us
    ppermute x2, waiting for transfers between devices, shifted(): return lax.ppermute(value, axis, pairs)  6.27 us
    ppermute x2, starting transfers between devices, shifted(): return lax.ppermute(value, axis, pairs)  4.37 us
  transfers between devices with their start and end apart: 16, of which 9 were waited for; matrix products, arithmetic and copies ran while one was open for 0% of the time, Pallas kernels for 30%

profile of v7, /device:TPU:0, one launch (start us, length us, event | category | flops | bytes accessed | tf_op | source)
XLA Modules:
  0.0 37.5 jit_solution(666652781058397224)
XLA Ops:
  0.0 0.5 %collective-permute-start.1 = (bf16[128,2048]{1,0:T(8,128)(2,1)}, bf16[128,2048]{1,0:T(8,128)(2,1)S(1)}, u32[]{:S(2)}, u32[]{:S(2)}) collective-permute-start(bf16[128,2048]{1,0:T(8,128)(2,1)} %bitcast.5), channel_id=1, source_target_pairs={{0,1},{1,0},{2,3},{3,2},{4,5},{5,4},{6,7},{7,6},{8,9},{9,8},{10,11... | collective-permute-start | bytes 1572872 | tf_op jit(solution)/shard_map/layer_one/ppermute | solution.py:31
  0.5 0.0 copy-start
  0.5 2.4 %layer_one.4 = (bf16[128,2048]{1,0:T(8,128)(2,1)S(1)}, bf16[4096,384]{1,0:T(8,128)(2,1)S(1)}, f32[128,384]{1,0:T(8,128)S(1)}, f32[128,128]{1,0:T(8,128)S(1)}, s3...) custom-call(s32[4]{0:T(128)} %bitcast.3, bf16[1,128,2048]{2,1,0:T(8,128)(2,1)} %own_hbm.1, ...), custom_call_target="tpu_custom_call" | custom-call | tf_op jit(solution)/shard_map/layer_one/pallas_call | solution.py:73
  2.9 0.1 collective-permute-start
  3.0 0.0 collective-permute-done.1.oth_ref
  3.0 0.8 %layer_one.5.mix_own_ref = bf16[128,128]{1,0:T(8,128)(2,1)S(1)} custom-call(s32[128,128]{1,0:T(8,128)S(1)} %get-tuple-element.34.live_ref, bf16[128,2048]{1,0:T(8,128)(2,1)S(1)} %collective-permute-done.1.oth_ref, bf16[4096,384]{1,0:T(8,128)(2,1)S(1)} %get-tuple-element.41.w_ref.refs_1_.refs_2_.w_own_ref, f32[128,384]{1,0:T(8,128)S(1)} %get-tuple-element.36.qkv_ref, ...), custom_call_target="tpu_custom_call" | custom-call | tf_op jit(solution)/shard_map/layer_one/pallas_call | solution.py:73
  3.8 0.5 %collective-permute-start.2 = (bf16[128,128]{1,0:T(8,128)(2,1)S(1)}, bf16[128,128]{1,0:T(8,128)(2,1)S(1)}, u32[]{:S(2)}, u32[]{:S(2)}) collective-permute-start(bf16[128,128]{1,0:T(8,128)(2,1)S(1)} %layer_one.5.mix_own_ref), channel_id=1, source_target_pairs={{0,1},{1,0},{2,3},{3,2},{4,5},{5,4},{6,7},{7,6},{8,9},{9,8},{10,11... | collective-permute-start | bytes 98312 | tf_op jit(solution)/shard_map/layer_one/ppermute | solution.py:31
  4.3 0.5 %collective-permute-done.refs_0_ = bf16[128,2048]{1,0:T(8,128)(2,1)S(1)} collective-permute-done((bf16[128,2048]{1,0:T(8,128)(2,1)S(1)}, bf16[128,2048]{1,0:T(8,128)(2,1)S(1)}, u32[]{:S(2)}, u32[]{:S(2)}) %collective-permute-start) | collective-permute-done | bytes 524320 | tf_op jit(solution)/shard_map/layer_one/ppermute | solution.py:31
  4.8 0.3 collective-permute-done.2.mix_oth_ref
  5.2 0.3 layer_one.7
  5.4 0.4 %collective-permute-start.8 = (bf16[4096,384]{1,0:T(8,128)(2,1)S(1)}, bf16[4096,384]{1,0:T(8,128)(2,1)S(1)}, u32[]{:S(2)}, u32[]{:S(2)}) collective-permute-start(bf16[4096,384]{1,0:T(8,128)(2,1)S(1)} %get-tuple-element.41.w_ref.refs_1_.refs_2_.w_own_ref), channel_id=1, source_target_pairs={{0,1},{1,0},{2,3},{3,2},{4,5},{5,4},{6,7},{7,6},{8,9},{9,8},{10,11... | collective-permute-start | bytes 9437192 | tf_op jit(solution)/shard_map/weights/ppermute | solution.py:31
  5.8 2.7 %collective-permute-start.5 = (bf16[128,1152]{1,0:T(8,128)(2,1)S(1)}, bf16[128,1152]{1,0:T(8,128)(2,1)S(1)}, u32[]{:S(2)}, u32[]{:S(2)}) collective-permute-start(bf16[128,1152]{1,0:T(8,128)(2,1)S(1)} %layer_one.7), channel_id=1, source_target_pairs={{0,8},{8,16},{16,24},{24,0},{1,9},{9,17},{17,25},{25,1},{2,10},{10... | collective-permute-start | bytes 884744 | tf_op jit(solution)/shard_map/hop/ppermute | solution.py:26
  8.6 0.0 copy-done
  8.6 4.0 %weights.2 = (bf16[2048,1024]{1,0:T(8,128)(2,1)S(1)}, f32[256,512]{1,0:T(8,128)S(1)}, bf16[256,512]{1,0:T(8,128)(2,1)S(1)}, s32[128,128]{1,0:T(8,128)S(1)}) custom-call(s32[4]{0:T(128)S(1)} %bitcast.4, bf16[128,2048]{1,0:T(8,128)(2,1)S(1)} %get-tuple-element.30.w_own_ref, bf16[2048,1024]{1,0:T(8,128)(2,1)} %e_hbm.1, ...), custom_call_target="tpu_custom_call" | custom-call | tf_op jit(solution)/shard_map/weights/pallas_call | solution.py:73
  12.6 0.1 collective-permute-start.4
  12.7 0.2 layer_one.6
  13.0 1.6 %collective-permute-start.3 = (bf16[128,896]{1,0:T(8,128)(2,1)S(1)}, bf16[128,896]{1,0:T(8,128)(2,1)S(1)}, u32[]{:S(2)}, u32[]{:S(2)}) collective-permute-start(bf16[128,896]{1,0:T(8,128)(2,1)S(1)} %layer_one.6), channel_id=1, source_target_pairs={{0,8},{8,16},{16,24},{24,0},{1,9},{9,17},{17,25},{25,1},{2,10},{10... | collective-permute-start | bytes 688136 | tf_op jit(solution)/shard_map/hop/ppermute | solution.py:26
  14.6 3.7 %collective-permute-done.5.x_ref.refs_0_ = bf16[128,1152]{1,0:T(8,128)(2,1)S(1)} collective-permute-done((bf16[128,1152]{1,0:T(8,128)(2,1)S(1)}, bf16[128,1152]{1,0:T(8,128)(2,1)S(1)}, u32[]{:S(2)}, u32[]{:S(2)}) %collective-permute-start.5) | collective-permute-done | bytes 294944 | tf_op jit(solution)/shard_map/hop/ppermute | solution.py:26
  18.3 0.1 collective-permute-start.7
  18.4 0.6 %collective-permute-start.6 = (bf16[128,512]{1,0:T(8,128)(2,1)S(1)}, bf16[128,512]{1,0:T(8,128)(2,1)S(1)}, u32[]{:S(2)}, u32[]{:S(2)}) collective-permute-start(bf16[128,512]{1,0:T(8,128)(2,1)S(1)} %slice.8), channel_id=1, source_target_pairs={{0,1},{1,0},{2,3},{3,2},{4,5},{5,4},{6,7},{7,6},{8,9},{9,8},{10,11... | collective-permute-start | bytes 393224 | tf_op jit(solution)/shard_map/layer_two/ppermute | solution.py:31
  19.0 0.0 collective-permute-done.4.recv_ref
  19.0 0.5 %layer_two.7.embed_ref = f32[128,1024]{1,0:T(8,128)S(1)} custom-call(bf16[128,1152]{1,0:T(8,128)(2,1)S(1)} %collective-permute-done.5.x_ref.refs_0_, bf16[2048,1024]{1,0:T(8,128)(2,1)S(1)} %get-tuple-element.40.e_ref), custom_call_target="tpu_custom_call" | custom-call | tf_op jit(solution)/shard_map/layer_two/pallas_call | solution.py:73
  19.6 0.0 collective-permute-done.8.refs_2_.refs_3_.w_oth_ref
  19.6 0.4 %layer_two.8 = (f32[128,768]{1,0:T(8,128)S(1)}, f32[128,128]{1,0:T(8,128)S(1)}) custom-call(bf16[128,1152]{1,0:T(8,128)(2,1)S(1)} %collective-permute-done.5.x_ref.refs_0_, bf16[4096,384]{1,0:T(8,128)(2,1)S(1)} %get-tuple-element.41.w_ref.refs_1_.refs_2_.w_own_ref, bf16[4096,384]{1,0:T(8,128)(2,1)S(1)} %collective-permute-done.8.refs_2_.refs_3_.w_oth_ref), custom_call_target="tpu_custom_call" | custom-call | tf_op jit(solution)/shard_map/layer_two/pallas_call | solution.py:73
  20.0 0.0 collective-permute-done.6.refs_0_
  20.0 0.0 collective-permute-done.7.refs_1_
  20.0 0.4 %layer_two.9 = (f32[128,768]{1,0:T(8,128)S(1)}, f32[128,128]{1,0:T(8,128)S(1)}) custom-call(bf16[128,512]{1,0:T(8,128)(2,1)S(1)} %collective-permute-done.6.refs_0_, bf16[128,640]{1,0:T(8,128)(2,1)S(1)} %collective-permute-done.7.refs_1_, bf16[4096,384]{1,0:T(8,128)(2,1)S(1)} %get-tuple-element.41.w_ref.refs_1_.refs_2_.w_own_ref, ...), custom_call_target="tpu_custom_call" | custom-call | tf_op jit(solution)/shard_map/layer_two/pallas_call | solution.py:73
  20.5 2.6 %collective-permute-done.3.x_ref.refs_0_ = bf16[128,896]{1,0:T(8,128)(2,1)S(1)} collective-permute-done((bf16[128,896]{1,0:T(8,128)(2,1)S(1)}, bf16[128,896]{1,0:T(8,128)(2,1)S(1)}, u32[]{:S(2)}, u32[]{:S(2)}) %collective-permute-start.3) | collective-permute-done | bytes 229408 | tf_op jit(solution)/shard_map/hop/ppermute | solution.py:26
  23.0 0.0 collective-permute-start.10
  23.0 0.5 %layer_two.10 = (f32[128,512]{1,0:T(8,128)S(1)}, bf16[128,512]{1,0:T(8,128)(2,1)S(1)}) custom-call(bf16[128,896]{1,0:T(8,128)(2,1)S(1)} %collective-permute-done.3.x_ref.refs_0_, bf16[2048,1024]{1,0:T(8,128)(2,1)S(1)} %get-tuple-element.40.e_ref, f32[128,1024]{1,0:T(8,128)S(1)} %layer_two.7.embed_ref), custom_call_target="tpu_custom_call" | custom-call | tf_op jit(solution)/shard_map/layer_two/pallas_call | solution.py:73
  23.5 0.6 %collective-permute-start.9 = (bf16[128,512]{1,0:T(8,128)(2,1)S(1)}, bf16[128,512]{1,0:T(8,128)(2,1)S(1)}, u32[]{:S(2)}, u32[]{:S(2)}) collective-permute-start(bf16[128,512]{1,0:T(8,128)(2,1)S(1)} %get-tuple-element.49), channel_id=1, source_target_pairs={{0,1},{1,0},{2,3},{3,2},{4,5},{5,4},{6,7},{7,6},{8,9},{9,8},{10,11... | collective-permute-start | bytes 393224 | tf_op jit(solution)/shard_map/layer_two/ppermute | solution.py:31
  24.1 0.4 %layer_two.11 = (f32[128,768]{1,0:T(8,128)S(1)}, f32[128,128]{1,0:T(8,128)S(1)}) custom-call(bf16[128,896]{1,0:T(8,128)(2,1)S(1)} %collective-permute-done.3.x_ref.refs_0_, bf16[4096,384]{1,0:T(8,128)(2,1)S(1)} %get-tuple-element.41.w_ref.refs_1_.refs_2_.w_own_ref, bf16[4096,384]{1,0:T(8,128)(2,1)S(1)} %collective-permute-done.8.refs_2_.refs_3_.w_oth_ref, ...), custom_call_target="tpu_custom_call" | custom-call | tf_op jit(solution)/shard_map/layer_two/pallas_call | solution.py:73
  24.5 0.1 collective-permute-done.10.x_ref
  24.5 0.8 %layer_two.12.mixed_ref = bf16[128,256]{1,0:T(8,128)(2,1)S(1)} custom-call(s32[128,128]{1,0:T(8,128)S(1)} %get-tuple-element.32.live_ref, bf16[128,896]{1,0:T(8,128)(2,1)S(1)} %collective-permute-done.10.x_ref, bf16[4096,384]{1,0:T(8,128)(2,1)S(1)} %get-tuple-element.41.w_ref.refs_1_.refs_2_.w_own_ref, ...), custom_call_target="tpu_custom_call" | custom-call | tf_op jit(solution)/shard_map/layer_two/pallas_call | solution.py:73
  25.4 0.0 collective-permute-done.9.recv_ref
  25.4 0.2 layer_two.13.refs_0_.refs_1_
  25.6 2.5 %collective-permute-start.14 = (bf16[128,512]{1,0:T(8,128)(2,1)S(1)}, bf16[128,512]{1,0:T(8,128)(2,1)S(1)}, u32[]{:S(2)}, u32[]{:S(2)}) collective-permute-start(bf16[128,512]{1,0:T(8,128)(2,1)S(1)} %layer_two.13.refs_0_.refs_1_), channel_id=1, source_target_pairs={{0,6},{2,4},{4,2},{6,0},{1,7},{3,5},{5,3},{7,1},{8,14},{10,12},{12... | collective-permute-start | bytes 393224 | tf_op jit(solution)/shard_map/moments/ppermute | solution.py:31
  28.1 0.5 %collective-permute-start.11 = (bf16[128,512]{1,0:T(8,128)(2,1)S(1)}, bf16[128,512]{1,0:T(8,128)(2,1)S(1)}, u32[]{:S(2)}, u32[]{:S(2)}) collective-permute-start(bf16[128,512]{1,0:T(8,128)(2,1)S(1)} %layer_two.13.refs_0_.refs_1_), channel_id=1, source_target_pairs={{0,4},{2,6},{4,0},{6,2},{1,5},{3,7},{5,1},{7,3},{8,12},{10,14},{12... | collective-permute-start | bytes 393224 | tf_op jit(solution)/shard_map/moments/ppermute | solution.py:31
  28.6 0.5 %collective-permute-start.12 = (bf16[128,512]{1,0:T(8,128)(2,1)S(1)}, bf16[128,512]{1,0:T(8,128)(2,1)S(1)}, u32[]{:S(2)}, u32[]{:S(2)}) collective-permute-start(bf16[128,512]{1,0:T(8,128)(2,1)S(1)} %layer_two.13.refs_0_.refs_1_), channel_id=1, source_target_pairs={{0,2},{2,0},{4,6},{6,4},{1,3},{3,1},{5,7},{7,5},{8,10},{10,8},{12,... | collective-permute-start | bytes 393224 | tf_op jit(solution)/shard_map/moments/ppermute | solution.py:31
  29.1 3.2 %collective-permute-done.14.refs_2_.refs_1_ = bf16[128,512]{1,0:T(8,128)(2,1)S(1)} collective-permute-done((bf16[128,512]{1,0:T(8,128)(2,1)S(1)}, bf16[128,512]{1,0:T(8,128)(2,1)S(1)}, u32[]{:S(2)}, u32[]{:S(2)}) %collective-permute-start.14) | collective-permute-done | bytes 131104 | tf_op jit(solution)/shard_map/moments/ppermute | solution.py:31
  32.4 0.2 moments.5.gram_own_ref
  32.6 0.1 collective-permute-start.15
  32.7 2.2 %collective-permute-done.11.refs_1_.refs_0_ = bf16[128,512]{1,0:T(8,128)(2,1)S(1)} collective-permute-done((bf16[128,512]{1,0:T(8,128)(2,1)S(1)}, bf16[128,512]{1,0:T(8,128)(2,1)S(1)}, u32[]{:S(2)}, u32[]{:S(2)}) %collective-permute-start.11) | collective-permute-done | bytes 131104 | tf_op jit(solution)/shard_map/moments/ppermute | solution.py:31
  34.9 0.1 collective-permute-done.12.refs_2_.refs_1_
  35.0 0.2 moments.4.gram_own_ref
  35.2 0.1 collective-permute-start.13
  35.3 0.0 collective-permute-done.15.gram_oth_ref
  35.3 0.2 moments.6.refs_2_
  35.5 1.1 %collective-permute-done.13.gram_oth_ref = f32[128,256]{1,0:T(8,128)S(1)} collective-permute-done((f32[128,256]{1,0:T(8,128)S(1)}, f32[128,256]{1,0:T(8,128)S(1)}, u32[]{:S(2)}, u32[]{:S(2)}) %collective-permute-start.13) | collective-permute-done | bytes 131104 | tf_op jit(solution)/shard_map/moments/ppermute | solution.py:31
  36.6 0.9 %moments.7 = f32[128,512]{1,0:T(8,128)} custom-call(f32[128,256]{1,0:T(8,128)S(1)} %moments.4.gram_own_ref, f32[128,256]{1,0:T(8,128)S(1)} %collective-permute-done.13.gram_oth_ref, bf16[128,512]{1,0:T(8,128)(2,1)S(1)} %collective-permute-done.11.refs_1_.refs_0_, bf16[128,512]{1,0:T(8,128)(2,1)S(1)} %collective-permute-done.12.refs_2_.refs_1_, ...), custom_call_target="tpu_custom_call" | custom-call | tf_op jit(solution)/shard_map/moments/pallas_call | solution.py:73
  (3 shorter events, 0.1 us)
Async XLA Ops:
  0.0 3.0 %collective-permute-start.1 = (bf16[128,2048]{1,0:T(8,128)(2,1)}, bf16[128,2048]{1,0:T(8,128)(2,1)S(1)}, u32[]{:S(2)}, u32[]{:S(2)}) collective-permute-start(bf16[128,2048]{1,0:T(8,128)(2,1)} %bitcast.5), channel_id=1, source_target_pairs={{0,1},{1,0},{2,3},{3,2},{4,5},{5,4},{6,7},{7,6},{8,9},{9,8},{10,11... | collective-permute-start | bytes 1572872 | tf_op jit(solution)/shard_map/layer_one/ppermute | solution.py:31
  0.5 8.1 %copy-start = (s32[4,1]{0,1:T(1,128)S(1)}, s32[4,1]{0,1:T(1,128)}, u32[]{:S(2)}) copy-start(s32[4,1]{0,1:T(1,128)} %param.8) | copy-start | bytes 52
  2.9 2.0 %collective-permute-start = (bf16[128,2048]{1,0:T(8,128)(2,1)S(1)}, bf16[128,2048]{1,0:T(8,128)(2,1)S(1)}, u32[]{:S(2)}, u32[]{:S(2)}) collective-permute-start(bf16[128,2048]{1,0:T(8,128)(2,1)S(1)} %get-tuple-element.31), channel_id=1, source_target_pairs={{0,1},{1,0},{2,3},{3,2},{4,5},{5,4},{6,7},{7,6},{8,9},{9,8},{10,11... | collective-permute-start | bytes 1572872 | tf_op jit(solution)/shard_map/layer_one/ppermute | solution.py:31
  3.8 1.4 %collective-permute-start.2 = (bf16[128,128]{1,0:T(8,128)(2,1)S(1)}, bf16[128,128]{1,0:T(8,128)(2,1)S(1)}, u32[]{:S(2)}, u32[]{:S(2)}) collective-permute-start(bf16[128,128]{1,0:T(8,128)(2,1)S(1)} %layer_one.5.mix_own_ref), channel_id=1, source_target_pairs={{0,1},{1,0},{2,3},{3,2},{4,5},{5,4},{6,7},{7,6},{8,9},{9,8},{10,11... | collective-permute-start | bytes 98312 | tf_op jit(solution)/shard_map/layer_one/ppermute | solution.py:31
  5.4 14.1 %collective-permute-start.8 = (bf16[4096,384]{1,0:T(8,128)(2,1)S(1)}, bf16[4096,384]{1,0:T(8,128)(2,1)S(1)}, u32[]{:S(2)}, u32[]{:S(2)}) collective-permute-start(bf16[4096,384]{1,0:T(8,128)(2,1)S(1)} %get-tuple-element.41.w_ref.refs_1_.refs_2_.w_own_ref), channel_id=1, source_target_pairs={{0,1},{1,0},{2,3},{3,2},{4,5},{5,4},{6,7},{7,6},{8,9},{9,8},{10,11... | collective-permute-start | bytes 9437192 | tf_op jit(solution)/shard_map/weights/ppermute | solution.py:31
  5.8 12.5 %collective-permute-start.5 = (bf16[128,1152]{1,0:T(8,128)(2,1)S(1)}, bf16[128,1152]{1,0:T(8,128)(2,1)S(1)}, u32[]{:S(2)}, u32[]{:S(2)}) collective-permute-start(bf16[128,1152]{1,0:T(8,128)(2,1)S(1)} %layer_one.7), channel_id=1, source_target_pairs={{0,8},{8,16},{16,24},{24,0},{1,9},{9,17},{17,25},{25,1},{2,10},{10... | collective-permute-start | bytes 884744 | tf_op jit(solution)/shard_map/hop/ppermute | solution.py:26
  12.6 6.4 %collective-permute-start.4 = (bf16[256,512]{1,0:T(8,128)(2,1)S(1)}, bf16[256,512]{1,0:T(8,128)(2,1)S(1)}, u32[]{:S(2)}, u32[]{:S(2)}) collective-permute-start(bf16[256,512]{1,0:T(8,128)(2,1)S(1)} %get-tuple-element.39), channel_id=1, source_target_pairs={{0,1},{1,0},{2,3},{3,2},{4,5},{5,4},{6,7},{7,6},{8,9},{9,8},{10,11... | collective-permute-start | bytes 786440 | tf_op jit(solution)/shard_map/weights/ppermute | solution.py:31
  13.0 10.1 %collective-permute-start.3 = (bf16[128,896]{1,0:T(8,128)(2,1)S(1)}, bf16[128,896]{1,0:T(8,128)(2,1)S(1)}, u32[]{:S(2)}, u32[]{:S(2)}) collective-permute-start(bf16[128,896]{1,0:T(8,128)(2,1)S(1)} %layer_one.6), channel_id=1, source_target_pairs={{0,8},{8,16},{16,24},{24,0},{1,9},{9,17},{17,25},{25,1},{2,10},{10... | collective-permute-start | bytes 688136 | tf_op jit(solution)/shard_map/hop/ppermute | solution.py:26
  18.3 1.7 %collective-permute-start.7 = (bf16[128,640]{1,0:T(8,128)(2,1)S(1)}, bf16[128,640]{1,0:T(8,128)(2,1)S(1)}, u32[]{:S(2)}, u32[]{:S(2)}) collective-permute-start(bf16[128,640]{1,0:T(8,128)(2,1)S(1)} %slice.9), channel_id=1, source_target_pairs={{0,1},{1,0},{2,3},{3,2},{4,5},{5,4},{6,7},{7,6},{8,9},{9,8},{10,11... | collective-permute-start | bytes 491528 | tf_op jit(solution)/shard_map/layer_two/ppermute | solution.py:31
  18.4 1.6 %collective-permute-start.6 = (bf16[128,512]{1,0:T(8,128)(2,1)S(1)}, bf16[128,512]{1,0:T(8,128)(2,1)S(1)}, u32[]{:S(2)}, u32[]{:S(2)}) collective-permute-start(bf16[128,512]{1,0:T(8,128)(2,1)S(1)} %slice.8), channel_id=1, source_target_pairs={{0,1},{1,0},{2,3},{3,2},{4,5},{5,4},{6,7},{7,6},{8,9},{9,8},{10,11... | collective-permute-start | bytes 393224 | tf_op jit(solution)/shard_map/layer_two/ppermute | solution.py:31
  23.0 1.5 %collective-permute-start.10 = (bf16[128,896]{1,0:T(8,128)(2,1)S(1)}, bf16[128,896]{1,0:T(8,128)(2,1)S(1)}, u32[]{:S(2)}, u32[]{:S(2)}) collective-permute-start(bf16[128,896]{1,0:T(8,128)(2,1)S(1)} %collective-permute-done.3.x_ref.refs_0_), channel_id=1, source_target_pairs={{0,1},{1,0},{2,3},{3,2},{4,5},{5,4},{6,7},{7,6},{8,9},{9,8},{10,11... | collective-permute-start | bytes 688136 | tf_op jit(solution)/shard_map/layer_two/ppermute | solution.py:31
  23.5 1.9 %collective-permute-start.9 = (bf16[128,512]{1,0:T(8,128)(2,1)S(1)}, bf16[128,512]{1,0:T(8,128)(2,1)S(1)}, u32[]{:S(2)}, u32[]{:S(2)}) collective-permute-start(bf16[128,512]{1,0:T(8,128)(2,1)S(1)} %get-tuple-element.49), channel_id=1, source_target_pairs={{0,1},{1,0},{2,3},{3,2},{4,5},{5,4},{6,7},{7,6},{8,9},{9,8},{10,11... | collective-permute-start | bytes 393224 | tf_op jit(solution)/shard_map/layer_two/ppermute | solution.py:31
  25.6 6.8 %collective-permute-start.14 = (bf16[128,512]{1,0:T(8,128)(2,1)S(1)}, bf16[128,512]{1,0:T(8,128)(2,1)S(1)}, u32[]{:S(2)}, u32[]{:S(2)}) collective-permute-start(bf16[128,512]{1,0:T(8,128)(2,1)S(1)} %layer_two.13.refs_0_.refs_1_), channel_id=1, source_target_pairs={{0,6},{2,4},{4,2},{6,0},{1,7},{3,5},{5,3},{7,1},{8,14},{10,12},{12... | collective-permute-start | bytes 393224 | tf_op jit(solution)/shard_map/moments/ppermute | solution.py:31
  28.1 6.8 %collective-permute-start.11 = (bf16[128,512]{1,0:T(8,128)(2,1)S(1)}, bf16[128,512]{1,0:T(8,128)(2,1)S(1)}, u32[]{:S(2)}, u32[]{:S(2)}) collective-permute-start(bf16[128,512]{1,0:T(8,128)(2,1)S(1)} %layer_two.13.refs_0_.refs_1_), channel_id=1, source_target_pairs={{0,4},{2,6},{4,0},{6,2},{1,5},{3,7},{5,1},{7,3},{8,12},{10,14},{12... | collective-permute-start | bytes 393224 | tf_op jit(solution)/shard_map/moments/ppermute | solution.py:31
  28.6 6.4 %collective-permute-start.12 = (bf16[128,512]{1,0:T(8,128)(2,1)S(1)}, bf16[128,512]{1,0:T(8,128)(2,1)S(1)}, u32[]{:S(2)}, u32[]{:S(2)}) collective-permute-start(bf16[128,512]{1,0:T(8,128)(2,1)S(1)} %layer_two.13.refs_0_.refs_1_), channel_id=1, source_target_pairs={{0,2},{2,0},{4,6},{6,4},{1,3},{3,1},{5,7},{7,5},{8,10},{10,8},{12,... | collective-permute-start | bytes 393224 | tf_op jit(solution)/shard_map/moments/ppermute | solution.py:31
  32.6 2.7 %collective-permute-start.15 = (f32[128,256]{1,0:T(8,128)S(1)}, f32[128,256]{1,0:T(8,128)S(1)}, u32[]{:S(2)}, u32[]{:S(2)}) collective-permute-start(f32[128,256]{1,0:T(8,128)S(1)} %moments.5.gram_own_ref), channel_id=1, source_target_pairs={{0,1},{1,0},{2,3},{3,2},{4,5},{5,4},{6,7},{7,6},{8,9},{9,8},{10,11... | collective-permute-start | bytes 393224 | tf_op jit(solution)/shard_map/moments/ppermute | solution.py:31
  35.2 1.4 %collective-permute-start.13 = (f32[128,256]{1,0:T(8,128)S(1)}, f32[128,256]{1,0:T(8,128)S(1)}, u32[]{:S(2)}, u32[]{:S(2)}) collective-permute-start(f32[128,256]{1,0:T(8,128)S(1)} %moments.4.gram_own_ref), channel_id=1, source_target_pairs={{0,1},{1,0},{2,3},{3,2},{4,5},{5,4},{6,7},{7,6},{8,9},{9,8},{10,11... | collective-permute-start | bytes 393224 | tf_op jit(solution)/shard_map/moments/ppermute | solution.py:31

commit v8 on v7

--- a/solution.py
+++ b/solution.py
@@ -90,22 +90,28 @@
     return lax.rsqrt(jnp.sum(square, axis=-1, keepdims=True) * (1.0 / features) + EPSILON)
 
 
-def softmax_mix(qkv, live_len):
-    query, key, value = (qkv[:, at : at + HD].astype(BF16) for at in range(0, QKV, HD))
-    rows = query.shape[0]
-    scores = dot_t(query, key) * (1.0 / math.sqrt(HD))
-    key_pos = lax.broadcasted_iota(jnp.int32, (rows, rows), 1)
-    scores = jnp.where(key_pos < live_len, scores, -1e30)
+def softmax_mix(heads, live_len):
+    parts = [[qkv[:, at : at + HD].astype(BF16) for at in range(0, QKV, HD)] for qkv in heads]
+    rows = live_len.shape[0]
+    scores = jnp.concatenate([dot_t(query, key) for query, key, _ in parts], axis=0)
+    live = jnp.concatenate([live_len] * len(parts), axis=0)
+    key_pos = lax.broadcasted_iota(jnp.int32, scores.shape, 1)
+    scores = jnp.where(key_pos < live, scores * (1.0 / math.sqrt(HD)), -1e30)
     weights = jnp.exp(scores - jnp.max(scores, axis=-1, keepdims=True))
     total = jnp.sum(weights, axis=-1, keepdims=True)
-    return (dot(weights.astype(BF16), value) / total).astype(BF16)
+    weights = weights.astype(BF16)
+    mixed = [
+        dot(weights[at * rows : (at + 1) * rows], value) / total[at * rows : (at + 1) * rows]
+        for at, (_, _, value) in enumerate(parts)
+    ]
+    return jnp.concatenate(mixed, axis=1).astype(BF16)
 
 
 def load_body(
     lens_hbm, own_hbm, wq_hbm, wk_hbm, wv_hbm, wo_hbm,
     own_ref, w_ref, qkv_ref, square_ref, live_ref, *rest,
 ):
-    wo_own_ref, *wo_send_refs, sems, lens_ref = rest
+    *wo_send_refs, sems, lens_ref = rest
     half = own_ref.shape[1]
     core = lax.axis_index("tensor")
     pairs = [(lens_hbm, lens_ref), (own_hbm.at[0], own_ref)]
@@ -116,7 +122,6 @@
     for at, ref in enumerate(wo_send_refs):
         width = ref.shape[1]
         pairs.append((wo_hbm.at[0, :, span((1 - core) * half + at * width, width)], ref))
-    pairs.append((wo_hbm.at[0, :, span(core * half, half)], wo_own_ref))
     copies = [
         pltpu.make_async_copy(source, target, sems.at[index])
         for index, (source, target) in enumerate(pairs)
@@ -141,34 +146,29 @@
     oth = oth_ref[...]
     qkv = qkv_ref[...] + dot(oth, w_ref[span((1 - core) * half, half), :])
     scale = rms_scale(square_ref[...] + lane_sums(oth), 2 * half)
-    mixed_ref[...] = softmax_mix(qkv * scale, live_ref[...])
+    mixed_ref[...] = softmax_mix([qkv * scale], live_ref[...])
 
 
 def update_body(lower, own_ref, mix_own_ref, mix_oth_ref, w_own_ref, *refs):
     w_oth_refs, out_ref = refs[:-1], refs[-1]
     cols = slice(lower, lower + out_ref.shape[1])
     w_oth = jnp.concatenate([ref[...] for ref in w_oth_refs], axis=1)
-    weight = jnp.concatenate([w_own_ref[:, cols], w_oth[:, cols]], axis=0)
+    start = lax.axis_index("tensor") * own_ref.shape[1] + lower
+    w_own = w_own_ref[0, :, pl.ds(pl.multiple_of(start, HD), out_ref.shape[1])]
+    weight = jnp.concatenate([w_own, w_oth[:, cols]], axis=0)
     mixed = jnp.concatenate([mix_own_ref[...], mix_oth_ref[...]], axis=1)
     out_ref[...] = (own_ref[:, cols].astype(F32) + dot(mixed, weight)).astype(BF16)
 
 
-def combine_body(lens_ref, w_own_ref, e_hbm, *refs):
-    w_oth_refs, (e_ref, mine_ref, send_ref, live_ref, sems) = refs[:WO_PARTS], refs[WO_PARTS:]
-    blocks = sems.shape[0]
-    depth = e_ref.shape[0] // blocks
-    copies = []
-    for block in range(blocks):
-        rows = slice(block * depth, (block + 1) * depth)
-        copies.append(pltpu.make_async_copy(e_hbm.at[rows, :], e_ref.at[rows, :], sems.at[block]))
-        copies[-1].start()
+def combine_body(lens_ref, w_own_ref, e_ref, *refs):
+    w_oth_refs, (mine_ref, send_ref, live_ref) = refs[:WO_PARTS], refs[WO_PARTS:]
     cols = mine_ref.shape[1]
     core = lax.axis_index("tensor")
     w_oth = jnp.concatenate([ref[...] for ref in w_oth_refs], axis=1)
-    weight = jnp.concatenate([w_own_ref[...], w_oth], axis=0)
+    half = w_oth.shape[1]
+    w_own = w_own_ref[0, :, span(lax.axis_index("tensor") * half, half)]
+    weight = jnp.concatenate([w_own, w_oth], axis=0)
     live_ref[...] = jnp.full(live_ref.shape, lens_ref[hop_anchor()], jnp.int32)
-    for copy in copies:
-        copy.wait()
     mine_ref[...] = dot(weight, e_ref[:, span(core * cols, cols)])
     send_ref[...] = dot(weight, e_ref[:, span((1 - core) * cols, cols)]).astype(BF16)
 
@@ -216,10 +216,7 @@
 ):
     qkv, square = heads_sums(lower, half, False, [x_ref], w_own_ref, w_oth_ref)
     qkv = (qkv + sum_ref[...]) * rms_scale(square + square_ref[...], 2 * half)
-    live = live_ref[...]
-    for head in range(2):
-        at = head * QKV
-        mixed_ref[:, head * HD : (head + 1) * HD] = softmax_mix(qkv[:, at : at + QKV], live)
+    mixed_ref[...] = softmax_mix([qkv[:, :QKV], qkv[:, QKV:]], live_ref[...])
 
 
 def combine_sum_body(mine_ref, recv_ref, out_ref):
@@ -241,12 +238,13 @@
     own, embeds, out_ref = refs[0][...], refs[1:-1], refs[-1]
     rows = own.shape[0]
     for at, embed in enumerate(embeds):
-        out_ref[:, at * rows : (at + 1) * rows] = dot_t(own, embed[...])
+        product = dot_t(own, embed[...])
+        out_ref[:, at * rows : (at + 1) * rows] = product.astype(out_ref.dtype)
 
 
 def result_sums(tokens, first, gram_own_ref, gram_oth_ref, embeds):
     rows = embeds[0].shape[0]
-    gram = (gram_own_ref[...] + gram_oth_ref[...]) * (1.0 / tokens)
+    gram = (gram_own_ref[...].astype(F32) + gram_oth_ref[...].astype(F32)) * (1.0 / tokens)
     if first:
         row = lax.broadcasted_iota(jnp.int32, gram.shape, 0)
         col = lax.broadcasted_iota(jnp.int32, gram.shape, 1)
@@ -292,7 +290,7 @@
 
     with jax.named_scope("layer_one"):
         oth = exchanged(own_in, "tensor", 1)
-        own, w_own, qkv, square, live, wo_own, *wo_send = call(
+        own, w_own, qkv, square, live, *wo_send = call(
             load_body,
             [
                 shape(rows, half),
@@ -300,11 +298,10 @@
                 shape(rows, QKV, dtype=F32),
                 shape(rows, HD, dtype=F32),
                 shape(rows, HD, dtype=jnp.int32),
-                shape(HD, half),
             ]
             + [shape(HD, half // WO_PARTS)] * WO_PARTS,
             "hhhhhh",
-            9 + WO_PARTS,
+            8 + WO_PARTS,
             scratch=(pltpu.SMEM(lens.shape, jnp.int32),),
         )(lens, tokens, w_query, w_key, w_value, w_out)
         wo_oth = [exchanged(part, "tensor", 1) for part in wo_send]
@@ -312,23 +309,23 @@
         mixed_oth = exchanged(mixed, "tensor", 1)
         state = [
             call(functools.partial(update_body, lower), shape(rows, width), "v" * (4 + WO_PARTS))(
-                own, mixed, mixed_oth, wo_own, *wo_oth
+                own, mixed, mixed_oth, w_out, *wo_oth
             )
             for lower, width in zip(lowers, widths)
         ]
     with jax.named_scope("weights"):
         w_oth = exchanged(after(w_own, state[0]), "tensor", 1)
+    ready = state[0]
     with jax.named_scope("hop"):
         state = [shifted(piece, "section", 1) for piece in state]
     with jax.named_scope("weights"):
-        w_embed_own, c_mine, c_send, live = call(
+        w_embed_own = after(w_embed, ready)
+        c_mine, c_send, live = call(
             combine_body,
-            [shape(*w_embed.shape)]
-            + [shape(2 * HD, cols, dtype=F32), shape(2 * HD, cols)]
+            [shape(2 * HD, cols, dtype=F32), shape(2 * HD, cols)]
             + [shape(rows, HD, dtype=jnp.int32)],
-            "svh" + "v" * WO_PARTS,
-            4,
-        )(lens, wo_own, w_embed, *wo_oth)
+            "svv" + "v" * WO_PARTS,
+        )(lens, w_out, w_embed_own, *wo_oth)
         combined = call(combine_sum_body, shape(2 * HD, cols), "vv")(
             c_mine, exchanged(c_send, "tensor", 1)
         )
@@ -380,7 +377,8 @@
         embeds = [embed] + [exchanged(embed, "dp", mask) for mask in DP_ORDER(group_count)]
         sums = ()
         for part in (embeds[:2], embeds[2:]):
-            gram = call(gram_body, shape(rows, rows * len(part), dtype=F32), "v" * (1 + len(part)))(
+            kind = BF16 if sums else F32
+            gram = call(gram_body, shape(rows, rows * len(part), dtype=kind), "v" * (1 + len(part)))(
                 embed, *part
             )
             operands = (gram, exchanged(gram, "tensor", 1), *part, *sums)

time: 37.7 us -> 37.3 us (0.989)
  Pallas kernels: 12.5 us -> 10 us
  waiting for transfers between devices: 13.9 us -> 16 us
    pallas_call x17, Pallas kernels: 12.5 us -> 10 us  [call(): return lambda *operands: kernel(*map(place, operands, spaces))]
    ppermute x2, waiting for transfers between devices: 6.27 us -> 8.46 us  [shifted(): return lax.ppermute(value, axis, pairs)]
  transfers between devices with their start and end apart: 16 -> 16, of which waited for: 9 -> 8; matrix products, arithmetic and copies ran while one was open for 0% -> 0% of each run, Pallas kernels for 30% -> 23%
where the time goes in v8:
time: 37.3 us; the launch traced here: 37.1 us
  waiting for transfers between devices  16 us (43%)
  starting transfers between devices  10.9 us (29%)
  Pallas kernels  10 us (27%)
    pallas_call x17, Pallas kernels, call(): return lambda *operands: kernel(*map(place, operands, spaces))  10 us
    ppermute x2, waiting for transfers between devices, shifted(): return lax.ppermute(value, axis, pairs)  8.46 us
    ppermute x14, waiting for transfers between devices, exchanged(): lax.ppermute(value, axis, [(source, source ^ mask) for source in range(co...  7.49 us
    ppermute x14, starting transfers between devices, exchanged(): lax.ppermute(value, axis, [(source, source ^ mask) for source in range(co...  6.53 us
    ppermute x2, starting transfers between devices, shifted(): return lax.ppermute(value, axis, pairs)  4.37 us
  transfers between devices with their start and end apart: 16, of which 8 were waited for; matrix products, arithmetic and copies ran while one was open for 0% of the time, Pallas kernels for 23%

profile of v8, /device:TPU:0, one launch (start us, length us, event | category | flops | bytes accessed | tf_op | source)
XLA Modules:
  0.0 37.1 jit_solution(12258457881184329254)
XLA Ops:
  0.0 0.5 %collective-permute-start = (bf16[128,2048]{1,0:T(8,128)(2,1)}, bf16[128,2048]{1,0:T(8,128)(2,1)S(1)}, u32[]{:S(2)}, u32[]{:S(2)}) collective-permute-start(bf16[128,2048]{1,0:T(8,128)(2,1)} %bitcast.5), channel_id=1, source_target_pairs={{0,1},{1,0},{2,3},{3,2},{4,5},{5,4},{6,7},{7,6},{8,9},{9,8},{10,11... | collective-permute-start | bytes 1572872 | tf_op jit(solution)/shard_map/layer_one/ppermute | solution.py:31
  0.5 2.2 %layer_one.4 = (bf16[128,2048]{1,0:T(8,128)(2,1)S(1)}, bf16[4096,384]{1,0:T(8,128)(2,1)S(1)}, f32[128,384]{1,0:T(8,128)S(1)}, f32[128,128]{1,0:T(8,128)S(1)}, s3...) custom-call(s32[4]{0:T(128)} %bitcast.3, bf16[1,128,2048]{2,1,0:T(8,128)(2,1)} %own_hbm.1, ...), custom_call_target="tpu_custom_call" | custom-call | tf_op jit(solution)/shard_map/layer_one/pallas_call | solution.py:73
  2.7 0.0 copy-start.1
  2.7 0.1 collective-permute-start.2
  2.8 0.0 collective-permute-done.oth_ref
  2.8 0.0 copy-start
  2.8 0.0 copy-start.2
  2.8 0.8 %layer_one.5.mix_own_ref = bf16[128,128]{1,0:T(8,128)(2,1)S(1)} custom-call(s32[128,128]{1,0:T(8,128)S(1)} %get-tuple-element.30.live_ref, bf16[128,2048]{1,0:T(8,128)(2,1)S(1)} %collective-permute-done.oth_ref, bf16[4096,384]{1,0:T(8,128)(2,1)S(1)} %get-tuple-element.39.w_ref.refs_1_.refs_2_.w_own_ref, f32[128,384]{1,0:T(8,128)S(1)} %get-tuple-element.32.qkv_ref, ...), custom_call_target="tpu_custom_call" | custom-call | tf_op jit(solution)/shard_map/layer_one/pallas_call | solution.py:73
  3.6 0.5 %collective-permute-start.1 = (bf16[128,128]{1,0:T(8,128)(2,1)S(1)}, bf16[128,128]{1,0:T(8,128)(2,1)S(1)}, u32[]{:S(2)}, u32[]{:S(2)}) collective-permute-start(bf16[128,128]{1,0:T(8,128)(2,1)S(1)} %layer_one.5.mix_own_ref), channel_id=1, source_target_pairs={{0,1},{1,0},{2,3},{3,2},{4,5},{5,4},{6,7},{7,6},{8,9},{9,8},{10,11... | collective-permute-start | bytes 98312 | tf_op jit(solution)/shard_map/layer_one/ppermute | solution.py:31
  4.1 0.5 %collective-permute-done.2.refs_0_ = bf16[128,2048]{1,0:T(8,128)(2,1)S(1)} collective-permute-done((bf16[128,2048]{1,0:T(8,128)(2,1)S(1)}, bf16[128,2048]{1,0:T(8,128)(2,1)S(1)}, u32[]{:S(2)}, u32[]{:S(2)}) %collective-permute-start.2) | collective-permute-done | bytes 524320 | tf_op jit(solution)/shard_map/layer_one/ppermute | solution.py:31
  4.7 0.3 collective-permute-done.1.mix_oth_ref
  5.0 0.0 copy-done.1
  5.0 0.3 layer_one.6
  5.3 0.4 %collective-permute-start.8 = (bf16[4096,384]{1,0:T(8,128)(2,1)S(1)}, bf16[4096,384]{1,0:T(8,128)(2,1)S(1)}, u32[]{:S(2)}, u32[]{:S(2)}) collective-permute-start(bf16[4096,384]{1,0:T(8,128)(2,1)S(1)} %get-tuple-element.39.w_ref.refs_1_.refs_2_.w_own_ref), channel_id=1, source_target_pairs={{0,1},{1,0},{2,3},{3,2},{4,5},{5,4},{6,7},{7,6},{8,9},{9,8},{10,11... | collective-permute-start | bytes 9437192 | tf_op jit(solution)/shard_map/weights/ppermute | solution.py:31
  5.7 2.7 %collective-permute-start.5 = (bf16[128,1152]{1,0:T(8,128)(2,1)S(1)}, bf16[128,1152]{1,0:T(8,128)(2,1)S(1)}, u32[]{:S(2)}, u32[]{:S(2)}) collective-permute-start(bf16[128,1152]{1,0:T(8,128)(2,1)S(1)} %layer_one.6), channel_id=1, source_target_pairs={{0,8},{8,16},{16,24},{24,0},{1,9},{9,17},{17,25},{25,1},{2,10},{10... | collective-permute-start | bytes 884744 | tf_op jit(solution)/shard_map/hop/ppermute | solution.py:26
  8.4 0.0 copy-done
  8.4 0.0 copy-done.2
  8.4 1.8 %weights.2 = (f32[256,512]{1,0:T(8,128)S(1)}, bf16[256,512]{1,0:T(8,128)(2,1)S(1)}, s32[128,128]{1,0:T(8,128)S(1)}) custom-call(s32[4]{0:T(128)S(1)} %bitcast.4, bf16[1,128,4096]{2,1,0:T(8,128)(2,1)S(1)} %copy-done.1, bf16[2048,1024]{1,0:T(8,128)(2,1)S(1)} %copy-done, bf16[128,2048]{1,0:T(8,128)(2,1)S(1)} %collective-permute-done.2.refs_0_), custom_call_target="tpu_custom_call" | custom-call | tf_op jit(solution)/shard_map/weights/pallas_call | solution.py:73
  10.2 0.1 collective-permute-start.4
  10.4 0.2 layer_one.7
  10.6 1.6 %collective-permute-start.3 = (bf16[128,896]{1,0:T(8,128)(2,1)S(1)}, bf16[128,896]{1,0:T(8,128)(2,1)S(1)}, u32[]{:S(2)}, u32[]{:S(2)}) collective-permute-start(bf16[128,896]{1,0:T(8,128)(2,1)S(1)} %layer_one.7), channel_id=1, source_target_pairs={{0,8},{8,16},{16,24},{24,0},{1,9},{9,17},{17,25},{25,1},{2,10},{10... | collective-permute-start | bytes 688136 | tf_op jit(solution)/shard_map/hop/ppermute | solution.py:26
  12.2 6.1 %collective-permute-done.5.x_ref.refs_0_ = bf16[128,1152]{1,0:T(8,128)(2,1)S(1)} collective-permute-done((bf16[128,1152]{1,0:T(8,128)(2,1)S(1)}, bf16[128,1152]{1,0:T(8,128)(2,1)S(1)}, u32[]{:S(2)}, u32[]{:S(2)}) %collective-permute-start.5) | collective-permute-done | bytes 294944 | tf_op jit(solution)/shard_map/hop/ppermute | solution.py:26
  18.3 0.1 collective-permute-start.7
  18.4 0.6 %collective-permute-start.6 = (bf16[128,512]{1,0:T(8,128)(2,1)S(1)}, bf16[128,512]{1,0:T(8,128)(2,1)S(1)}, u32[]{:S(2)}, u32[]{:S(2)}) collective-permute-start(bf16[128,512]{1,0:T(8,128)(2,1)S(1)} %slice.8), channel_id=1, source_target_pairs={{0,1},{1,0},{2,3},{3,2},{4,5},{5,4},{6,7},{7,6},{8,9},{9,8},{10,11... | collective-permute-start | bytes 393224 | tf_op jit(solution)/shard_map/layer_two/ppermute | solution.py:31
  19.0 0.0 collective-permute-done.4.recv_ref
  19.0 0.5 %layer_two.7.embed_ref = f32[128,1024]{1,0:T(8,128)S(1)} custom-call(bf16[128,1152]{1,0:T(8,128)(2,1)S(1)} %collective-permute-done.5.x_ref.refs_0_, bf16[2048,1024]{1,0:T(8,128)(2,1)S(1)} %copy-done), custom_call_target="tpu_custom_call" | custom-call | tf_op jit(solution)/shard_map/layer_two/pallas_call | solution.py:73
  19.5 0.0 collective-permute-done.8.refs_2_.refs_3_.w_oth_ref
  19.5 0.4 %layer_two.8 = (f32[128,768]{1,0:T(8,128)S(1)}, f32[128,128]{1,0:T(8,128)S(1)}) custom-call(bf16[128,1152]{1,0:T(8,128)(2,1)S(1)} %collective-permute-done.5.x_ref.refs_0_, bf16[4096,384]{1,0:T(8,128)(2,1)S(1)} %get-tuple-element.39.w_ref.refs_1_.refs_2_.w_own_ref, bf16[4096,384]{1,0:T(8,128)(2,1)S(1)} %collective-permute-done.8.refs_2_.refs_3_.w_oth_ref), custom_call_target="tpu_custom_call" | custom-call | tf_op jit(solution)/shard_map/layer_two/pallas_call | solution.py:73
  20.0 0.0 collective-permute-done.6.refs_0_
  20.0 0.0 collective-permute-done.7.refs_1_
  20.0 0.4 %layer_two.9 = (f32[128,768]{1,0:T(8,128)S(1)}, f32[128,128]{1,0:T(8,128)S(1)}) custom-call(bf16[128,512]{1,0:T(8,128)(2,1)S(1)} %collective-permute-done.6.refs_0_, bf16[128,640]{1,0:T(8,128)(2,1)S(1)} %collective-permute-done.7.refs_1_, bf16[4096,384]{1,0:T(8,128)(2,1)S(1)} %get-tuple-element.39.w_ref.refs_1_.refs_2_.w_own_ref, ...), custom_call_target="tpu_custom_call" | custom-call | tf_op jit(solution)/shard_map/layer_two/pallas_call | solution.py:73
  20.5 2.4 %collective-permute-done.3.x_ref.refs_0_ = bf16[128,896]{1,0:T(8,128)(2,1)S(1)} collective-permute-done((bf16[128,896]{1,0:T(8,128)(2,1)S(1)}, bf16[128,896]{1,0:T(8,128)(2,1)S(1)}, u32[]{:S(2)}, u32[]{:S(2)}) %collective-permute-start.3) | collective-permute-done | bytes 229408 | tf_op jit(solution)/shard_map/hop/ppermute | solution.py:26
  22.9 0.0 collective-permute-start.10
  22.9 0.4 %layer_two.10 = (f32[128,512]{1,0:T(8,128)S(1)}, bf16[128,512]{1,0:T(8,128)(2,1)S(1)}) custom-call(bf16[128,896]{1,0:T(8,128)(2,1)S(1)} %collective-permute-done.3.x_ref.refs_0_, bf16[2048,1024]{1,0:T(8,128)(2,1)S(1)} %copy-done, f32[128,1024]{1,0:T(8,128)S(1)} %layer_two.7.embed_ref), custom_call_target="tpu_custom_call" | custom-call | tf_op jit(solution)/shard_map/layer_two/pallas_call | solution.py:73
  23.3 0.6 %collective-permute-start.9 = (bf16[128,512]{1,0:T(8,128)(2,1)S(1)}, bf16[128,512]{1,0:T(8,128)(2,1)S(1)}, u32[]{:S(2)}, u32[]{:S(2)}) collective-permute-start(bf16[128,512]{1,0:T(8,128)(2,1)S(1)} %get-tuple-element.47), channel_id=1, source_target_pairs={{0,1},{1,0},{2,3},{3,2},{4,5},{5,4},{6,7},{7,6},{8,9},{9,8},{10,11... | collective-permute-start | bytes 393224 | tf_op jit(solution)/shard_map/layer_two/ppermute | solution.py:31
  23.9 0.4 %layer_two.11 = (f32[128,768]{1,0:T(8,128)S(1)}, f32[128,128]{1,0:T(8,128)S(1)}) custom-call(bf16[128,896]{1,0:T(8,128)(2,1)S(1)} %collective-permute-done.3.x_ref.refs_0_, bf16[4096,384]{1,0:T(8,128)(2,1)S(1)} %get-tuple-element.39.w_ref.refs_1_.refs_2_.w_own_ref, bf16[4096,384]{1,0:T(8,128)(2,1)S(1)} %collective-permute-done.8.refs_2_.refs_3_.w_oth_ref, ...), custom_call_target="tpu_custom_call" | custom-call | tf_op jit(solution)/shard_map/layer_two/pallas_call | solution.py:73
  24.3 0.1 collective-permute-done.10.x_ref
  24.4 0.7 %layer_two.12.mixed_ref = bf16[128,256]{1,0:T(8,128)(2,1)S(1)} custom-call(s32[128,128]{1,0:T(8,128)S(1)} %get-tuple-element.36.live_ref, bf16[128,896]{1,0:T(8,128)(2,1)S(1)} %collective-permute-done.10.x_ref, bf16[4096,384]{1,0:T(8,128)(2,1)S(1)} %get-tuple-element.39.w_ref.refs_1_.refs_2_.w_own_ref, ...), custom_call_target="tpu_custom_call" | custom-call | tf_op jit(solution)/shard_map/layer_two/pallas_call | solution.py:73
  25.1 0.0 collective-permute-done.9.recv_ref
  25.1 0.2 layer_two.13.refs_0_.refs_1_
  25.3 2.5 %collective-permute-start.14 = (bf16[128,512]{1,0:T(8,128)(2,1)S(1)}, bf16[128,512]{1,0:T(8,128)(2,1)S(1)}, u32[]{:S(2)}, u32[]{:S(2)}) collective-permute-start(bf16[128,512]{1,0:T(8,128)(2,1)S(1)} %layer_two.13.refs_0_.refs_1_), channel_id=1, source_target_pairs={{0,6},{2,4},{4,2},{6,0},{1,7},{3,5},{5,3},{7,1},{8,14},{10,12},{12... | collective-permute-start | bytes 393224 | tf_op jit(solution)/shard_map/moments/ppermute | solution.py:31
  27.8 0.5 %collective-permute-start.12 = (bf16[128,512]{1,0:T(8,128)(2,1)S(1)}, bf16[128,512]{1,0:T(8,128)(2,1)S(1)}, u32[]{:S(2)}, u32[]{:S(2)}) collective-permute-start(bf16[128,512]{1,0:T(8,128)(2,1)S(1)} %layer_two.13.refs_0_.refs_1_), channel_id=1, source_target_pairs={{0,2},{2,0},{4,6},{6,4},{1,3},{3,1},{5,7},{7,5},{8,10},{10,8},{12,... | collective-permute-start | bytes 393224 | tf_op jit(solution)/shard_map/moments/ppermute | solution.py:31
  28.4 0.5 %collective-permute-start.11 = (bf16[128,512]{1,0:T(8,128)(2,1)S(1)}, bf16[128,512]{1,0:T(8,128)(2,1)S(1)}, u32[]{:S(2)}, u32[]{:S(2)}) collective-permute-start(bf16[128,512]{1,0:T(8,128)(2,1)S(1)} %layer_two.13.refs_0_.refs_1_), channel_id=1, source_target_pairs={{0,4},{2,6},{4,0},{6,2},{1,5},{3,7},{5,1},{7,3},{8,12},{10,14},{12... | collective-permute-start | bytes 393224 | tf_op jit(solution)/shard_map/moments/ppermute | solution.py:31
  28.9 3.8 %collective-permute-done.14.refs_2_.refs_1_ = bf16[128,512]{1,0:T(8,128)(2,1)S(1)} collective-permute-done((bf16[128,512]{1,0:T(8,128)(2,1)S(1)}, bf16[128,512]{1,0:T(8,128)(2,1)S(1)}, u32[]{:S(2)}, u32[]{:S(2)}) %collective-permute-start.14) | collective-permute-done | bytes 131104 | tf_op jit(solution)/shard_map/moments/ppermute | solution.py:31
  32.6 0.2 moments.5.gram_own_ref
  32.9 0.1 collective-permute-start.15
  32.9 1.7 %collective-permute-done.12.refs_2_.refs_1_ = bf16[128,512]{1,0:T(8,128)(2,1)S(1)} collective-permute-done((bf16[128,512]{1,0:T(8,128)(2,1)S(1)}, bf16[128,512]{1,0:T(8,128)(2,1)S(1)}, u32[]{:S(2)}, u32[]{:S(2)}) %collective-permute-start.12) | collective-permute-done | bytes 131104 | tf_op jit(solution)/shard_map/moments/ppermute | solution.py:31
  34.7 0.0 collective-permute-done.11.refs_1_.refs_0_
  34.7 0.2 moments.4.gram_own_ref
  34.9 0.1 collective-permute-start.13
  35.0 0.0 collective-permute-done.15.gram_oth_ref
  35.0 0.2 moments.6.refs_2_
  35.2 1.0 %collective-permute-done.13.gram_oth_ref = bf16[128,256]{1,0:T(8,128)(2,1)S(1)} collective-permute-done((bf16[128,256]{1,0:T(8,128)(2,1)S(1)}, bf16[128,256]{1,0:T(8,128)(2,1)S(1)}, u32[]{:S(2)}, u32[]{:S(2)}) %collective-permute-start.13) | collective-permute-done | bytes 65568 | tf_op jit(solution)/shard_map/moments/ppermute | solution.py:31
  36.2 0.9 %moments.7 = f32[128,512]{1,0:T(8,128)} custom-call(bf16[128,256]{1,0:T(8,128)(2,1)S(1)} %moments.4.gram_own_ref, bf16[128,256]{1,0:T(8,128)(2,1)S(1)} %collective-permute-done.13.gram_oth_ref, bf16[128,512]{1,0:T(8,128)(2,1)S(1)} %collective-permute-done.11.refs_1_.refs_0_, bf16[128,512]{1,0:T(8,128)(2,1)S(1)} %collective-permute-done.12.refs_2_.refs_1_, ...), custom_call_target="tpu_custom_call" | custom-call | tf_op jit(solution)/shard_map/moments/pallas_call | solution.py:73
  (3 shorter events, 0.1 us)
Async XLA Ops:
  0.0 2.8 %collective-permute-start = (bf16[128,2048]{1,0:T(8,128)(2,1)}, bf16[128,2048]{1,0:T(8,128)(2,1)S(1)}, u32[]{:S(2)}, u32[]{:S(2)}) collective-permute-start(bf16[128,2048]{1,0:T(8,128)(2,1)} %bitcast.5), channel_id=1, source_target_pairs={{0,1},{1,0},{2,3},{3,2},{4,5},{5,4},{6,7},{7,6},{8,9},{9,8},{10,11... | collective-permute-start | bytes 1572872 | tf_op jit(solution)/shard_map/layer_one/ppermute | solution.py:31
  2.7 2.3 %copy-start.1 = (bf16[1,128,4096]{2,1,0:T(8,128)(2,1)S(1)}, bf16[1,128,4096]{2,1,0:T(8,128)(2,1)}, u32[]{:S(2)}) copy-start(bf16[1,128,4096]{2,1,0:T(8,128)(2,1)} %w_own_ref.5) | copy-start | bytes 3145732
  2.7 2.0 %collective-permute-start.2 = (bf16[128,2048]{1,0:T(8,128)(2,1)S(1)}, bf16[128,2048]{1,0:T(8,128)(2,1)S(1)}, u32[]{:S(2)}, u32[]{:S(2)}) collective-permute-start(bf16[128,2048]{1,0:T(8,128)(2,1)S(1)} %get-tuple-element.34), channel_id=1, source_target_pairs={{0,1},{1,0},{2,3},{3,2},{4,5},{5,4},{6,7},{7,6},{8,9},{9,8},{10,11... | collective-permute-start | bytes 1572872 | tf_op jit(solution)/shard_map/layer_one/ppermute | solution.py:31
  2.8 5.6 %copy-start = (bf16[2048,1024]{1,0:T(8,128)(2,1)S(1)}, bf16[2048,1024]{1,0:T(8,128)(2,1)}, u32[]{:S(2)}) copy-start(bf16[2048,1024]{1,0:T(8,128)(2,1)} %e_ref.2) | copy-start | bytes 12582916
  2.8 5.6 %copy-start.2 = (s32[4,1]{0,1:T(1,128)S(1)}, s32[4,1]{0,1:T(1,128)}, u32[]{:S(2)}) copy-start(s32[4,1]{0,1:T(1,128)} %param.8) | copy-start | bytes 52
  3.6 1.4 %collective-permute-start.1 = (bf16[128,128]{1,0:T(8,128)(2,1)S(1)}, bf16[128,128]{1,0:T(8,128)(2,1)S(1)}, u32[]{:S(2)}, u32[]{:S(2)}) collective-permute-start(bf16[128,128]{1,0:T(8,128)(2,1)S(1)} %layer_one.5.mix_own_ref), channel_id=1, source_target_pairs={{0,1},{1,0},{2,3},{3,2},{4,5},{5,4},{6,7},{7,6},{8,9},{9,8},{10,11... | collective-permute-start | bytes 98312 | tf_op jit(solution)/shard_map/layer_one/ppermute | solution.py:31
  5.3 14.3 %collective-permute-start.8 = (bf16[4096,384]{1,0:T(8,128)(2,1)S(1)}, bf16[4096,384]{1,0:T(8,128)(2,1)S(1)}, u32[]{:S(2)}, u32[]{:S(2)}) collective-permute-start(bf16[4096,384]{1,0:T(8,128)(2,1)S(1)} %get-tuple-element.39.w_ref.refs_1_.refs_2_.w_own_ref), channel_id=1, source_target_pairs={{0,1},{1,0},{2,3},{3,2},{4,5},{5,4},{6,7},{7,6},{8,9},{9,8},{10,11... | collective-permute-start | bytes 9437192 | tf_op jit(solution)/shard_map/weights/ppermute | solution.py:31
  5.7 12.6 %collective-permute-start.5 = (bf16[128,1152]{1,0:T(8,128)(2,1)S(1)}, bf16[128,1152]{1,0:T(8,128)(2,1)S(1)}, u32[]{:S(2)}, u32[]{:S(2)}) collective-permute-start(bf16[128,1152]{1,0:T(8,128)(2,1)S(1)} %layer_one.6), channel_id=1, source_target_pairs={{0,8},{8,16},{16,24},{24,0},{1,9},{9,17},{17,25},{25,1},{2,10},{10... | collective-permute-start | bytes 884744 | tf_op jit(solution)/shard_map/hop/ppermute | solution.py:26
  10.2 8.7 %collective-permute-start.4 = (bf16[256,512]{1,0:T(8,128)(2,1)S(1)}, bf16[256,512]{1,0:T(8,128)(2,1)S(1)}, u32[]{:S(2)}, u32[]{:S(2)}) collective-permute-start(bf16[256,512]{1,0:T(8,128)(2,1)S(1)} %get-tuple-element.38), channel_id=1, source_target_pairs={{0,1},{1,0},{2,3},{3,2},{4,5},{5,4},{6,7},{7,6},{8,9},{9,8},{10,11... | collective-permute-start | bytes 786440 | tf_op jit(solution)/shard_map/weights/ppermute | solution.py:31
  10.6 12.3 %collective-permute-start.3 = (bf16[128,896]{1,0:T(8,128)(2,1)S(1)}, bf16[128,896]{1,0:T(8,128)(2,1)S(1)}, u32[]{:S(2)}, u32[]{:S(2)}) collective-permute-start(bf16[128,896]{1,0:T(8,128)(2,1)S(1)} %layer_one.7), channel_id=1, source_target_pairs={{0,8},{8,16},{16,24},{24,0},{1,9},{9,17},{17,25},{25,1},{2,10},{10... | collective-permute-start | bytes 688136 | tf_op jit(solution)/shard_map/hop/ppermute | solution.py:26
  18.3 1.7 %collective-permute-start.7 = (bf16[128,640]{1,0:T(8,128)(2,1)S(1)}, bf16[128,640]{1,0:T(8,128)(2,1)S(1)}, u32[]{:S(2)}, u32[]{:S(2)}) collective-permute-start(bf16[128,640]{1,0:T(8,128)(2,1)S(1)} %slice.9), channel_id=1, source_target_pairs={{0,1},{1,0},{2,3},{3,2},{4,5},{5,4},{6,7},{7,6},{8,9},{9,8},{10,11... | collective-permute-start | bytes 491528 | tf_op jit(solution)/shard_map/layer_two/ppermute | solution.py:31
  18.4 1.6 %collective-permute-start.6 = (bf16[128,512]{1,0:T(8,128)(2,1)S(1)}, bf16[128,512]{1,0:T(8,128)(2,1)S(1)}, u32[]{:S(2)}, u32[]{:S(2)}) collective-permute-start(bf16[128,512]{1,0:T(8,128)(2,1)S(1)} %slice.8), channel_id=1, source_target_pairs={{0,1},{1,0},{2,3},{3,2},{4,5},{5,4},{6,7},{7,6},{8,9},{9,8},{10,11... | collective-permute-start | bytes 393224 | tf_op jit(solution)/shard_map/layer_two/ppermute | solution.py:31
  22.9 1.5 %collective-permute-start.10 = (bf16[128,896]{1,0:T(8,128)(2,1)S(1)}, bf16[128,896]{1,0:T(8,128)(2,1)S(1)}, u32[]{:S(2)}, u32[]{:S(2)}) collective-permute-start(bf16[128,896]{1,0:T(8,128)(2,1)S(1)} %collective-permute-done.3.x_ref.refs_0_), channel_id=1, source_target_pairs={{0,1},{1,0},{2,3},{3,2},{4,5},{5,4},{6,7},{7,6},{8,9},{9,8},{10,11... | collective-permute-start | bytes 688136 | tf_op jit(solution)/shard_map/layer_two/ppermute | solution.py:31
  23.3 1.8 %collective-permute-start.9 = (bf16[128,512]{1,0:T(8,128)(2,1)S(1)}, bf16[128,512]{1,0:T(8,128)(2,1)S(1)}, u32[]{:S(2)}, u32[]{:S(2)}) collective-permute-start(bf16[128,512]{1,0:T(8,128)(2,1)S(1)} %get-tuple-element.47), channel_id=1, source_target_pairs={{0,1},{1,0},{2,3},{3,2},{4,5},{5,4},{6,7},{7,6},{8,9},{9,8},{10,11... | collective-permute-start | bytes 393224 | tf_op jit(solution)/shard_map/layer_two/ppermute | solution.py:31
  25.3 7.3 %collective-permute-start.14 = (bf16[128,512]{1,0:T(8,128)(2,1)S(1)}, bf16[128,512]{1,0:T(8,128)(2,1)S(1)}, u32[]{:S(2)}, u32[]{:S(2)}) collective-permute-start(bf16[128,512]{1,0:T(8,128)(2,1)S(1)} %layer_two.13.refs_0_.refs_1_), channel_id=1, source_target_pairs={{0,6},{2,4},{4,2},{6,0},{1,7},{3,5},{5,3},{7,1},{8,14},{10,12},{12... | collective-permute-start | bytes 393224 | tf_op jit(solution)/shard_map/moments/ppermute | solution.py:31
  27.8 6.9 %collective-permute-start.12 = (bf16[128,512]{1,0:T(8,128)(2,1)S(1)}, bf16[128,512]{1,0:T(8,128)(2,1)S(1)}, u32[]{:S(2)}, u32[]{:S(2)}) collective-permute-start(bf16[128,512]{1,0:T(8,128)(2,1)S(1)} %layer_two.13.refs_0_.refs_1_), channel_id=1, source_target_pairs={{0,2},{2,0},{4,6},{6,4},{1,3},{3,1},{5,7},{7,5},{8,10},{10,8},{12,... | collective-permute-start | bytes 393224 | tf_op jit(solution)/shard_map/moments/ppermute | solution.py:31
  28.4 6.3 %collective-permute-start.11 = (bf16[128,512]{1,0:T(8,128)(2,1)S(1)}, bf16[128,512]{1,0:T(8,128)(2,1)S(1)}, u32[]{:S(2)}, u32[]{:S(2)}) collective-permute-start(bf16[128,512]{1,0:T(8,128)(2,1)S(1)} %layer_two.13.refs_0_.refs_1_), channel_id=1, source_target_pairs={{0,4},{2,6},{4,0},{6,2},{1,5},{3,7},{5,1},{7,3},{8,12},{10,14},{12... | collective-permute-start | bytes 393224 | tf_op jit(solution)/shard_map/moments/ppermute | solution.py:31
  32.9 2.1 %collective-permute-start.15 = (f32[128,256]{1,0:T(8,128)S(1)}, f32[128,256]{1,0:T(8,128)S(1)}, u32[]{:S(2)}, u32[]{:S(2)}) collective-permute-start(f32[128,256]{1,0:T(8,128)S(1)} %moments.5.gram_own_ref), channel_id=1, source_target_pairs={{0,1},{1,0},{2,3},{3,2},{4,5},{5,4},{6,7},{7,6},{8,9},{9,8},{10,11... | collective-permute-start | bytes 393224 | tf_op jit(solution)/shard_map/moments/ppermute | solution.py:31
  34.9 1.3 %collective-permute-start.13 = (bf16[128,256]{1,0:T(8,128)(2,1)S(1)}, bf16[128,256]{1,0:T(8,128)(2,1)S(1)}, u32[]{:S(2)}, u32[]{:S(2)}) collective-permute-start(bf16[128,256]{1,0:T(8,128)(2,1)S(1)} %moments.4.gram_own_ref), channel_id=1, source_target_pairs={{0,1},{1,0},{2,3},{3,2},{4,5},{5,4},{6,7},{7,6},{8,9},{9,8},{10,11... | collective-permute-start | bytes 196616 | tf_op jit(solution)/shard_map/moments/ppermute | solution.py:31

commit v9 on v8

--- a/solution.py
+++ b/solution.py
@@ -17,7 +17,6 @@
 SHARES = (9, 7)
 WO_PARTS = 1
 SWAP_CUTS = 2
-DP_ORDER = lambda count: reversed(range(1, count))
 
 
 def shifted(value, axis, steps):
@@ -29,6 +28,13 @@
 def exchanged(value, axis, mask):
     count = lax.axis_size(axis)
     return lax.ppermute(value, axis, [(source, source ^ mask) for source in range(count)])
+
+
+def exchanged_by_core(value, masks):
+    cores = len(masks)
+    count = lax.axis_size("dp") * cores
+    pairs = [(source, source ^ (masks[source % cores] * cores)) for source in range(count)]
+    return lax.ppermute(value, ("dp", "tensor"), pairs)
 
 
 def after(value, *others):
@@ -244,7 +250,12 @@
 
 def result_sums(tokens, first, gram_own_ref, gram_oth_ref, embeds):
     rows = embeds[0].shape[0]
-    gram = (gram_own_ref[...].astype(F32) + gram_oth_ref[...].astype(F32)) * (1.0 / tokens)
+    gram_oth = gram_oth_ref[...].astype(F32)
+    if not first:
+        starts = range(0, gram_oth.shape[1], rows)
+        blocks = [gram_oth[:, at : at + rows] for at in starts]
+        gram_oth = jnp.concatenate(blocks[::-1], axis=1)
+    gram = (gram_own_ref[...].astype(F32) + gram_oth) * (1.0 / tokens)
     if first:
         row = lax.broadcasted_iota(jnp.int32, gram.shape, 0)
         col = lax.broadcasted_iota(jnp.int32, gram.shape, 1)
@@ -374,7 +385,9 @@
         )(live, *oth, w_own, w_oth, *sums)
         embed = call(embed_body, shape(rows, cols), "v" * 5)(live, e_mine, e_recv, mixed, combined)
     with jax.named_scope("moments"):
-        embeds = [embed] + [exchanged(embed, "dp", mask) for mask in DP_ORDER(group_count)]
+        first, *rest = reversed(range(1, group_count))
+        embeds = [embed, exchanged(embed, "dp", first)]
+        embeds += [exchanged_by_core(embed, pair) for pair in zip(rest, reversed(rest))]
         sums = ()
         for part in (embeds[:2], embeds[2:]):
             kind = BF16 if sums else F32

time: 37.3 us -> 37.3 us (level)
    ppermute x0 -> x2, waiting for transfers between devices: none -> 2.3 us  [exchanged_by_core(): return lax.ppermute(value, ('dp', 'tensor'), pairs)]
    ppermute x14 -> x12, waiting for transfers between devices: 7.49 us -> 5.22 us  [exchanged(): lax.ppermute(value, axis, [(source, source ^ mask) for source in range(co...]
    ppermute x0 -> x2, starting transfers between devices: none -> 1.04 us  [exchanged_by_core(): return lax.ppermute(value, ('dp', 'tensor'), pairs)]
    ppermute x14 -> x12, starting transfers between devices: 6.53 us -> 5.49 us  [exchanged(): lax.ppermute(value, axis, [(source, source ^ mask) for source in range(co...]
where the time goes in v9:
time: 37.3 us; the launch traced here: 37.2 us
  waiting for transfers between devices  16 us (43%)
  starting transfers between devices  10.9 us (29%)
  Pallas kernels  10 us (27%)
    pallas_call x17, Pallas kernels, call(): return lambda *operands: kernel(*map(place, operands, spaces))  10 us
    ppermute x2, waiting for transfers between devices, shifted(): return lax.ppermute(value, axis, pairs)  8.46 us
    ppermute x12, starting transfers between devices, exchanged(): lax.ppermute(value, axis, [(source, source ^ mask) for source in range(co...  5.49 us
    ppermute x12, waiting for transfers between devices, exchanged(): lax.ppermute(value, axis, [(source, source ^ mask) for source in range(co...  5.22 us
    ppermute x2, starting transfers between devices, shifted(): return lax.ppermute(value, axis, pairs)  4.37 us
    ppermute x2, waiting for transfers between devices, exchanged_by_core(): return lax.ppermute(value, ('dp', 'tensor'), pairs)  2.3 us
    ppermute x2, starting transfers between devices, exchanged_by_core(): return lax.ppermute(value, ('dp', 'tensor'), pairs)  1.04 us
  transfers between devices with their start and end apart: 16, of which 8 were waited for; matrix products, arithmetic and copies ran while one was open for 0% of the time, Pallas kernels for 23%

profile of v9, /device:TPU:0, one launch (start us, length us, event | category | flops | bytes accessed | tf_op | source)
XLA Modules:
  0.0 37.2 jit_solution(12316904426084923721)
XLA Ops:
  0.0 0.5 %collective-permute-start = (bf16[128,2048]{1,0:T(8,128)(2,1)}, bf16[128,2048]{1,0:T(8,128)(2,1)S(1)}, u32[]{:S(2)}, u32[]{:S(2)}) collective-permute-start(bf16[128,2048]{1,0:T(8,128)(2,1)} %bitcast.5), channel_id=1, source_target_pairs={{0,1},{1,0},{2,3},{3,2},{4,5},{5,4},{6,7},{7,6},{8,9},{9,8},{10,11... | collective-permute-start | bytes 1572872 | tf_op jit(solution)/shard_map/layer_one/ppermute | solution.py:30
  0.5 2.2 %layer_one.4 = (bf16[128,2048]{1,0:T(8,128)(2,1)S(1)}, bf16[4096,384]{1,0:T(8,128)(2,1)S(1)}, f32[128,384]{1,0:T(8,128)S(1)}, f32[128,128]{1,0:T(8,128)S(1)}, s3...) custom-call(s32[4]{0:T(128)} %bitcast.3, bf16[1,128,2048]{2,1,0:T(8,128)(2,1)} %own_hbm.1, ...), custom_call_target="tpu_custom_call" | custom-call | tf_op jit(solution)/shard_map/layer_one/pallas_call | solution.py:79
  2.7 0.0 copy-start.1
  2.7 0.1 collective-permute-start.2
  2.8 0.0 collective-permute-done.oth_ref
  2.8 0.0 copy-start
  2.8 0.0 copy-start.2
  2.8 0.8 %layer_one.5.mix_own_ref = bf16[128,128]{1,0:T(8,128)(2,1)S(1)} custom-call(s32[128,128]{1,0:T(8,128)S(1)} %get-tuple-element.30.live_ref, bf16[128,2048]{1,0:T(8,128)(2,1)S(1)} %collective-permute-done.oth_ref, bf16[4096,384]{1,0:T(8,128)(2,1)S(1)} %get-tuple-element.39.w_ref.refs_1_.refs_2_.w_own_ref, f32[128,384]{1,0:T(8,128)S(1)} %get-tuple-element.32.qkv_ref, ...), custom_call_target="tpu_custom_call" | custom-call | tf_op jit(solution)/shard_map/layer_one/pallas_call | solution.py:79
  3.6 0.5 %collective-permute-start.1 = (bf16[128,128]{1,0:T(8,128)(2,1)S(1)}, bf16[128,128]{1,0:T(8,128)(2,1)S(1)}, u32[]{:S(2)}, u32[]{:S(2)}) collective-permute-start(bf16[128,128]{1,0:T(8,128)(2,1)S(1)} %layer_one.5.mix_own_ref), channel_id=1, source_target_pairs={{0,1},{1,0},{2,3},{3,2},{4,5},{5,4},{6,7},{7,6},{8,9},{9,8},{10,11... | collective-permute-start | bytes 98312 | tf_op jit(solution)/shard_map/layer_one/ppermute | solution.py:30
  4.1 0.5 %collective-permute-done.2.refs_0_ = bf16[128,2048]{1,0:T(8,128)(2,1)S(1)} collective-permute-done((bf16[128,2048]{1,0:T(8,128)(2,1)S(1)}, bf16[128,2048]{1,0:T(8,128)(2,1)S(1)}, u32[]{:S(2)}, u32[]{:S(2)}) %collective-permute-start.2) | collective-permute-done | bytes 524320 | tf_op jit(solution)/shard_map/layer_one/ppermute | solution.py:30
  4.7 0.3 collective-permute-done.1.mix_oth_ref
  5.0 0.0 copy-done.1
  5.0 0.3 layer_one.6
  5.3 0.4 %collective-permute-start.8 = (bf16[4096,384]{1,0:T(8,128)(2,1)S(1)}, bf16[4096,384]{1,0:T(8,128)(2,1)S(1)}, u32[]{:S(2)}, u32[]{:S(2)}) collective-permute-start(bf16[4096,384]{1,0:T(8,128)(2,1)S(1)} %get-tuple-element.39.w_ref.refs_1_.refs_2_.w_own_ref), channel_id=1, source_target_pairs={{0,1},{1,0},{2,3},{3,2},{4,5},{5,4},{6,7},{7,6},{8,9},{9,8},{10,11... | collective-permute-start | bytes 9437192 | tf_op jit(solution)/shard_map/weights/ppermute | solution.py:30
  5.7 2.7 %collective-permute-start.5 = (bf16[128,1152]{1,0:T(8,128)(2,1)S(1)}, bf16[128,1152]{1,0:T(8,128)(2,1)S(1)}, u32[]{:S(2)}, u32[]{:S(2)}) collective-permute-start(bf16[128,1152]{1,0:T(8,128)(2,1)S(1)} %layer_one.6), channel_id=1, source_target_pairs={{0,8},{8,16},{16,24},{24,0},{1,9},{9,17},{17,25},{25,1},{2,10},{10... | collective-permute-start | bytes 884744 | tf_op jit(solution)/shard_map/hop/ppermute | solution.py:25
  8.4 0.0 copy-done
  8.4 0.0 copy-done.2
  8.4 1.8 %weights.2 = (f32[256,512]{1,0:T(8,128)S(1)}, bf16[256,512]{1,0:T(8,128)(2,1)S(1)}, s32[128,128]{1,0:T(8,128)S(1)}) custom-call(s32[4]{0:T(128)S(1)} %bitcast.4, bf16[1,128,4096]{2,1,0:T(8,128)(2,1)S(1)} %copy-done.1, bf16[2048,1024]{1,0:T(8,128)(2,1)S(1)} %copy-done, bf16[128,2048]{1,0:T(8,128)(2,1)S(1)} %collective-permute-done.2.refs_0_), custom_call_target="tpu_custom_call" | custom-call | tf_op jit(solution)/shard_map/weights/pallas_call | solution.py:79
  10.2 0.1 collective-permute-start.4
  10.4 0.2 layer_one.7
  10.6 1.6 %collective-permute-start.3 = (bf16[128,896]{1,0:T(8,128)(2,1)S(1)}, bf16[128,896]{1,0:T(8,128)(2,1)S(1)}, u32[]{:S(2)}, u32[]{:S(2)}) collective-permute-start(bf16[128,896]{1,0:T(8,128)(2,1)S(1)} %layer_one.7), channel_id=1, source_target_pairs={{0,8},{8,16},{16,24},{24,0},{1,9},{9,17},{17,25},{25,1},{2,10},{10... | collective-permute-start | bytes 688136 | tf_op jit(solution)/shard_map/hop/ppermute | solution.py:25
  12.2 6.1 %collective-permute-done.5.x_ref.refs_0_ = bf16[128,1152]{1,0:T(8,128)(2,1)S(1)} collective-permute-done((bf16[128,1152]{1,0:T(8,128)(2,1)S(1)}, bf16[128,1152]{1,0:T(8,128)(2,1)S(1)}, u32[]{:S(2)}, u32[]{:S(2)}) %collective-permute-start.5) | collective-permute-done | bytes 294944 | tf_op jit(solution)/shard_map/hop/ppermute | solution.py:25
  18.3 0.1 collective-permute-start.7
  18.4 0.6 %collective-permute-start.6 = (bf16[128,512]{1,0:T(8,128)(2,1)S(1)}, bf16[128,512]{1,0:T(8,128)(2,1)S(1)}, u32[]{:S(2)}, u32[]{:S(2)}) collective-permute-start(bf16[128,512]{1,0:T(8,128)(2,1)S(1)} %slice.8), channel_id=1, source_target_pairs={{0,1},{1,0},{2,3},{3,2},{4,5},{5,4},{6,7},{7,6},{8,9},{9,8},{10,11... | collective-permute-start | bytes 393224 | tf_op jit(solution)/shard_map/layer_two/ppermute | solution.py:30
  19.0 0.0 collective-permute-done.4.recv_ref
  19.0 0.5 %layer_two.7.embed_ref = f32[128,1024]{1,0:T(8,128)S(1)} custom-call(bf16[128,1152]{1,0:T(8,128)(2,1)S(1)} %collective-permute-done.5.x_ref.refs_0_, bf16[2048,1024]{1,0:T(8,128)(2,1)S(1)} %copy-done), custom_call_target="tpu_custom_call" | custom-call | tf_op jit(solution)/shard_map/layer_two/pallas_call | solution.py:79
  19.5 0.0 collective-permute-done.8.refs_2_.refs_3_.w_oth_ref
  19.5 0.4 %layer_two.8 = (f32[128,768]{1,0:T(8,128)S(1)}, f32[128,128]{1,0:T(8,128)S(1)}) custom-call(bf16[128,1152]{1,0:T(8,128)(2,1)S(1)} %collective-permute-done.5.x_ref.refs_0_, bf16[4096,384]{1,0:T(8,128)(2,1)S(1)} %get-tuple-element.39.w_ref.refs_1_.refs_2_.w_own_ref, bf16[4096,384]{1,0:T(8,128)(2,1)S(1)} %collective-permute-done.8.refs_2_.refs_3_.w_oth_ref), custom_call_target="tpu_custom_call" | custom-call | tf_op jit(solution)/shard_map/layer_two/pallas_call | solution.py:79
  20.0 0.0 collective-permute-done.6.refs_0_
  20.0 0.0 collective-permute-done.7.refs_1_
  20.0 0.4 %layer_two.9 = (f32[128,768]{1,0:T(8,128)S(1)}, f32[128,128]{1,0:T(8,128)S(1)}) custom-call(bf16[128,512]{1,0:T(8,128)(2,1)S(1)} %collective-permute-done.6.refs_0_, bf16[128,640]{1,0:T(8,128)(2,1)S(1)} %collective-permute-done.7.refs_1_, bf16[4096,384]{1,0:T(8,128)(2,1)S(1)} %get-tuple-element.39.w_ref.refs_1_.refs_2_.w_own_ref, ...), custom_call_target="tpu_custom_call" | custom-call | tf_op jit(solution)/shard_map/layer_two/pallas_call | solution.py:79
  20.5 2.4 %collective-permute-done.3.x_ref.refs_0_ = bf16[128,896]{1,0:T(8,128)(2,1)S(1)} collective-permute-done((bf16[128,896]{1,0:T(8,128)(2,1)S(1)}, bf16[128,896]{1,0:T(8,128)(2,1)S(1)}, u32[]{:S(2)}, u32[]{:S(2)}) %collective-permute-start.3) | collective-permute-done | bytes 229408 | tf_op jit(solution)/shard_map/hop/ppermute | solution.py:25
  22.9 0.0 collective-permute-start.10
  22.9 0.4 %layer_two.10 = (f32[128,512]{1,0:T(8,128)S(1)}, bf16[128,512]{1,0:T(8,128)(2,1)S(1)}) custom-call(bf16[128,896]{1,0:T(8,128)(2,1)S(1)} %collective-permute-done.3.x_ref.refs_0_, bf16[2048,1024]{1,0:T(8,128)(2,1)S(1)} %copy-done, f32[128,1024]{1,0:T(8,128)S(1)} %layer_two.7.embed_ref), custom_call_target="tpu_custom_call" | custom-call | tf_op jit(solution)/shard_map/layer_two/pallas_call | solution.py:79
  23.3 0.6 %collective-permute-start.9 = (bf16[128,512]{1,0:T(8,128)(2,1)S(1)}, bf16[128,512]{1,0:T(8,128)(2,1)S(1)}, u32[]{:S(2)}, u32[]{:S(2)}) collective-permute-start(bf16[128,512]{1,0:T(8,128)(2,1)S(1)} %get-tuple-element.47), channel_id=1, source_target_pairs={{0,1},{1,0},{2,3},{3,2},{4,5},{5,4},{6,7},{7,6},{8,9},{9,8},{10,11... | collective-permute-start | bytes 393224 | tf_op jit(solution)/shard_map/layer_two/ppermute | solution.py:30
  23.9 0.4 %layer_two.11 = (f32[128,768]{1,0:T(8,128)S(1)}, f32[128,128]{1,0:T(8,128)S(1)}) custom-call(bf16[128,896]{1,0:T(8,128)(2,1)S(1)} %collective-permute-done.3.x_ref.refs_0_, bf16[4096,384]{1,0:T(8,128)(2,1)S(1)} %get-tuple-element.39.w_ref.refs_1_.refs_2_.w_own_ref, bf16[4096,384]{1,0:T(8,128)(2,1)S(1)} %collective-permute-done.8.refs_2_.refs_3_.w_oth_ref, ...), custom_call_target="tpu_custom_call" | custom-call | tf_op jit(solution)/shard_map/layer_two/pallas_call | solution.py:79
  24.3 0.1 collective-permute-done.10.x_ref
  24.4 0.7 %layer_two.12.mixed_ref = bf16[128,256]{1,0:T(8,128)(2,1)S(1)} custom-call(s32[128,128]{1,0:T(8,128)S(1)} %get-tuple-element.36.live_ref, bf16[128,896]{1,0:T(8,128)(2,1)S(1)} %collective-permute-done.10.x_ref, bf16[4096,384]{1,0:T(8,128)(2,1)S(1)} %get-tuple-element.39.w_ref.refs_1_.refs_2_.w_own_ref, ...), custom_call_target="tpu_custom_call" | custom-call | tf_op jit(solution)/shard_map/layer_two/pallas_call | solution.py:79
  25.1 0.0 collective-permute-done.9.recv_ref
  25.1 0.2 layer_two.13.refs_0_.refs_1_
  25.3 2.5 %collective-permute-start.14 = (bf16[128,512]{1,0:T(8,128)(2,1)S(1)}, bf16[128,512]{1,0:T(8,128)(2,1)S(1)}, u32[]{:S(2)}, u32[]{:S(2)}) collective-permute-start(bf16[128,512]{1,0:T(8,128)(2,1)S(1)} %layer_two.13.refs_0_.refs_1_), channel_id=1, source_target_pairs={{0,6},{2,4},{4,2},{6,0},{1,7},{3,5},{5,3},{7,1},{8,14},{10,12},{12... | collective-permute-start | bytes 393224 | tf_op jit(solution)/shard_map/moments/ppermute | solution.py:30
  27.8 0.5 %collective-permute-start.12 = (bf16[128,512]{1,0:T(8,128)(2,1)S(1)}, bf16[128,512]{1,0:T(8,128)(2,1)S(1)}, u32[]{:S(2)}, u32[]{:S(2)}) collective-permute-start(bf16[128,512]{1,0:T(8,128)(2,1)S(1)} %layer_two.13.refs_0_.refs_1_), channel_id=1, source_target_pairs={{0,2},{1,5},{2,0},{3,7},{4,6},{5,1},{6,4},{7,3},{8,10},{9,13},{10,... | collective-permute-start | bytes 393224 | tf_op jit(solution)/shard_map/moments/ppermute | solution.py:37
  28.4 0.5 %collective-permute-start.11 = (bf16[128,512]{1,0:T(8,128)(2,1)S(1)}, bf16[128,512]{1,0:T(8,128)(2,1)S(1)}, u32[]{:S(2)}, u32[]{:S(2)}) collective-permute-start(bf16[128,512]{1,0:T(8,128)(2,1)S(1)} %layer_two.13.refs_0_.refs_1_), channel_id=1, source_target_pairs={{0,4},{1,3},{2,6},{3,1},{4,0},{5,7},{6,2},{7,5},{8,12},{9,11},{10,... | collective-permute-start | bytes 393224 | tf_op jit(solution)/shard_map/moments/ppermute | solution.py:37
  28.9 3.2 %collective-permute-done.14.refs_2_.refs_1_ = bf16[128,512]{1,0:T(8,128)(2,1)S(1)} collective-permute-done((bf16[128,512]{1,0:T(8,128)(2,1)S(1)}, bf16[128,512]{1,0:T(8,128)(2,1)S(1)}, u32[]{:S(2)}, u32[]{:S(2)}) %collective-permute-start.14) | collective-permute-done | bytes 131104 | tf_op jit(solution)/shard_map/moments/ppermute | solution.py:30
  32.1 0.2 moments.5.gram_own_ref
  32.3 0.1 collective-permute-start.15
  32.4 2.3 %collective-permute-done.12.refs_2_.refs_1_ = bf16[128,512]{1,0:T(8,128)(2,1)S(1)} collective-permute-done((bf16[128,512]{1,0:T(8,128)(2,1)S(1)}, bf16[128,512]{1,0:T(8,128)(2,1)S(1)}, u32[]{:S(2)}, u32[]{:S(2)}) %collective-permute-start.12) | collective-permute-done | bytes 131104 | tf_op jit(solution)/shard_map/moments/ppermute | solution.py:37
  34.7 0.0 collective-permute-done.11.refs_1_.refs_0_
  34.7 0.2 moments.4.gram_own_ref
  35.0 0.1 collective-permute-start.13
  35.0 0.0 collective-permute-done.15.gram_oth_ref
  35.0 0.2 moments.6.refs_2_
  35.2 1.0 %collective-permute-done.13.gram_oth_ref = bf16[128,256]{1,0:T(8,128)(2,1)S(1)} collective-permute-done((bf16[128,256]{1,0:T(8,128)(2,1)S(1)}, bf16[128,256]{1,0:T(8,128)(2,1)S(1)}, u32[]{:S(2)}, u32[]{:S(2)}) %collective-permute-start.13) | collective-permute-done | bytes 65568 | tf_op jit(solution)/shard_map/moments/ppermute | solution.py:30
  36.3 0.9 %moments.7 = f32[128,512]{1,0:T(8,128)} custom-call(bf16[128,256]{1,0:T(8,128)(2,1)S(1)} %moments.4.gram_own_ref, bf16[128,256]{1,0:T(8,128)(2,1)S(1)} %collective-permute-done.13.gram_oth_ref, bf16[128,512]{1,0:T(8,128)(2,1)S(1)} %collective-permute-done.11.refs_1_.refs_0_, bf16[128,512]{1,0:T(8,128)(2,1)S(1)} %collective-permute-done.12.refs_2_.refs_1_, ...), custom_call_target="tpu_custom_call" | custom-call | tf_op jit(solution)/shard_map/moments/pallas_call | solution.py:79
  (3 shorter events, 0.1 us)
Async XLA Ops:
  0.0 2.8 %collective-permute-start = (bf16[128,2048]{1,0:T(8,128)(2,1)}, bf16[128,2048]{1,0:T(8,128)(2,1)S(1)}, u32[]{:S(2)}, u32[]{:S(2)}) collective-permute-start(bf16[128,2048]{1,0:T(8,128)(2,1)} %bitcast.5), channel_id=1, source_target_pairs={{0,1},{1,0},{2,3},{3,2},{4,5},{5,4},{6,7},{7,6},{8,9},{9,8},{10,11... | collective-permute-start | bytes 1572872 | tf_op jit(solution)/shard_map/layer_one/ppermute | solution.py:30
  2.7 2.3 %copy-start.1 = (bf16[1,128,4096]{2,1,0:T(8,128)(2,1)S(1)}, bf16[1,128,4096]{2,1,0:T(8,128)(2,1)}, u32[]{:S(2)}) copy-start(bf16[1,128,4096]{2,1,0:T(8,128)(2,1)} %w_own_ref.5) | copy-start | bytes 3145732
  2.7 2.0 %collective-permute-start.2 = (bf16[128,2048]{1,0:T(8,128)(2,1)S(1)}, bf16[128,2048]{1,0:T(8,128)(2,1)S(1)}, u32[]{:S(2)}, u32[]{:S(2)}) collective-permute-start(bf16[128,2048]{1,0:T(8,128)(2,1)S(1)} %get-tuple-element.34), channel_id=1, source_target_pairs={{0,1},{1,0},{2,3},{3,2},{4,5},{5,4},{6,7},{7,6},{8,9},{9,8},{10,11... | collective-permute-start | bytes 1572872 | tf_op jit(solution)/shard_map/layer_one/ppermute | solution.py:30
  2.8 5.6 %copy-start = (bf16[2048,1024]{1,0:T(8,128)(2,1)S(1)}, bf16[2048,1024]{1,0:T(8,128)(2,1)}, u32[]{:S(2)}) copy-start(bf16[2048,1024]{1,0:T(8,128)(2,1)} %e_ref.2) | copy-start | bytes 12582916
  2.8 5.6 %copy-start.2 = (s32[4,1]{0,1:T(1,128)S(1)}, s32[4,1]{0,1:T(1,128)}, u32[]{:S(2)}) copy-start(s32[4,1]{0,1:T(1,128)} %param.8) | copy-start | bytes 52
  3.6 1.4 %collective-permute-start.1 = (bf16[128,128]{1,0:T(8,128)(2,1)S(1)}, bf16[128,128]{1,0:T(8,128)(2,1)S(1)}, u32[]{:S(2)}, u32[]{:S(2)}) collective-permute-start(bf16[128,128]{1,0:T(8,128)(2,1)S(1)} %layer_one.5.mix_own_ref), channel_id=1, source_target_pairs={{0,1},{1,0},{2,3},{3,2},{4,5},{5,4},{6,7},{7,6},{8,9},{9,8},{10,11... | collective-permute-start | bytes 98312 | tf_op jit(solution)/shard_map/layer_one/ppermute | solution.py:30
  5.3 14.3 %collective-permute-start.8 = (bf16[4096,384]{1,0:T(8,128)(2,1)S(1)}, bf16[4096,384]{1,0:T(8,128)(2,1)S(1)}, u32[]{:S(2)}, u32[]{:S(2)}) collective-permute-start(bf16[4096,384]{1,0:T(8,128)(2,1)S(1)} %get-tuple-element.39.w_ref.refs_1_.refs_2_.w_own_ref), channel_id=1, source_target_pairs={{0,1},{1,0},{2,3},{3,2},{4,5},{5,4},{6,7},{7,6},{8,9},{9,8},{10,11... | collective-permute-start | bytes 9437192 | tf_op jit(solution)/shard_map/weights/ppermute | solution.py:30
  5.7 12.6 %collective-permute-start.5 = (bf16[128,1152]{1,0:T(8,128)(2,1)S(1)}, bf16[128,1152]{1,0:T(8,128)(2,1)S(1)}, u32[]{:S(2)}, u32[]{:S(2)}) collective-permute-start(bf16[128,1152]{1,0:T(8,128)(2,1)S(1)} %layer_one.6), channel_id=1, source_target_pairs={{0,8},{8,16},{16,24},{24,0},{1,9},{9,17},{17,25},{25,1},{2,10},{10... | collective-permute-start | bytes 884744 | tf_op jit(solution)/shard_map/hop/ppermute | solution.py:25
  10.2 8.7 %collective-permute-start.4 = (bf16[256,512]{1,0:T(8,128)(2,1)S(1)}, bf16[256,512]{1,0:T(8,128)(2,1)S(1)}, u32[]{:S(2)}, u32[]{:S(2)}) collective-permute-start(bf16[256,512]{1,0:T(8,128)(2,1)S(1)} %get-tuple-element.38), channel_id=1, source_target_pairs={{0,1},{1,0},{2,3},{3,2},{4,5},{5,4},{6,7},{7,6},{8,9},{9,8},{10,11... | collective-permute-start | bytes 786440 | tf_op jit(solution)/shard_map/weights/ppermute | solution.py:30
  10.6 12.3 %collective-permute-start.3 = (bf16[128,896]{1,0:T(8,128)(2,1)S(1)}, bf16[128,896]{1,0:T(8,128)(2,1)S(1)}, u32[]{:S(2)}, u32[]{:S(2)}) collective-permute-start(bf16[128,896]{1,0:T(8,128)(2,1)S(1)} %layer_one.7), channel_id=1, source_target_pairs={{0,8},{8,16},{16,24},{24,0},{1,9},{9,17},{17,25},{25,1},{2,10},{10... | collective-permute-start | bytes 688136 | tf_op jit(solution)/shard_map/hop/ppermute | solution.py:25
  18.3 1.7 %collective-permute-start.7 = (bf16[128,640]{1,0:T(8,128)(2,1)S(1)}, bf16[128,640]{1,0:T(8,128)(2,1)S(1)}, u32[]{:S(2)}, u32[]{:S(2)}) collective-permute-start(bf16[128,640]{1,0:T(8,128)(2,1)S(1)} %slice.9), channel_id=1, source_target_pairs={{0,1},{1,0},{2,3},{3,2},{4,5},{5,4},{6,7},{7,6},{8,9},{9,8},{10,11... | collective-permute-start | bytes 491528 | tf_op jit(solution)/shard_map/layer_two/ppermute | solution.py:30
  18.4 1.6 %collective-permute-start.6 = (bf16[128,512]{1,0:T(8,128)(2,1)S(1)}, bf16[128,512]{1,0:T(8,128)(2,1)S(1)}, u32[]{:S(2)}, u32[]{:S(2)}) collective-permute-start(bf16[128,512]{1,0:T(8,128)(2,1)S(1)} %slice.8), channel_id=1, source_target_pairs={{0,1},{1,0},{2,3},{3,2},{4,5},{5,4},{6,7},{7,6},{8,9},{9,8},{10,11... | collective-permute-start | bytes 393224 | tf_op jit(solution)/shard_map/layer_two/ppermute | solution.py:30
  22.9 1.5 %collective-permute-start.10 = (bf16[128,896]{1,0:T(8,128)(2,1)S(1)}, bf16[128,896]{1,0:T(8,128)(2,1)S(1)}, u32[]{:S(2)}, u32[]{:S(2)}) collective-permute-start(bf16[128,896]{1,0:T(8,128)(2,1)S(1)} %collective-permute-done.3.x_ref.refs_0_), channel_id=1, source_target_pairs={{0,1},{1,0},{2,3},{3,2},{4,5},{5,4},{6,7},{7,6},{8,9},{9,8},{10,11... | collective-permute-start | bytes 688136 | tf_op jit(solution)/shard_map/layer_two/ppermute | solution.py:30
  23.3 1.8 %collective-permute-start.9 = (bf16[128,512]{1,0:T(8,128)(2,1)S(1)}, bf16[128,512]{1,0:T(8,128)(2,1)S(1)}, u32[]{:S(2)}, u32[]{:S(2)}) collective-permute-start(bf16[128,512]{1,0:T(8,128)(2,1)S(1)} %get-tuple-element.47), channel_id=1, source_target_pairs={{0,1},{1,0},{2,3},{3,2},{4,5},{5,4},{6,7},{7,6},{8,9},{9,8},{10,11... | collective-permute-start | bytes 393224 | tf_op jit(solution)/shard_map/layer_two/ppermute | solution.py:30
  25.3 6.8 %collective-permute-start.14 = (bf16[128,512]{1,0:T(8,128)(2,1)S(1)}, bf16[128,512]{1,0:T(8,128)(2,1)S(1)}, u32[]{:S(2)}, u32[]{:S(2)}) collective-permute-start(bf16[128,512]{1,0:T(8,128)(2,1)S(1)} %layer_two.13.refs_0_.refs_1_), channel_id=1, source_target_pairs={{0,6},{2,4},{4,2},{6,0},{1,7},{3,5},{5,3},{7,1},{8,14},{10,12},{12... | collective-permute-start | bytes 393224 | tf_op jit(solution)/shard_map/moments/ppermute | solution.py:30
  27.8 6.9 %collective-permute-start.12 = (bf16[128,512]{1,0:T(8,128)(2,1)S(1)}, bf16[128,512]{1,0:T(8,128)(2,1)S(1)}, u32[]{:S(2)}, u32[]{:S(2)}) collective-permute-start(bf16[128,512]{1,0:T(8,128)(2,1)S(1)} %layer_two.13.refs_0_.refs_1_), channel_id=1, source_target_pairs={{0,2},{1,5},{2,0},{3,7},{4,6},{5,1},{6,4},{7,3},{8,10},{9,13},{10,... | collective-permute-start | bytes 393224 | tf_op jit(solution)/shard_map/moments/ppermute | solution.py:37
  28.4 6.3 %collective-permute-start.11 = (bf16[128,512]{1,0:T(8,128)(2,1)S(1)}, bf16[128,512]{1,0:T(8,128)(2,1)S(1)}, u32[]{:S(2)}, u32[]{:S(2)}) collective-permute-start(bf16[128,512]{1,0:T(8,128)(2,1)S(1)} %layer_two.13.refs_0_.refs_1_), channel_id=1, source_target_pairs={{0,4},{1,3},{2,6},{3,1},{4,0},{5,7},{6,2},{7,5},{8,12},{9,11},{10,... | collective-permute-start | bytes 393224 | tf_op jit(solution)/shard_map/moments/ppermute | solution.py:37
  32.3 2.7 %collective-permute-start.15 = (f32[128,256]{1,0:T(8,128)S(1)}, f32[128,256]{1,0:T(8,128)S(1)}, u32[]{:S(2)}, u32[]{:S(2)}) collective-permute-start(f32[128,256]{1,0:T(8,128)S(1)} %moments.5.gram_own_ref), channel_id=1, source_target_pairs={{0,1},{1,0},{2,3},{3,2},{4,5},{5,4},{6,7},{7,6},{8,9},{9,8},{10,11... | collective-permute-start | bytes 393224 | tf_op jit(solution)/shard_map/moments/ppermute | solution.py:30
  35.0 1.3 %collective-permute-start.13 = (bf16[128,256]{1,0:T(8,128)(2,1)S(1)}, bf16[128,256]{1,0:T(8,128)(2,1)S(1)}, u32[]{:S(2)}, u32[]{:S(2)}) collective-permute-start(bf16[128,256]{1,0:T(8,128)(2,1)S(1)} %moments.4.gram_own_ref), channel_id=1, source_target_pairs={{0,1},{1,0},{2,3},{3,2},{4,5},{5,4},{6,7},{7,6},{8,9},{9,8},{10,11... | collective-permute-start | bytes 196616 | tf_op jit(solution)/shard_map/moments/ppermute | solution.py:30

commit v10 on v8

--- a/solution.py
+++ b/solution.py
@@ -14,9 +14,9 @@
 BF16 = jnp.bfloat16
 F32 = jnp.float32
 VMEM_BYTES = 18 * 1024 * 1024
-SHARES = (9, 7)
+SHARES = (5, 5, 6)
 WO_PARTS = 1
-SWAP_CUTS = 2
+SWAP_CUTS = 1
 DP_ORDER = lambda count: reversed(range(1, count))
 
 

time: 37.3 us -> 37.2 us (level)
  waiting for transfers between devices: 16 us -> 14.1 us
  starting transfers between devices: 10.9 us -> 11.9 us
  Pallas kernels: 10 us -> 10.8 us
    ppermute x2 -> x3, waiting for transfers between devices: 8.46 us -> 6.58 us  [shifted(): return lax.ppermute(value, axis, pairs)]
    ppermute x2 -> x3, starting transfers between devices: 4.37 us -> 5.99 us  [shifted(): return lax.ppermute(value, axis, pairs)]
    pallas_call x17 -> x21, Pallas kernels: 10 us -> 10.8 us  [call(): return lambda *operands: kernel(*map(place, operands, spaces))]
    ppermute x14, starting transfers between devices: 6.53 us -> 5.87 us  [exchanged(): lax.ppermute(value, axis, [(source, source ^ mask) for source in range(co...]
  transfers between devices with their start and end apart: 16 -> 17, of which waited for: 8 -> 9; matrix products, arithmetic and copies ran while one was open for 0% -> 0% of each run, Pallas kernels for 23% -> 26%
where the time goes in v10:
time: 37.2 us; the launch traced here: 37.1 us
  waiting for transfers between devices  14.1 us (38%)
  starting transfers between devices  11.9 us (32%)
  Pallas kernels  10.8 us (29%)
    pallas_call x21, Pallas kernels, call(): return lambda *operands: kernel(*map(place, operands, spaces))  10.8 us
    ppermute x14, waiting for transfers between devices, exchanged(): lax.ppermute(value, axis, [(source, source ^ mask) for source in range(co...  7.57 us
    ppermute x3, waiting for transfers between devices, shifted(): return lax.ppermute(value, axis, pairs)  6.58 us
    ppermute x3, starting transfers between devices, shifted(): return lax.ppermute(value, axis, pairs)  5.99 us
    ppermute x14, starting transfers between devices, exchanged(): lax.ppermute(value, axis, [(source, source ^ mask) for source in range(co...  5.87 us
  transfers between devices with their start and end apart: 17, of which 9 were waited for; matrix products, arithmetic and copies ran while one was open for 0% of the time, Pallas kernels for 26%

profile of v10, /device:TPU:0, one launch (start us, length us, event | category | flops | bytes accessed | tf_op | source)
XLA Modules:
  0.0 37.1 jit_solution(7821142839090420309)
XLA Ops:
  0.0 0.5 %collective-permute-start = (bf16[128,2048]{1,0:T(8,128)(2,1)}, bf16[128,2048]{1,0:T(8,128)(2,1)S(1)}, u32[]{:S(2)}, u32[]{:S(2)}) collective-permute-start(bf16[128,2048]{1,0:T(8,128)(2,1)} %bitcast.5), channel_id=1, source_target_pairs={{0,1},{1,0},{2,3},{3,2},{4,5},{5,4},{6,7},{7,6},{8,9},{9,8},{10,11... | collective-permute-start | bytes 1572872 | tf_op jit(solution)/shard_map/layer_one/ppermute | solution.py:31
  0.5 2.2 %layer_one.5 = (bf16[128,2048]{1,0:T(8,128)(2,1)S(1)}, bf16[4096,384]{1,0:T(8,128)(2,1)S(1)}, f32[128,384]{1,0:T(8,128)S(1)}, f32[128,128]{1,0:T(8,128)S(1)}, s3...) custom-call(s32[4]{0:T(128)} %bitcast.3, bf16[1,128,2048]{2,1,0:T(8,128)(2,1)} %own_hbm.1, ...), custom_call_target="tpu_custom_call" | custom-call | tf_op jit(solution)/shard_map/layer_one/pallas_call | solution.py:73
  2.7 0.0 copy-start.1
  2.7 0.1 collective-permute-start.2
  2.8 0.0 collective-permute-done.oth_ref
  2.8 0.8 %layer_one.6.mix_own_ref = bf16[128,128]{1,0:T(8,128)(2,1)S(1)} custom-call(s32[128,128]{1,0:T(8,128)S(1)} %get-tuple-element.34.live_ref, bf16[128,2048]{1,0:T(8,128)(2,1)S(1)} %collective-permute-done.oth_ref, bf16[4096,384]{1,0:T(8,128)(2,1)S(1)} %get-tuple-element.43.w_ref.refs_1_.w_own_ref, f32[128,384]{1,0:T(8,128)S(1)} %get-tuple-element.36.qkv_ref, ...), custom_call_target="tpu_custom_call" | custom-call | tf_op jit(solution)/shard_map/layer_one/pallas_call | solution.py:73
  3.6 0.0 copy-start
  3.6 0.0 copy-start.2
  3.6 0.5 %collective-permute-start.1 = (bf16[128,128]{1,0:T(8,128)(2,1)S(1)}, bf16[128,128]{1,0:T(8,128)(2,1)S(1)}, u32[]{:S(2)}, u32[]{:S(2)}) collective-permute-start(bf16[128,128]{1,0:T(8,128)(2,1)S(1)} %layer_one.6.mix_own_ref), channel_id=1, source_target_pairs={{0,1},{1,0},{2,3},{3,2},{4,5},{5,4},{6,7},{7,6},{8,9},{9,8},{10,11... | collective-permute-start | bytes 98312 | tf_op jit(solution)/shard_map/layer_one/ppermute | solution.py:31
  4.2 0.5 %collective-permute-done.2.refs_0_ = bf16[128,2048]{1,0:T(8,128)(2,1)S(1)} collective-permute-done((bf16[128,2048]{1,0:T(8,128)(2,1)S(1)}, bf16[128,2048]{1,0:T(8,128)(2,1)S(1)}, u32[]{:S(2)}, u32[]{:S(2)}) %collective-permute-start.2) | collective-permute-done | bytes 524320 | tf_op jit(solution)/shard_map/layer_one/ppermute | solution.py:31
  4.7 0.3 collective-permute-done.1.mix_oth_ref
  5.0 0.0 copy-done.1
  5.0 0.2 layer_one.7
  5.2 0.4 %collective-permute-start.8 = (bf16[4096,384]{1,0:T(8,128)(2,1)S(1)}, bf16[4096,384]{1,0:T(8,128)(2,1)S(1)}, u32[]{:S(2)}, u32[]{:S(2)}) collective-permute-start(bf16[4096,384]{1,0:T(8,128)(2,1)S(1)} %get-tuple-element.43.w_ref.refs_1_.w_own_ref), channel_id=1, source_target_pairs={{0,1},{1,0},{2,3},{3,2},{4,5},{5,4},{6,7},{7,6},{8,9},{9,8},{10,11... | collective-permute-start | bytes 9437192 | tf_op jit(solution)/shard_map/weights/ppermute | solution.py:31
  5.7 2.7 %collective-permute-start.6 = (bf16[128,640]{1,0:T(8,128)(2,1)S(1)}, bf16[128,640]{1,0:T(8,128)(2,1)S(1)}, u32[]{:S(2)}, u32[]{:S(2)}) collective-permute-start(bf16[128,640]{1,0:T(8,128)(2,1)S(1)} %layer_one.7), channel_id=1, source_target_pairs={{0,8},{8,16},{16,24},{24,0},{1,9},{9,17},{17,25},{25,1},{2,10},{10... | collective-permute-start | bytes 491528 | tf_op jit(solution)/shard_map/hop/ppermute | solution.py:26
  8.4 0.2 layer_one.9
  8.6 1.6 %collective-permute-start.5 = (bf16[128,640]{1,0:T(8,128)(2,1)S(1)}, bf16[128,640]{1,0:T(8,128)(2,1)S(1)}, u32[]{:S(2)}, u32[]{:S(2)}) collective-permute-start(bf16[128,640]{1,0:T(8,128)(2,1)S(1)} %layer_one.9), channel_id=1, source_target_pairs={{0,8},{8,16},{16,24},{24,0},{1,9},{9,17},{17,25},{25,1},{2,10},{10... | collective-permute-start | bytes 491528 | tf_op jit(solution)/shard_map/hop/ppermute | solution.py:26
  10.3 0.0 copy-done
  10.3 0.0 copy-done.2
  10.3 1.8 %weights.2 = (f32[256,512]{1,0:T(8,128)S(1)}, bf16[256,512]{1,0:T(8,128)(2,1)S(1)}, s32[128,128]{1,0:T(8,128)S(1)}) custom-call(s32[4]{0:T(128)S(1)} %bitcast.4, bf16[1,128,4096]{2,1,0:T(8,128)(2,1)S(1)} %copy-done.1, bf16[2048,1024]{1,0:T(8,128)(2,1)S(1)} %copy-done, bf16[128,2048]{1,0:T(8,128)(2,1)S(1)} %collective-permute-done.2.refs_0_), custom_call_target="tpu_custom_call" | custom-call | tf_op jit(solution)/shard_map/weights/pallas_call | solution.py:73
  12.1 0.1 collective-permute-start.4
  12.2 0.2 layer_one.8
  12.4 1.6 %collective-permute-start.3 = (bf16[128,768]{1,0:T(8,128)(2,1)S(1)}, bf16[128,768]{1,0:T(8,128)(2,1)S(1)}, u32[]{:S(2)}, u32[]{:S(2)}) collective-permute-start(bf16[128,768]{1,0:T(8,128)(2,1)S(1)} %layer_one.8), channel_id=1, source_target_pairs={{0,8},{8,16},{16,24},{24,0},{1,9},{9,17},{17,25},{25,1},{2,10},{10... | collective-permute-start | bytes 589832 | tf_op jit(solution)/shard_map/hop/ppermute | solution.py:26
  14.0 1.4 %collective-permute-done.6.x_ref.refs_0_ = bf16[128,640]{1,0:T(8,128)(2,1)S(1)} collective-permute-done((bf16[128,640]{1,0:T(8,128)(2,1)S(1)}, bf16[128,640]{1,0:T(8,128)(2,1)S(1)}, u32[]{:S(2)}, u32[]{:S(2)}) %collective-permute-start.6) | collective-permute-done | bytes 163872 | tf_op jit(solution)/shard_map/hop/ppermute | solution.py:26
  15.5 0.0 collective-permute-start.9
  15.5 3.5 %collective-permute-done.5.x_ref.refs_0_ = bf16[128,640]{1,0:T(8,128)(2,1)S(1)} collective-permute-done((bf16[128,640]{1,0:T(8,128)(2,1)S(1)}, bf16[128,640]{1,0:T(8,128)(2,1)S(1)}, u32[]{:S(2)}, u32[]{:S(2)}) %collective-permute-start.5) | collective-permute-done | bytes 163872 | tf_op jit(solution)/shard_map/hop/ppermute | solution.py:26
  19.0 0.0 collective-permute-start.7
  19.0 0.4 %layer_two.10.refs_0_ = f32[128,1024]{1,0:T(8,128)S(1)} custom-call(bf16[128,640]{1,0:T(8,128)(2,1)S(1)} %collective-permute-done.6.x_ref.refs_0_, bf16[2048,1024]{1,0:T(8,128)(2,1)S(1)} %copy-done), custom_call_target="tpu_custom_call" | custom-call | tf_op jit(solution)/shard_map/layer_two/pallas_call | solution.py:73
  19.4 0.4 %layer_two.11.embed_ref = f32[128,1024]{1,0:T(8,128)S(1)} custom-call(bf16[128,640]{1,0:T(8,128)(2,1)S(1)} %collective-permute-done.5.x_ref.refs_0_, bf16[2048,1024]{1,0:T(8,128)(2,1)S(1)} %copy-done, f32[128,1024]{1,0:T(8,128)S(1)} %layer_two.10.refs_0_), custom_call_target="tpu_custom_call" | custom-call | tf_op jit(solution)/shard_map/layer_two/pallas_call | solution.py:73
  19.7 0.0 collective-permute-done.4.recv_ref
  19.8 0.0 collective-permute-done.8.refs_2_.w_oth_ref
  19.8 0.3 layer_two.12
  20.2 0.0 collective-permute-done.9.refs_0_
  20.2 0.3 layer_two.13
  20.5 0.3 layer_two.14
  20.9 0.0 collective-permute-done.7.refs_0_
  20.9 0.3 layer_two.15
  21.2 1.6 %collective-permute-done.3.x_ref.refs_0_ = bf16[128,768]{1,0:T(8,128)(2,1)S(1)} collective-permute-done((bf16[128,768]{1,0:T(8,128)(2,1)S(1)}, bf16[128,768]{1,0:T(8,128)(2,1)S(1)}, u32[]{:S(2)}, u32[]{:S(2)}) %collective-permute-start.3) | collective-permute-done | bytes 196640 | tf_op jit(solution)/shard_map/hop/ppermute | solution.py:26
  22.9 0.0 collective-permute-start.11
  22.9 0.4 %layer_two.16 = (f32[128,512]{1,0:T(8,128)S(1)}, bf16[128,512]{1,0:T(8,128)(2,1)S(1)}) custom-call(bf16[128,768]{1,0:T(8,128)(2,1)S(1)} %collective-permute-done.3.x_ref.refs_0_, bf16[2048,1024]{1,0:T(8,128)(2,1)S(1)} %copy-done, f32[128,1024]{1,0:T(8,128)S(1)} %layer_two.11.embed_ref), custom_call_target="tpu_custom_call" | custom-call | tf_op jit(solution)/shard_map/layer_two/pallas_call | solution.py:73
  23.2 0.6 %collective-permute-start.10 = (bf16[128,512]{1,0:T(8,128)(2,1)S(1)}, bf16[128,512]{1,0:T(8,128)(2,1)S(1)}, u32[]{:S(2)}, u32[]{:S(2)}) collective-permute-start(bf16[128,512]{1,0:T(8,128)(2,1)S(1)} %get-tuple-element.55), channel_id=1, source_target_pairs={{0,1},{1,0},{2,3},{3,2},{4,5},{5,4},{6,7},{7,6},{8,9},{9,8},{10,11... | collective-permute-start | bytes 393224 | tf_op jit(solution)/shard_map/layer_two/ppermute | solution.py:31
  23.8 0.3 layer_two.17
  24.2 0.1 collective-permute-done.11.x_ref
  24.3 0.7 %layer_two.18.mixed_ref = bf16[128,256]{1,0:T(8,128)(2,1)S(1)} custom-call(s32[128,128]{1,0:T(8,128)S(1)} %get-tuple-element.40.live_ref, bf16[128,768]{1,0:T(8,128)(2,1)S(1)} %collective-permute-done.11.x_ref, bf16[4096,384]{1,0:T(8,128)(2,1)S(1)} %get-tuple-element.43.w_ref.refs_1_.w_own_ref, ...), custom_call_target="tpu_custom_call" | custom-call | tf_op jit(solution)/shard_map/layer_two/pallas_call | solution.py:73
  25.0 0.0 collective-permute-done.10.recv_ref
  25.0 0.2 layer_two.19.refs_0_.refs_1_
  25.2 2.5 %collective-permute-start.15 = (bf16[128,512]{1,0:T(8,128)(2,1)S(1)}, bf16[128,512]{1,0:T(8,128)(2,1)S(1)}, u32[]{:S(2)}, u32[]{:S(2)}) collective-permute-start(bf16[128,512]{1,0:T(8,128)(2,1)S(1)} %layer_two.19.refs_0_.refs_1_), channel_id=1, source_target_pairs={{0,6},{2,4},{4,2},{6,0},{1,7},{3,5},{5,3},{7,1},{8,14},{10,12},{12... | collective-permute-start | bytes 393224 | tf_op jit(solution)/shard_map/moments/ppermute | solution.py:31
  27.7 0.5 %collective-permute-start.13 = (bf16[128,512]{1,0:T(8,128)(2,1)S(1)}, bf16[128,512]{1,0:T(8,128)(2,1)S(1)}, u32[]{:S(2)}, u32[]{:S(2)}) collective-permute-start(bf16[128,512]{1,0:T(8,128)(2,1)S(1)} %layer_two.19.refs_0_.refs_1_), channel_id=1, source_target_pairs={{0,2},{2,0},{4,6},{6,4},{1,3},{3,1},{5,7},{7,5},{8,10},{10,8},{12,... | collective-permute-start | bytes 393224 | tf_op jit(solution)/shard_map/moments/ppermute | solution.py:31
  28.3 0.5 %collective-permute-start.12 = (bf16[128,512]{1,0:T(8,128)(2,1)S(1)}, bf16[128,512]{1,0:T(8,128)(2,1)S(1)}, u32[]{:S(2)}, u32[]{:S(2)}) collective-permute-start(bf16[128,512]{1,0:T(8,128)(2,1)S(1)} %layer_two.19.refs_0_.refs_1_), channel_id=1, source_target_pairs={{0,4},{2,6},{4,0},{6,2},{1,5},{3,7},{5,1},{7,3},{8,12},{10,14},{12... | collective-permute-start | bytes 393224 | tf_op jit(solution)/shard_map/moments/ppermute | solution.py:31
  28.8 3.8 %collective-permute-done.15.refs_2_.refs_1_ = bf16[128,512]{1,0:T(8,128)(2,1)S(1)} collective-permute-done((bf16[128,512]{1,0:T(8,128)(2,1)S(1)}, bf16[128,512]{1,0:T(8,128)(2,1)S(1)}, u32[]{:S(2)}, u32[]{:S(2)}) %collective-permute-start.15) | collective-permute-done | bytes 131104 | tf_op jit(solution)/shard_map/moments/ppermute | solution.py:31
  32.5 0.2 moments.5.gram_own_ref
  32.8 0.1 collective-permute-start.16
  32.8 1.8 %collective-permute-done.13.refs_2_.refs_1_ = bf16[128,512]{1,0:T(8,128)(2,1)S(1)} collective-permute-done((bf16[128,512]{1,0:T(8,128)(2,1)S(1)}, bf16[128,512]{1,0:T(8,128)(2,1)S(1)}, u32[]{:S(2)}, u32[]{:S(2)}) %collective-permute-start.13) | collective-permute-done | bytes 131104 | tf_op jit(solution)/shard_map/moments/ppermute | solution.py:31
  34.6 0.0 collective-permute-done.12.refs_1_.refs_0_
  34.6 0.2 moments.4.gram_own_ref
  34.8 0.1 collective-permute-start.14
  34.9 0.0 collective-permute-done.16.gram_oth_ref
  34.9 0.2 moments.6.refs_2_
  35.1 1.0 %collective-permute-done.14.gram_oth_ref = bf16[128,256]{1,0:T(8,128)(2,1)S(1)} collective-permute-done((bf16[128,256]{1,0:T(8,128)(2,1)S(1)}, bf16[128,256]{1,0:T(8,128)(2,1)S(1)}, u32[]{:S(2)}, u32[]{:S(2)}) %collective-permute-start.14) | collective-permute-done | bytes 65568 | tf_op jit(solution)/shard_map/moments/ppermute | solution.py:31
  36.2 0.9 %moments.7 = f32[128,512]{1,0:T(8,128)} custom-call(bf16[128,256]{1,0:T(8,128)(2,1)S(1)} %moments.4.gram_own_ref, bf16[128,256]{1,0:T(8,128)(2,1)S(1)} %collective-permute-done.14.gram_oth_ref, bf16[128,512]{1,0:T(8,128)(2,1)S(1)} %collective-permute-done.12.refs_1_.refs_0_, bf16[128,512]{1,0:T(8,128)(2,1)S(1)} %collective-permute-done.13.refs_2_.refs_1_, ...), custom_call_target="tpu_custom_call" | custom-call | tf_op jit(solution)/shard_map/moments/pallas_call | solution.py:73
  (1 shorter events, 0.0 us)
Async XLA Ops:
  0.0 2.8 %collective-permute-start = (bf16[128,2048]{1,0:T(8,128)(2,1)}, bf16[128,2048]{1,0:T(8,128)(2,1)S(1)}, u32[]{:S(2)}, u32[]{:S(2)}) collective-permute-start(bf16[128,2048]{1,0:T(8,128)(2,1)} %bitcast.5), channel_id=1, source_target_pairs={{0,1},{1,0},{2,3},{3,2},{4,5},{5,4},{6,7},{7,6},{8,9},{9,8},{10,11... | collective-permute-start | bytes 1572872 | tf_op jit(solution)/shard_map/layer_one/ppermute | solution.py:31
  2.7 2.3 %copy-start.1 = (bf16[1,128,4096]{2,1,0:T(8,128)(2,1)S(1)}, bf16[1,128,4096]{2,1,0:T(8,128)(2,1)}, u32[]{:S(2)}) copy-start(bf16[1,128,4096]{2,1,0:T(8,128)(2,1)} %w_own_ref.7) | copy-start | bytes 3145732
  2.7 2.0 %collective-permute-start.2 = (bf16[128,2048]{1,0:T(8,128)(2,1)S(1)}, bf16[128,2048]{1,0:T(8,128)(2,1)S(1)}, u32[]{:S(2)}, u32[]{:S(2)}) collective-permute-start(bf16[128,2048]{1,0:T(8,128)(2,1)S(1)} %get-tuple-element.38), channel_id=1, source_target_pairs={{0,1},{1,0},{2,3},{3,2},{4,5},{5,4},{6,7},{7,6},{8,9},{9,8},{10,11... | collective-permute-start | bytes 1572872 | tf_op jit(solution)/shard_map/layer_one/ppermute | solution.py:31
  3.6 6.6 %copy-start = (bf16[2048,1024]{1,0:T(8,128)(2,1)S(1)}, bf16[2048,1024]{1,0:T(8,128)(2,1)}, u32[]{:S(2)}) copy-start(bf16[2048,1024]{1,0:T(8,128)(2,1)} %e_ref.3) | copy-start | bytes 12582916
  3.6 6.6 %copy-start.2 = (s32[4,1]{0,1:T(1,128)S(1)}, s32[4,1]{0,1:T(1,128)}, u32[]{:S(2)}) copy-start(s32[4,1]{0,1:T(1,128)} %param.8) | copy-start | bytes 52
  3.6 1.4 %collective-permute-start.1 = (bf16[128,128]{1,0:T(8,128)(2,1)S(1)}, bf16[128,128]{1,0:T(8,128)(2,1)S(1)}, u32[]{:S(2)}, u32[]{:S(2)}) collective-permute-start(bf16[128,128]{1,0:T(8,128)(2,1)S(1)} %layer_one.6.mix_own_ref), channel_id=1, source_target_pairs={{0,1},{1,0},{2,3},{3,2},{4,5},{5,4},{6,7},{7,6},{8,9},{9,8},{10,11... | collective-permute-start | bytes 98312 | tf_op jit(solution)/shard_map/layer_one/ppermute | solution.py:31
  5.2 14.6 %collective-permute-start.8 = (bf16[4096,384]{1,0:T(8,128)(2,1)S(1)}, bf16[4096,384]{1,0:T(8,128)(2,1)S(1)}, u32[]{:S(2)}, u32[]{:S(2)}) collective-permute-start(bf16[4096,384]{1,0:T(8,128)(2,1)S(1)} %get-tuple-element.43.w_ref.refs_1_.w_own_ref), channel_id=1, source_target_pairs={{0,1},{1,0},{2,3},{3,2},{4,5},{5,4},{6,7},{7,6},{8,9},{9,8},{10,11... | collective-permute-start | bytes 9437192 | tf_op jit(solution)/shard_map/weights/ppermute | solution.py:31
  5.7 9.8 %collective-permute-start.6 = (bf16[128,640]{1,0:T(8,128)(2,1)S(1)}, bf16[128,640]{1,0:T(8,128)(2,1)S(1)}, u32[]{:S(2)}, u32[]{:S(2)}) collective-permute-start(bf16[128,640]{1,0:T(8,128)(2,1)S(1)} %layer_one.7), channel_id=1, source_target_pairs={{0,8},{8,16},{16,24},{24,0},{1,9},{9,17},{17,25},{25,1},{2,10},{10... | collective-permute-start | bytes 491528 | tf_op jit(solution)/shard_map/hop/ppermute | solution.py:26
  8.6 10.4 %collective-permute-start.5 = (bf16[128,640]{1,0:T(8,128)(2,1)S(1)}, bf16[128,640]{1,0:T(8,128)(2,1)S(1)}, u32[]{:S(2)}, u32[]{:S(2)}) collective-permute-start(bf16[128,640]{1,0:T(8,128)(2,1)S(1)} %layer_one.9), channel_id=1, source_target_pairs={{0,8},{8,16},{16,24},{24,0},{1,9},{9,17},{17,25},{25,1},{2,10},{10... | collective-permute-start | bytes 491528 | tf_op jit(solution)/shard_map/hop/ppermute | solution.py:26
  12.1 7.7 %collective-permute-start.4 = (bf16[256,512]{1,0:T(8,128)(2,1)S(1)}, bf16[256,512]{1,0:T(8,128)(2,1)S(1)}, u32[]{:S(2)}, u32[]{:S(2)}) collective-permute-start(bf16[256,512]{1,0:T(8,128)(2,1)S(1)} %get-tuple-element.42), channel_id=1, source_target_pairs={{0,1},{1,0},{2,3},{3,2},{4,5},{5,4},{6,7},{7,6},{8,9},{9,8},{10,11... | collective-permute-start | bytes 786440 | tf_op jit(solution)/shard_map/weights/ppermute | solution.py:31
  12.4 10.5 %collective-permute-start.3 = (bf16[128,768]{1,0:T(8,128)(2,1)S(1)}, bf16[128,768]{1,0:T(8,128)(2,1)S(1)}, u32[]{:S(2)}, u32[]{:S(2)}) collective-permute-start(bf16[128,768]{1,0:T(8,128)(2,1)S(1)} %layer_one.8), channel_id=1, source_target_pairs={{0,8},{8,16},{16,24},{24,0},{1,9},{9,17},{17,25},{25,1},{2,10},{10... | collective-permute-start | bytes 589832 | tf_op jit(solution)/shard_map/hop/ppermute | solution.py:26
  15.5 4.7 %collective-permute-start.9 = (bf16[128,640]{1,0:T(8,128)(2,1)S(1)}, bf16[128,640]{1,0:T(8,128)(2,1)S(1)}, u32[]{:S(2)}, u32[]{:S(2)}) collective-permute-start(bf16[128,640]{1,0:T(8,128)(2,1)S(1)} %collective-permute-done.6.x_ref.refs_0_), channel_id=1, source_target_pairs={{0,1},{1,0},{2,3},{3,2},{4,5},{5,4},{6,7},{7,6},{8,9},{9,8},{10,11... | collective-permute-start | bytes 491528 | tf_op jit(solution)/shard_map/layer_two/ppermute | solution.py:31
  19.0 1.9 %collective-permute-start.7 = (bf16[128,640]{1,0:T(8,128)(2,1)S(1)}, bf16[128,640]{1,0:T(8,128)(2,1)S(1)}, u32[]{:S(2)}, u32[]{:S(2)}) collective-permute-start(bf16[128,640]{1,0:T(8,128)(2,1)S(1)} %collective-permute-done.5.x_ref.refs_0_), channel_id=1, source_target_pairs={{0,1},{1,0},{2,3},{3,2},{4,5},{5,4},{6,7},{7,6},{8,9},{9,8},{10,11... | collective-permute-start | bytes 491528 | tf_op jit(solution)/shard_map/layer_two/ppermute | solution.py:31
  22.9 1.4 %collective-permute-start.11 = (bf16[128,768]{1,0:T(8,128)(2,1)S(1)}, bf16[128,768]{1,0:T(8,128)(2,1)S(1)}, u32[]{:S(2)}, u32[]{:S(2)}) collective-permute-start(bf16[128,768]{1,0:T(8,128)(2,1)S(1)} %collective-permute-done.3.x_ref.refs_0_), channel_id=1, source_target_pairs={{0,1},{1,0},{2,3},{3,2},{4,5},{5,4},{6,7},{7,6},{8,9},{9,8},{10,11... | collective-permute-start | bytes 589832 | tf_op jit(solution)/shard_map/layer_two/ppermute | solution.py:31
  23.2 1.8 %collective-permute-start.10 = (bf16[128,512]{1,0:T(8,128)(2,1)S(1)}, bf16[128,512]{1,0:T(8,128)(2,1)S(1)}, u32[]{:S(2)}, u32[]{:S(2)}) collective-permute-start(bf16[128,512]{1,0:T(8,128)(2,1)S(1)} %get-tuple-element.55), channel_id=1, source_target_pairs={{0,1},{1,0},{2,3},{3,2},{4,5},{5,4},{6,7},{7,6},{8,9},{9,8},{10,11... | collective-permute-start | bytes 393224 | tf_op jit(solution)/shard_map/layer_two/ppermute | solution.py:31
  25.2 7.3 %collective-permute-start.15 = (bf16[128,512]{1,0:T(8,128)(2,1)S(1)}, bf16[128,512]{1,0:T(8,128)(2,1)S(1)}, u32[]{:S(2)}, u32[]{:S(2)}) collective-permute-start(bf16[128,512]{1,0:T(8,128)(2,1)S(1)} %layer_two.19.refs_0_.refs_1_), channel_id=1, source_target_pairs={{0,6},{2,4},{4,2},{6,0},{1,7},{3,5},{5,3},{7,1},{8,14},{10,12},{12... | collective-permute-start | bytes 393224 | tf_op jit(solution)/shard_map/moments/ppermute | solution.py:31
  27.7 6.9 %collective-permute-start.13 = (bf16[128,512]{1,0:T(8,128)(2,1)S(1)}, bf16[128,512]{1,0:T(8,128)(2,1)S(1)}, u32[]{:S(2)}, u32[]{:S(2)}) collective-permute-start(bf16[128,512]{1,0:T(8,128)(2,1)S(1)} %layer_two.19.refs_0_.refs_1_), channel_id=1, source_target_pairs={{0,2},{2,0},{4,6},{6,4},{1,3},{3,1},{5,7},{7,5},{8,10},{10,8},{12,... | collective-permute-start | bytes 393224 | tf_op jit(solution)/shard_map/moments/ppermute | solution.py:31
  28.3 6.3 %collective-permute-start.12 = (bf16[128,512]{1,0:T(8,128)(2,1)S(1)}, bf16[128,512]{1,0:T(8,128)(2,1)S(1)}, u32[]{:S(2)}, u32[]{:S(2)}) collective-permute-start(bf16[128,512]{1,0:T(8,128)(2,1)S(1)} %layer_two.19.refs_0_.refs_1_), channel_id=1, source_target_pairs={{0,4},{2,6},{4,0},{6,2},{1,5},{3,7},{5,1},{7,3},{8,12},{10,14},{12... | collective-permute-start | bytes 393224 | tf_op jit(solution)/shard_map/moments/ppermute | solution.py:31
  32.8 2.2 %collective-permute-start.16 = (f32[128,256]{1,0:T(8,128)S(1)}, f32[128,256]{1,0:T(8,128)S(1)}, u32[]{:S(2)}, u32[]{:S(2)}) collective-permute-start(f32[128,256]{1,0:T(8,128)S(1)} %moments.5.gram_own_ref), channel_id=1, source_target_pairs={{0,1},{1,0},{2,3},{3,2},{4,5},{5,4},{6,7},{7,6},{8,9},{9,8},{10,11... | collective-permute-start | bytes 393224 | tf_op jit(solution)/shard_map/moments/ppermute | solution.py:31
  34.8 1.3 %collective-permute-start.14 = (bf16[128,256]{1,0:T(8,128)(2,1)S(1)}, bf16[128,256]{1,0:T(8,128)(2,1)S(1)}, u32[]{:S(2)}, u32[]{:S(2)}) collective-permute-start(bf16[128,256]{1,0:T(8,128)(2,1)S(1)} %moments.4.gram_own_ref), channel_id=1, source_target_pairs={{0,1},{1,0},{2,3},{3,2},{4,5},{5,4},{6,7},{7,6},{8,9},{9,8},{10,11... | collective-permute-start | bytes 196616 | tf_op jit(solution)/shard_map/moments/ppermute | solution.py:31

commit v11 on v10

--- a/solution.py
+++ b/solution.py
@@ -149,15 +149,17 @@
     mixed_ref[...] = softmax_mix([qkv * scale], live_ref[...])
 
 
-def update_body(lower, own_ref, mix_own_ref, mix_oth_ref, w_own_ref, *refs):
-    w_oth_refs, out_ref = refs[:-1], refs[-1]
+def held_body(own_ref, mixed_ref, w_ref, held_ref):
+    half = own_ref.shape[1]
+    weight = w_ref[0, :, span(lax.axis_index("tensor") * half, half)]
+    held_ref[...] = own_ref[...].astype(F32) + dot(mixed_ref[...], weight)
+
+
+def update_body(lower, held_ref, mixed_ref, *refs):
+    w_refs, out_ref = refs[:-1], refs[-1]
     cols = slice(lower, lower + out_ref.shape[1])
-    w_oth = jnp.concatenate([ref[...] for ref in w_oth_refs], axis=1)
-    start = lax.axis_index("tensor") * own_ref.shape[1] + lower
-    w_own = w_own_ref[0, :, pl.ds(pl.multiple_of(start, HD), out_ref.shape[1])]
-    weight = jnp.concatenate([w_own, w_oth[:, cols]], axis=0)
-    mixed = jnp.concatenate([mix_own_ref[...], mix_oth_ref[...]], axis=1)
-    out_ref[...] = (own_ref[:, cols].astype(F32) + dot(mixed, weight)).astype(BF16)
+    weight = jnp.concatenate([ref[...] for ref in w_refs], axis=1)
+    out_ref[...] = (held_ref[:, cols] + dot(mixed_ref[...], weight[:, cols])).astype(BF16)
 
 
 def combine_body(lens_ref, w_own_ref, e_ref, *refs):
@@ -307,9 +309,10 @@
         wo_oth = [exchanged(part, "tensor", 1) for part in wo_send]
         mixed = call(first_body, shape(rows, HD), "vvvvv")(live, oth, w_own, qkv, square)
         mixed_oth = exchanged(mixed, "tensor", 1)
+        held = call(held_body, shape(rows, half, dtype=F32), "vvv")(own, mixed, w_out)
         state = [
-            call(functools.partial(update_body, lower), shape(rows, width), "v" * (4 + WO_PARTS))(
-                own, mixed, mixed_oth, w_out, *wo_oth
+            call(functools.partial(update_body, lower), shape(rows, width), "v" * (2 + WO_PARTS))(
+                held, mixed_oth, *wo_oth
             )
             for lower, width in zip(lowers, widths)
         ]

time: 37.2 us -> 37.2 us (level)
    pallas_call x21 -> x22, Pallas kernels: 10.8 us -> 11 us  [call(): return lambda *operands: kernel(*map(place, operands, spaces))]
where the time goes in v11:
time: 37.2 us; the launch traced here: 37 us
  waiting for transfers between devices  13.9 us (37%)
  starting transfers between devices  11.9 us (32%)
  Pallas kernels  11 us (30%)
    pallas_call x22, Pallas kernels, call(): return lambda *operands: kernel(*map(place, operands, spaces))  11 us
    ppermute x14, waiting for transfers between devices, exchanged(): lax.ppermute(value, axis, [(source, source ^ mask) for source in range(co...  7.27 us
    ppermute x3, waiting for transfers between devices, shifted(): return lax.ppermute(value, axis, pairs)  6.68 us
    ppermute x3, starting transfers between devices, shifted(): return lax.ppermute(value, axis, pairs)  5.99 us
    ppermute x14, starting transfers between devices, exchanged(): lax.ppermute(value, axis, [(source, source ^ mask) for source in range(co...  5.86 us
  transfers between devices with their start and end apart: 17, of which 9 were waited for; matrix products, arithmetic and copies ran while one was open for 0% of the time, Pallas kernels for 26%

profile of v11, /device:TPU:0, one launch (start us, length us, event | category | flops | bytes accessed | tf_op | source)
XLA Modules:
  0.0 37.0 jit_solution(11913609662791998578)
XLA Ops:
  0.0 0.5 %collective-permute-start = (bf16[128,2048]{1,0:T(8,128)(2,1)}, bf16[128,2048]{1,0:T(8,128)(2,1)S(1)}, u32[]{:S(2)}, u32[]{:S(2)}) collective-permute-start(bf16[128,2048]{1,0:T(8,128)(2,1)} %bitcast.5), channel_id=1, source_target_pairs={{0,1},{1,0},{2,3},{3,2},{4,5},{5,4},{6,7},{7,6},{8,9},{9,8},{10,11... | collective-permute-start | bytes 1572872 | tf_op jit(solution)/shard_map/layer_one/ppermute | solution.py:31
  0.5 2.2 %layer_one.6 = (bf16[128,2048]{1,0:T(8,128)(2,1)S(1)}, bf16[4096,384]{1,0:T(8,128)(2,1)S(1)}, f32[128,384]{1,0:T(8,128)S(1)}, f32[128,128]{1,0:T(8,128)S(1)}, s3...) custom-call(s32[4]{0:T(128)} %bitcast.3, bf16[1,128,2048]{2,1,0:T(8,128)(2,1)} %own_hbm.1, ...), custom_call_target="tpu_custom_call" | custom-call | tf_op jit(solution)/shard_map/layer_one/pallas_call | solution.py:73
  2.7 0.0 copy-start.1
  2.7 0.1 collective-permute-start.2
  2.8 0.0 collective-permute-done.oth_ref
  2.8 0.8 %layer_one.7.mixed_ref = bf16[128,128]{1,0:T(8,128)(2,1)S(1)} custom-call(s32[128,128]{1,0:T(8,128)S(1)} %get-tuple-element.34.live_ref, bf16[128,2048]{1,0:T(8,128)(2,1)S(1)} %collective-permute-done.oth_ref, bf16[4096,384]{1,0:T(8,128)(2,1)S(1)} %get-tuple-element.43.w_ref.refs_1_.w_own_ref, f32[128,384]{1,0:T(8,128)S(1)} %get-tuple-element.36.qkv_ref, ...), custom_call_target="tpu_custom_call" | custom-call | tf_op jit(solution)/shard_map/layer_one/pallas_call | solution.py:73
  3.6 0.0 copy-start
  3.6 0.0 copy-start.2
  3.6 0.5 %collective-permute-start.1 = (bf16[128,128]{1,0:T(8,128)(2,1)S(1)}, bf16[128,128]{1,0:T(8,128)(2,1)S(1)}, u32[]{:S(2)}, u32[]{:S(2)}) collective-permute-start(bf16[128,128]{1,0:T(8,128)(2,1)S(1)} %layer_one.7.mixed_ref), channel_id=1, source_target_pairs={{0,1},{1,0},{2,3},{3,2},{4,5},{5,4},{6,7},{7,6},{8,9},{9,8},{10,11... | collective-permute-start | bytes 98312 | tf_op jit(solution)/shard_map/layer_one/ppermute | solution.py:31
  4.2 0.0 copy-done.1
  4.2 0.3 layer_one.8.held_ref
  4.5 0.2 collective-permute-done.2.refs_0_
  4.7 0.3 collective-permute-done.1.mixed_ref
  5.0 0.2 layer_one.9
  5.2 0.4 %collective-permute-start.8 = (bf16[4096,384]{1,0:T(8,128)(2,1)S(1)}, bf16[4096,384]{1,0:T(8,128)(2,1)S(1)}, u32[]{:S(2)}, u32[]{:S(2)}) collective-permute-start(bf16[4096,384]{1,0:T(8,128)(2,1)S(1)} %get-tuple-element.43.w_ref.refs_1_.w_own_ref), channel_id=1, source_target_pairs={{0,1},{1,0},{2,3},{3,2},{4,5},{5,4},{6,7},{7,6},{8,9},{9,8},{10,11... | collective-permute-start | bytes 9437192 | tf_op jit(solution)/shard_map/weights/ppermute | solution.py:31
  5.6 2.7 %collective-permute-start.6 = (bf16[128,640]{1,0:T(8,128)(2,1)S(1)}, bf16[128,640]{1,0:T(8,128)(2,1)S(1)}, u32[]{:S(2)}, u32[]{:S(2)}) collective-permute-start(bf16[128,640]{1,0:T(8,128)(2,1)S(1)} %layer_one.9), channel_id=1, source_target_pairs={{0,8},{8,16},{16,24},{24,0},{1,9},{9,17},{17,25},{25,1},{2,10},{10... | collective-permute-start | bytes 491528 | tf_op jit(solution)/shard_map/hop/ppermute | solution.py:26
  8.4 0.2 layer_one.11
  8.5 1.6 %collective-permute-start.5 = (bf16[128,640]{1,0:T(8,128)(2,1)S(1)}, bf16[128,640]{1,0:T(8,128)(2,1)S(1)}, u32[]{:S(2)}, u32[]{:S(2)}) collective-permute-start(bf16[128,640]{1,0:T(8,128)(2,1)S(1)} %layer_one.11), channel_id=1, source_target_pairs={{0,8},{8,16},{16,24},{24,0},{1,9},{9,17},{17,25},{25,1},{2,10},{10... | collective-permute-start | bytes 491528 | tf_op jit(solution)/shard_map/hop/ppermute | solution.py:26
  10.2 0.0 copy-done
  10.2 0.0 copy-done.2
  10.2 1.8 %weights.2 = (f32[256,512]{1,0:T(8,128)S(1)}, bf16[256,512]{1,0:T(8,128)(2,1)S(1)}, s32[128,128]{1,0:T(8,128)S(1)}) custom-call(s32[4]{0:T(128)S(1)} %bitcast.4, bf16[1,128,4096]{2,1,0:T(8,128)(2,1)S(1)} %copy-done.1, bf16[2048,1024]{1,0:T(8,128)(2,1)S(1)} %copy-done, bf16[128,2048]{1,0:T(8,128)(2,1)S(1)} %collective-permute-done.2.refs_0_), custom_call_target="tpu_custom_call" | custom-call | tf_op jit(solution)/shard_map/weights/pallas_call | solution.py:73
  12.0 0.1 collective-permute-start.4
  12.1 0.2 layer_one.10
  12.3 1.6 %collective-permute-start.3 = (bf16[128,768]{1,0:T(8,128)(2,1)S(1)}, bf16[128,768]{1,0:T(8,128)(2,1)S(1)}, u32[]{:S(2)}, u32[]{:S(2)}) collective-permute-start(bf16[128,768]{1,0:T(8,128)(2,1)S(1)} %layer_one.10), channel_id=1, source_target_pairs={{0,8},{8,16},{16,24},{24,0},{1,9},{9,17},{17,25},{25,1},{2,10},{10... | collective-permute-start | bytes 589832 | tf_op jit(solution)/shard_map/hop/ppermute | solution.py:26
  13.9 1.5 %collective-permute-done.6.x_ref.refs_0_ = bf16[128,640]{1,0:T(8,128)(2,1)S(1)} collective-permute-done((bf16[128,640]{1,0:T(8,128)(2,1)S(1)}, bf16[128,640]{1,0:T(8,128)(2,1)S(1)}, u32[]{:S(2)}, u32[]{:S(2)}) %collective-permute-start.6) | collective-permute-done | bytes 163872 | tf_op jit(solution)/shard_map/hop/ppermute | solution.py:26
  15.4 0.0 collective-permute-start.9
  15.4 3.5 %collective-permute-done.5.x_ref.refs_0_ = bf16[128,640]{1,0:T(8,128)(2,1)S(1)} collective-permute-done((bf16[128,640]{1,0:T(8,128)(2,1)S(1)}, bf16[128,640]{1,0:T(8,128)(2,1)S(1)}, u32[]{:S(2)}, u32[]{:S(2)}) %collective-permute-start.5) | collective-permute-done | bytes 163872 | tf_op jit(solution)/shard_map/hop/ppermute | solution.py:26
  18.9 0.0 collective-permute-start.7
  18.9 0.4 layer_two.10.refs_0_
  19.3 0.4 %layer_two.11.embed_ref = f32[128,1024]{1,0:T(8,128)S(1)} custom-call(bf16[128,640]{1,0:T(8,128)(2,1)S(1)} %collective-permute-done.5.x_ref.refs_0_, bf16[2048,1024]{1,0:T(8,128)(2,1)S(1)} %copy-done, f32[128,1024]{1,0:T(8,128)S(1)} %layer_two.10.refs_0_), custom_call_target="tpu_custom_call" | custom-call | tf_op jit(solution)/shard_map/layer_two/pallas_call | solution.py:73
  19.7 0.0 collective-permute-done.4.recv_ref
  19.8 0.0 collective-permute-done.8.refs_2_.w_oth_ref
  19.8 0.3 layer_two.12
  20.1 0.0 collective-permute-done.9.refs_0_
  20.1 0.3 layer_two.13
  20.5 0.3 layer_two.14
  20.8 0.0 collective-permute-done.7.refs_0_
  20.8 0.3 layer_two.15
  21.2 1.6 %collective-permute-done.3.x_ref.refs_0_ = bf16[128,768]{1,0:T(8,128)(2,1)S(1)} collective-permute-done((bf16[128,768]{1,0:T(8,128)(2,1)S(1)}, bf16[128,768]{1,0:T(8,128)(2,1)S(1)}, u32[]{:S(2)}, u32[]{:S(2)}) %collective-permute-start.3) | collective-permute-done | bytes 196640 | tf_op jit(solution)/shard_map/hop/ppermute | solution.py:26
  22.8 0.0 collective-permute-start.11
  22.8 0.4 %layer_two.16 = (f32[128,512]{1,0:T(8,128)S(1)}, bf16[128,512]{1,0:T(8,128)(2,1)S(1)}) custom-call(bf16[128,768]{1,0:T(8,128)(2,1)S(1)} %collective-permute-done.3.x_ref.refs_0_, bf16[2048,1024]{1,0:T(8,128)(2,1)S(1)} %copy-done, f32[128,1024]{1,0:T(8,128)S(1)} %layer_two.11.embed_ref), custom_call_target="tpu_custom_call" | custom-call | tf_op jit(solution)/shard_map/layer_two/pallas_call | solution.py:73
  23.2 0.6 %collective-permute-start.10 = (bf16[128,512]{1,0:T(8,128)(2,1)S(1)}, bf16[128,512]{1,0:T(8,128)(2,1)S(1)}, u32[]{:S(2)}, u32[]{:S(2)}) collective-permute-start(bf16[128,512]{1,0:T(8,128)(2,1)S(1)} %get-tuple-element.55), channel_id=1, source_target_pairs={{0,1},{1,0},{2,3},{3,2},{4,5},{5,4},{6,7},{7,6},{8,9},{9,8},{10,11... | collective-permute-start | bytes 393224 | tf_op jit(solution)/shard_map/layer_two/ppermute | solution.py:31
  23.8 0.3 layer_two.17
  24.1 0.1 collective-permute-done.11.x_ref
  24.3 0.7 %layer_two.18.mixed_ref = bf16[128,256]{1,0:T(8,128)(2,1)S(1)} custom-call(s32[128,128]{1,0:T(8,128)S(1)} %get-tuple-element.40.live_ref, bf16[128,768]{1,0:T(8,128)(2,1)S(1)} %collective-permute-done.11.x_ref, bf16[4096,384]{1,0:T(8,128)(2,1)S(1)} %get-tuple-element.43.w_ref.refs_1_.w_own_ref, ...), custom_call_target="tpu_custom_call" | custom-call | tf_op jit(solution)/shard_map/layer_two/pallas_call | solution.py:73
  25.0 0.0 collective-permute-done.10.recv_ref
  25.0 0.2 layer_two.19.refs_0_.refs_1_
  25.2 2.5 %collective-permute-start.15 = (bf16[128,512]{1,0:T(8,128)(2,1)S(1)}, bf16[128,512]{1,0:T(8,128)(2,1)S(1)}, u32[]{:S(2)}, u32[]{:S(2)}) collective-permute-start(bf16[128,512]{1,0:T(8,128)(2,1)S(1)} %layer_two.19.refs_0_.refs_1_), channel_id=1, source_target_pairs={{0,6},{2,4},{4,2},{6,0},{1,7},{3,5},{5,3},{7,1},{8,14},{10,12},{12... | collective-permute-start | bytes 393224 | tf_op jit(solution)/shard_map/moments/ppermute | solution.py:31
  27.7 0.5 %collective-permute-start.13 = (bf16[128,512]{1,0:T(8,128)(2,1)S(1)}, bf16[128,512]{1,0:T(8,128)(2,1)S(1)}, u32[]{:S(2)}, u32[]{:S(2)}) collective-permute-start(bf16[128,512]{1,0:T(8,128)(2,1)S(1)} %layer_two.19.refs_0_.refs_1_), channel_id=1, source_target_pairs={{0,2},{2,0},{4,6},{6,4},{1,3},{3,1},{5,7},{7,5},{8,10},{10,8},{12,... | collective-permute-start | bytes 393224 | tf_op jit(solution)/shard_map/moments/ppermute | solution.py:31
  28.2 0.5 %collective-permute-start.12 = (bf16[128,512]{1,0:T(8,128)(2,1)S(1)}, bf16[128,512]{1,0:T(8,128)(2,1)S(1)}, u32[]{:S(2)}, u32[]{:S(2)}) collective-permute-start(bf16[128,512]{1,0:T(8,128)(2,1)S(1)} %layer_two.19.refs_0_.refs_1_), channel_id=1, source_target_pairs={{0,4},{2,6},{4,0},{6,2},{1,5},{3,7},{5,1},{7,3},{8,12},{10,14},{12... | collective-permute-start | bytes 393224 | tf_op jit(solution)/shard_map/moments/ppermute | solution.py:31
  28.8 3.8 %collective-permute-done.15.refs_2_.refs_1_ = bf16[128,512]{1,0:T(8,128)(2,1)S(1)} collective-permute-done((bf16[128,512]{1,0:T(8,128)(2,1)S(1)}, bf16[128,512]{1,0:T(8,128)(2,1)S(1)}, u32[]{:S(2)}, u32[]{:S(2)}) %collective-permute-start.15) | collective-permute-done | bytes 131104 | tf_op jit(solution)/shard_map/moments/ppermute | solution.py:31
  32.5 0.2 moments.5.gram_own_ref
  32.7 0.1 collective-permute-start.16
  32.8 1.8 %collective-permute-done.13.refs_2_.refs_1_ = bf16[128,512]{1,0:T(8,128)(2,1)S(1)} collective-permute-done((bf16[128,512]{1,0:T(8,128)(2,1)S(1)}, bf16[128,512]{1,0:T(8,128)(2,1)S(1)}, u32[]{:S(2)}, u32[]{:S(2)}) %collective-permute-start.13) | collective-permute-done | bytes 131104 | tf_op jit(solution)/shard_map/moments/ppermute | solution.py:31
  34.6 0.0 collective-permute-done.12.refs_1_.refs_0_
  34.6 0.2 moments.4.gram_own_ref
  34.8 0.1 collective-permute-start.14
  34.9 0.0 collective-permute-done.16.gram_oth_ref
  34.9 0.2 moments.6.refs_2_
  35.1 1.0 %collective-permute-done.14.gram_oth_ref = bf16[128,256]{1,0:T(8,128)(2,1)S(1)} collective-permute-done((bf16[128,256]{1,0:T(8,128)(2,1)S(1)}, bf16[128,256]{1,0:T(8,128)(2,1)S(1)}, u32[]{:S(2)}, u32[]{:S(2)}) %collective-permute-start.14) | collective-permute-done | bytes 65568 | tf_op jit(solution)/shard_map/moments/ppermute | solution.py:31
  36.1 0.9 %moments.7 = f32[128,512]{1,0:T(8,128)} custom-call(bf16[128,256]{1,0:T(8,128)(2,1)S(1)} %moments.4.gram_own_ref, bf16[128,256]{1,0:T(8,128)(2,1)S(1)} %collective-permute-done.14.gram_oth_ref, bf16[128,512]{1,0:T(8,128)(2,1)S(1)} %collective-permute-done.12.refs_1_.refs_0_, bf16[128,512]{1,0:T(8,128)(2,1)S(1)} %collective-permute-done.13.refs_2_.refs_1_, ...), custom_call_target="tpu_custom_call" | custom-call | tf_op jit(solution)/shard_map/moments/pallas_call | solution.py:73
  (1 shorter events, 0.0 us)
Async XLA Ops:
  0.0 2.8 %collective-permute-start = (bf16[128,2048]{1,0:T(8,128)(2,1)}, bf16[128,2048]{1,0:T(8,128)(2,1)S(1)}, u32[]{:S(2)}, u32[]{:S(2)}) collective-permute-start(bf16[128,2048]{1,0:T(8,128)(2,1)} %bitcast.5), channel_id=1, source_target_pairs={{0,1},{1,0},{2,3},{3,2},{4,5},{5,4},{6,7},{7,6},{8,9},{9,8},{10,11... | collective-permute-start | bytes 1572872 | tf_op jit(solution)/shard_map/layer_one/ppermute | solution.py:31
  2.7 1.5 %copy-start.1 = (bf16[1,128,4096]{2,1,0:T(8,128)(2,1)S(1)}, bf16[1,128,4096]{2,1,0:T(8,128)(2,1)}, u32[]{:S(2)}) copy-start(bf16[1,128,4096]{2,1,0:T(8,128)(2,1)} %w_own_ref.1) | copy-start | bytes 3145732
  2.7 2.0 %collective-permute-start.2 = (bf16[128,2048]{1,0:T(8,128)(2,1)S(1)}, bf16[128,2048]{1,0:T(8,128)(2,1)S(1)}, u32[]{:S(2)}, u32[]{:S(2)}) collective-permute-start(bf16[128,2048]{1,0:T(8,128)(2,1)S(1)} %get-tuple-element.38), channel_id=1, source_target_pairs={{0,1},{1,0},{2,3},{3,2},{4,5},{5,4},{6,7},{7,6},{8,9},{9,8},{10,11... | collective-permute-start | bytes 1572872 | tf_op jit(solution)/shard_map/layer_one/ppermute | solution.py:31
  3.6 6.6 %copy-start = (bf16[2048,1024]{1,0:T(8,128)(2,1)S(1)}, bf16[2048,1024]{1,0:T(8,128)(2,1)}, u32[]{:S(2)}) copy-start(bf16[2048,1024]{1,0:T(8,128)(2,1)} %e_ref.3) | copy-start | bytes 12582916
  3.6 6.5 %copy-start.2 = (s32[4,1]{0,1:T(1,128)S(1)}, s32[4,1]{0,1:T(1,128)}, u32[]{:S(2)}) copy-start(s32[4,1]{0,1:T(1,128)} %param.8) | copy-start | bytes 52
  3.6 1.4 %collective-permute-start.1 = (bf16[128,128]{1,0:T(8,128)(2,1)S(1)}, bf16[128,128]{1,0:T(8,128)(2,1)S(1)}, u32[]{:S(2)}, u32[]{:S(2)}) collective-permute-start(bf16[128,128]{1,0:T(8,128)(2,1)S(1)} %layer_one.7.mixed_ref), channel_id=1, source_target_pairs={{0,1},{1,0},{2,3},{3,2},{4,5},{5,4},{6,7},{7,6},{8,9},{9,8},{10,11... | collective-permute-start | bytes 98312 | tf_op jit(solution)/shard_map/layer_one/ppermute | solution.py:31
  5.2 14.6 %collective-permute-start.8 = (bf16[4096,384]{1,0:T(8,128)(2,1)S(1)}, bf16[4096,384]{1,0:T(8,128)(2,1)S(1)}, u32[]{:S(2)}, u32[]{:S(2)}) collective-permute-start(bf16[4096,384]{1,0:T(8,128)(2,1)S(1)} %get-tuple-element.43.w_ref.refs_1_.w_own_ref), channel_id=1, source_target_pairs={{0,1},{1,0},{2,3},{3,2},{4,5},{5,4},{6,7},{7,6},{8,9},{9,8},{10,11... | collective-permute-start | bytes 9437192 | tf_op jit(solution)/shard_map/weights/ppermute | solution.py:31
  5.6 9.8 %collective-permute-start.6 = (bf16[128,640]{1,0:T(8,128)(2,1)S(1)}, bf16[128,640]{1,0:T(8,128)(2,1)S(1)}, u32[]{:S(2)}, u32[]{:S(2)}) collective-permute-start(bf16[128,640]{1,0:T(8,128)(2,1)S(1)} %layer_one.9), channel_id=1, source_target_pairs={{0,8},{8,16},{16,24},{24,0},{1,9},{9,17},{17,25},{25,1},{2,10},{10... | collective-permute-start | bytes 491528 | tf_op jit(solution)/shard_map/hop/ppermute | solution.py:26
  8.5 10.4 %collective-permute-start.5 = (bf16[128,640]{1,0:T(8,128)(2,1)S(1)}, bf16[128,640]{1,0:T(8,128)(2,1)S(1)}, u32[]{:S(2)}, u32[]{:S(2)}) collective-permute-start(bf16[128,640]{1,0:T(8,128)(2,1)S(1)} %layer_one.11), channel_id=1, source_target_pairs={{0,8},{8,16},{16,24},{24,0},{1,9},{9,17},{17,25},{25,1},{2,10},{10... | collective-permute-start | bytes 491528 | tf_op jit(solution)/shard_map/hop/ppermute | solution.py:26
  12.0 7.7 %collective-permute-start.4 = (bf16[256,512]{1,0:T(8,128)(2,1)S(1)}, bf16[256,512]{1,0:T(8,128)(2,1)S(1)}, u32[]{:S(2)}, u32[]{:S(2)}) collective-permute-start(bf16[256,512]{1,0:T(8,128)(2,1)S(1)} %get-tuple-element.42), channel_id=1, source_target_pairs={{0,1},{1,0},{2,3},{3,2},{4,5},{5,4},{6,7},{7,6},{8,9},{9,8},{10,11... | collective-permute-start | bytes 786440 | tf_op jit(solution)/shard_map/weights/ppermute | solution.py:31
  12.3 10.5 %collective-permute-start.3 = (bf16[128,768]{1,0:T(8,128)(2,1)S(1)}, bf16[128,768]{1,0:T(8,128)(2,1)S(1)}, u32[]{:S(2)}, u32[]{:S(2)}) collective-permute-start(bf16[128,768]{1,0:T(8,128)(2,1)S(1)} %layer_one.10), channel_id=1, source_target_pairs={{0,8},{8,16},{16,24},{24,0},{1,9},{9,17},{17,25},{25,1},{2,10},{10... | collective-permute-start | bytes 589832 | tf_op jit(solution)/shard_map/hop/ppermute | solution.py:26
  15.4 4.7 %collective-permute-start.9 = (bf16[128,640]{1,0:T(8,128)(2,1)S(1)}, bf16[128,640]{1,0:T(8,128)(2,1)S(1)}, u32[]{:S(2)}, u32[]{:S(2)}) collective-permute-start(bf16[128,640]{1,0:T(8,128)(2,1)S(1)} %collective-permute-done.6.x_ref.refs_0_), channel_id=1, source_target_pairs={{0,1},{1,0},{2,3},{3,2},{4,5},{5,4},{6,7},{7,6},{8,9},{9,8},{10,11... | collective-permute-start | bytes 491528 | tf_op jit(solution)/shard_map/layer_two/ppermute | solution.py:31
  18.9 1.9 %collective-permute-start.7 = (bf16[128,640]{1,0:T(8,128)(2,1)S(1)}, bf16[128,640]{1,0:T(8,128)(2,1)S(1)}, u32[]{:S(2)}, u32[]{:S(2)}) collective-permute-start(bf16[128,640]{1,0:T(8,128)(2,1)S(1)} %collective-permute-done.5.x_ref.refs_0_), channel_id=1, source_target_pairs={{0,1},{1,0},{2,3},{3,2},{4,5},{5,4},{6,7},{7,6},{8,9},{9,8},{10,11... | collective-permute-start | bytes 491528 | tf_op jit(solution)/shard_map/layer_two/ppermute | solution.py:31
  22.8 1.4 %collective-permute-start.11 = (bf16[128,768]{1,0:T(8,128)(2,1)S(1)}, bf16[128,768]{1,0:T(8,128)(2,1)S(1)}, u32[]{:S(2)}, u32[]{:S(2)}) collective-permute-start(bf16[128,768]{1,0:T(8,128)(2,1)S(1)} %collective-permute-done.3.x_ref.refs_0_), channel_id=1, source_target_pairs={{0,1},{1,0},{2,3},{3,2},{4,5},{5,4},{6,7},{7,6},{8,9},{9,8},{10,11... | collective-permute-start | bytes 589832 | tf_op jit(solution)/shard_map/layer_two/ppermute | solution.py:31
  23.2 1.8 %collective-permute-start.10 = (bf16[128,512]{1,0:T(8,128)(2,1)S(1)}, bf16[128,512]{1,0:T(8,128)(2,1)S(1)}, u32[]{:S(2)}, u32[]{:S(2)}) collective-permute-start(bf16[128,512]{1,0:T(8,128)(2,1)S(1)} %get-tuple-element.55), channel_id=1, source_target_pairs={{0,1},{1,0},{2,3},{3,2},{4,5},{5,4},{6,7},{7,6},{8,9},{9,8},{10,11... | collective-permute-start | bytes 393224 | tf_op jit(solution)/shard_map/layer_two/ppermute | solution.py:31
  25.2 7.3 %collective-permute-start.15 = (bf16[128,512]{1,0:T(8,128)(2,1)S(1)}, bf16[128,512]{1,0:T(8,128)(2,1)S(1)}, u32[]{:S(2)}, u32[]{:S(2)}) collective-permute-start(bf16[128,512]{1,0:T(8,128)(2,1)S(1)} %layer_two.19.refs_0_.refs_1_), channel_id=1, source_target_pairs={{0,6},{2,4},{4,2},{6,0},{1,7},{3,5},{5,3},{7,1},{8,14},{10,12},{12... | collective-permute-start | bytes 393224 | tf_op jit(solution)/shard_map/moments/ppermute | solution.py:31
  27.7 6.9 %collective-permute-start.13 = (bf16[128,512]{1,0:T(8,128)(2,1)S(1)}, bf16[128,512]{1,0:T(8,128)(2,1)S(1)}, u32[]{:S(2)}, u32[]{:S(2)}) collective-permute-start(bf16[128,512]{1,0:T(8,128)(2,1)S(1)} %layer_two.19.refs_0_.refs_1_), channel_id=1, source_target_pairs={{0,2},{2,0},{4,6},{6,4},{1,3},{3,1},{5,7},{7,5},{8,10},{10,8},{12,... | collective-permute-start | bytes 393224 | tf_op jit(solution)/shard_map/moments/ppermute | solution.py:31
  28.2 6.3 %collective-permute-start.12 = (bf16[128,512]{1,0:T(8,128)(2,1)S(1)}, bf16[128,512]{1,0:T(8,128)(2,1)S(1)}, u32[]{:S(2)}, u32[]{:S(2)}) collective-permute-start(bf16[128,512]{1,0:T(8,128)(2,1)S(1)} %layer_two.19.refs_0_.refs_1_), channel_id=1, source_target_pairs={{0,4},{2,6},{4,0},{6,2},{1,5},{3,7},{5,1},{7,3},{8,12},{10,14},{12... | collective-permute-start | bytes 393224 | tf_op jit(solution)/shard_map/moments/ppermute | solution.py:31
  32.7 2.2 %collective-permute-start.16 = (f32[128,256]{1,0:T(8,128)S(1)}, f32[128,256]{1,0:T(8,128)S(1)}, u32[]{:S(2)}, u32[]{:S(2)}) collective-permute-start(f32[128,256]{1,0:T(8,128)S(1)} %moments.5.gram_own_ref), channel_id=1, source_target_pairs={{0,1},{1,0},{2,3},{3,2},{4,5},{5,4},{6,7},{7,6},{8,9},{9,8},{10,11... | collective-permute-start | bytes 393224 | tf_op jit(solution)/shard_map/moments/ppermute | solution.py:31
  34.8 1.3 %collective-permute-start.14 = (bf16[128,256]{1,0:T(8,128)(2,1)S(1)}, bf16[128,256]{1,0:T(8,128)(2,1)S(1)}, u32[]{:S(2)}, u32[]{:S(2)}) collective-permute-start(bf16[128,256]{1,0:T(8,128)(2,1)S(1)} %moments.4.gram_own_ref), channel_id=1, source_target_pairs={{0,1},{1,0},{2,3},{3,2},{4,5},{5,4},{6,7},{7,6},{8,9},{9,8},{10,11... | collective-permute-start | bytes 196616 | tf_op jit(solution)/shard_map/moments/ppermute | solution.py:31
